TPU v7x, 32 devices: a whole 2x2x4 slice. The times are simulated.
32 devices in a mesh: groups: 2 (over y), tm: 4 (over x, core), space: 4 (over z).
Axes of the slice: x: 2, y: 2, z: 4, core: 2. Of those that a mesh axis runs over, the one named last changes fastest.
Arguments:
- forcing: float32 [32, 4, 64, 1024], P('groups', 'tm', None, 'space'), parts along dimension 0, may hold values from -6 to 6
- iterate: float32 [32, 4, 64, 1024], P('groups', 'tm', None, 'space'), parts along dimension 0, may hold values from -6 to 6
- kappa_mean: float32 [1024], P('space'), may hold values from 0.2 to 2
- kappa_modes: float32 [16, 1024], P(None, 'space'), may hold values from -0.1125 to 0.1125
- grad_mats: float32 [3, 64, 64], replicated, may hold values from -0.4375 to 0.4375
- face_mats: float32 [3, 64, 64], replicated, may hold values from -0.1875 to 0.1875
- lattice_shift: float32 [32], P('groups'), parts along dimension 0, may hold values from 0 to 1
- gen_vector: int32 [16], replicated, may hold values from 1 to 15, as said below
- sweep_counts: int32 [4], replicated, may hold values from 1 to 3, as said below
- face_nbr: int32 [6, 1024], P(None, 'space'), may hold values from -1 to 383, as said below
- halo_send: int32 [2, 256], P(None, 'space'), may hold values from 0 to 255, as said below
Outputs:
- correction: float32 [32, 4, 64, 1024], P('groups', 'tm', None, 'space'), parts along dimension 0
There are 2 independent parts, one for each index of `groups`. A program takes and returns all parts, laid end to end along the dimension named above; an argument that names none is the same for every part. Nothing has to cross between parts.
Inputs may be any that keep to these rules, and one draw needn't show every extreme that they name: `gen_vector`: odd numbers below 16; the first entry is 1 and the second 16 - 1. `sweep_counts`: frequencies k and 4 - k take equal counts; some frequency takes 3 and some 1. `face_nbr`: faces 0 to 5 are -x, +x, -y, +y, -z, +z; an entry below 256 is an element of the same slab in its local numbering, 256 + i the i-th entry of row 1 of the slab below, 320 + i the i-th entry of row 0 of the slab above, -1 the domain's boundary; across face f of e lies an element whose face f xor 1 leads back to e. `halo_send`: each slab's 64 entries in each row are distinct local numbers below 256, listing every element that faces the slab below (row 0) or above (row 1); local number 0 faces the slab below and 255 the slab above.
All inputs are finite; a program needn't handle non-finite values.
Results may differ from a plain program's by a relative error of at most 0.0003.
Values sent between devices are 32-bit elements; how exact they have to be, the bound alone decides.
No kernel may reach another device: no remote copies, remote signals or barrier semaphores. Data moves between devices by JAX's collectives and lax.ppermute only.
A program may use at most 128 MiB of HBM per device.

v0:
```python
import math

import jax
import jax.numpy as jnp
from jax import lax
from jax.sharding import PartitionSpec as P

MAXS = 3


alpha_circ = 0.05
time_step = 0.1
relax_rho = 2.3
highest = lax.Precision.HIGHEST


def with_halo(cells, sides, width):
    for axis, dim in sides:
        count = lax.axis_size(axis)
        ends = count - 1
        head = lax.slice_in_dim(cells, 0, width, axis=dim)
        tail = lax.slice_in_dim(cells, cells.shape[dim] - width, cells.shape[dim], axis=dim)
        cells = jnp.concatenate(
            [
                lax.ppermute(tail, axis, [(i, (i + 1) % count) for i in range(ends)]),
                cells,
                lax.ppermute(head, axis, [((i + 1) % count, i) for i in range(ends)]),
            ],
            axis=dim,
        )
    return cells


def from_behind(value, axis, steps):
    count = lax.axis_size(axis)
    first, last = (max(0, -steps), min(count, count - steps))
    return lax.ppermute(value, axis, [(source, source + steps) for source in range(first, last)])


def lattice_points(gen_vector, lattice_shift, number, modulus):
    position = jnp.arange(number, dtype=jnp.int32)
    residue = position[:, None] * gen_vector[None, :] % modulus
    shifted = residue.astype(lattice_shift.dtype) / modulus + lattice_shift[None, :]
    fraction = shifted - jnp.floor(shifted)
    return 0.5 - jnp.abs(2.0 * fraction - 1.0)


def conductivity(points, kappa_mean, kappa_modes):
    return kappa_mean[None, :] * (1.0 + jnp.dot(points, kappa_modes, precision=highest))


def volume_block(grad_mats):
    return jnp.eye(grad_mats.shape[1], dtype=grad_mats.dtype) + jnp.einsum(
        "dca,dcb->ab", grad_mats, grad_mats, precision=highest
    )


def face_blocks(face_mats):
    return [
        face_mats[0].T,
        face_mats[0],
        face_mats[1].T,
        face_mats[1],
        face_mats[2].T,
        face_mats[2],
    ]


def face_coefs(conduct, conduct_nbr, inside):
    coupling = jnp.where(inside[None], 0.5 * (conduct[:, None, :] + conduct_nbr), 0.0)
    diag_coef = conduct + jnp.sum(jnp.where(inside[None], coupling, conduct[:, None, :]), axis=1)
    return (coupling, diag_coef)


def stiffness(source, extended, nbr_safe, coupling, diag_coef, volume, blocks):
    summed = diag_coef[None, :, None, None, :] * jnp.einsum(
        "ab,csgbe->csgae", volume, source, precision=highest
    )
    for which_face in range(6):
        across = jnp.take(extended, nbr_safe[which_face], axis=4)
        term = jnp.einsum("ab,csgbe->csgae", blocks[which_face], across, precision=highest)
        summed = summed + coupling[None, :, which_face, None, None, :] * term
    return summed


def shifted_terms(frequency, total_steps, diag_coef):
    magnitude = alpha_circ ** (1.0 / total_steps)
    phase_angle = frequency.astype(diag_coef.dtype) * (2.0 * math.pi / total_steps)
    shift_real = 1.0 - magnitude * jnp.cos(phase_angle)
    shift_imag = magnitude * jnp.sin(phase_angle)
    denom_real = shift_real[None, :, None] + time_step * relax_rho * diag_coef[:, None, :]
    denom_imag = jnp.broadcast_to(shift_imag[None, :, None], denom_real.shape)
    modulus = denom_real * denom_real + denom_imag * denom_imag
    return (shift_real, shift_imag, denom_real / modulus, -denom_imag / modulus)


def times_theta(theta_real, theta_imag, source):
    rate_real = theta_real[:, :, None, :]
    rate_imag = theta_imag[:, :, None, :]
    return jnp.stack(
        [
            rate_real * source[0] - rate_imag * source[1],
            rate_real * source[1] + rate_imag * source[0],
        ]
    )


def operator_image(current, applied, shift_real, shift_imag):
    scale_real = shift_real[None, :, None, None]
    scale_imag = shift_imag[None, :, None, None]
    return (
        jnp.stack(
            [
                scale_real * current[0] - scale_imag * current[1],
                scale_real * current[1] + scale_imag * current[0],
            ]
        )
        + time_step * applied
    )


def dft_tables(length, dtype):
    position = jnp.arange(length, dtype=jnp.int32)
    phase_angle = (position[:, None] * position[None, :] % length).astype(dtype) * (
        2.0 * math.pi / length
    )
    return (jnp.cos(phase_angle), jnp.sin(phase_angle))


def per_device(
    forcing,
    iterate,
    kappa_mean,
    kappa_modes,
    grad_mats,
    face_mats,
    lattice_shift,
    gen_vector,
    sweep_counts,
    face_nbr,
    halo_send,
):
    samples, steps_dev, dof_count, elements = forcing.shape
    halo_len = halo_send.shape[1]
    time_devs = lax.axis_size("tm")
    total_steps = steps_dev * time_devs
    time_rank = lax.axis_index("tm")
    conduct = conductivity(
        lattice_points(gen_vector, lattice_shift, samples, samples), kappa_mean, kappa_modes
    )
    send_ids = jnp.concatenate([halo_send[0], halo_send[1]])
    field_rows = samples * steps_dev * dof_count
    packed = jnp.concatenate(
        [
            jnp.take(iterate, send_ids, axis=3).reshape(field_rows, 2 * halo_len),
            jnp.take(conduct, send_ids, axis=1),
        ],
        axis=0,
    )
    padded = with_halo(packed, (("space", 1),), halo_len)
    rim_cells = jnp.concatenate([padded[:, :halo_len], padded[:, 3 * halo_len :]], axis=1)
    iterate_rims = rim_cells[:field_rows].reshape(samples, steps_dev, dof_count, 2 * halo_len)
    conduct_ext = jnp.concatenate([conduct, rim_cells[field_rows:]], axis=1)
    inside = face_nbr >= 0
    nbr_safe = jnp.maximum(face_nbr, 0)
    coupling, diag_coef = face_coefs(conduct, jnp.take(conduct_ext, nbr_safe, axis=1), inside)
    volume = volume_block(grad_mats)
    blocks = face_blocks(face_mats)
    extended = jnp.concatenate([iterate, iterate_rims], axis=3)
    applied = stiffness(
        iterate[None], extended[None], nbr_safe, coupling, diag_coef, volume, blocks
    )[0]
    last_step = from_behind(iterate, "tm", 1)
    earlier = jnp.concatenate([last_step, iterate[:, : steps_dev - 1]], axis=1)
    residual = forcing - iterate - time_step * applied + earlier
    global_steps = (time_rank * steps_dev + jnp.arange(steps_dev, dtype=jnp.int32)).astype(
        forcing.dtype
    )
    weight = jnp.exp(math.log(alpha_circ) / total_steps * global_steps)
    scaled = residual * weight[None, :, None, None]
    every_frequency = jnp.arange(total_steps, dtype=jnp.int32)
    per_sample = samples // time_devs
    by_sample = lax.all_to_all(scaled, "tm", split_axis=0, concat_axis=1, tiled=True)
    cosine, sine_table = dft_tables(total_steps, forcing.dtype)
    spectrum = jnp.stack(
        [
            jnp.einsum("kn,snde->skde", cosine, by_sample, precision=highest),
            -jnp.einsum("kn,snde->skde", sine_table, by_sample, precision=highest),
        ]
    )
    first_sample = time_rank * per_sample
    coupling_part = lax.dynamic_slice_in_dim(coupling, first_sample, per_sample, 0)
    diag_part = lax.dynamic_slice_in_dim(diag_coef, first_sample, per_sample, 0)
    counts_here = jnp.sum(
        jnp.where(every_frequency[:, None] == every_frequency[None, :], sweep_counts[None, :], 0),
        axis=1,
    )
    shift_real, shift_imag, theta_real, theta_imag = shifted_terms(
        every_frequency, total_steps, diag_part
    )

    def sweep(sweep_turn, current):
        outgoing = jnp.take(current, send_ids, axis=4)
        arrived = with_halo(outgoing, (("space", 4),), halo_len)
        extended_now = jnp.concatenate(
            [current, arrived[..., :halo_len], arrived[..., 3 * halo_len :]], axis=4
        )
        applied_now = stiffness(
            current, extended_now, nbr_safe, coupling_part, diag_part, volume, blocks
        )
        image = operator_image(current, applied_now, shift_real, shift_imag)
        updated = current + times_theta(theta_real, theta_imag, spectrum - image)
        active = (sweep_turn + 1 < counts_here)[None, None, :, None, None]
        return jnp.where(active, updated, current)

    solved = lax.fori_loop(0, MAXS - 1, sweep, times_theta(theta_real, theta_imag, spectrum))
    series = (
        jnp.einsum("kn,skde->snde", cosine, solved[0], precision=highest)
        - jnp.einsum("kn,skde->snde", sine_table, solved[1], precision=highest)
    ) / total_steps
    restored = lax.all_to_all(series, "tm", split_axis=1, concat_axis=0, tiled=True)
    unweight = jnp.exp(-math.log(alpha_circ) / total_steps * global_steps)
    return restored * unweight[None, :, None, None]


def solution(mesh):
    placed = (
        P("groups", "tm", None, "space"),
        P("groups", "tm", None, "space"),
        P("space"),
        P(None, "space"),
        P(),
        P(),
        P("groups"),
        P(),
        P(),
        P(None, "space"),
        P(None, "space"),
    )
    return jax.shard_map(
        per_device,
        mesh=mesh,
        in_specs=placed,
        out_specs=P("groups", "tm", None, "space"),
        check_vma=False,
    )
```

profile of v0, /device:TPU:0, one launch (start us, length us, event | category | flops | bytes accessed | tf_op | source)
XLA Modules:
  0.0 463.2 jit_solution(14099119046675125229)
XLA Ops:
  3.3 2.5 copy.141
  9.4 4.9 %collective-permute-start.2 = (f32[1040,64]{0,1:T(8,128)S(1)}, f32[1040,64]{0,1:T(8,128)S(1)}, u32[]{:S(2)}, u32[]{:S(2)}) collective-permute-start(f32[1040,64]{0,1:T(8,128)S(1)} %copy.145), channel_id=1, source_target_pairs={{0,1},{1,2},{2,3},{4,5},{5,6},{6,7},{8,9},{9,10},{10,11},{12,13},{... | collective-permute-start | bytes 798728 | tf_op jit(solution)/shard_map/ppermute | solution.py:25
  15.9 2.4 collective-permute-start.4
  33.3 3.8 gather_fusion.9
  39.3 2.5 gather_fusion.10
  41.8 2.5 gather_fusion.12
  44.3 2.5 gather_fusion.11
  46.8 2.6 gather_fusion.13
  49.5 2.5 gather_fusion.14
  54.0 4.0 fusion.100
  58.3 4.0 fusion.94
  62.7 4.0 fusion.97
  70.0 4.2 fusion.91
  74.2 2.5 gather_fusion.15
  76.7 4.7 %fusion.88 = f32[1,16,1,256,64]{3,4,1,2,0:T(8,128)S(1)} fusion(f32[16,64,256]{1,0,2:T(8,128)} %fusion.35, f32[16,256]{1,0:T(8,128)S(1)} %get-tuple-element.622, f32[3,64,64]{2,1,0:T(8,128)S(1)} %copy-done.27), kind=kOutput, calls=%fused_computation.144 | convolution fusion | flops 201588736 | bytes 2146304 | tf_op jit(solution)/shard_map/ab,csgbe->csgae/dot_general | solution.py:81
  81.9 3.0 fusion.85
  84.9 4.4 fusion.84
  89.4 3.9 all-to-all-start
  94.4 13.3 %all-to-all-done = f32[16,1,64,256]{3,2,1,0:T(8,128)S(1)} async-done(((f32[16,1,64,256]{3,2,1,0:T(8,128)}), f32[16,1,64,256]{3,2,1,0:T(8,128)S(1)}, u32[]{:S(2)}, u32[]{:S(2)}) %all-to-all-start) | async-done | bytes 1048608 | tf_op jit(solution)/shard_map/all_to_all | solution.py:183
  107.7 2.5 fusion.111
  110.2 2.6 convolution_negate_fusion
  116.8 320.5 %while.16 = (s32[]{:T(128)}, f32[2,4,4,64,256]{4,3,2,1,0:T(8,128)S(1)}, s32[4]{0:T(128)S(1)}, f32[4,256]{1,0:T(4,128)S(1)}, f32[64,64]{1,0:T(8,128)S(1)}, /*inde...) while((s32[]{:T(128)}, ...), condition=%wide.region_3.6_spmd.clone.clone.clone, body=%wide.region_2.5_spmd.clone.clone.clone.sunk | while | flops 2837227264 | bytes 203764112 | solution.py:216
  117.3 3.2 copy.289
  120.5 5.6 %gather_fusion = f32[128,2,4,4,64]{4,3,2,1,0:T(4,128)} fusion(f32[2,4,4,64,256]{3,2,4,1,0:T(4,128)} %copy.289, s32[1024]{0:T(1024)S(1)} %pad_clamp_fusion.22), kind=kCustom, calls=%fused_computation.12.clone.clone.clone.1 | custom fusion | bytes 2097664 | tf_op jit(solution)/shard_map/while/body/eval_jaxpr/jit(_take)/gather | solution.py:203
  130.1 5.3 %collective-permute-start = (f32[2,4,4,64,64]{3,2,1,0,4:T(4,128)}, f32[2,4,4,64,64]{3,2,1,0,4:T(4,128)}, u32[]{:S(2)}, u32[]{:S(2)}) collective-permute-start(f32[2,4,4,64,64]{3,2,1,0,4:T(4,128)} %get-tuple-element.783), channel_id=1, source_target_pairs={{0,1},{1,2},{2,3},{4,5},{5,6},{6,7},{8,9},{9,10},{10,11},{12,13},{... | collective-permute-start | bytes 1572872 | tf_op jit(solution)/shard_map/while/body/eval_jaxpr/ppermute | solution.py:25
  138.5 3.3 fusion.256
  141.8 15.1 %collective-permute-done = f32[2,4,4,64,64]{3,2,1,0,4:T(4,128)} collective-permute-done((f32[2,4,4,64,64]{3,2,1,0,4:T(4,128)}, f32[2,4,4,64,64]{3,2,1,0,4:T(4,128)}, u32[]{:S(2)}, u32[]{:S(2)}) %collective-permute-start) | collective-permute-done | bytes 524320 | tf_op jit(solution)/shard_map/while/body/eval_jaxpr/ppermute | solution.py:25
  156.9 5.1 %collective-permute-done.1 = f32[2,4,4,64,64]{3,2,1,0,4:T(4,128)} collective-permute-done((f32[2,4,4,64,64]{3,2,1,0,4:T(4,128)}, f32[2,4,4,64,64]{3,2,1,0,4:T(4,128)}, u32[]{:S(2)}, u32[]{:S(2)}) %collective-permute-start.1) | collective-permute-done | bytes 524320 | tf_op jit(solution)/shard_map/while/body/eval_jaxpr/ppermute | solution.py:27
  162.0 6.6 %pad_maximum_fusion.7 = f32[2,4,4,64,384]{3,2,4,1,0:T(4,128)} fusion(f32[2,4,4,64,256]{3,2,4,1,0:T(4,128)S(1)} %copy-done.2, f32[2,4,4,64,64]{3,2,1,0,4:T(4,128)} %collective-permute-done, f32[2,4,4,64,64]{3,2,1,0,4:T(4,128)} %collective-permute-done.1), kind=kLoop, calls=%fused_computation.20.clone.1 | loop fusion | flops 1572864 | bytes 6291456 | tf_op jit(solution)/shard_map/while/body/eval_jaxpr/concatenate | solution.py:205
  168.6 8.4 %gather_fusion.2 = f32[256,2,4,4,64]{4,3,2,1,0:T(4,128)} fusion(f32[2,4,4,64,384]{3,2,4,1,0:T(4,128)} %pad_maximum_fusion.7, s32[1024]{0:T(1024)S(1)} %pad_clamp_fusion.24), kind=kCustom, calls=%fused_computation.9.clone.clone.1 | custom fusion | bytes 4195328 | tf_op jit(solution)/shard_map/while/body/eval_jaxpr/jit(_take)/gather | solution.py:80
  177.0 8.3 %gather_fusion.3 = f32[256,2,4,4,64]{4,3,2,1,0:T(4,128)} fusion(f32[2,4,4,64,384]{3,2,4,1,0:T(4,128)} %pad_maximum_fusion.7, s32[1024]{0:T(1024)S(1)} %pad_clamp_fusion.25), kind=kCustom, calls=%fused_computation.8.clone.clone.1 | custom fusion | bytes 4195328 | tf_op jit(solution)/shard_map/while/body/eval_jaxpr/jit(_take)/gather | solution.py:80
  185.3 8.4 %gather_fusion.4 = f32[256,2,4,4,64]{4,3,2,1,0:T(4,128)} fusion(f32[2,4,4,64,384]{3,2,4,1,0:T(4,128)} %pad_maximum_fusion.7, s32[1024]{0:T(1024)S(1)} %pad_clamp_fusion.26), kind=kCustom, calls=%fused_computation.7.clone.clone.1 | custom fusion | bytes 4195328 | tf_op jit(solution)/shard_map/while/body/eval_jaxpr/jit(_take)/gather | solution.py:80
  193.7 8.7 %gather_fusion.5 = f32[256,2,4,4,64]{4,3,2,1,0:T(4,128)} fusion(f32[2,4,4,64,384]{3,2,4,1,0:T(4,128)} %pad_maximum_fusion.7, s32[1024]{0:T(1024)S(1)} %pad_clamp_fusion.27), kind=kCustom, calls=%fused_computation.1.clone.clone.1 | custom fusion | bytes 4195328 | tf_op jit(solution)/shard_map/while/body/eval_jaxpr/jit(_take)/gather | solution.py:80
  202.3 8.4 %gather_fusion.1 = f32[256,2,4,4,64]{4,3,2,1,0:T(4,128)} fusion(f32[2,4,4,64,384]{3,2,4,1,0:T(4,128)} %pad_maximum_fusion.7, s32[1024]{0:T(1024)S(1)} %pad_clamp_fusion.23), kind=kCustom, calls=%fused_computation.10.clone.clone.1 | custom fusion | bytes 4195328 | tf_op jit(solution)/shard_map/while/body/eval_jaxpr/jit(_take)/gather | solution.py:80
  210.8 8.4 %gather_fusion.6 = f32[256,2,4,4,64]{4,3,2,1,0:T(4,128)} fusion(f32[2,4,4,64,384]{3,2,4,1,0:T(4,128)} %pad_maximum_fusion.7, s32[1024]{0:T(1024)S(1)} %pad_clamp_fusion.28), kind=kCustom, calls=%fused_computation.11.clone.clone.1 | custom fusion | bytes 4195328 | tf_op jit(solution)/shard_map/while/body/eval_jaxpr/jit(_take)/gather | solution.py:80
  219.2 3.3 select_bitcast_fusion.17
  222.5 7.1 %fusion.252 = f32[2,4,4,256,64]{3,4,2,1,0:T(8,128)S(1)} fusion(f32[2,4,4,64,256]{3,2,1,0,4:T(4,128)S(1)} %select_bitcast_fusion.17, f32[64,64]{1,0:T(8,128)S(1)} %get-tuple-element.852), kind=kOutput, calls=%fused_computation.25.clone.1 | convolution fusion | flops 402653184 | bytes 4210688 | tf_op jit(solution)/shard_map/while/body/eval_jaxpr/ab,csgbe->csgae/dot_general | solution.py:81
  231.6 7.1 %fusion.253 = f32[2,4,4,256,64]{3,4,2,1,0:T(8,128)S(1)} fusion(f32[2,4,4,64,256]{3,2,1,0,4:T(4,128)S(1)} %select_bitcast_fusion.18, f32[64,64]{1,0:T(8,128)S(1)} %get-tuple-element.851), kind=kOutput, calls=%fused_computation.27.clone.1 | convolution fusion | flops 402653184 | bytes 4210688 | tf_op jit(solution)/shard_map/while/body/eval_jaxpr/ab,csgbe->csgae/dot_general | solution.py:81
  240.4 7.1 %fusion.254 = f32[2,4,4,256,64]{3,4,2,1,0:T(8,128)S(1)} fusion(f32[2,4,4,64,256]{3,2,1,0,4:T(4,128)S(1)} %select_bitcast_fusion.19, f32[64,64]{1,0:T(8,128)S(1)} %get-tuple-element.850), kind=kOutput, calls=%fused_computation.29.clone.1 | convolution fusion | flops 402653184 | bytes 4210688 | tf_op jit(solution)/shard_map/while/body/eval_jaxpr/ab,csgbe->csgae/dot_general | solution.py:81
  249.3 7.1 %fusion.255 = f32[2,4,4,256,64]{3,4,2,1,0:T(8,128)S(1)} fusion(f32[2,4,4,64,256]{3,2,1,0,4:T(4,128)S(1)} %select_bitcast_fusion.20, f32[64,64]{1,0:T(8,128)S(1)} %get-tuple-element.849), kind=kOutput, calls=%fused_computation.31.clone.1 | convolution fusion | flops 402653184 | bytes 4210688 | tf_op jit(solution)/shard_map/while/body/eval_jaxpr/ab,csgbe->csgae/dot_general | solution.py:81
  258.2 7.1 %fusion.251 = f32[2,4,4,256,64]{3,4,2,1,0:T(8,128)S(1)} fusion(f32[2,4,4,64,256]{3,2,1,0,4:T(4,128)S(1)} %select_bitcast_fusion.16, f32[64,64]{1,0:T(8,128)S(1)} %get-tuple-element.853), kind=kOutput, calls=%fused_computation.23.clone.1 | convolution fusion | flops 402653184 | bytes 4210688 | tf_op jit(solution)/shard_map/while/body/eval_jaxpr/ab,csgbe->csgae/dot_general | solution.py:81
  267.9 7.2 %fusion.257 = f32[2,4,4,64,256]{4,3,2,1,0:T(8,128)S(1)} fusion(f32[2,4,4,64,256]{4,3,2,1,0:T(8,128)S(1)} %copy-done.10, f32[1,4,4,64,256]{4,3,2,1,0:T(8,128)S(1)} %copy-done.9, f32[1,4,4,64,256]{4,3,2,1,0:T(8,128)S(1)} %get-tuple-element.782, f32[2,4,4,256,64]{3,4,2,1,0:T(8,128)S(1)} %fusion.251, f32[2,4,4,256,64]{3,4,2,1,0:T(8,128)S(1)} %fusion.252, ...), kind=kOutput, calls=%fused_computation.41.clone.1 | convolution fusion | flops 411566080 | bytes 21016576 | tf_op jit(solution)/shard_map/while/body/eval_jaxpr/ab,csgbe->csgae/dot_general | solution.py:81
  276.6 3.2 copy.289
  279.8 5.6 %gather_fusion = f32[128,2,4,4,64]{4,3,2,1,0:T(4,128)} fusion(f32[2,4,4,64,256]{3,2,4,1,0:T(4,128)} %copy.289, s32[1024]{0:T(1024)S(1)} %pad_clamp_fusion.22), kind=kCustom, calls=%fused_computation.12.clone.clone.clone.1 | custom fusion | bytes 2097664 | tf_op jit(solution)/shard_map/while/body/eval_jaxpr/jit(_take)/gather | solution.py:203
  289.3 3.5 collective-permute-start
  295.9 3.3 fusion.256
  299.2 13.9 %collective-permute-done = f32[2,4,4,64,64]{3,2,1,0,4:T(4,128)} collective-permute-done((f32[2,4,4,64,64]{3,2,1,0,4:T(4,128)}, f32[2,4,4,64,64]{3,2,1,0,4:T(4,128)}, u32[]{:S(2)}, u32[]{:S(2)}) %collective-permute-start) | collective-permute-done | bytes 524320 | tf_op jit(solution)/shard_map/while/body/eval_jaxpr/ppermute | solution.py:25
  313.1 5.1 %collective-permute-done.1 = f32[2,4,4,64,64]{3,2,1,0,4:T(4,128)} collective-permute-done((f32[2,4,4,64,64]{3,2,1,0,4:T(4,128)}, f32[2,4,4,64,64]{3,2,1,0,4:T(4,128)}, u32[]{:S(2)}, u32[]{:S(2)}) %collective-permute-start.1) | collective-permute-done | bytes 524320 | tf_op jit(solution)/shard_map/while/body/eval_jaxpr/ppermute | solution.py:27
  318.2 6.6 %pad_maximum_fusion.7 = f32[2,4,4,64,384]{3,2,4,1,0:T(4,128)} fusion(f32[2,4,4,64,256]{3,2,4,1,0:T(4,128)S(1)} %copy-done.2, f32[2,4,4,64,64]{3,2,1,0,4:T(4,128)} %collective-permute-done, f32[2,4,4,64,64]{3,2,1,0,4:T(4,128)} %collective-permute-done.1), kind=kLoop, calls=%fused_computation.20.clone.1 | loop fusion | flops 1572864 | bytes 6291456 | tf_op jit(solution)/shard_map/while/body/eval_jaxpr/concatenate | solution.py:205
  324.8 8.4 %gather_fusion.2 = f32[256,2,4,4,64]{4,3,2,1,0:T(4,128)} fusion(f32[2,4,4,64,384]{3,2,4,1,0:T(4,128)} %pad_maximum_fusion.7, s32[1024]{0:T(1024)S(1)} %pad_clamp_fusion.24), kind=kCustom, calls=%fused_computation.9.clone.clone.1 | custom fusion | bytes 4195328 | tf_op jit(solution)/shard_map/while/body/eval_jaxpr/jit(_take)/gather | solution.py:80
  333.2 8.3 %gather_fusion.3 = f32[256,2,4,4,64]{4,3,2,1,0:T(4,128)} fusion(f32[2,4,4,64,384]{3,2,4,1,0:T(4,128)} %pad_maximum_fusion.7, s32[1024]{0:T(1024)S(1)} %pad_clamp_fusion.25), kind=kCustom, calls=%fused_computation.8.clone.clone.1 | custom fusion | bytes 4195328 | tf_op jit(solution)/shard_map/while/body/eval_jaxpr/jit(_take)/gather | solution.py:80
  341.5 8.4 %gather_fusion.4 = f32[256,2,4,4,64]{4,3,2,1,0:T(4,128)} fusion(f32[2,4,4,64,384]{3,2,4,1,0:T(4,128)} %pad_maximum_fusion.7, s32[1024]{0:T(1024)S(1)} %pad_clamp_fusion.26), kind=kCustom, calls=%fused_computation.7.clone.clone.1 | custom fusion | bytes 4195328 | tf_op jit(solution)/shard_map/while/body/eval_jaxpr/jit(_take)/gather | solution.py:80
  349.9 8.7 %gather_fusion.5 = f32[256,2,4,4,64]{4,3,2,1,0:T(4,128)} fusion(f32[2,4,4,64,384]{3,2,4,1,0:T(4,128)} %pad_maximum_fusion.7, s32[1024]{0:T(1024)S(1)} %pad_clamp_fusion.27), kind=kCustom, calls=%fused_computation.1.clone.clone.1 | custom fusion | bytes 4195328 | tf_op jit(solution)/shard_map/while/body/eval_jaxpr/jit(_take)/gather | solution.py:80
  358.5 8.4 %gather_fusion.1 = f32[256,2,4,4,64]{4,3,2,1,0:T(4,128)} fusion(f32[2,4,4,64,384]{3,2,4,1,0:T(4,128)} %pad_maximum_fusion.7, s32[1024]{0:T(1024)S(1)} %pad_clamp_fusion.23), kind=kCustom, calls=%fused_computation.10.clone.clone.1 | custom fusion | bytes 4195328 | tf_op jit(solution)/shard_map/while/body/eval_jaxpr/jit(_take)/gather | solution.py:80
  367.0 8.4 %gather_fusion.6 = f32[256,2,4,4,64]{4,3,2,1,0:T(4,128)} fusion(f32[2,4,4,64,384]{3,2,4,1,0:T(4,128)} %pad_maximum_fusion.7, s32[1024]{0:T(1024)S(1)} %pad_clamp_fusion.28), kind=kCustom, calls=%fused_computation.11.clone.clone.1 | custom fusion | bytes 4195328 | tf_op jit(solution)/shard_map/while/body/eval_jaxpr/jit(_take)/gather | solution.py:80
  375.4 3.3 select_bitcast_fusion.17
  378.7 7.1 %fusion.252 = f32[2,4,4,256,64]{3,4,2,1,0:T(8,128)S(1)} fusion(f32[2,4,4,64,256]{3,2,1,0,4:T(4,128)S(1)} %select_bitcast_fusion.17, f32[64,64]{1,0:T(8,128)S(1)} %get-tuple-element.852), kind=kOutput, calls=%fused_computation.25.clone.1 | convolution fusion | flops 402653184 | bytes 4210688 | tf_op jit(solution)/shard_map/while/body/eval_jaxpr/ab,csgbe->csgae/dot_general | solution.py:81
  387.8 7.1 %fusion.253 = f32[2,4,4,256,64]{3,4,2,1,0:T(8,128)S(1)} fusion(f32[2,4,4,64,256]{3,2,1,0,4:T(4,128)S(1)} %select_bitcast_fusion.18, f32[64,64]{1,0:T(8,128)S(1)} %get-tuple-element.851), kind=kOutput, calls=%fused_computation.27.clone.1 | convolution fusion | flops 402653184 | bytes 4210688 | tf_op jit(solution)/shard_map/while/body/eval_jaxpr/ab,csgbe->csgae/dot_general | solution.py:81
  396.6 7.1 %fusion.254 = f32[2,4,4,256,64]{3,4,2,1,0:T(8,128)S(1)} fusion(f32[2,4,4,64,256]{3,2,1,0,4:T(4,128)S(1)} %select_bitcast_fusion.19, f32[64,64]{1,0:T(8,128)S(1)} %get-tuple-element.850), kind=kOutput, calls=%fused_computation.29.clone.1 | convolution fusion | flops 402653184 | bytes 4210688 | tf_op jit(solution)/shard_map/while/body/eval_jaxpr/ab,csgbe->csgae/dot_general | solution.py:81
  405.5 7.1 %fusion.255 = f32[2,4,4,256,64]{3,4,2,1,0:T(8,128)S(1)} fusion(f32[2,4,4,64,256]{3,2,1,0,4:T(4,128)S(1)} %select_bitcast_fusion.20, f32[64,64]{1,0:T(8,128)S(1)} %get-tuple-element.849), kind=kOutput, calls=%fused_computation.31.clone.1 | convolution fusion | flops 402653184 | bytes 4210688 | tf_op jit(solution)/shard_map/while/body/eval_jaxpr/ab,csgbe->csgae/dot_general | solution.py:81
  414.4 7.1 %fusion.251 = f32[2,4,4,256,64]{3,4,2,1,0:T(8,128)S(1)} fusion(f32[2,4,4,64,256]{3,2,1,0,4:T(4,128)S(1)} %select_bitcast_fusion.16, f32[64,64]{1,0:T(8,128)S(1)} %get-tuple-element.853), kind=kOutput, calls=%fused_computation.23.clone.1 | convolution fusion | flops 402653184 | bytes 4210688 | tf_op jit(solution)/shard_map/while/body/eval_jaxpr/ab,csgbe->csgae/dot_general | solution.py:81
  424.1 7.2 %fusion.257 = f32[2,4,4,64,256]{4,3,2,1,0:T(8,128)S(1)} fusion(f32[2,4,4,64,256]{4,3,2,1,0:T(8,128)S(1)} %copy-done.10, f32[1,4,4,64,256]{4,3,2,1,0:T(8,128)S(1)} %copy-done.9, f32[1,4,4,64,256]{4,3,2,1,0:T(8,128)S(1)} %get-tuple-element.782, f32[2,4,4,256,64]{3,4,2,1,0:T(8,128)S(1)} %fusion.251, f32[2,4,4,256,64]{3,4,2,1,0:T(8,128)S(1)} %fusion.252, ...), kind=kOutput, calls=%fused_computation.41.clone.1 | convolution fusion | flops 411566080 | bytes 21016576 | tf_op jit(solution)/shard_map/while/body/eval_jaxpr/ab,csgbe->csgae/dot_general | solution.py:81
  443.9 3.5 all-to-all-start.1
  447.5 14.4 %all-to-all-done.1 = f32[4,4,64,256]{3,2,0,1:T(8,128)S(1)} async-done(((f32[4,4,64,256]{3,2,0,1:T(8,128)}), f32[4,4,64,256]{3,2,0,1:T(8,128)S(1)}, u32[]{:S(2)}, u32[]{:S(2)}) %all-to-all-start.1) | async-done | bytes 1048608 | tf_op jit(solution)/shard_map/all_to_all | solution.py:221
  (252 shorter events, 79.1 us)
Async XLA Ops:
  0.0 28.6 %copy-start = (f32[3,64,64]{2,1,0:T(8,128)S(1)}, f32[3,64,64]{2,1,0:T(8,128)}, u32[]{:S(2)}) copy-start(f32[3,64,64]{2,1,0:T(8,128)} %param.21) | copy-start | bytes 147460
  1.8 27.8 %copy-start.29 = (f32[16,256]{1,0:T(8,128)}, f32[16,256]{1,0:T(8,128)S(1)}, u32[]{:S(2)}) copy-start(f32[16,256]{1,0:T(8,128)S(1)} %fusion.104) | copy-start | bytes 49156
  5.9 3.3 copy-start.11
  7.9 10.4 %copy-start.31 = (s32[6,256]{1,0:T(8,128)S(1)}, s32[6,256]{1,0:T(8,128)}, u32[]{:S(2)}) copy-start(s32[6,256]{1,0:T(8,128)} %param.26) | copy-start | bytes 18436
  7.9 17.4 %copy-start.26 = (f32[3,64,64]{2,1,0:T(8,128)S(1)}, f32[3,64,64]{2,1,0:T(8,128)}, u32[]{:S(2)}) copy-start(f32[3,64,64]{2,1,0:T(8,128)} %param.22) | copy-start | bytes 147460
  9.4 19.5 %collective-permute-start.2 = (f32[1040,64]{0,1:T(8,128)S(1)}, f32[1040,64]{0,1:T(8,128)S(1)}, u32[]{:S(2)}, u32[]{:S(2)}) collective-permute-start(f32[1040,64]{0,1:T(8,128)S(1)} %copy.145), channel_id=1, source_target_pairs={{0,1},{1,2},{2,3},{4,5},{5,6},{6,7},{8,9},{9,10},{10,11},{12,13},{... | collective-permute-start | bytes 798728 | tf_op jit(solution)/shard_map/ppermute | solution.py:25
  14.6 14.6 %collective-permute-start.3 = (f32[1040,64]{0,1:T(8,128)S(1)}, f32[1040,64]{0,1:T(8,128)S(1)}, u32[]{:S(2)}, u32[]{:S(2)}) collective-permute-start(f32[1040,64]{0,1:T(8,128)S(1)} %copy.146), channel_id=1, source_target_pairs={{1,0},{2,1},{3,2},{5,4},{6,5},{7,6},{9,8},{10,9},{11,10},{13,12},{... | collective-permute-start | bytes 798728 | tf_op jit(solution)/shard_map/ppermute | solution.py:27
  15.9 69.0 %collective-permute-start.4 = (f32[16,1,64,256]{3,2,0,1:T(8,128)}, f32[16,1,64,256]{3,2,0,1:T(8,128)}, u32[]{:S(2)}, u32[]{:S(2)}) collective-permute-start(f32[16,1,64,256]{3,2,0,1:T(8,128)} %bitcast.12), channel_id=1, source_target_pairs={{0,4},{4,8},{8,12},{1,5},{5,9},{9,13},{2,6},{6,10},{10,14},{3,7},{... | collective-permute-start | bytes 3145736 | tf_op jit(solution)/shard_map/ppermute | solution.py:37
  39.3 5.0 %copy-start.28 = (f32[16,6,256]{2,0,1:T(8,128)}, f32[16,6,256]{2,0,1:T(8,128)S(1)}, u32[]{:S(2)}) copy-start(f32[16,6,256]{2,0,1:T(8,128)S(1)} %get-tuple-element.585) | copy-start | bytes 294916
  46.8 5.2 %copy-start.36 = (pred[256]{0:T(512)(128)(4,1)S(1)}, pred[256]{0:T(512)(128)(4,1)}, u32[]{:S(2)}) copy-start(pred[256]{0:T(512)(128)(4,1)} %compare_and_fusion.12) | copy-start | bytes 772
  52.0 2.0 copy-start.27
  54.0 4.0 copy-start.15
  54.0 4.0 copy-start.37
  58.3 4.0 copy-start.14
  58.3 4.0 copy-start.35
  62.7 4.0 copy-start.13
  62.7 4.0 copy-start.33
  66.7 1.6 copy-start.12
  66.7 1.6 copy-start.34
  70.0 6.7 %copy-start.30 = (f32[16,256]{1,0:T(8,128)S(1)}, f32[16,256]{1,0:T(8,128)}, u32[]{:S(2)}) copy-start(f32[16,256]{1,0:T(8,128)} %copy-done.29) | copy-start | bytes 49156
  76.7 4.7 %copy-start.16 = (f32[256,16,64]{2,1,0:T(8,128)S(1)}, f32[256,16,64]{2,1,0:T(8,128)}, u32[]{:S(2)}) copy-start(f32[256,16,64]{2,1,0:T(8,128)} %gather_fusion.15) | copy-start | bytes 3145732
  76.7 4.7 %copy-start.32 = (pred[256]{0:T(512)(128)(4,1)S(1)}, pred[256]{0:T(512)(128)(4,1)}, u32[]{:S(2)}) copy-start(pred[256]{0:T(512)(128)(4,1)} %compare_and_fusion.7) | copy-start | bytes 772
  81.5 3.4 copy-start.20
  81.5 3.4 copy-start.25
  81.8 3.1 copy-start.17
  81.9 3.1 copy-start.18
  81.9 3.1 copy-start.19
  89.4 4.0 copy-start.39
  89.4 18.3 %all-to-all-start = ((f32[16,1,64,256]{3,2,1,0:T(8,128)}), f32[16,1,64,256]{3,2,1,0:T(8,128)S(1)}, u32[]{:S(2)}, u32[]{:S(2)}) async-start(f32[16,1,64,256]{3,2,1,0:T(8,128)} %fusion.84), calls=%async_computation | async-start | bytes 2097152 | tf_op jit(solution)/shard_map/all_to_all | solution.py:183
  116.0 0.8 copy-start.21
  116.0 0.8 copy-start.22
  116.0 0.8 copy-start.23
  116.1 0.8 copy-start.24
  116.1 0.8 copy-start.38
  130.1 26.9 %collective-permute-start = (f32[2,4,4,64,64]{3,2,1,0,4:T(4,128)}, f32[2,4,4,64,64]{3,2,1,0,4:T(4,128)}, u32[]{:S(2)}, u32[]{:S(2)}) collective-permute-start(f32[2,4,4,64,64]{3,2,1,0,4:T(4,128)} %get-tuple-element.783), channel_id=1, source_target_pairs={{0,1},{1,2},{2,3},{4,5},{5,6},{6,7},{8,9},{9,10},{10,11},{12,13},{... | collective-permute-start | bytes 1572872 | tf_op jit(solution)/shard_map/while/body/eval_jaxpr/ppermute | solution.py:25
  135.4 26.6 %collective-permute-start.1 = (f32[2,4,4,64,64]{3,2,1,0,4:T(4,128)}, f32[2,4,4,64,64]{3,2,1,0,4:T(4,128)}, u32[]{:S(2)}, u32[]{:S(2)}) collective-permute-start(f32[2,4,4,64,64]{3,2,1,0,4:T(4,128)} %get-tuple-element.784), channel_id=1, source_target_pairs={{1,0},{2,1},{3,2},{5,4},{6,5},{7,6},{9,8},{10,9},{11,10},{13,12},{... | collective-permute-start | bytes 1572872 | tf_op jit(solution)/shard_map/while/body/eval_jaxpr/ppermute | solution.py:27
  138.4 23.6 %copy-start.2 = (f32[2,4,4,64,256]{3,2,4,1,0:T(4,128)S(1)}, f32[2,4,4,64,256]{3,2,4,1,0:T(4,128)}, u32[]{:S(2)}) copy-start(f32[2,4,4,64,256]{3,2,4,1,0:T(4,128)} %copy.289) | copy-start | bytes 6291460 | tf_op jit(solution)/shard_map/while
  222.5 7.2 %copy-start.7 = (f32[256,2,4,4,64]{4,3,2,1,0:T(4,128)S(1)}, f32[256,2,4,4,64]{4,3,2,1,0:T(4,128)}, u32[]{:S(2)}) copy-start(f32[256,2,4,4,64]{4,3,2,1,0:T(4,128)} %gather_fusion.3) | copy-start | bytes 6291460 | tf_op jit(solution)/shard_map/while
  231.6 7.2 %copy-start.6 = (f32[256,2,4,4,64]{4,3,2,1,0:T(4,128)S(1)}, f32[256,2,4,4,64]{4,3,2,1,0:T(4,128)}, u32[]{:S(2)}) copy-start(f32[256,2,4,4,64]{4,3,2,1,0:T(4,128)} %gather_fusion.4) | copy-start | bytes 6291460 | tf_op jit(solution)/shard_map/while
  240.4 7.2 %copy-start.5 = (f32[256,2,4,4,64]{4,3,2,1,0:T(4,128)S(1)}, f32[256,2,4,4,64]{4,3,2,1,0:T(4,128)}, u32[]{:S(2)}) copy-start(f32[256,2,4,4,64]{4,3,2,1,0:T(4,128)} %gather_fusion.5) | copy-start | bytes 6291460 | tf_op jit(solution)/shard_map/while
  249.3 7.2 %copy-start.4 = (f32[256,2,4,4,64]{4,3,2,1,0:T(4,128)S(1)}, f32[256,2,4,4,64]{4,3,2,1,0:T(4,128)}, u32[]{:S(2)}) copy-start(f32[256,2,4,4,64]{4,3,2,1,0:T(4,128)} %gather_fusion.1) | copy-start | bytes 6291460 | tf_op jit(solution)/shard_map/while
  258.2 7.2 %copy-start.3 = (f32[256,2,4,4,64]{4,3,2,1,0:T(4,128)S(1)}, f32[256,2,4,4,64]{4,3,2,1,0:T(4,128)}, u32[]{:S(2)}) copy-start(f32[256,2,4,4,64]{4,3,2,1,0:T(4,128)} %gather_fusion.6) | copy-start | bytes 6291460 | tf_op jit(solution)/shard_map/while
  265.4 1.6 copy-start.8
  265.4 1.8 copy-start.9
  265.4 2.5 copy-start.10
  289.3 23.8 %collective-permute-start = (f32[2,4,4,64,64]{3,2,1,0,4:T(4,128)}, f32[2,4,4,64,64]{3,2,1,0,4:T(4,128)}, u32[]{:S(2)}, u32[]{:S(2)}) collective-permute-start(f32[2,4,4,64,64]{3,2,1,0,4:T(4,128)} %get-tuple-element.783), channel_id=1, source_target_pairs={{0,1},{1,2},{2,3},{4,5},{5,6},{6,7},{8,9},{9,10},{10,11},{12,13},{... | collective-permute-start | bytes 1572872 | tf_op jit(solution)/shard_map/while/body/eval_jaxpr/ppermute | solution.py:25
  292.8 25.4 %collective-permute-start.1 = (f32[2,4,4,64,64]{3,2,1,0,4:T(4,128)}, f32[2,4,4,64,64]{3,2,1,0,4:T(4,128)}, u32[]{:S(2)}, u32[]{:S(2)}) collective-permute-start(f32[2,4,4,64,64]{3,2,1,0,4:T(4,128)} %get-tuple-element.784), channel_id=1, source_target_pairs={{1,0},{2,1},{3,2},{5,4},{6,5},{7,6},{9,8},{10,9},{11,10},{13,12},{... | collective-permute-start | bytes 1572872 | tf_op jit(solution)/shard_map/while/body/eval_jaxpr/ppermute | solution.py:27
  295.8 22.4 %copy-start.2 = (f32[2,4,4,64,256]{3,2,4,1,0:T(4,128)S(1)}, f32[2,4,4,64,256]{3,2,4,1,0:T(4,128)}, u32[]{:S(2)}) copy-start(f32[2,4,4,64,256]{3,2,4,1,0:T(4,128)} %copy.289) | copy-start | bytes 6291460 | tf_op jit(solution)/shard_map/while
  378.7 7.2 %copy-start.7 = (f32[256,2,4,4,64]{4,3,2,1,0:T(4,128)S(1)}, f32[256,2,4,4,64]{4,3,2,1,0:T(4,128)}, u32[]{:S(2)}) copy-start(f32[256,2,4,4,64]{4,3,2,1,0:T(4,128)} %gather_fusion.3) | copy-start | bytes 6291460 | tf_op jit(solution)/shard_map/while
  387.8 7.2 %copy-start.6 = (f32[256,2,4,4,64]{4,3,2,1,0:T(4,128)S(1)}, f32[256,2,4,4,64]{4,3,2,1,0:T(4,128)}, u32[]{:S(2)}) copy-start(f32[256,2,4,4,64]{4,3,2,1,0:T(4,128)} %gather_fusion.4) | copy-start | bytes 6291460 | tf_op jit(solution)/shard_map/while
  396.6 7.2 %copy-start.5 = (f32[256,2,4,4,64]{4,3,2,1,0:T(4,128)S(1)}, f32[256,2,4,4,64]{4,3,2,1,0:T(4,128)}, u32[]{:S(2)}) copy-start(f32[256,2,4,4,64]{4,3,2,1,0:T(4,128)} %gather_fusion.5) | copy-start | bytes 6291460 | tf_op jit(solution)/shard_map/while
  405.5 7.2 %copy-start.4 = (f32[256,2,4,4,64]{4,3,2,1,0:T(4,128)S(1)}, f32[256,2,4,4,64]{4,3,2,1,0:T(4,128)}, u32[]{:S(2)}) copy-start(f32[256,2,4,4,64]{4,3,2,1,0:T(4,128)} %gather_fusion.1) | copy-start | bytes 6291460 | tf_op jit(solution)/shard_map/while
  414.4 7.2 %copy-start.3 = (f32[256,2,4,4,64]{4,3,2,1,0:T(4,128)S(1)}, f32[256,2,4,4,64]{4,3,2,1,0:T(4,128)}, u32[]{:S(2)}) copy-start(f32[256,2,4,4,64]{4,3,2,1,0:T(4,128)} %gather_fusion.6) | copy-start | bytes 6291460 | tf_op jit(solution)/shard_map/while
  421.6 1.6 copy-start.8
  421.6 1.8 copy-start.9
  421.6 2.5 copy-start.10
  442.8 20.2 %copy-start.1 = (f32[3,64,64]{2,1,0:T(8,128)S(1)}, f32[3,64,64]{2,1,0:T(8,128)}, u32[]{:S(2)}) copy-start(f32[3,64,64]{2,1,0:T(8,128)} %param.21) | copy-start | bytes 147460
  443.9 18.0 %all-to-all-start.1 = ((f32[4,4,64,256]{3,2,0,1:T(8,128)}), f32[4,4,64,256]{3,2,0,1:T(8,128)S(1)}, u32[]{:S(2)}, u32[]{:S(2)}) async-start(f32[4,4,64,256]{3,2,0,1:T(8,128)} %copy.181), calls=%async_computation.1 | async-start | bytes 2097152 | tf_op jit(solution)/shard_map/all_to_all | solution.py:221
where the time goes:
time: 469 us; the launch traced here: 463 us
  local copies, waits for them, and re-layouts  163 us (35%)
  matrix products  131 us (28%)
  waiting for transfers between devices  67 us (14%)
  other arithmetic  66.9 us (14%)
  starting transfers between devices  27.5 us (6%)
  loops' own time  6.72 us (1%)
    gather x18, local copies, waits for them, and re-layouts, stiffness(): across = jnp.take(extended, nbr_safe[which_face], axis=4)  116 us
    dot_general x18, matrix products, stiffness(): jnp.einsum('ab,csgbe->csgae', blocks[which_face], across, precision=highest)  110 us
    ppermute x3, waiting for transfers between devices, with_halo(): lax.ppermute(tail, axis, [(i, (i + 1) % count) for i in range(ends)])  29.1 us
    select_n x30, other arithmetic, stiffness(): across = jnp.take(extended, nbr_safe[which_face], axis=4)  23.7 us
    all_to_all x1, waiting for transfers between devices, per_device(): lax.all_to_all(series, 'tm', split_axis=1, concat_axis=0, tiled=True)  14.4 us
    ppermute x3, starting transfers between devices, with_halo(): lax.ppermute(tail, axis, [(i, (i + 1) % count) for i in range(ends)])  13.8 us
    all_to_all x1, waiting for transfers between devices, per_device(): lax.all_to_all(scaled, 'tm', split_axis=0, concat_axis=1, tiled=True)  13.3 us
    concatenate x2, other arithmetic, sweep(): jnp.concatenate([current, arrived[..., :halo_len], arrived[..., 3 * halo_...  13.1 us
  transfers between devices with their start and end apart: 9, of which 6 were waited for; matrix products, arithmetic and copies ran while one was open for 16% of the time, Pallas kernels for 0%

commit v1 on v0

v1 whole, which is shorter than its diff:
```python
import functools
import math

import jax
import jax.numpy as jnp
from jax import lax
from jax.experimental import pallas as pl
from jax.experimental.pallas import tpu as pltpu
from jax.sharding import PartitionSpec as P

MAXS = 3
alpha_circ = 0.05
time_step = 0.1
relax_rho = 2.3
highest = lax.Precision.HIGHEST
f32, bf16, i32 = jnp.float32, jnp.bfloat16, jnp.int32
FACES = 6


def dot(a, b):
    return jnp.dot(a, b, preferred_element_type=f32)


def split(x):
    hi = x.astype(bf16)
    return hi, (x - hi.astype(f32)).astype(bf16)


def exact_select(x, onehot):
    a, b = split(x)
    c = (x - a.astype(f32) - b.astype(f32)).astype(bf16)
    return dot(a, onehot) + (dot(b, onehot) + dot(c, onehot))


def times_block(stacked, x):
    rows = stacked.shape[0] // 2
    hi, lo = split(x)
    both = dot(stacked, hi)
    return both[:rows] + (both[rows:] + dot(stacked[:rows], lo))


def rows_iota(shape):
    return lax.broadcasted_iota(i32, shape, 0)


def halo_onehot(nbr_row, base, halo):
    elems = nbr_row.shape[1]
    entry = nbr_row - base
    here = (entry >= 0) & (entry < halo)
    entry = jnp.where(here, entry, -2 * halo)
    row = rows_iota((2 * halo, elems))
    left = (row == entry).astype(f32).astype(bf16)
    right = (row == entry + halo).astype(f32).astype(bf16)
    return jnp.concatenate([left, right], axis=1)


def space_even():
    return lax.rem(lax.axis_index("space"), 2) == 0


def sides(even, elems, halo):
    below, above = elems, elems + halo
    return (
        (jnp.where(even, 5, 4), jnp.where(even, above, below)),
        (jnp.where(even, 4, 5), jnp.where(even, below, above)),
    )


def pack_fields(ref, send, outs):
    half = ref.shape[0] // 2
    dofs, elems = ref.shape[1], ref.shape[2]
    group = 4
    width = send.shape[1] // 2
    for j in range(0, half, group):
        left = ref[j : j + group].reshape(group * dofs, elems)
        right = ref[half + j : half + j + group].reshape(group * dofs, elems)
        hi, lo = split(jnp.concatenate([left, right], axis=1))
        got = dot(hi, send) + dot(lo, send)
        for which, out in enumerate(outs):
            out[j * dofs : (j + group) * dofs, :] = got[:, which * width : (which + 1) * width]


def prepare_kernel(
    iterate, halo_send, shift, gen, mean, modes, pack0, pack1, send_out, conduct_out
):
    samples, dofs, elems = iterate.shape
    halo = halo_send.shape[1]
    even = space_even()
    down = jnp.concatenate([halo_send[0:1, :]] * 2, axis=1)
    up = jnp.concatenate([halo_send[1:2, :]] * 2, axis=1)
    lane = lax.broadcasted_iota(i32, (1, 2 * halo), 1)
    row = rows_iota((2 * elems, 2 * halo))
    for which in range(2):
        ids = jnp.where(even == (which == 0), up, down)
        ids = jnp.where(lane < halo, ids, ids + elems)
        send_out[:, which * 2 * halo : (which + 1) * 2 * halo] = (
            (row == ids).astype(f32).astype(bf16)
        )
    position = rows_iota((samples, gen.shape[1]))
    residue = lax.rem(position * gen[...], samples)
    shifted = residue.astype(f32) / samples + shift[...]
    fraction = shifted - jnp.floor(shifted)
    points = 0.5 - jnp.abs(2.0 * fraction - 1.0)
    conduct = mean[...] * (
        1.0 + jnp.dot(points, modes[...], precision=highest, preferred_element_type=f32)
    )
    conduct_out[...] = conduct
    send = send_out[...]
    pack_fields(iterate, send, (pack0, pack1))
    half = samples // 2
    got = exact_select(jnp.concatenate([conduct[:half], conduct[half:]], axis=1), send)
    pack0[half * dofs :, :] = got[:, : 2 * halo]
    pack1[half * dofs :, :] = got[:, 2 * halo :]


def local_part(fields, coef_row, picks, blocks, out, high, low, group):
    dofs, elems = fields.shape[1], fields.shape[2]
    for first in range(0, fields.shape[0], group):
        slots = range(group)
        value = fields[first : first + group]
        hi, lo = split(value.reshape(group * dofs, elems))
        for j in slots:
            a, b = split(value[j] * coef_row(FACES, first + j))
            high[first + j, 0:dofs, :] = a
            low[first + j, 0:dofs, :] = b
        for f in range(FACES):
            pick = picks[:, f * elems : (f + 1) * elems]
            got = (dot(hi, pick) + dot(lo, pick)).reshape(group, dofs, elems)
            at = (f + 1) * dofs
            for j in slots:
                a, b = split(got[j] * coef_row(f, first + j))
                high[first + j, at : at + dofs, :] = a
                low[first + j, at : at + dofs, :] = b
        stacked = blocks[...]
        for j in slots:
            both = dot(stacked, high[first + j])
            out[first + j] = both[:dofs] + (
                both[dofs:] + dot(stacked[:dofs], low[first + j])
            )


def first_local_kernel(
    iterate,
    conduct_ref,
    face_nbr,
    grads,
    face_mats,
    out,
    coefs,
    picks,
    blocks,
    face_blocks,
    halo_picks,
    general,
    high,
    low,
    wide,
):
    samples, dofs, elems = iterate.shape
    halo = halo_picks.shape[1] // 2
    even = space_even()
    row = rows_iota((elems, elems))
    for f in range(FACES):
        picks[:, f * elems : (f + 1) * elems] = (
            (row == face_nbr[f : f + 1, :]).astype(f32).astype(bf16)
        )
    conduct = conduct_ref[...]
    diag = conduct
    for f in range(FACES):
        nbr = face_nbr[f : f + 1, :]
        across = exact_select(conduct, picks[:, f * elems : (f + 1) * elems])
        inside = (nbr >= 0) & (nbr < elems)
        coupling = jnp.where(inside, 0.5 * (conduct + across), 0.0)
        coefs[f] = coupling
        diag = diag + jnp.where(nbr < 0, conduct, coupling)
    coefs[FACES] = diag
    coefs[FACES + 1] = conduct
    volume = (rows_iota((dofs, dofs)) == lax.broadcasted_iota(i32, (dofs, dofs), 1)).astype(f32)
    for d in range(grads.shape[0]):
        volume = volume + lax.dot_general(
            grads[d], grads[d], (((0,), (0,)), ((), ())), precision=highest,
            preferred_element_type=f32,
        )
    wide[...] = jnp.zeros(wide.shape, f32)
    wide[0:dofs, 0:dofs] = volume
    for f in range(FACES):
        block = face_mats[f // 2]
        at = (f + 1) * dofs
        wide[at : at + dofs, 0:dofs] = block if f % 2 == 0 else block.T
    turned = wide[...].T[:dofs, :]
    hi, lo = split(turned)
    blocks[0:dofs, :] = hi
    blocks[dofs:, :] = lo
    for f in range(FACES):
        block = face_mats[f // 2]
        hi, lo = split(block.T if f % 2 == 0 else block)
        face_blocks[f, 0:dofs, :] = hi
        face_blocks[f, dofs:, :] = lo
    for which, (face, base) in enumerate(sides(even, elems, halo)):
        nbr = jnp.where(face == 4, face_nbr[4:5, :], face_nbr[5:6, :])
        halo_picks[which] = halo_onehot(nbr, base, halo)
    crossing = jnp.max(jnp.where(face_nbr[0:4, :] >= elems, 1, 0))
    crossing = crossing + jnp.max(jnp.where(face_nbr[4:5, :] >= elems + halo, 1, 0))
    fifth = face_nbr[5:6, :]
    crossing = crossing + jnp.max(
        jnp.where((fifth >= elems) & (fifth < elems + halo), 1, 0)
    )
    general[0] = crossing
    local_part(
        iterate, lambda f, j: coefs[f, j : j + 1, :], picks, blocks, out, high, low, 4
    )


def halo_blocks(arrived, block, pick, turned):
    dofs = block.shape[1]
    pairs = turned.shape[0] // dofs
    width = turned.shape[1]
    for j in range(0, pairs, 2):
        both = jnp.concatenate(
            [
                arrived[j * dofs : (j + 1) * dofs, :],
                arrived[(j + 1) * dofs : (j + 2) * dofs, :],
            ],
            axis=1,
        )
        got = times_block(block, both)
        turned[j * dofs : (j + 1) * dofs, :] = got[:, :width]
        turned[(j + 1) * dofs : (j + 2) * dofs, :] = got[:, width:]
    hi, lo = split(turned[...])
    return dot(hi, pick) + dot(lo, pick)


def other_sides(general, even, face_nbr, halo, body):
    elems = face_nbr.shape[1]

    @pl.when(general[0] > 0)
    def _():
        for which, (usual, base) in enumerate(sides(even, elems, halo)):

            def step(face, carry, which=which, usual=usual, base=base):
                @pl.when(face != usual)
                def _():
                    body(which, face, halo_onehot(face_nbr[pl.ds(face, 1), :], base, halo))

                return carry

            lax.fori_loop(0, FACES, step, 0)


def add_halo(arrived, even, general, face_nbr, face_blocks, halo_picks, coef_row, total, turned):
    elems = face_nbr.shape[1]
    halo = halo_picks.shape[1] // 2
    half = total.shape[0] // 2
    dofs = total.shape[1]
    usual = sides(even, elems, halo)
    picked = [
        halo_blocks(arrived[w], face_blocks[usual[w][0]], halo_picks[w], turned)
        for w in range(2)
    ]
    for j in range(2 * half):
        rows = slice((j % half) * dofs, (j % half + 1) * dofs)
        cols = slice((j // half) * elems, (j // half + 1) * elems)
        value = total[j]
        for w in range(2):
            value = value + coef_row(usual[w][0], j) * picked[w][rows, cols]
        total[j] = value

    def body(which, face, pick):
        got = halo_blocks(arrived[which], face_blocks[face], pick, turned)
        for j in range(2 * half):
            rows = slice((j % half) * dofs, (j % half + 1) * dofs)
            cols = slice((j // half) * elems, (j // half + 1) * elems)
            total[j] = total[j] + coef_row(face, j) * got[rows, cols]

    other_sides(general, even, face_nbr, halo, body)


def residual_kernel(
    forcing,
    iterate,
    earlier,
    local,
    arrived0,
    arrived1,
    coefs_in,
    face_nbr,
    blocks,
    face_blocks,
    halo_picks,
    general,
    out,
    coefs,
    total,
    turned,
    extra,
    *,
    total_steps,
):
    samples, dofs, elems = forcing.shape
    halo = halo_picks.shape[1] // 2
    half = samples // 2
    even = space_even()
    arrived = (arrived0, arrived1)
    coefs[...] = coefs_in[...]
    conduct = coefs_in[FACES + 1]
    extra[...] = jnp.zeros(extra.shape, f32)

    def add_coupling(which, face, pick):
        got = exact_select(arrived[which][half * dofs :, :], pick)
        nbr = face_nbr[pl.ds(face, 1), :]
        base = sides(even, elems, halo)[which][1]
        here = (nbr >= base) & (nbr < base + halo)
        across = jnp.concatenate([got[:, :elems], got[:, elems:]], axis=0)
        coupling = jnp.where(here, 0.5 * (conduct + across), 0.0)
        coefs[face] = coefs[face] + coupling
        extra[...] = extra[...] + coupling

    for which, (face, _) in enumerate(sides(even, elems, halo)):
        add_coupling(which, face, halo_picks[which])
    other_sides(general, even, face_nbr, halo, add_coupling)
    coefs[FACES] = coefs[FACES] + extra[...]
    volume = blocks[:, 0 : 2 * dofs][:, :dofs]
    for j in range(samples):
        total[j] = local[j] + times_block(volume, iterate[j] * extra[j : j + 1, :])
    add_halo(
        arrived,
        even,
        general,
        face_nbr,
        face_blocks,
        halo_picks,
        lambda f, j: coefs[f, j : j + 1, :],
        total,
        turned,
    )
    step = lax.axis_index("tm")
    weight = jnp.float32(0.0)
    for n in range(total_steps):
        weight = jnp.where(step == n, jnp.float32(alpha_circ ** (n / total_steps)), weight)
    for j in range(samples):
        out[j] = weight * (
            (forcing[j] - iterate[j]) - time_step * total[j] + earlier[j]
        )


def real_fields(total_steps):
    order = [(0, False)]
    if total_steps % 2 == 0:
        order.append((total_steps // 2, False))
    for k in range(1, (total_steps + 1) // 2):
        order += [(k, False), (k, True)]
    return order


def cos_sin(k, n, total_steps):
    turn = 2.0 * math.pi * ((k * n) % total_steps) / total_steps
    c, s = math.cos(turn), math.sin(turn)
    snap = lambda v: float(round(v)) if abs(v - round(v)) < 1e-12 else v
    return snap(c), snap(s)


def weighted(terms):
    total = None
    for constant, value in terms:
        if constant == 0.0:
            continue
        if total is None:
            total = value if constant == 1.0 else constant * value
        elif constant == 1.0:
            total = total + value
        elif constant == -1.0:
            total = total - value
        else:
            total = total + constant * value
    return total


def shift_of(k, total_steps):
    magnitude = alpha_circ ** (1.0 / total_steps)
    c, s = cos_sin(k, 1, total_steps)
    return 1.0 - magnitude * c, magnitude * s


def theta_rows(k, total_steps, diag):
    shift_real, shift_imag = shift_of(k, total_steps)
    denom = shift_real + (time_step * relax_rho) * diag
    if shift_imag == 0.0:
        return 1.0 / denom, None
    modulus = denom * denom + shift_imag * shift_imag
    return denom / modulus, -shift_imag / modulus


def frequencies(total_steps):
    order = real_fields(total_steps)
    return [
        (k, at, order.index((k, True)) if (k, True) in order else None)
        for at, (k, imag) in enumerate(order)
        if not imag
    ]


def my_first(samples):
    return lax.axis_index("tm") * samples


def spectrum_kernel(pieces, coefs, send_ref, spectrum, first_w, pack0, pack1):
    total_steps, samples, dofs, elems = pieces.shape
    first = my_first(samples)
    for s in range(samples):
        diag = coefs[FACES, pl.ds(first + s, 1), :]
        base = s * total_steps
        for k, re, im in frequencies(total_steps):
            tables = [cos_sin(k, n, total_steps) for n in range(total_steps)]
            real = weighted([(tables[n][0], pieces[n, s]) for n in range(total_steps)])
            rate_real, rate_imag = theta_rows(k, total_steps, diag)
            spectrum[base + re] = real
            if im is None:
                first_w[base + re] = rate_real * real
            else:
                imag = weighted([(-tables[n][1], pieces[n, s]) for n in range(total_steps)])
                spectrum[base + im] = imag
                first_w[base + re] = rate_real * real - rate_imag * imag
                first_w[base + im] = rate_real * imag + rate_imag * real
    pack_fields(first_w, send_ref[...], (pack0, pack1))


def sweep_local_kernel(fields, coefs, picks, blocks, out, high, low, *, total_steps):
    first = my_first(fields.shape[0] // total_steps)
    local_part(
        fields,
        lambda f, j: coefs[f, pl.ds(first + j // total_steps, 1), :],
        picks,
        blocks,
        out,
        high,
        low,
        4,
    )


def updated_fields(current, spectrum, total, coefs, counts, turn, total_steps, store):
    samples = current.shape[0] // total_steps
    first = my_first(samples)
    for s in range(samples):
        diag = coefs[FACES, pl.ds(first + s, 1), :]
        base = s * total_steps
        for k, re, im in frequencies(total_steps):
            active = counts[k] > turn + 1
            shift_real, shift_imag = shift_of(k, total_steps)
            rate_real, rate_imag = theta_rows(k, total_steps, diag)
            value = current[base + re]
            rest = spectrum[base + re] - (shift_real * value + time_step * total[base + re])
            if im is None:
                store(base + re, jnp.where(active, value + rate_real * rest, value))
            else:
                other = current[base + im]
                rest = rest + shift_imag * other
                rest_imag = spectrum[base + im] - (
                    shift_real * other + shift_imag * value + time_step * total[base + im]
                )
                store(
                    base + re,
                    jnp.where(active, value + (rate_real * rest - rate_imag * rest_imag), value),
                )
                store(
                    base + im,
                    jnp.where(active, other + (rate_real * rest_imag + rate_imag * rest), other),
                )


def sweep_update_kernel(
    counts,
    general,
    current,
    spectrum,
    local,
    arrived0,
    arrived1,
    coefs,
    face_nbr,
    face_blocks,
    halo_picks,
    *rest,
    turn,
    total_steps,
    last,
):
    even = space_even()
    if last:
        series, total, turned, solved = rest
    else:
        send_ref, solved, pack0, pack1, total, turned = rest
    fields, dofs, elems = current.shape
    samples = fields // total_steps
    first = my_first(samples)
    total[...] = local[...]
    add_halo(
        (arrived0, arrived1),
        even,
        general,
        face_nbr,
        face_blocks,
        halo_picks,
        lambda f, j: coefs[f, pl.ds(first + j // total_steps, 1), :],
        total,
        turned,
    )

    def store(at, value):
        solved[at] = value

    updated_fields(current, spectrum, total, coefs, counts, turn, total_steps, store)
    if not last:
        pack_fields(solved, send_ref[...], (pack0, pack1))
        return
    for s in range(samples):
        base = s * total_steps
        for n in range(total_steps):
            scale = alpha_circ ** (-n / total_steps) / total_steps
            terms = []
            for k, re, im in frequencies(total_steps):
                c, sn = cos_sin(k, n, total_steps)
                if im is None:
                    terms.append((c, solved[base + re]))
                else:
                    terms += [(2.0 * c, solved[base + re]), (-2.0 * sn, solved[base + im])]
            series[n, s] = scale * weighted(terms)


vmem = pl.BlockSpec(memory_space=pltpu.VMEM)
smem = pl.BlockSpec(memory_space=pltpu.SMEM)


def run(kernel, inputs, outs, scratch=(), in_smem=(), out_smem=(), flops=10**9):
    spec = lambda i, small: smem if i in small else vmem
    return pl.pallas_call(
        kernel,
        out_shape=[jax.ShapeDtypeStruct(*o) for o in outs],
        in_specs=[spec(i, in_smem) for i in range(len(inputs))],
        out_specs=[spec(i, out_smem) for i in range(len(outs))],
        scratch_shapes=[pltpu.VMEM(*s) for s in scratch],
        compiler_params=pltpu.CompilerParams(vmem_limit_bytes=40 << 20),
        cost_estimate=pl.CostEstimate(flops=flops, bytes_accessed=1 << 22, transcendentals=0),
    )(*inputs)


def neighbour_swap(value, start):
    count = lax.axis_size("space")
    pairs = []
    for low in range(start, count - 1, 2):
        pairs += [(low, low + 1), (low + 1, low)]
    return lax.ppermute(value, "space", pairs)


def per_device(
    forcing,
    iterate,
    kappa_mean,
    kappa_modes,
    grad_mats,
    face_mats,
    lattice_shift,
    gen_vector,
    sweep_counts,
    face_nbr,
    halo_send,
):
    samples, steps_dev, dofs, elems = forcing.shape
    halo = halo_send.shape[1]
    devs = lax.axis_size("tm")
    total_steps = steps_dev * devs
    part = samples // devs
    half = samples // 2
    cube = (samples, dofs, elems)
    forcing = forcing.reshape(cube)
    iterate = iterate.reshape(cube)
    earlier = lax.ppermute(iterate, "tm", [(i, i + 1) for i in range(devs - 1)])

    rows = half * dofs
    pack0, pack1, send, conduct = run(
        prepare_kernel,
        (
            iterate,
            halo_send,
            lattice_shift.reshape(1, -1),
            gen_vector.reshape(1, -1),
            kappa_mean.reshape(1, -1),
            kappa_modes,
        ),
        [
            ((rows + half, 2 * halo), f32),
            ((rows + half, 2 * halo), f32),
            ((2 * elems, 4 * halo), bf16),
            ((samples, elems), f32),
        ],
    )
    arrived0 = neighbour_swap(pack0, 0)
    arrived1 = neighbour_swap(pack1, 1)
    blocks_wide = (FACES + 1) * dofs
    splits = [((samples, blocks_wide, elems), bf16)] * 2
    local, coefs, picks, blocks, face_blocks, halo_picks, general = run(
        first_local_kernel,
        (iterate, conduct, face_nbr, grad_mats, face_mats),
        [
            (cube, f32),
            ((FACES + 2, samples, elems), f32),
            ((elems, FACES * elems), bf16),
            ((2 * dofs, blocks_wide), bf16),
            ((FACES, 2 * dofs, dofs), bf16),
            ((2, 2 * halo, 2 * elems), bf16),
            ((1,), i32),
        ],
        splits + [((blocks_wide, 2 * dofs), f32)],
        out_smem=(6,),
    )
    turned = ((rows, 2 * halo), f32)
    scaled, coefs = run(
        functools.partial(residual_kernel, total_steps=total_steps),
        (
            forcing,
            iterate,
            earlier,
            local,
            arrived0,
            arrived1,
            coefs,
            face_nbr,
            blocks,
            face_blocks,
            halo_picks,
            general,
        ),
        [(cube, f32), ((FACES + 2, samples, elems), f32)],
        [(cube, f32), turned, ((samples, elems), f32)],
        in_smem=(11,),
    )
    pieces = lax.all_to_all(scaled, "tm", split_axis=0, concat_axis=0, tiled=True)
    pieces = pieces.reshape(total_steps, part, dofs, elems)
    packs = [((rows, 2 * halo), f32)] * 2
    spectrum, current, pack0, pack1 = run(
        spectrum_kernel,
        (pieces, coefs, send),
        [(cube, f32), (cube, f32)] + packs,
    )
    for turn in range(MAXS - 1):
        arrived0 = neighbour_swap(pack0, 0)
        arrived1 = neighbour_swap(pack1, 1)
        (local,) = run(
            functools.partial(sweep_local_kernel, total_steps=total_steps),
            (current, coefs, picks, blocks),
            [(cube, f32)],
            splits,
        )
        last = turn == MAXS - 2
        inputs = (
            sweep_counts,
            general,
            current,
            spectrum,
            local,
            arrived0,
            arrived1,
            coefs,
            face_nbr,
            face_blocks,
            halo_picks,
        )
        kernel = functools.partial(
            sweep_update_kernel, turn=turn, total_steps=total_steps, last=last
        )
        if last:
            (series,) = run(
                kernel,
                inputs,
                [((total_steps, part, dofs, elems), f32)],
                [(cube, f32), turned, (cube, f32)],
                in_smem=(0, 1),
            )
        else:
            current, pack0, pack1 = run(
                kernel,
                inputs + (send,),
                [(cube, f32)] + packs,
                [(cube, f32), turned],
                in_smem=(0, 1),
            )
    series = series.reshape(cube)
    restored = lax.all_to_all(series, "tm", split_axis=0, concat_axis=0, tiled=True)
    return restored.reshape(samples, steps_dev, dofs, elems)


def solution(mesh):
    placed = (
        P("groups", "tm", None, "space"),
        P("groups", "tm", None, "space"),
        P("space"),
        P(None, "space"),
        P(),
        P(),
        P("groups"),
        P(),
        P(),
        P(None, "space"),
        P(None, "space"),
    )
    return jax.shard_map(
        per_device,
        mesh=mesh,
        in_specs=placed,
        out_specs=P("groups", "tm", None, "space"),
        check_vma=False,
    )
```

time: 469 us -> 80 us (0.17); the launches traced: 463 us -> 79 us
  local copies, waits for them, and re-layouts: 163 us -> 3.62 us
  matrix products: 131 us -> 0 us
  other arithmetic: 66.9 us -> 0 us
  waiting for transfers between devices: 67 us -> 4.66 us
  blocking collectives: 0 us -> 37.4 us
  Pallas kernels: 0 us -> 19.8 us
  starting transfers between devices: 27.5 us -> 13.4 us
  loops' own time: 6.72 us -> 0 us
    gather x25 -> x0, local copies, waits for them, and re-layouts: 135 us -> none  [the longest x18 116 us: stiffness(): across = jnp.take(extended, nbr_safe[which_face], axis=4)]
    dot_general x27 -> x0, matrix products: 131 us -> none  [the longest x18 110 us: stiffness(): jnp.einsum('ab,csgbe->csgae', blocks[which_face], across, precision=highest)]
    all_to_all x0 -> x2, blocking collectives: none -> 37.4 us  [the longest x1 20.5 us: per_device(): lax.all_to_all(scaled, 'tm', split_axis=0, concat_axis=0, tiled=True)]
    ppermute x7, waiting for transfers between devices: 39.3 us -> 4.66 us  [the longest x6 4.66 us: neighbour_swap(): return lax.ppermute(value, 'space', pairs)]
    select_n x39 -> x0, other arithmetic: 30.4 us -> none  [the longest x30 23.7 us: stiffness(): across = jnp.take(extended, nbr_safe[which_face], axis=4)]
    all_to_all x2 -> x0, waiting for transfers between devices: 27.7 us -> none  [the longest x1 14.4 us: per_device(): lax.all_to_all(series, 'tm', split_axis=1, concat_axis=0, tiled=True)]
    pallas_call x0 -> x8, Pallas kernels: none -> 19.8 us  [run(): pl.pallas_call(kernel, out_shape=[jax.ShapeDtypeStruct(*o) for o in outs]...]
    concatenate x5 -> x0, other arithmetic: 13.6 us -> none  [the longest x2 13.1 us: sweep(): jnp.concatenate([current, arrived[..., :halo_len], arrived[..., 3 * halo_...]
  transfers between devices with their start and end apart: 9 -> 7, of which waited for: 6 -> 3; matrix products, arithmetic and copies ran while one was open for 16% -> 0% of each run, Pallas kernels for 0% -> 14%
where the time goes in v1:
time: 80 us; the launch traced here: 79 us
  blocking collectives  37.4 us (47%)
  Pallas kernels  19.8 us (25%)
  starting transfers between devices  13.4 us (17%)
  waiting for transfers between devices  4.66 us (6%)
  local copies, waits for them, and re-layouts  3.62 us (5%)
    all_to_all x1, blocking collectives, per_device(): lax.all_to_all(scaled, 'tm', split_axis=0, concat_axis=0, tiled=True)  20.5 us
    pallas_call x8, Pallas kernels, run(): pl.pallas_call(kernel, out_shape=[jax.ShapeDtypeStruct(*o) for o in outs]...  19.8 us
    all_to_all x1, blocking collectives, per_device(): lax.all_to_all(series, 'tm', split_axis=0, concat_axis=0, tiled=True)  16.9 us
    ppermute x6, starting transfers between devices, neighbour_swap(): return lax.ppermute(value, 'space', pairs)  10.9 us
    ppermute x6, waiting for transfers between devices, neighbour_swap(): return lax.ppermute(value, 'space', pairs)  4.66 us
    unnamed x23, local copies, waits for them, and re-layouts  3.62 us
    ppermute x1, starting transfers between devices, per_device(): earlier = lax.ppermute(iterate, 'tm', [(i, i + 1) for i in range(devs - 1)])  2.41 us
  transfers between devices with their start and end apart: 7, of which 3 were waited for; matrix products, arithmetic and copies ran while one was open for 0% of the time, Pallas kernels for 14%

profile of v1, /device:TPU:0, one launch (start us, length us, event | category | flops | bytes accessed | tf_op | source)
XLA Modules:
  0.0 79.0 jit_solution(3744668137648066927)
XLA Ops:
  0.0 2.4 %collective-permute-start = (f32[16,64,256]{2,1,0:T(8,128)}, f32[16,64,256]{2,1,0:T(8,128)S(1)}, u32[]{:S(2)}, u32[]{:S(2)}) collective-permute-start(f32[16,64,256]{2,1,0:T(8,128)} %bitcast.10), channel_id=1, source_target_pairs={{0,4},{4,8},{8,12},{1,5},{5,9},{9,13},{2,6},{6,10},{10,14},{3,7},{... | collective-permute-start | bytes 3145736 | tf_op jit(solution)/shard_map/ppermute | solution.py:577
  2.4 0.0 copy-start.8
  2.4 0.0 copy-start.10
  2.4 0.0 copy-start.7
  2.4 0.0 copy-start.9
  2.5 0.6 copy-done.8
  3.1 0.0 copy-done.10
  3.1 0.0 copy-done.7
  3.1 0.0 copy-done.9
  3.1 0.0 copy-start
  3.1 1.2 %copy-done = f32[16,1,64,256]{3,2,1,0:T(8,128)S(1)} copy-done((f32[16,1,64,256]{3,2,1,0:T(8,128)S(1)}, f32[16,1,64,256]{3,2,1,0:T(8,128)}, u32[]{:S(2)}) %copy-start) | copy-done | bytes 1048600
  4.4 0.0 copy-start.6
  4.4 0.7 copy-done.6
  5.1 0.0 copy-start.2
  5.1 0.0 copy-start.4
  5.1 0.0 copy-start.5
  5.1 0.6 shard_map.109
  5.7 2.5 %collective-permute-start.1 = (f32[520,128]{1,0:T(8,128)S(1)}, f32[520,128]{1,0:T(8,128)S(1)}, u32[]{:S(2)}, u32[]{:S(2)}) collective-permute-start(f32[520,128]{1,0:T(8,128)S(1)} %get-tuple-element.28), channel_id=1, source_target_pairs={{0,1},{1,0},{2,3},{3,2},{4,5},{5,4},{6,7},{7,6},{8,9},{9,8},{10,11... | collective-permute-start | bytes 798728 | tf_op jit(solution)/shard_map/ppermute | solution.py:552
  8.2 0.7 collective-permute-start.2
  8.9 0.0 copy-done.2
  8.9 0.0 copy-done.4
  8.9 0.0 copy-done.5
  8.9 0.0 copy-start.1
  8.9 4.0 %shard_map.110 = (f32[16,64,256]{2,1,0:T(8,128)S(1)}, f32[8,16,256]{2,1,0:T(8,128)S(1)}, bf16[256,1536]{1,0:T(8,128)(2,1)S(1)}, bf16[128,448]{1,0:T(8,128)(2,1)S...) custom-call(f32[16,64,256]{2,1,0:T(8,128)S(1)} %bitcast.12, ...), custom_call_target="tpu_custom_call" | custom-call | flops 1000000000 | bytes 4194304 | tf_op jit(solution)/shard_map/pallas_call | solution.py:536
  13.0 1.3 %collective-permute-done.1.arrived0 = f32[520,128]{1,0:T(8,128)S(1)} collective-permute-done((f32[520,128]{1,0:T(8,128)S(1)}, f32[520,128]{1,0:T(8,128)S(1)}, u32[]{:S(2)}, u32[]{:S(2)}) %collective-permute-start.1) | collective-permute-done | bytes 266272 | tf_op jit(solution)/shard_map/ppermute | solution.py:552
  14.3 0.0 collective-permute-done.2.arrived1
  14.3 0.0 collective-permute-done.earlier
  14.3 0.0 copy-done.1
  14.3 2.5 %shard_map.111 = (f32[16,64,256]{2,1,0:T(8,128)S(1)}, f32[8,16,256]{2,1,0:T(8,128)S(1)}) custom-call(f32[16,64,256]{2,1,0:T(8,128)S(1)} %bitcast.14, f32[16,64,256]{2,1,0:T(8,128)S(1)} %bitcast.13, f32[16,64,256]{2,1,0:T(8,128)S(1)} %collective-permute-done.earlier, f32[16,64,256]{2,1,0:T(8,128)S(1)} %get-tuple-element.27.local, ...), custom_call_target="tpu_custom_call" | custom-call | flops 1000000000 | bytes 4194304 | tf_op jit(solution)/shard_map/pallas_call | solution.py:536
  16.8 20.5 %all_to_all.10 = f32[16,64,256]{2,1,0:T(8,128)S(1)} all-to-all(f32[16,64,256]{2,1,0:T(8,128)S(1)} %get-tuple-element.34), channel_id=1, replica_groups=mesh['groups'=2,'tm'=4,'space'=4] {'tm'}, dimensions={0} | all-to-all | bytes 2097152 | tf_op jit(solution)/shard_map/all_to_all | solution.py:637
  37.3 0.6 shard_map.112
  37.9 2.0 %collective-permute-start.3 = (f32[512,128]{1,0:T(8,128)S(1)}, f32[512,128]{1,0:T(8,128)S(1)}, u32[]{:S(2)}, u32[]{:S(2)}) collective-permute-start(f32[512,128]{1,0:T(8,128)S(1)} %get-tuple-element.40), channel_id=1, source_target_pairs={{0,1},{1,0},{2,3},{3,2},{4,5},{5,4},{6,7},{7,6},{8,9},{9,8},{10,11... | collective-permute-start | bytes 786440 | tf_op jit(solution)/shard_map/ppermute | solution.py:552
  39.8 0.7 collective-permute-start.4
  40.5 3.1 %shard_map.113.local = f32[16,64,256]{2,1,0:T(8,128)S(1)} custom-call(f32[16,64,256]{2,1,0:T(8,128)S(1)} %get-tuple-element.37.fields.current, f32[8,16,256]{2,1,0:T(8,128)S(1)} %get-tuple-element.35.coefs, bf16[256,1536]{1,0:T(8,128)(2,1)S(1)} %get-tuple-element.39.picks, bf16[128,448]{1,0:T(8,128)(2,1)S(1)} %get-tuple-element.31.blocks), custom_call_target="tpu_custom_call" | custom-call | flops 1000000000 | bytes 4194304 | tf_op jit(solution)/shard_map/pallas_call | solution.py:536
  43.7 0.0 copy-start.3
  43.7 2.1 %collective-permute-done.3.arrived0 = f32[512,128]{1,0:T(8,128)S(1)} collective-permute-done((f32[512,128]{1,0:T(8,128)S(1)}, f32[512,128]{1,0:T(8,128)S(1)}, u32[]{:S(2)}, u32[]{:S(2)}) %collective-permute-start.3) | collective-permute-done | bytes 262176 | tf_op jit(solution)/shard_map/ppermute | solution.py:552
  45.8 0.0 collective-permute-done.4.arrived1
  45.8 0.0 copy-done.3
  45.8 3.1 %shard_map.114 = (f32[16,64,256]{2,1,0:T(8,128)S(1)}, f32[512,128]{1,0:T(8,128)S(1)}, f32[512,128]{1,0:T(8,128)S(1)}) custom-call(s32[4]{0:T(128)S(1)} %copy-done.3, s32[1]{0:T(128)} %get-tuple-element.26.general, f32[16,64,256]{2,1,0:T(8,128)S(1)} %get-tuple-element.37.fields.current, f32[16,64,256]{2,1,0:T(8,128)S(1)} %get-tuple-element.38.spectrum, ...), custom_call_target="tpu_custom_call" | custom-call | flops 1000000000 | bytes 4194304 | tf_op jit(solution)/shard_map/pallas_call | solution.py:536
  48.9 4.5 %collective-permute-start.5 = (f32[512,128]{1,0:T(8,128)S(1)}, f32[512,128]{1,0:T(8,128)S(1)}, u32[]{:S(2)}, u32[]{:S(2)}) collective-permute-start(f32[512,128]{1,0:T(8,128)S(1)} %get-tuple-element.43), channel_id=1, source_target_pairs={{0,1},{1,0},{2,3},{3,2},{4,5},{5,4},{6,7},{7,6},{8,9},{9,8},{10,11... | collective-permute-start | bytes 786440 | tf_op jit(solution)/shard_map/ppermute | solution.py:552
  53.4 0.7 collective-permute-start.6
  54.1 3.1 %shard_map.115.local = f32[16,64,256]{2,1,0:T(8,128)S(1)} custom-call(f32[16,64,256]{2,1,0:T(8,128)S(1)} %get-tuple-element.42.fields.current, f32[8,16,256]{2,1,0:T(8,128)S(1)} %get-tuple-element.35.coefs, bf16[256,1536]{1,0:T(8,128)(2,1)S(1)} %get-tuple-element.39.picks, bf16[128,448]{1,0:T(8,128)(2,1)S(1)} %get-tuple-element.31.blocks), custom_call_target="tpu_custom_call" | custom-call | flops 1000000000 | bytes 4194304 | tf_op jit(solution)/shard_map/pallas_call | solution.py:536
  57.2 1.2 %collective-permute-done.5.arrived0 = f32[512,128]{1,0:T(8,128)S(1)} collective-permute-done((f32[512,128]{1,0:T(8,128)S(1)}, f32[512,128]{1,0:T(8,128)S(1)}, u32[]{:S(2)}, u32[]{:S(2)}) %collective-permute-start.5) | collective-permute-done | bytes 262176 | tf_op jit(solution)/shard_map/ppermute | solution.py:552
  58.4 0.0 collective-permute-done.6.arrived1
  58.4 2.7 %shard_map.116 = f32[4,4,64,256]{3,2,1,0:T(8,128)S(1)} custom-call(s32[4]{0:T(128)S(1)} %copy-done.3, s32[1]{0:T(128)} %get-tuple-element.26.general, f32[16,64,256]{2,1,0:T(8,128)S(1)} %get-tuple-element.42.fields.current, f32[16,64,256]{2,1,0:T(8,128)S(1)} %get-tuple-element.38.spectrum, f32[16,64,256]{2,1,0:T(8,128)S(1)} %shard_map.115.local, ...), custom_call_target="tpu_custom_call" | custom-call | flops 1000000000 | bytes 4194304 | tf_op jit(solution)/shard_map/pallas_call | solution.py:536
  61.1 16.9 %all_to_all.11 = f32[16,64,256]{2,1,0:T(8,128)S(1)} all-to-all(f32[16,64,256]{2,1,0:T(8,128)S(1)} %bitcast.8), channel_id=1, replica_groups=mesh['groups'=2,'tm'=4,'space'=4] {'tm'}, dimensions={0} | all-to-all | bytes 2097152 | tf_op jit(solution)/shard_map/all_to_all | solution.py:688
  78.0 1.0 %copy.13 = f32[16,1,64,256]{3,2,1,0:T(8,128)} copy(f32[16,1,64,256]{3,2,1,0:T(8,128)S(1)} %bitcast.18) | data formatting | bytes 2097152
Async XLA Ops:
  0.0 14.3 %collective-permute-start = (f32[16,64,256]{2,1,0:T(8,128)}, f32[16,64,256]{2,1,0:T(8,128)S(1)}, u32[]{:S(2)}, u32[]{:S(2)}) collective-permute-start(f32[16,64,256]{2,1,0:T(8,128)} %bitcast.10), channel_id=1, source_target_pairs={{0,4},{4,8},{8,12},{1,5},{5,9},{9,13},{2,6},{6,10},{10,14},{3,7},{... | collective-permute-start | bytes 3145736 | tf_op jit(solution)/shard_map/ppermute | solution.py:577
  2.4 0.7 copy-start.8
  2.4 0.7 copy-start.10
  2.4 0.7 copy-start.7
  2.4 0.7 copy-start.9
  3.1 1.2 %copy-start = (f32[16,1,64,256]{3,2,1,0:T(8,128)S(1)}, f32[16,1,64,256]{3,2,1,0:T(8,128)}, u32[]{:S(2)}) copy-start(f32[16,1,64,256]{3,2,1,0:T(8,128)} %param.12) | copy-start | bytes 3145732
  4.4 0.7 copy-start.6
  5.1 3.8 %copy-start.2 = (s32[6,256]{1,0:T(8,128)S(1)}, s32[6,256]{1,0:T(8,128)}, u32[]{:S(2)}) copy-start(s32[6,256]{1,0:T(8,128)} %face_nbr.7) | copy-start | bytes 18436
  5.1 3.8 %copy-start.4 = (f32[3,64,64]{2,1,0:T(8,128)S(1)}, f32[3,64,64]{2,1,0:T(8,128)}, u32[]{:S(2)}) copy-start(f32[3,64,64]{2,1,0:T(8,128)} %grads.1) | copy-start | bytes 147460
  5.1 3.8 %copy-start.5 = (f32[3,64,64]{2,1,0:T(8,128)S(1)}, f32[3,64,64]{2,1,0:T(8,128)}, u32[]{:S(2)}) copy-start(f32[3,64,64]{2,1,0:T(8,128)} %face_mats.1) | copy-start | bytes 147460
  5.7 8.6 %collective-permute-start.1 = (f32[520,128]{1,0:T(8,128)S(1)}, f32[520,128]{1,0:T(8,128)S(1)}, u32[]{:S(2)}, u32[]{:S(2)}) collective-permute-start(f32[520,128]{1,0:T(8,128)S(1)} %get-tuple-element.28), channel_id=1, source_target_pairs={{0,1},{1,0},{2,3},{3,2},{4,5},{5,4},{6,7},{7,6},{8,9},{9,8},{10,11... | collective-permute-start | bytes 798728 | tf_op jit(solution)/shard_map/ppermute | solution.py:552
  8.2 6.1 %collective-permute-start.2 = (f32[520,128]{1,0:T(8,128)S(1)}, f32[520,128]{1,0:T(8,128)S(1)}, u32[]{:S(2)}, u32[]{:S(2)}) collective-permute-start(f32[520,128]{1,0:T(8,128)S(1)} %get-tuple-element.29), channel_id=1, source_target_pairs={{1,2},{2,1},{5,6},{6,5},{9,10},{10,9},{13,14},{14,13},{17,18},{18,... | collective-permute-start | bytes 798728 | tf_op jit(solution)/shard_map/ppermute | solution.py:552
  8.9 5.4 %copy-start.1 = (f32[16,1,64,256]{3,2,1,0:T(8,128)S(1)}, f32[16,1,64,256]{3,2,1,0:T(8,128)}, u32[]{:S(2)}) copy-start(f32[16,1,64,256]{3,2,1,0:T(8,128)} %param.11) | copy-start | bytes 3145732
  37.9 7.9 %collective-permute-start.3 = (f32[512,128]{1,0:T(8,128)S(1)}, f32[512,128]{1,0:T(8,128)S(1)}, u32[]{:S(2)}, u32[]{:S(2)}) collective-permute-start(f32[512,128]{1,0:T(8,128)S(1)} %get-tuple-element.40), channel_id=1, source_target_pairs={{0,1},{1,0},{2,3},{3,2},{4,5},{5,4},{6,7},{7,6},{8,9},{9,8},{10,11... | collective-permute-start | bytes 786440 | tf_op jit(solution)/shard_map/ppermute | solution.py:552
  39.8 5.9 %collective-permute-start.4 = (f32[512,128]{1,0:T(8,128)S(1)}, f32[512,128]{1,0:T(8,128)S(1)}, u32[]{:S(2)}, u32[]{:S(2)}) collective-permute-start(f32[512,128]{1,0:T(8,128)S(1)} %get-tuple-element.41), channel_id=1, source_target_pairs={{1,2},{2,1},{5,6},{6,5},{9,10},{10,9},{13,14},{14,13},{17,18},{18,... | collective-permute-start | bytes 786440 | tf_op jit(solution)/shard_map/ppermute | solution.py:552
  43.7 2.1 %copy-start.3 = (s32[4]{0:T(128)S(1)}, s32[4]{0:T(128)}, u32[]{:S(2)}) copy-start(s32[4]{0:T(128)} %counts.3) | copy-start | bytes 52
  48.9 9.5 %collective-permute-start.5 = (f32[512,128]{1,0:T(8,128)S(1)}, f32[512,128]{1,0:T(8,128)S(1)}, u32[]{:S(2)}, u32[]{:S(2)}) collective-permute-start(f32[512,128]{1,0:T(8,128)S(1)} %get-tuple-element.43), channel_id=1, source_target_pairs={{0,1},{1,0},{2,3},{3,2},{4,5},{5,4},{6,7},{7,6},{8,9},{9,8},{10,11... | collective-permute-start | bytes 786440 | tf_op jit(solution)/shard_map/ppermute | solution.py:552
  53.4 5.0 %collective-permute-start.6 = (f32[512,128]{1,0:T(8,128)S(1)}, f32[512,128]{1,0:T(8,128)S(1)}, u32[]{:S(2)}, u32[]{:S(2)}) collective-permute-start(f32[512,128]{1,0:T(8,128)S(1)} %get-tuple-element.44), channel_id=1, source_target_pairs={{1,2},{2,1},{5,6},{6,5},{9,10},{10,9},{13,14},{14,13},{17,18},{18,... | collective-permute-start | bytes 786440 | tf_op jit(solution)/shard_map/ppermute | solution.py:552

commit v2 on v1

--- a/solution.py
+++ b/solution.py
@@ -15,6 +15,7 @@
 highest = lax.Precision.HIGHEST
 f32, bf16, i32 = jnp.float32, jnp.bfloat16, jnp.int32
 FACES = 6
+GROUPS = 1
 
 
 def dot(a, b):
@@ -55,7 +56,7 @@
 
 
 def space_even():
-    return lax.rem(lax.axis_index("space"), 2) == 0
+    return lax.rem(lax.axis_index("space") + lax.axis_index("tm"), 2) == 0
 
 
 def sides(even, elems, halo):
@@ -66,25 +67,79 @@
     )
 
 
-def pack_fields(ref, send, outs):
-    half = ref.shape[0] // 2
-    dofs, elems = ref.shape[1], ref.shape[2]
-    group = 4
+def group_size(count):
+    return next(size for size in (4, 3, 2, 1) if count % size == 0)
+
+
+def pack_group(ref, left, right, send, first, outs):
+    dofs = ref.shape[1]
     width = send.shape[1] // 2
-    for j in range(0, half, group):
-        left = ref[j : j + group].reshape(group * dofs, elems)
-        right = ref[half + j : half + j + group].reshape(group * dofs, elems)
-        hi, lo = split(jnp.concatenate([left, right], axis=1))
-        got = dot(hi, send) + dot(lo, send)
-        for which, out in enumerate(outs):
-            out[j * dofs : (j + group) * dofs, :] = got[:, which * width : (which + 1) * width]
+    sides_by_side = [jnp.concatenate([ref[i] for i in side], axis=0) for side in (left, right)]
+    hi, lo = split(jnp.concatenate(sides_by_side, axis=1))
+    got = dot(hi, send) + dot(lo, send)
+    rows = slice(first * dofs, (first + len(left)) * dofs)
+    for which, out in enumerate(outs):
+        out[rows, :] = got[:, which * width : (which + 1) * width]
+
+
+def pack_fields(ref, fields, send, outs):
+    half = len(fields) // 2
+    size = group_size(half)
+    for j in range(0, half, size):
+        pack_group(
+            ref, fields[j : j + size], fields[half + j : half + j + size], send, j, outs
+        )
 
 
 def prepare_kernel(
-    iterate, halo_send, shift, gen, mean, modes, pack0, pack1, send_out, conduct_out
+    iterate_in,
+    halo_send_in,
+    shift_in,
+    gen_in,
+    mean_in,
+    modes_in,
+    pack0,
+    pack1,
+    send_out,
+    conduct_out,
+    iterate,
+    halo_send,
+    shift,
+    gen,
+    mean,
+    modes,
+    small_done,
+    field_done,
 ):
     samples, dofs, elems = iterate.shape
     halo = halo_send.shape[1]
+    half = samples // 2
+    size = group_size(half)
+    small = [
+        pltpu.make_async_copy(source, target, small_done.at[i])
+        for i, (source, target) in enumerate(
+            (
+                (halo_send_in, halo_send),
+                (shift_in, shift),
+                (gen_in, gen),
+                (mean_in, mean),
+                (modes_in, modes),
+            )
+        )
+    ]
+    large = []
+    for j in range(0, half, size):
+        for at in (j, half + j):
+            part = pl.ds(at, size)
+            large.append(
+                pltpu.make_async_copy(
+                    iterate_in.at[part], iterate.at[part], field_done.at[len(large)]
+                )
+            )
+    for copy in small + large:
+        copy.start()
+    for copy in small:
+        copy.wait()
     even = space_even()
     down = jnp.concatenate([halo_send[0:1, :]] * 2, axis=1)
     up = jnp.concatenate([halo_send[1:2, :]] * 2, axis=1)
@@ -106,37 +161,39 @@
     )
     conduct_out[...] = conduct
     send = send_out[...]
-    pack_fields(iterate, send, (pack0, pack1))
-    half = samples // 2
     got = exact_select(jnp.concatenate([conduct[:half], conduct[half:]], axis=1), send)
     pack0[half * dofs :, :] = got[:, : 2 * halo]
     pack1[half * dofs :, :] = got[:, 2 * halo :]
-
-
-def local_part(fields, coef_row, picks, blocks, out, high, low, group):
+    for at, j in enumerate(range(0, half, size)):
+        large[2 * at].wait()
+        large[2 * at + 1].wait()
+        left = list(range(j, j + size))
+        pack_group(iterate, left, [half + i for i in left], send, j, (pack0, pack1))
+
+
+def local_part(fields, slots, coef_row, picks, blocks, out, high, low):
     dofs, elems = fields.shape[1], fields.shape[2]
-    for first in range(0, fields.shape[0], group):
-        slots = range(group)
-        value = fields[first : first + group]
-        hi, lo = split(value.reshape(group * dofs, elems))
-        for j in slots:
-            a, b = split(value[j] * coef_row(FACES, first + j))
-            high[first + j, 0:dofs, :] = a
-            low[first + j, 0:dofs, :] = b
+    size = group_size(len(slots))
+    for first in range(0, len(slots), size):
+        group = range(first, first + size)
+        values = [fields[slots[t]] for t in group]
+        hi, lo = split(jnp.concatenate(values, axis=0))
+        for t, value in zip(group, values):
+            a, b = split(value * coef_row(FACES, t))
+            high[t, 0:dofs, :] = a
+            low[t, 0:dofs, :] = b
         for f in range(FACES):
             pick = picks[:, f * elems : (f + 1) * elems]
-            got = (dot(hi, pick) + dot(lo, pick)).reshape(group, dofs, elems)
+            got = dot(hi, pick) + dot(lo, pick)
             at = (f + 1) * dofs
-            for j in slots:
-                a, b = split(got[j] * coef_row(f, first + j))
-                high[first + j, at : at + dofs, :] = a
-                low[first + j, at : at + dofs, :] = b
+            for i, t in enumerate(group):
+                a, b = split(got[i * dofs : (i + 1) * dofs] * coef_row(f, t))
+                high[t, at : at + dofs, :] = a
+                low[t, at : at + dofs, :] = b
         stacked = blocks[...]
-        for j in slots:
-            both = dot(stacked, high[first + j])
-            out[first + j] = both[:dofs] + (
-                both[dofs:] + dot(stacked[:dofs], low[first + j])
-            )
+        for t in group:
+            both = dot(stacked, high[t])
+            out[slots[t]] = both[:dofs] + (both[dofs:] + dot(stacked[:dofs], low[t]))
 
 
 def first_local_kernel(
@@ -145,6 +202,7 @@
     face_nbr,
     grads,
     face_mats,
+    counts_in,
     out,
     coefs,
     picks,
@@ -152,10 +210,13 @@
     face_blocks,
     halo_picks,
     general,
+    counts,
     high,
     low,
     wide,
 ):
+    for k in range(counts.shape[0]):
+        counts[k] = counts_in[0, k]
     samples, dofs, elems = iterate.shape
     halo = halo_picks.shape[1] // 2
     even = space_even()
@@ -207,7 +268,14 @@
     )
     general[0] = crossing
     local_part(
-        iterate, lambda f, j: coefs[f, j : j + 1, :], picks, blocks, out, high, low, 4
+        iterate,
+        list(range(samples)),
+        lambda f, t: coefs[f, t : t + 1, :],
+        picks,
+        blocks,
+        out,
+        high,
+        low,
     )
 
 
@@ -215,17 +283,12 @@
     dofs = block.shape[1]
     pairs = turned.shape[0] // dofs
     width = turned.shape[1]
-    for j in range(0, pairs, 2):
-        both = jnp.concatenate(
-            [
-                arrived[j * dofs : (j + 1) * dofs, :],
-                arrived[(j + 1) * dofs : (j + 2) * dofs, :],
-            ],
-            axis=1,
-        )
-        got = times_block(block, both)
-        turned[j * dofs : (j + 1) * dofs, :] = got[:, :width]
-        turned[(j + 1) * dofs : (j + 2) * dofs, :] = got[:, width:]
+    size = 2 if pairs % 2 == 0 else 1
+    for j in range(0, pairs, size):
+        rows = [slice((j + i) * dofs, (j + i + 1) * dofs) for i in range(size)]
+        got = times_block(block, jnp.concatenate([arrived[r, :] for r in rows], axis=1))
+        for i, r in enumerate(rows):
+            turned[r, :] = got[:, i * width : (i + 1) * width]
     hi, lo = split(turned[...])
     return dot(hi, pick) + dot(lo, pick)
 
@@ -247,30 +310,33 @@
             lax.fori_loop(0, FACES, step, 0)
 
 
-def add_halo(arrived, even, general, face_nbr, face_blocks, halo_picks, coef_row, total, turned):
+def add_halo(
+    arrived, even, general, face_nbr, face_blocks, halo_picks, slots, coef_row, total, turned
+):
     elems = face_nbr.shape[1]
     halo = halo_picks.shape[1] // 2
-    half = total.shape[0] // 2
     dofs = total.shape[1]
+    half = turned.shape[0] // dofs
     usual = sides(even, elems, halo)
     picked = [
         halo_blocks(arrived[w], face_blocks[usual[w][0]], halo_picks[w], turned)
         for w in range(2)
     ]
-    for j in range(2 * half):
-        rows = slice((j % half) * dofs, (j % half + 1) * dofs)
-        cols = slice((j // half) * elems, (j // half + 1) * elems)
-        value = total[j]
+
+    def place(t):
+        row, col = t % half * dofs, t // half * elems
+        return slice(row, row + dofs), slice(col, col + elems)
+
+    for t, field in enumerate(slots):
+        value = total[field]
         for w in range(2):
-            value = value + coef_row(usual[w][0], j) * picked[w][rows, cols]
-        total[j] = value
+            value = value + coef_row(usual[w][0], t) * picked[w][place(t)]
+        total[field] = value
 
     def body(which, face, pick):
         got = halo_blocks(arrived[which], face_blocks[face], pick, turned)
-        for j in range(2 * half):
-            rows = slice((j % half) * dofs, (j % half + 1) * dofs)
-            cols = slice((j // half) * elems, (j // half + 1) * elems)
-            total[j] = total[j] + coef_row(face, j) * got[rows, cols]
+        for t, field in enumerate(slots):
+            total[field] = total[field] + coef_row(face, t) * got[place(t)]
 
     other_sides(general, even, face_nbr, halo, body)
 
@@ -288,14 +354,12 @@
     face_blocks,
     halo_picks,
     general,
-    out,
-    coefs,
-    total,
-    turned,
-    extra,
-    *,
+    *rest,
     total_steps,
+    groups,
 ):
+    outs = rest[: groups * total_steps]
+    coefs, total, turned, extra = rest[groups * total_steps :]
     samples, dofs, elems = forcing.shape
     halo = halo_picks.shape[1] // 2
     half = samples // 2
@@ -329,7 +393,8 @@
         face_nbr,
         face_blocks,
         halo_picks,
-        lambda f, j: coefs[f, j : j + 1, :],
+        list(range(samples)),
+        lambda f, t: coefs[f, t : t + 1, :],
         total,
         turned,
     )
@@ -337,10 +402,21 @@
     weight = jnp.float32(0.0)
     for n in range(total_steps):
         weight = jnp.where(step == n, jnp.float32(alpha_circ ** (n / total_steps)), weight)
-    for j in range(samples):
-        out[j] = weight * (
-            (forcing[j] - iterate[j]) - time_step * total[j] + earlier[j]
-        )
+    gate = jnp.where(step > 0, weight, 0.0)
+    size = samples // (groups * total_steps)
+    for which, out in enumerate(outs):
+        at, turn = divmod(which, total_steps)
+        for i in range(size):
+            j = (partner(step, turn, total_steps) * groups + at) * size + i
+            out[i] = weight * (
+                (forcing[j] - iterate[j]) - time_step * total[j]
+            ) + gate * earlier[j]
+
+
+def partner(rank, turn, count):
+    if count & (count - 1) == 0:
+        return rank ^ turn
+    return lax.rem(turn + count - rank, count)
 
 
 def real_fields(total_steps):
@@ -399,13 +475,41 @@
     ]
 
 
-def my_first(samples):
-    return lax.axis_index("tm") * samples
-
-
-def spectrum_kernel(pieces, coefs, send_ref, spectrum, first_w, pack0, pack1):
-    total_steps, samples, dofs, elems = pieces.shape
-    first = my_first(samples)
+def kept_slots(counts, samples, total_steps):
+    skip = jnp.int32(0)
+    for k, re, _ in frequencies(total_steps):
+        skip = jnp.where(counts[k] == 1, re, skip)
+    kept = total_steps - 1
+    slots = []
+    for t in range(samples * kept):
+        s, i = divmod(t, kept)
+        slots.append(s * total_steps + jnp.where(skip <= i, i + 1, i))
+    return slots
+
+
+def even_slots(slots):
+    return slots + slots[: len(slots) % 2]
+
+
+def my_first(samples, at, groups):
+    return (lax.axis_index("tm") * groups + at) * samples
+
+
+def sample_row(coefs, total_steps, first):
+    kept = total_steps - 1
+    return lambda f, t: coefs[f, pl.ds(first + t // kept, 1), :]
+
+
+def spectrum_kernel(counts, coefs, send_ref, *rest, total_steps, at, groups):
+    arrived, (spectrum, first_w, pack0, pack1, pieces) = (
+        rest[:total_steps],
+        rest[total_steps:],
+    )
+    samples = arrived[0].shape[0]
+    first = my_first(samples, at, groups)
+    rank = lax.axis_index("tm")
+    for turn, piece in enumerate(arrived):
+        pieces[partner(rank, turn, total_steps)] = piece[...]
     for s in range(samples):
         diag = coefs[FACES, pl.ds(first + s, 1), :]
         base = s * total_steps
@@ -421,26 +525,28 @@
                 spectrum[base + im] = imag
                 first_w[base + re] = rate_real * real - rate_imag * imag
                 first_w[base + im] = rate_real * imag + rate_imag * real
-    pack_fields(first_w, send_ref[...], (pack0, pack1))
-
-
-def sweep_local_kernel(fields, coefs, picks, blocks, out, high, low, *, total_steps):
-    first = my_first(fields.shape[0] // total_steps)
+    slots = kept_slots(counts, samples, total_steps)
+    pack_fields(first_w, even_slots(slots), send_ref[...], (pack0, pack1))
+
+
+def sweep_local_kernel(
+    counts, fields, coefs, picks, blocks, out, high, low, *, total_steps, at, groups
+):
+    samples = fields.shape[0] // total_steps
     local_part(
         fields,
-        lambda f, j: coefs[f, pl.ds(first + j // total_steps, 1), :],
+        kept_slots(counts, samples, total_steps),
+        sample_row(coefs, total_steps, my_first(samples, at, groups)),
         picks,
         blocks,
         out,
         high,
         low,
-        4,
-    )
-
-
-def updated_fields(current, spectrum, total, coefs, counts, turn, total_steps, store):
+    )
+
+
+def updated_fields(current, spectrum, total, coefs, counts, turn, total_steps, first, store):
     samples = current.shape[0] // total_steps
-    first = my_first(samples)
     for s in range(samples):
         diag = coefs[FACES, pl.ds(first + s, 1), :]
         base = s * total_steps
@@ -484,15 +590,18 @@
     turn,
     total_steps,
     last,
+    at,
+    groups,
 ):
     even = space_even()
     if last:
-        series, total, turned, solved = rest
+        outs, (total, turned, solved) = rest[:total_steps], rest[total_steps:]
     else:
         send_ref, solved, pack0, pack1, total, turned = rest
-    fields, dofs, elems = current.shape
+    fields = current.shape[0]
     samples = fields // total_steps
-    first = my_first(samples)
+    first = my_first(samples, at, groups)
+    slots = kept_slots(counts, samples, total_steps)
     total[...] = local[...]
     add_halo(
         (arrived0, arrived1),
@@ -501,18 +610,20 @@
         face_nbr,
         face_blocks,
         halo_picks,
-        lambda f, j: coefs[f, pl.ds(first + j // total_steps, 1), :],
+        slots,
+        sample_row(coefs, total_steps, first),
         total,
         turned,
     )
 
-    def store(at, value):
-        solved[at] = value
-
-    updated_fields(current, spectrum, total, coefs, counts, turn, total_steps, store)
+    def store(field, value):
+        solved[field] = value
+
+    updated_fields(current, spectrum, total, coefs, counts, turn, total_steps, first, store)
     if not last:
-        pack_fields(solved, send_ref[...], (pack0, pack1))
+        pack_fields(solved, even_slots(slots), send_ref[...], (pack0, pack1))
         return
+    rank = lax.axis_index("tm")
     for s in range(samples):
         base = s * total_steps
         for n in range(total_steps):
@@ -524,32 +635,79 @@
                     terms.append((c, solved[base + re]))
                 else:
                     terms += [(2.0 * c, solved[base + re]), (-2.0 * sn, solved[base + im])]
-            series[n, s] = scale * weighted(terms)
+            total[n * samples + s] = scale * weighted(terms)
+    for turn_to, out in enumerate(outs):
+        step = partner(rank, turn_to, total_steps)
+        for s in range(samples):
+            out[s] = total[step * samples + s]
+
+
+def assemble_kernel(*rest, total_steps, groups):
+    pieces, (out, done) = rest[:-2], rest[-2:]
+    size = pieces[0].shape[0]
+    rank = lax.axis_index("tm")
+    copies = []
+    for which, piece in enumerate(pieces):
+        at, turn = divmod(which, total_steps)
+        first = (partner(rank, turn, total_steps) * groups + at) * size
+        copies.append(
+            pltpu.make_async_copy(piece, out.at[pl.ds(first, size)], done.at[which])
+        )
+    for copy in copies:
+        copy.start()
+    for copy in copies:
+        copy.wait()
 
 
 vmem = pl.BlockSpec(memory_space=pltpu.VMEM)
 smem = pl.BlockSpec(memory_space=pltpu.SMEM)
 
 
-def run(kernel, inputs, outs, scratch=(), in_smem=(), out_smem=(), flops=10**9):
-    spec = lambda i, small: smem if i in small else vmem
+def run(
+    kernel, inputs, outs, scratch=(), in_smem=(), out_smem=(), in_hbm=(), out_hbm=(), flops=10**9
+):
+    def spec(i, small, outside=()):
+        if i in outside:
+            return pl.BlockSpec(memory_space=pltpu.HBM)
+        return smem if i in small else vmem
+
+    inputs = [
+        pltpu.with_memory_space_constraint(value, pltpu.HBM) if i in in_hbm else value
+        for i, value in enumerate(inputs)
+    ]
     return pl.pallas_call(
         kernel,
         out_shape=[jax.ShapeDtypeStruct(*o) for o in outs],
-        in_specs=[spec(i, in_smem) for i in range(len(inputs))],
-        out_specs=[spec(i, out_smem) for i in range(len(outs))],
-        scratch_shapes=[pltpu.VMEM(*s) for s in scratch],
+        in_specs=[spec(i, in_smem, in_hbm) for i in range(len(inputs))],
+        out_specs=[spec(i, out_smem, out_hbm) for i in range(len(outs))],
+        scratch_shapes=[pltpu.VMEM(*s) if isinstance(s, tuple) else s for s in scratch],
         compiler_params=pltpu.CompilerParams(vmem_limit_bytes=40 << 20),
         cost_estimate=pl.CostEstimate(flops=flops, bytes_accessed=1 << 22, transcendentals=0),
     )(*inputs)
 
 
 def neighbour_swap(value, start):
-    count = lax.axis_size("space")
+    axes = ("groups", "tm", "space")
+    parts, devs, count = (lax.axis_size(axis) for axis in axes)
     pairs = []
-    for low in range(start, count - 1, 2):
-        pairs += [(low, low + 1), (low + 1, low)]
-    return lax.ppermute(value, "space", pairs)
+    for part in range(parts):
+        for tm in range(devs):
+            for space in range(count):
+                step = 1 if (space + tm + start) % 2 == 0 else -1
+                to_part, to_space = part, space + step
+                if not 0 <= to_space < count:
+                    to_part, to_space = part ^ 1, space
+                if to_part < parts:
+                    pairs.append(
+                        ((part * devs + tm) * count + space, (to_part * devs + tm) * count + to_space)
+                    )
+    return lax.ppermute(value, axes, pairs)
+
+
+def time_swap(value, turn):
+    count = lax.axis_size("tm")
+    pairs = [(i, int(partner(i, turn, count))) for i in range(count)]
+    return value if turn == 0 else lax.ppermute(value, "tm", pairs)
 
 
 def per_device(
@@ -574,10 +732,10 @@
     cube = (samples, dofs, elems)
     forcing = forcing.reshape(cube)
     iterate = iterate.reshape(cube)
-    earlier = lax.ppermute(iterate, "tm", [(i, i + 1) for i in range(devs - 1)])
-
+    earlier = lax.ppermute(iterate, "tm", [(i, (i + 1) % devs) for i in range(devs)])
     rows = half * dofs
-    pack0, pack1, send, conduct = run(
+    copies = 2 * (half // group_size(half))
+    pack0, pack1, send, conduct, iterate = run(
         prepare_kernel,
         (
             iterate,
@@ -592,15 +750,26 @@
             ((rows + half, 2 * halo), f32),
             ((2 * elems, 4 * halo), bf16),
             ((samples, elems), f32),
+            (cube, f32),
         ],
+        [
+            (halo_send.shape, i32),
+            ((1, lattice_shift.shape[0]), f32),
+            ((1, gen_vector.shape[0]), i32),
+            ((1, elems), f32),
+            (kappa_modes.shape, f32),
+            pltpu.SemaphoreType.DMA((5,)),
+            pltpu.SemaphoreType.DMA((copies,)),
+        ],
+        in_hbm=range(6),
     )
     arrived0 = neighbour_swap(pack0, 0)
     arrived1 = neighbour_swap(pack1, 1)
     blocks_wide = (FACES + 1) * dofs
-    splits = [((samples, blocks_wide, elems), bf16)] * 2
-    local, coefs, picks, blocks, face_blocks, halo_picks, general = run(
+    splits = lambda count: [((count, blocks_wide, elems), bf16)] * 2
+    local, coefs, picks, blocks, face_blocks, halo_picks, general, counts = run(
         first_local_kernel,
-        (iterate, conduct, face_nbr, grad_mats, face_mats),
+        (iterate, conduct, face_nbr, grad_mats, face_mats, sweep_counts.reshape(1, -1)),
         [
             (cube, f32),
             ((FACES + 2, samples, elems), f32),
@@ -609,13 +778,17 @@
             ((FACES, 2 * dofs, dofs), bf16),
             ((2, 2 * halo, 2 * elems), bf16),
             ((1,), i32),
+            (sweep_counts.shape, i32),
         ],
-        splits + [((blocks_wide, 2 * dofs), f32)],
-        out_smem=(6,),
-    )
-    turned = ((rows, 2 * halo), f32)
-    scaled, coefs = run(
-        functools.partial(residual_kernel, total_steps=total_steps),
+        splits(samples) + [((blocks_wide, 2 * dofs), f32)],
+        out_smem=(6, 7),
+        flops=4 * 10**9,
+    )
+    groups = GROUPS if part % GROUPS == 0 else 1
+    share = part // groups
+    piece = ((share, dofs, elems), f32)
+    *scaled, coefs = run(
+        functools.partial(residual_kernel, total_steps=total_steps, groups=groups),
         (
             forcing,
             iterate,
@@ -630,63 +803,76 @@
             halo_picks,
             general,
         ),
-        [(cube, f32), ((FACES + 2, samples, elems), f32)],
-        [(cube, f32), turned, ((samples, elems), f32)],
+        [piece] * (groups * devs) + [((FACES + 2, samples, elems), f32)],
+        [(cube, f32), ((rows, 2 * halo), f32), ((samples, elems), f32)],
         in_smem=(11,),
     )
-    pieces = lax.all_to_all(scaled, "tm", split_axis=0, concat_axis=0, tiled=True)
-    pieces = pieces.reshape(total_steps, part, dofs, elems)
-    packs = [((rows, 2 * halo), f32)] * 2
-    spectrum, current, pack0, pack1 = run(
-        spectrum_kernel,
-        (pieces, coefs, send),
-        [(cube, f32), (cube, f32)] + packs,
-    )
-    for turn in range(MAXS - 1):
-        arrived0 = neighbour_swap(pack0, 0)
-        arrived1 = neighbour_swap(pack1, 1)
-        (local,) = run(
-            functools.partial(sweep_local_kernel, total_steps=total_steps),
-            (current, coefs, picks, blocks),
-            [(cube, f32)],
-            splits,
+    fields = share * total_steps
+    swept = share * (total_steps - 1)
+    some = (fields, dofs, elems)
+    turned = ((((swept + 1) // 2) * dofs, 2 * halo), f32)
+    restored = []
+    for at in range(groups):
+        mine = dict(total_steps=total_steps, at=at, groups=groups)
+        pieces = [time_swap(scaled[at * devs + turn], turn) for turn in range(devs)]
+        spectrum, current, pack0, pack1 = run(
+            functools.partial(spectrum_kernel, **mine),
+            (counts, coefs, send, *pieces),
+            [(some, f32), (some, f32), turned, turned],
+            [((total_steps, share, dofs, elems), f32)],
+            in_smem=(0,),
         )
-        last = turn == MAXS - 2
-        inputs = (
-            sweep_counts,
-            general,
-            current,
-            spectrum,
-            local,
-            arrived0,
-            arrived1,
-            coefs,
-            face_nbr,
-            face_blocks,
-            halo_picks,
-        )
-        kernel = functools.partial(
-            sweep_update_kernel, turn=turn, total_steps=total_steps, last=last
-        )
-        if last:
-            (series,) = run(
-                kernel,
-                inputs,
-                [((total_steps, part, dofs, elems), f32)],
-                [(cube, f32), turned, (cube, f32)],
-                in_smem=(0, 1),
+        for turn in range(MAXS - 1):
+            arrived0 = neighbour_swap(pack0, 0)
+            arrived1 = neighbour_swap(pack1, 1)
+            (local,) = run(
+                functools.partial(sweep_local_kernel, **mine),
+                (counts, current, coefs, picks, blocks),
+                [(some, f32)],
+                splits(swept),
+                in_smem=(0,),
+                flops=3 * 10**9 // groups,
             )
-        else:
-            current, pack0, pack1 = run(
-                kernel,
-                inputs + (send,),
-                [(cube, f32)] + packs,
-                [(cube, f32), turned],
-                in_smem=(0, 1),
+            last = turn == MAXS - 2
+            inputs = (
+                counts,
+                general,
+                current,
+                spectrum,
+                local,
+                arrived0,
+                arrived1,
+                coefs,
+                face_nbr,
+                face_blocks,
+                halo_picks,
             )
-    series = series.reshape(cube)
-    restored = lax.all_to_all(series, "tm", split_axis=0, concat_axis=0, tiled=True)
-    return restored.reshape(samples, steps_dev, dofs, elems)
+            kernel = functools.partial(sweep_update_kernel, turn=turn, last=last, **mine)
+            if last:
+                series = run(
+                    kernel,
+                    inputs,
+                    [piece] * devs,
+                    [(some, f32), turned, (some, f32)],
+                    in_smem=(0, 1),
+                )
+            else:
+                current, pack0, pack1 = run(
+                    kernel,
+                    inputs + (send,),
+                    [(some, f32), turned, turned],
+                    [(some, f32), turned],
+                    in_smem=(0, 1),
+                )
+        restored += [time_swap(series[turn], turn) for turn in range(devs)]
+    (out,) = run(
+        functools.partial(assemble_kernel, total_steps=total_steps, groups=groups),
+        tuple(restored),
+        [(cube, f32)],
+        [pltpu.SemaphoreType.DMA((len(restored),))],
+        out_hbm=(0,),
+    )
+    return out.reshape(samples, steps_dev, dofs, elems)
 
 
 def solution(mesh):

time: 80 us -> 69.1 us (0.86)
  blocking collectives: 37.4 us -> 0 us
  waiting for transfers between devices: 4.66 us -> 29.3 us
  Pallas kernels: 19.8 us -> 23 us
  local copies, waits for them, and re-layouts: 3.62 us -> 0.66 us
  starting transfers between devices: 13.4 us -> 15.5 us
    all_to_all x2 -> x0, blocking collectives: 37.4 us -> none  [the longest x1 20.5 us: per_device(): lax.all_to_all(scaled, 'tm', split_axis=0, concat_axis=0, tiled=True)]
    ppermute x7 -> x13, waiting for transfers between devices: 4.66 us -> 29.3 us  [the longest x6 23.8 us: time_swap(): return value if turn == 0 else lax.ppermute(value, 'tm', pairs)]
    pallas_call x8 -> x9, Pallas kernels: 19.8 us -> 23 us  [run(): pl.pallas_call(kernel, out_shape=[jax.ShapeDtypeStruct(*o) for o in outs]...]
    unnamed x23 -> x10, local copies, waits for them, and re-layouts: 3.62 us -> 0.66 us
    ppermute x7 -> x13, starting transfers between devices: 13.4 us -> 15.5 us  [the longest x6 10.5 us: neighbour_swap(): return lax.ppermute(value, axes, pairs)]
  transfers between devices with their start and end apart: 7 -> 13, of which waited for: 3 -> 9; matrix products, arithmetic and copies ran while one was open for 0% -> 0% of each run, Pallas kernels for 14% -> 18%
where the time goes in v2:
time: 69.1 us; the launch traced here: 68.8 us
  waiting for transfers between devices  29.3 us (42%)
  Pallas kernels  23 us (33%)
  starting transfers between devices  15.5 us (22%)
    ppermute x6, waiting for transfers between devices, time_swap(): return value if turn == 0 else lax.ppermute(value, 'tm', pairs)  23.8 us
    pallas_call x9, Pallas kernels, run(): pl.pallas_call(kernel, out_shape=[jax.ShapeDtypeStruct(*o) for o in outs]...  23 us
    ppermute x6, starting transfers between devices, neighbour_swap(): return lax.ppermute(value, axes, pairs)  10.5 us
    ppermute x6, starting transfers between devices, time_swap(): return value if turn == 0 else lax.ppermute(value, 'tm', pairs)  4.5 us
    ppermute x6, waiting for transfers between devices, neighbour_swap(): return lax.ppermute(value, axes, pairs)  4.35 us
  transfers between devices with their start and end apart: 13, of which 9 were waited for; matrix products, arithmetic and copies ran while one was open for 0% of the time, Pallas kernels for 18%

profile of v2, /device:TPU:0, one launch (start us, length us, event | category | flops | bytes accessed | tf_op | source)
XLA Modules:
  0.0 68.8 jit_solution(5196999645776935248)
XLA Ops:
  0.0 0.5 collective-permute-start
  0.5 0.0 copy-start.2
  0.5 0.0 copy-start.3
  0.5 2.4 %shard_map.109 = (f32[520,128]{1,0:T(8,128)S(1)}, f32[520,128]{1,0:T(8,128)S(1)}, bf16[512,256]{1,0:T(8,128)(2,1)S(1)}, f32[16,256]{1,0:T(8,128)S(1)}, f32[16,64,256]{2,1,0:T(8,128)S(1)}) custom-call(f32[16,64,256]{2,1,0:T(8,128)} %bitcast.12, s32[2,64]{1,0:T(2,128)} %halo_send_in.1, f32[1,16]{1,0:T(1,128)} %bitcast.14, s32[1,16]{1,0:T(1,128)} %bitcast.15, ...), custom_call_target="tpu_custom_call" | custom-call | flops 1000000000 | bytes 4194304 | tf_op jit(solution)/shard_map/pallas_call | solution.py:678
  2.9 0.0 copy-start.1
  2.9 2.6 %collective-permute-start.1 = (f32[520,128]{1,0:T(8,128)S(1)}, f32[520,128]{1,0:T(8,128)S(1)}, u32[]{:S(2)}, u32[]{:S(2)}) collective-permute-start(f32[520,128]{1,0:T(8,128)S(1)} %get-tuple-element.39), channel_id=1, source_target_pairs={{0,1},{1,0},{2,3},{3,2},{4,20},{5,6},{6,5},{7,23},{8,9},{9,8},{10,... | collective-permute-start | bytes 798728 | tf_op jit(solution)/shard_map/ppermute | solution.py:704
  5.5 1.5 %collective-permute-start.2 = (f32[520,128]{1,0:T(8,128)S(1)}, f32[520,128]{1,0:T(8,128)S(1)}, u32[]{:S(2)}, u32[]{:S(2)}) collective-permute-start(f32[520,128]{1,0:T(8,128)S(1)} %get-tuple-element.40), channel_id=1, source_target_pairs={{0,16},{1,2},{2,1},{3,19},{4,5},{5,4},{6,7},{7,6},{8,24},{9,10},{1... | collective-permute-start | bytes 798728 | tf_op jit(solution)/shard_map/ppermute | solution.py:704
  7.0 0.0 copy-start.4
  7.0 0.0 copy-done.2
  7.0 0.0 copy-done.3
  7.0 0.0 copy-done.1
  7.0 0.6 copy-done.4
  7.7 0.0 copy-start
  7.7 4.2 %shard_map.110 = (f32[16,64,256]{2,1,0:T(8,128)S(1)}, f32[8,16,256]{2,1,0:T(8,128)S(1)}, bf16[256,1536]{1,0:T(8,128)(2,1)S(1)}, bf16[128,448]{1,0:T(8,128)(2,1)S...) custom-call(f32[16,64,256]{2,1,0:T(8,128)S(1)} %get-tuple-element.34.iterate,, ...), custom_call_target="tpu_custom_call" | custom-call | flops 4000000000 | bytes 4194304 | tf_op jit(solution)/shard_map/pallas_call | solution.py:678
  11.9 0.0 collective-permute-done.1.arrived0
  11.9 2.0 %collective-permute-done.2.arrived1 = f32[520,128]{1,0:T(8,128)S(1)} collective-permute-done((f32[520,128]{1,0:T(8,128)S(1)}, f32[520,128]{1,0:T(8,128)S(1)}, u32[]{:S(2)}, u32[]{:S(2)}) %collective-permute-start.2) | collective-permute-done | bytes 266272 | tf_op jit(solution)/shard_map/ppermute | solution.py:704
  13.8 1.2 %collective-permute-done.earlier = f32[16,64,256]{2,1,0:T(8,128)S(1)} collective-permute-done((f32[16,64,256]{2,1,0:T(8,128)}, f32[16,64,256]{2,1,0:T(8,128)S(1)}, u32[]{:S(2)}, u32[]{:S(2)}) %collective-permute-start) | collective-permute-done | bytes 1048608 | tf_op jit(solution)/shard_map/ppermute | solution.py:735
  15.1 0.0 copy-done
  15.1 2.6 %shard_map.111 = (f32[4,64,256]{2,1,0:T(8,128)S(1)}, f32[4,64,256]{2,1,0:T(8,128)S(1)}, f32[4,64,256]{2,1,0:T(8,128)S(1)}, f32[4,64,256]{2,1,0:T(8,128)S(1)}, f32[8,16,256]{2,1,0:T(8,128)S(1)}) custom-call(f32[16,64,256]{2,1,0:T(8,128)S(1)} %bitcast.9, f32[16,64,256]{2,1,0:T(8,128)S(1)} %get-tuple-element.34.iterate, ...), custom_call_target="tpu_custom_call" | custom-call | flops 1000000000 | bytes 4194304 | tf_op jit(solution)/shard_map/pallas_call | solution.py:678
  17.7 0.1 collective-permute-start.3
  17.8 2.3 %collective-permute-start.4 = (f32[4,64,256]{2,1,0:T(8,128)S(1)}, f32[4,64,256]{2,1,0:T(8,128)S(1)}, u32[]{:S(2)}, u32[]{:S(2)}) collective-permute-start(f32[4,64,256]{2,1,0:T(8,128)S(1)} %get-tuple-element.49), channel_id=1, source_target_pairs={{0,8},{4,12},{8,0},{12,4},{1,9},{5,13},{9,1},{13,5},{2,10},{6,14},... | collective-permute-start | bytes 786440 | tf_op jit(solution)/shard_map/ppermute | solution.py:710
  20.1 0.1 collective-permute-start.5
  20.2 0.0 collective-permute-done.3.rest_1_
  20.2 7.1 %collective-permute-done.4.rest_2_ = f32[4,64,256]{2,1,0:T(8,128)S(1)} collective-permute-done((f32[4,64,256]{2,1,0:T(8,128)S(1)}, f32[4,64,256]{2,1,0:T(8,128)S(1)}, u32[]{:S(2)}, u32[]{:S(2)}) %collective-permute-start.4) | collective-permute-done | bytes 262176 | tf_op jit(solution)/shard_map/ppermute | solution.py:710
  27.3 5.1 %collective-permute-done.5.rest_3_ = f32[4,64,256]{2,1,0:T(8,128)S(1)} collective-permute-done((f32[4,64,256]{2,1,0:T(8,128)S(1)}, f32[4,64,256]{2,1,0:T(8,128)S(1)}, u32[]{:S(2)}, u32[]{:S(2)}) %collective-permute-start.5) | collective-permute-done | bytes 262176 | tf_op jit(solution)/shard_map/ppermute | solution.py:710
  32.4 1.2 %shard_map.112 = (f32[16,64,256]{2,1,0:T(8,128)S(1)}, f32[16,64,256]{2,1,0:T(8,128)S(1)}, f32[384,128]{1,0:T(8,128)S(1)}, f32[384,128]{1,0:T(8,128)S(1)}) custom-call(s32[4]{0:T(128)S(1)} %get-tuple-element.36.counts, f32[8,16,256]{2,1,0:T(8,128)S(1)} %get-tuple-element.45.coefs, bf16[512,256]{1,0:T(8,128)(2,1)S(1)} %get-tuple-element.46.send_ref.rest_0_, ...), custom_call_target="tpu_custom_call" | custom-call | flops 1000000000 | bytes 4194304 | tf_op jit(solution)/shard_map/pallas_call | solution.py:678
  33.6 1.7 %collective-permute-start.6 = (f32[384,128]{1,0:T(8,128)S(1)}, f32[384,128]{1,0:T(8,128)S(1)}, u32[]{:S(2)}, u32[]{:S(2)}) collective-permute-start(f32[384,128]{1,0:T(8,128)S(1)} %get-tuple-element.54), channel_id=1, source_target_pairs={{0,1},{1,0},{2,3},{3,2},{4,20},{5,6},{6,5},{7,23},{8,9},{9,8},{10,... | collective-permute-start | bytes 589832 | tf_op jit(solution)/shard_map/ppermute | solution.py:704
  35.3 1.5 %collective-permute-start.7 = (f32[384,128]{1,0:T(8,128)S(1)}, f32[384,128]{1,0:T(8,128)S(1)}, u32[]{:S(2)}, u32[]{:S(2)}) collective-permute-start(f32[384,128]{1,0:T(8,128)S(1)} %get-tuple-element.55), channel_id=1, source_target_pairs={{0,16},{1,2},{2,1},{3,19},{4,5},{5,4},{6,7},{7,6},{8,24},{9,10},{1... | collective-permute-start | bytes 589832 | tf_op jit(solution)/shard_map/ppermute | solution.py:704
  36.8 2.9 %shard_map.113.local = f32[16,64,256]{2,1,0:T(8,128)S(1)} custom-call(s32[4]{0:T(128)S(1)} %get-tuple-element.36.counts, f32[16,64,256]{2,1,0:T(8,128)S(1)} %get-tuple-element.51.fields.current, f32[8,16,256]{2,1,0:T(8,128)S(1)} %get-tuple-element.45.coefs, bf16[256,1536]{1,0:T(8,128)(2,1)S(1)} %get-tuple-element.53.picks, ...), custom_call_target="tpu_custom_call" | custom-call | flops 3000000000 | bytes 4194304 | tf_op jit(solution)/shard_map/pallas_call | solution.py:678
  39.8 1.1 %collective-permute-done.6.arrived0 = f32[384,128]{1,0:T(8,128)S(1)} collective-permute-done((f32[384,128]{1,0:T(8,128)S(1)}, f32[384,128]{1,0:T(8,128)S(1)}, u32[]{:S(2)}, u32[]{:S(2)}) %collective-permute-start.6) | collective-permute-done | bytes 196640 | tf_op jit(solution)/shard_map/ppermute | solution.py:704
  40.9 0.1 collective-permute-done.7.arrived1
  41.0 3.0 %shard_map.114 = (f32[16,64,256]{2,1,0:T(8,128)S(1)}, f32[384,128]{1,0:T(8,128)S(1)}, f32[384,128]{1,0:T(8,128)S(1)}) custom-call(s32[4]{0:T(128)S(1)} %get-tuple-element.36.counts, s32[1]{0:T(128)} %get-tuple-element.37.general, f32[16,64,256]{2,1,0:T(8,128)S(1)} %get-tuple-element.51.fields.current, f32[16,64,256]{2,1,0:T(8,128)S(1)} %get-tuple-element.52.spectrum, ...), custom_call_target="tpu_custom_call" | custom-call | flops 1000000000 | bytes 4194304 | tf_op jit(solution)/shard_map/pallas_call | solution.py:678
  44.1 1.6 %collective-permute-start.8 = (f32[384,128]{1,0:T(8,128)S(1)}, f32[384,128]{1,0:T(8,128)S(1)}, u32[]{:S(2)}, u32[]{:S(2)}) collective-permute-start(f32[384,128]{1,0:T(8,128)S(1)} %get-tuple-element.57), channel_id=1, source_target_pairs={{0,1},{1,0},{2,3},{3,2},{4,20},{5,6},{6,5},{7,23},{8,9},{9,8},{10,... | collective-permute-start | bytes 589832 | tf_op jit(solution)/shard_map/ppermute | solution.py:704
  45.7 1.5 %collective-permute-start.9 = (f32[384,128]{1,0:T(8,128)S(1)}, f32[384,128]{1,0:T(8,128)S(1)}, u32[]{:S(2)}, u32[]{:S(2)}) collective-permute-start(f32[384,128]{1,0:T(8,128)S(1)} %get-tuple-element.58), channel_id=1, source_target_pairs={{0,16},{1,2},{2,1},{3,19},{4,5},{5,4},{6,7},{7,6},{8,24},{9,10},{1... | collective-permute-start | bytes 589832 | tf_op jit(solution)/shard_map/ppermute | solution.py:704
  47.2 2.9 %shard_map.115.local = f32[16,64,256]{2,1,0:T(8,128)S(1)} custom-call(s32[4]{0:T(128)S(1)} %get-tuple-element.36.counts, f32[16,64,256]{2,1,0:T(8,128)S(1)} %get-tuple-element.56.fields.current, f32[8,16,256]{2,1,0:T(8,128)S(1)} %get-tuple-element.45.coefs, bf16[256,1536]{1,0:T(8,128)(2,1)S(1)} %get-tuple-element.53.picks, ...), custom_call_target="tpu_custom_call" | custom-call | flops 3000000000 | bytes 4194304 | tf_op jit(solution)/shard_map/pallas_call | solution.py:678
  50.1 1.1 %collective-permute-done.8.arrived0 = f32[384,128]{1,0:T(8,128)S(1)} collective-permute-done((f32[384,128]{1,0:T(8,128)S(1)}, f32[384,128]{1,0:T(8,128)S(1)}, u32[]{:S(2)}, u32[]{:S(2)}) %collective-permute-start.8) | collective-permute-done | bytes 196640 | tf_op jit(solution)/shard_map/ppermute | solution.py:704
  51.3 0.0 collective-permute-done.9.arrived1
  51.3 2.7 %shard_map.116 = (f32[4,64,256]{2,1,0:T(8,128)S(1)}, f32[4,64,256]{2,1,0:T(8,128)S(1)}, f32[4,64,256]{2,1,0:T(8,128)S(1)}, f32[4,64,256]{2,1,0:T(8,128)S(1)}) custom-call(s32[4]{0:T(128)S(1)} %get-tuple-element.36.counts, s32[1]{0:T(128)} %get-tuple-element.37.general, f32[16,64,256]{2,1,0:T(8,128)S(1)} %get-tuple-element.56.fields.current, ...), custom_call_target="tpu_custom_call" | custom-call | flops 1000000000 | bytes 4194304 | tf_op jit(solution)/shard_map/pallas_call | solution.py:678
  54.0 0.4 collective-permute-start.10
  54.5 1.5 %collective-permute-start.11 = (f32[4,64,256]{2,1,0:T(8,128)S(1)}, f32[4,64,256]{2,1,0:T(8,128)S(1)}, u32[]{:S(2)}, u32[]{:S(2)}) collective-permute-start(f32[4,64,256]{2,1,0:T(8,128)S(1)} %get-tuple-element.61), channel_id=1, source_target_pairs={{0,8},{4,12},{8,0},{12,4},{1,9},{5,13},{9,1},{13,5},{2,10},{6,14},... | collective-permute-start | bytes 786440 | tf_op jit(solution)/shard_map/ppermute | solution.py:710
  56.0 0.0 collective-permute-start.12
  56.0 0.0 collective-permute-done.10.rest_1_
  56.0 7.6 %collective-permute-done.11.rest_2_ = f32[4,64,256]{2,1,0:T(8,128)S(1)} collective-permute-done((f32[4,64,256]{2,1,0:T(8,128)S(1)}, f32[4,64,256]{2,1,0:T(8,128)S(1)}, u32[]{:S(2)}, u32[]{:S(2)}) %collective-permute-start.11) | collective-permute-done | bytes 262176 | tf_op jit(solution)/shard_map/ppermute | solution.py:710
  63.6 4.0 %collective-permute-done.12.rest_3_ = f32[4,64,256]{2,1,0:T(8,128)S(1)} collective-permute-done((f32[4,64,256]{2,1,0:T(8,128)S(1)}, f32[4,64,256]{2,1,0:T(8,128)S(1)}, u32[]{:S(2)}, u32[]{:S(2)}) %collective-permute-start.12) | collective-permute-done | bytes 262176 | tf_op jit(solution)/shard_map/ppermute | solution.py:710
  67.6 1.0 %shard_map.117 = f32[16,64,256]{2,1,0:T(8,128)} custom-call(f32[4,64,256]{2,1,0:T(8,128)S(1)} %get-tuple-element.59.rest_0_, f32[4,64,256]{2,1,0:T(8,128)S(1)} %collective-permute-done.10.rest_1_, f32[4,64,256]{2,1,0:T(8,128)S(1)} %collective-permute-done.11.rest_2_, f32[4,64,256]{2,1,0:T(8,128)S(1)} %collective-permute-done.12.rest_3_), custom_call_target="tpu_custom_call" | custom-call | flops 1000000000 | bytes 4194304 | tf_op jit(solution)/shard_map/pallas_call | solution.py:678
Async XLA Ops:
  0.0 15.1 %collective-permute-start = (f32[16,64,256]{2,1,0:T(8,128)}, f32[16,64,256]{2,1,0:T(8,128)S(1)}, u32[]{:S(2)}, u32[]{:S(2)}) collective-permute-start(f32[16,64,256]{2,1,0:T(8,128)} %bitcast.11), channel_id=1, source_target_pairs={{0,4},{4,8},{8,12},{12,0},{1,5},{5,9},{9,13},{13,1},{2,6},{6,10},{... | collective-permute-start | bytes 3145736 | tf_op jit(solution)/shard_map/ppermute | solution.py:735
  0.5 6.6 %copy-start.2 = (f32[3,64,64]{2,1,0:T(8,128)S(1)}, f32[3,64,64]{2,1,0:T(8,128)}, u32[]{:S(2)}) copy-start(f32[3,64,64]{2,1,0:T(8,128)} %grads.1) | copy-start | bytes 147460
  0.5 6.6 %copy-start.3 = (f32[3,64,64]{2,1,0:T(8,128)S(1)}, f32[3,64,64]{2,1,0:T(8,128)}, u32[]{:S(2)}) copy-start(f32[3,64,64]{2,1,0:T(8,128)} %face_mats.1) | copy-start | bytes 147460
  2.9 4.2 %copy-start.1 = (s32[6,256]{1,0:T(8,128)S(1)}, s32[6,256]{1,0:T(8,128)}, u32[]{:S(2)}) copy-start(s32[6,256]{1,0:T(8,128)} %face_nbr.7) | copy-start | bytes 18436
  2.9 9.0 %collective-permute-start.1 = (f32[520,128]{1,0:T(8,128)S(1)}, f32[520,128]{1,0:T(8,128)S(1)}, u32[]{:S(2)}, u32[]{:S(2)}) collective-permute-start(f32[520,128]{1,0:T(8,128)S(1)} %get-tuple-element.39), channel_id=1, source_target_pairs={{0,1},{1,0},{2,3},{3,2},{4,20},{5,6},{6,5},{7,23},{8,9},{9,8},{10,... | collective-permute-start | bytes 798728 | tf_op jit(solution)/shard_map/ppermute | solution.py:704
  5.5 8.3 %collective-permute-start.2 = (f32[520,128]{1,0:T(8,128)S(1)}, f32[520,128]{1,0:T(8,128)S(1)}, u32[]{:S(2)}, u32[]{:S(2)}) collective-permute-start(f32[520,128]{1,0:T(8,128)S(1)} %get-tuple-element.40), channel_id=1, source_target_pairs={{0,16},{1,2},{2,1},{3,19},{4,5},{5,4},{6,7},{7,6},{8,24},{9,10},{1... | collective-permute-start | bytes 798728 | tf_op jit(solution)/shard_map/ppermute | solution.py:704
  7.0 0.7 copy-start.4
  7.7 7.4 %copy-start = (f32[16,1,64,256]{3,2,1,0:T(8,128)S(1)}, f32[16,1,64,256]{3,2,1,0:T(8,128)}, u32[]{:S(2)}) copy-start(f32[16,1,64,256]{3,2,1,0:T(8,128)} %param.11) | copy-start | bytes 3145732
  17.7 2.5 %collective-permute-start.3 = (f32[4,64,256]{2,1,0:T(8,128)S(1)}, f32[4,64,256]{2,1,0:T(8,128)S(1)}, u32[]{:S(2)}, u32[]{:S(2)}) collective-permute-start(f32[4,64,256]{2,1,0:T(8,128)S(1)} %get-tuple-element.48), channel_id=1, source_target_pairs={{0,4},{4,0},{8,12},{12,8},{1,5},{5,1},{9,13},{13,9},{2,6},{6,2},{1... | collective-permute-start | bytes 786440 | tf_op jit(solution)/shard_map/ppermute | solution.py:710
  17.8 9.5 %collective-permute-start.4 = (f32[4,64,256]{2,1,0:T(8,128)S(1)}, f32[4,64,256]{2,1,0:T(8,128)S(1)}, u32[]{:S(2)}, u32[]{:S(2)}) collective-permute-start(f32[4,64,256]{2,1,0:T(8,128)S(1)} %get-tuple-element.49), channel_id=1, source_target_pairs={{0,8},{4,12},{8,0},{12,4},{1,9},{5,13},{9,1},{13,5},{2,10},{6,14},... | collective-permute-start | bytes 786440 | tf_op jit(solution)/shard_map/ppermute | solution.py:710
  20.1 12.3 %collective-permute-start.5 = (f32[4,64,256]{2,1,0:T(8,128)S(1)}, f32[4,64,256]{2,1,0:T(8,128)S(1)}, u32[]{:S(2)}, u32[]{:S(2)}) collective-permute-start(f32[4,64,256]{2,1,0:T(8,128)S(1)} %get-tuple-element.50), channel_id=1, source_target_pairs={{0,12},{4,8},{8,4},{12,0},{1,13},{5,9},{9,5},{13,1},{2,14},{6,10},... | collective-permute-start | bytes 786440 | tf_op jit(solution)/shard_map/ppermute | solution.py:710
  33.6 7.3 %collective-permute-start.6 = (f32[384,128]{1,0:T(8,128)S(1)}, f32[384,128]{1,0:T(8,128)S(1)}, u32[]{:S(2)}, u32[]{:S(2)}) collective-permute-start(f32[384,128]{1,0:T(8,128)S(1)} %get-tuple-element.54), channel_id=1, source_target_pairs={{0,1},{1,0},{2,3},{3,2},{4,20},{5,6},{6,5},{7,23},{8,9},{9,8},{10,... | collective-permute-start | bytes 589832 | tf_op jit(solution)/shard_map/ppermute | solution.py:704
  35.3 5.7 %collective-permute-start.7 = (f32[384,128]{1,0:T(8,128)S(1)}, f32[384,128]{1,0:T(8,128)S(1)}, u32[]{:S(2)}, u32[]{:S(2)}) collective-permute-start(f32[384,128]{1,0:T(8,128)S(1)} %get-tuple-element.55), channel_id=1, source_target_pairs={{0,16},{1,2},{2,1},{3,19},{4,5},{5,4},{6,7},{7,6},{8,24},{9,10},{1... | collective-permute-start | bytes 589832 | tf_op jit(solution)/shard_map/ppermute | solution.py:704
  44.1 7.2 %collective-permute-start.8 = (f32[384,128]{1,0:T(8,128)S(1)}, f32[384,128]{1,0:T(8,128)S(1)}, u32[]{:S(2)}, u32[]{:S(2)}) collective-permute-start(f32[384,128]{1,0:T(8,128)S(1)} %get-tuple-element.57), channel_id=1, source_target_pairs={{0,1},{1,0},{2,3},{3,2},{4,20},{5,6},{6,5},{7,23},{8,9},{9,8},{10,... | collective-permute-start | bytes 589832 | tf_op jit(solution)/shard_map/ppermute | solution.py:704
  45.7 5.7 %collective-permute-start.9 = (f32[384,128]{1,0:T(8,128)S(1)}, f32[384,128]{1,0:T(8,128)S(1)}, u32[]{:S(2)}, u32[]{:S(2)}) collective-permute-start(f32[384,128]{1,0:T(8,128)S(1)} %get-tuple-element.58), channel_id=1, source_target_pairs={{0,16},{1,2},{2,1},{3,19},{4,5},{5,4},{6,7},{7,6},{8,24},{9,10},{1... | collective-permute-start | bytes 589832 | tf_op jit(solution)/shard_map/ppermute | solution.py:704
  54.0 2.0 %collective-permute-start.10 = (f32[4,64,256]{2,1,0:T(8,128)S(1)}, f32[4,64,256]{2,1,0:T(8,128)S(1)}, u32[]{:S(2)}, u32[]{:S(2)}) collective-permute-start(f32[4,64,256]{2,1,0:T(8,128)S(1)} %get-tuple-element.60), channel_id=1, source_target_pairs={{0,4},{4,0},{8,12},{12,8},{1,5},{5,1},{9,13},{13,9},{2,6},{6,2},{1... | collective-permute-start | bytes 786440 | tf_op jit(solution)/shard_map/ppermute | solution.py:710
  54.5 9.2 %collective-permute-start.11 = (f32[4,64,256]{2,1,0:T(8,128)S(1)}, f32[4,64,256]{2,1,0:T(8,128)S(1)}, u32[]{:S(2)}, u32[]{:S(2)}) collective-permute-start(f32[4,64,256]{2,1,0:T(8,128)S(1)} %get-tuple-element.61), channel_id=1, source_target_pairs={{0,8},{4,12},{8,0},{12,4},{1,9},{5,13},{9,1},{13,5},{2,10},{6,14},... | collective-permute-start | bytes 786440 | tf_op jit(solution)/shard_map/ppermute | solution.py:710
  56.0 11.6 %collective-permute-start.12 = (f32[4,64,256]{2,1,0:T(8,128)S(1)}, f32[4,64,256]{2,1,0:T(8,128)S(1)}, u32[]{:S(2)}, u32[]{:S(2)}) collective-permute-start(f32[4,64,256]{2,1,0:T(8,128)S(1)} %get-tuple-element.62), channel_id=1, source_target_pairs={{0,12},{4,8},{8,4},{12,0},{1,13},{5,9},{9,5},{13,1},{2,14},{6,10},... | collective-permute-start | bytes 786440 | tf_op jit(solution)/shard_map/ppermute | solution.py:710

commit v3 on v2

--- a/solution.py
+++ b/solution.py
@@ -27,10 +27,13 @@
     return hi, (x - hi.astype(f32)).astype(bf16)
 
 
-def exact_select(x, onehot):
+def exact_select(x, onehot, across=0):
     a, b = split(x)
     c = (x - a.astype(f32) - b.astype(f32)).astype(bf16)
-    return dot(a, onehot) + (dot(b, onehot) + dot(c, onehot))
+    times = lambda v: lax.dot_general(
+        v, onehot, (((1,), (across,)), ((), ())), preferred_element_type=f32
+    )
+    return times(a) + (times(b) + times(c))
 
 
 def times_block(stacked, x):
@@ -98,11 +101,20 @@
     gen_in,
     mean_in,
     modes_in,
+    nbr_in,
+    grads_in,
+    face_mats_in,
+    counts_in,
     pack0,
     pack1,
     send_out,
     conduct_out,
-    iterate,
+    low,
+    high,
+    nbr,
+    grads,
+    face_mats,
+    counts,
     halo_send,
     shift,
     gen,
@@ -110,7 +122,9 @@
     modes,
     small_done,
     field_done,
+    later_done,
 ):
+    iterate = Halves(low, high)
     samples, dofs, elems = iterate.shape
     halo = halo_send.shape[1]
     half = samples // 2
@@ -129,14 +143,21 @@
     ]
     large = []
     for j in range(0, half, size):
-        for at in (j, half + j):
-            part = pl.ds(at, size)
+        for at, side in ((j, low), (half + j, high)):
             large.append(
                 pltpu.make_async_copy(
-                    iterate_in.at[part], iterate.at[part], field_done.at[len(large)]
+                    iterate_in.at[pl.ds(at, size)],
+                    side.at[pl.ds(j, size)],
+                    field_done.at[len(large)],
                 )
             )
-    for copy in small + large:
+    later = [
+        pltpu.make_async_copy(source, target, later_done.at[i])
+        for i, (source, target) in enumerate(
+            ((nbr_in, nbr), (grads_in, grads), (face_mats_in, face_mats), (counts_in, counts))
+        )
+    ]
+    for copy in small + large + later:
         copy.start()
     for copy in small:
         copy.wait()
@@ -169,6 +190,8 @@
         large[2 * at + 1].wait()
         left = list(range(j, j + size))
         pack_group(iterate, left, [half + i for i in left], send, j, (pack0, pack1))
+    for copy in later:
+        copy.wait()
 
 
 def local_part(fields, slots, coef_row, picks, blocks, out, high, low):
@@ -197,7 +220,8 @@
 
 
 def first_local_kernel(
-    iterate,
+    low_fields,
+    high_fields,
     conduct_ref,
     face_nbr,
     grads,
@@ -211,14 +235,16 @@
     halo_picks,
     general,
     counts,
+    facing,
     high,
     low,
     wide,
 ):
     for k in range(counts.shape[0]):
         counts[k] = counts_in[0, k]
+    iterate = Halves(low_fields, high_fields)
     samples, dofs, elems = iterate.shape
-    halo = halo_picks.shape[1] // 2
+    halo = halo_picks.shape[0] // 4
     even = space_even()
     row = rows_iota((elems, elems))
     for f in range(FACES):
@@ -259,7 +285,9 @@
         face_blocks[f, dofs:, :] = lo
     for which, (face, base) in enumerate(sides(even, elems, halo)):
         nbr = jnp.where(face == 4, face_nbr[4:5, :], face_nbr[5:6, :])
-        halo_picks[which] = halo_onehot(nbr, base, halo)
+        pick = halo_onehot(nbr, base, halo)
+        halo_picks[which * 2 * halo : (which + 1) * 2 * halo, :] = pick
+        facing[which] = exact_select(side_by_side(conduct), pick, 1)
     crossing = jnp.max(jnp.where(face_nbr[0:4, :] >= elems, 1, 0))
     crossing = crossing + jnp.max(jnp.where(face_nbr[4:5, :] >= elems + halo, 1, 0))
     fifth = face_nbr[5:6, :]
@@ -279,18 +307,50 @@
     )
 
 
-def halo_blocks(arrived, block, pick, turned):
+def side_by_side(x):
+    half = x.shape[0] // 2
+    return jnp.concatenate([x[:half], x[half:]], axis=1)
+
+
+def stacked_halves(x):
+    width = x.shape[1] // 2
+    return jnp.concatenate([x[:, :width], x[:, width:]], axis=0)
+
+
+def usual_halo(arrived, scales, blocks, picks):
+    dofs = blocks[0].shape[1]
+    columns = []
+    for which in range(2):
+        value = arrived[which]
+        width = value.shape[1]
+        pairs = scales[which].shape[0]
+        scaled = [
+            value[j * dofs : (j + 1) * dofs, :] * scales[which][j : j + 1, :]
+            for j in range(pairs)
+        ]
+        got = times_block(blocks[which], jnp.concatenate(scaled, axis=1))
+        columns.append(
+            jnp.concatenate([got[:, j * width : (j + 1) * width] for j in range(pairs)], axis=0)
+        )
+    hi, lo = split(jnp.concatenate(columns, axis=1))
+    return dot(hi, picks) + dot(lo, picks)
+
+
+class Halves:
+    def __init__(self, low, high):
+        self.low, self.high = low, high
+        self.shape = (2 * low.shape[0],) + tuple(low.shape[1:])
+
+    def __getitem__(self, at):
+        half = self.low.shape[0]
+        return self.low[at] if at < half else self.high[at - half]
+
+
+def other_halo(arrived, block, pick):
     dofs = block.shape[1]
-    pairs = turned.shape[0] // dofs
-    width = turned.shape[1]
-    size = 2 if pairs % 2 == 0 else 1
-    for j in range(0, pairs, size):
-        rows = [slice((j + i) * dofs, (j + i + 1) * dofs) for i in range(size)]
-        got = times_block(block, jnp.concatenate([arrived[r, :] for r in rows], axis=1))
-        for i, r in enumerate(rows):
-            turned[r, :] = got[:, i * width : (i + 1) * width]
-    hi, lo = split(turned[...])
-    return dot(hi, pick) + dot(lo, pick)
+    hi, lo = split(times_block(block, arrived))
+    got = dot(hi, pick) + dot(lo, pick)
+    return got
 
 
 def other_sides(general, even, face_nbr, halo, body):
@@ -310,41 +370,34 @@
             lax.fori_loop(0, FACES, step, 0)
 
 
-def add_halo(
-    arrived, even, general, face_nbr, face_blocks, halo_picks, slots, coef_row, total, turned
-):
+def pair_place(t, half, dofs, elems):
+    row, col = t % half * dofs, t // half * elems
+    return slice(row, row + dofs), slice(col, col + elems)
+
+
+def add_others(arrived, even, general, face_nbr, face_blocks, halo, half, slots, coef_row, factor, total):
     elems = face_nbr.shape[1]
-    halo = halo_picks.shape[1] // 2
     dofs = total.shape[1]
-    half = turned.shape[0] // dofs
-    usual = sides(even, elems, halo)
-    picked = [
-        halo_blocks(arrived[w], face_blocks[usual[w][0]], halo_picks[w], turned)
-        for w in range(2)
-    ]
-
-    def place(t):
-        row, col = t % half * dofs, t // half * elems
-        return slice(row, row + dofs), slice(col, col + elems)
-
-    for t, field in enumerate(slots):
-        value = total[field]
-        for w in range(2):
-            value = value + coef_row(usual[w][0], t) * picked[w][place(t)]
-        total[field] = value
 
     def body(which, face, pick):
-        got = halo_blocks(arrived[which], face_blocks[face], pick, turned)
-        for t, field in enumerate(slots):
-            total[field] = total[field] + coef_row(face, t) * got[place(t)]
+        block = face_blocks[face]
+        for j in range(half):
+            got = other_halo(arrived[which][j * dofs : (j + 1) * dofs, :], block, pick)
+            for t in (j, half + j):
+                if t < len(slots):
+                    cols = slice(t // half * elems, (t // half + 1) * elems)
+                    field = slots[t]
+                    total[field] = total[field] + factor * coef_row(face, t) * got[:, cols]
 
     other_sides(general, even, face_nbr, halo, body)
 
 
 def residual_kernel(
     forcing,
-    iterate,
-    earlier,
+    low_fields,
+    high_fields,
+    earlier_low,
+    earlier_high,
     local,
     arrived0,
     arrived1,
@@ -353,64 +406,90 @@
     blocks,
     face_blocks,
     halo_picks,
+    facing,
     general,
     *rest,
     total_steps,
     groups,
 ):
     outs = rest[: groups * total_steps]
-    coefs, total, turned, extra = rest[groups * total_steps :]
+    coefs, total, extra = rest[groups * total_steps :]
+    iterate = Halves(low_fields, high_fields)
     samples, dofs, elems = forcing.shape
-    halo = halo_picks.shape[1] // 2
+    halo = halo_picks.shape[0] // 4
     half = samples // 2
     even = space_even()
+    usual = sides(even, elems, halo)
     arrived = (arrived0, arrived1)
     coefs[...] = coefs_in[...]
     conduct = coefs_in[FACES + 1]
-    extra[...] = jnp.zeros(extra.shape, f32)
+    scales = [0.5 * (facing[w] + arrived[w][half * dofs :, :]) for w in range(2)]
+    couplings = [
+        stacked_halves(
+            exact_select(scales[w], halo_picks[w * 2 * halo : (w + 1) * 2 * halo, :])
+        )
+        for w in range(2)
+    ]
+    extra[...] = couplings[0] + couplings[1]
+    for w in range(2):
+        coefs[usual[w][0]] = coefs[usual[w][0]] + couplings[w]
 
     def add_coupling(which, face, pick):
         got = exact_select(arrived[which][half * dofs :, :], pick)
         nbr = face_nbr[pl.ds(face, 1), :]
-        base = sides(even, elems, halo)[which][1]
+        base = usual[which][1]
         here = (nbr >= base) & (nbr < base + halo)
-        across = jnp.concatenate([got[:, :elems], got[:, elems:]], axis=0)
-        coupling = jnp.where(here, 0.5 * (conduct + across), 0.0)
+        coupling = jnp.where(here, 0.5 * (conduct + stacked_halves(got)), 0.0)
         coefs[face] = coefs[face] + coupling
         extra[...] = extra[...] + coupling
 
-    for which, (face, _) in enumerate(sides(even, elems, halo)):
-        add_coupling(which, face, halo_picks[which])
     other_sides(general, even, face_nbr, halo, add_coupling)
     coefs[FACES] = coefs[FACES] + extra[...]
     volume = blocks[:, 0 : 2 * dofs][:, :dofs]
+    brought = usual_halo(
+        arrived, scales, [face_blocks[usual[w][0]] for w in range(2)], halo_picks[...]
+    )
     for j in range(samples):
-        total[j] = local[j] + times_block(volume, iterate[j] * extra[j : j + 1, :])
-    add_halo(
+        value = iterate[j]
+        total[j] = value + time_step * (
+            local[j]
+            + brought[pair_place(j, half, dofs, elems)]
+            + times_block(volume, value * extra[j : j + 1, :])
+        )
+    add_others(
         arrived,
         even,
         general,
         face_nbr,
         face_blocks,
-        halo_picks,
+        halo,
+        half,
         list(range(samples)),
         lambda f, t: coefs[f, t : t + 1, :],
+        time_step,
         total,
-        turned,
     )
     step = lax.axis_index("tm")
     weight = jnp.float32(0.0)
     for n in range(total_steps):
         weight = jnp.where(step == n, jnp.float32(alpha_circ ** (n / total_steps)), weight)
-    gate = jnp.where(step > 0, weight, 0.0)
+    gate_high = jnp.where(step > 0, weight, 0.0)
+    gate_low = jnp.where(step % 2 == 1, weight, 0.0) if two_chips(total_steps) else gate_high
     size = samples // (groups * total_steps)
     for which, out in enumerate(outs):
         at, turn = divmod(which, total_steps)
+        first = (partner(step, turn, total_steps) * groups + at) * size
         for i in range(size):
-            j = (partner(step, turn, total_steps) * groups + at) * size + i
-            out[i] = weight * (
-                (forcing[j] - iterate[j]) - time_step * total[j]
-            ) + gate * earlier[j]
+            j = first + i
+            inner = forcing[j] - total[j]
+            before = lax.rem(j, half)
+            late = j >= half
+            earlier = jnp.where(late, earlier_high[before], earlier_low[before])
+            out[i] = weight * inner + jnp.where(late, gate_high, gate_low) * earlier
+
+
+def two_chips(devs):
+    return devs == 4
 
 
 def partner(rank, turn, count):
@@ -500,7 +579,9 @@
     return lambda f, t: coefs[f, pl.ds(first + t // kept, 1), :]
 
 
-def spectrum_kernel(counts, coefs, send_ref, *rest, total_steps, at, groups):
+def spectrum_kernel(
+    counts, coefs, send_ref, own, near, *rest, total_steps, at, groups
+):
     arrived, (spectrum, first_w, pack0, pack1, pieces) = (
         rest[:total_steps],
         rest[total_steps:],
@@ -510,6 +591,13 @@
     rank = lax.axis_index("tm")
     for turn, piece in enumerate(arrived):
         pieces[partner(rank, turn, total_steps)] = piece[...]
+    if two_chips(total_steps):
+        here = at * samples
+        there = groups * samples + here
+        gate = jnp.where(rank < 2, jnp.float32(alpha_circ ** (2 / total_steps)), 0.0)
+        for s in range(samples):
+            before = jnp.where(rank == 0, near[here + s], own[there + s])
+            pieces[2, s] = pieces[2, s] + gate * before
     for s in range(samples):
         diag = coefs[FACES, pl.ds(first + s, 1), :]
         base = s * total_steps
@@ -530,62 +618,80 @@
 
 
 def sweep_local_kernel(
-    counts, fields, coefs, picks, blocks, out, high, low, *, total_steps, at, groups
+    counts,
+    fields,
+    spectrum,
+    coefs,
+    picks,
+    blocks,
+    halo_picks,
+    *rest,
+    total_steps,
+    at,
+    groups,
+    first_turn,
 ):
+    if first_turn:
+        out, thetas, scales, total, high, low = rest
+    else:
+        out, total, high, low = rest
+    elems = fields.shape[2]
     samples = fields.shape[0] // total_steps
-    local_part(
-        fields,
-        kept_slots(counts, samples, total_steps),
-        sample_row(coefs, total_steps, my_first(samples, at, groups)),
-        picks,
-        blocks,
-        out,
-        high,
-        low,
-    )
-
-
-def updated_fields(current, spectrum, total, coefs, counts, turn, total_steps, first, store):
-    samples = current.shape[0] // total_steps
+    first = my_first(samples, at, groups)
+    slots = kept_slots(counts, samples, total_steps)
+    row = sample_row(coefs, total_steps, first)
+    if first_turn:
+        halo = halo_picks.shape[0] // 4
+        half = scales.shape[1]
+        usual = sides(space_even(), elems, halo)
+        count = len(slots)
+        for w in range(2):
+            lines = [
+                row(usual[w][0], t if t < count else 0) for t in range(2 * half)
+            ]
+            sides_of = [jnp.concatenate(lines[:half], 0), jnp.concatenate(lines[half:], 0)]
+            scales[w] = time_step * exact_select(
+                jnp.concatenate(sides_of, axis=1),
+                halo_picks[w * 2 * halo : (w + 1) * 2 * halo, :],
+                1,
+            )
+        diag = jnp.concatenate(
+            [coefs[FACES, pl.ds(first + s, 1), :] for s in range(samples)], axis=0
+        )
+        for i, (k, _, im) in enumerate(frequencies(total_steps)):
+            rate_real, rate_imag = theta_rows(k, total_steps, diag)
+            thetas[2 * i] = rate_real
+            if im is not None:
+                thetas[2 * i + 1] = rate_imag
+    local_part(fields, slots, row, picks, blocks, total, high, low)
     for s in range(samples):
-        diag = coefs[FACES, pl.ds(first + s, 1), :]
         base = s * total_steps
         for k, re, im in frequencies(total_steps):
-            active = counts[k] > turn + 1
             shift_real, shift_imag = shift_of(k, total_steps)
-            rate_real, rate_imag = theta_rows(k, total_steps, diag)
-            value = current[base + re]
-            rest = spectrum[base + re] - (shift_real * value + time_step * total[base + re])
-            if im is None:
-                store(base + re, jnp.where(active, value + rate_real * rest, value))
-            else:
-                other = current[base + im]
-                rest = rest + shift_imag * other
-                rest_imag = spectrum[base + im] - (
+            value = fields[base + re]
+            kept = spectrum[base + re] - (shift_real * value + time_step * total[base + re])
+            if im is not None:
+                other = fields[base + im]
+                kept = kept + shift_imag * other
+                out[base + im] = spectrum[base + im] - (
                     shift_real * other + shift_imag * value + time_step * total[base + im]
                 )
-                store(
-                    base + re,
-                    jnp.where(active, value + (rate_real * rest - rate_imag * rest_imag), value),
-                )
-                store(
-                    base + im,
-                    jnp.where(active, other + (rate_real * rest_imag + rate_imag * rest), other),
-                )
+            out[base + re] = kept
 
 
 def sweep_update_kernel(
     counts,
     general,
     current,
-    spectrum,
-    local,
+    inner,
     arrived0,
     arrived1,
     coefs,
     face_nbr,
     face_blocks,
     halo_picks,
+    thetas,
+    scales,
     *rest,
     turn,
     total_steps,
@@ -595,31 +701,53 @@
 ):
     even = space_even()
     if last:
-        outs, (total, turned, solved) = rest[:total_steps], rest[total_steps:]
+        outs, (total, solved) = rest[:total_steps], rest[total_steps:]
     else:
-        send_ref, solved, pack0, pack1, total, turned = rest
-    fields = current.shape[0]
+        send_ref, solved, pack0, pack1, total = rest
+    fields, dofs, elems = current.shape
     samples = fields // total_steps
     first = my_first(samples, at, groups)
     slots = kept_slots(counts, samples, total_steps)
-    total[...] = local[...]
-    add_halo(
-        (arrived0, arrived1),
+    arrived = (arrived0, arrived1)
+    halo = halo_picks.shape[0] // 4
+    half = scales.shape[1]
+    usual = sides(even, elems, halo)
+    brought = usual_halo(
+        arrived,
+        [scales[w] for w in range(2)],
+        [face_blocks[usual[w][0]] for w in range(2)],
+        halo_picks[...],
+    )
+    for t, field in enumerate(slots):
+        total[field] = inner[field] - brought[pair_place(t, half, dofs, elems)]
+    add_others(
+        arrived,
         even,
         general,
         face_nbr,
         face_blocks,
-        halo_picks,
+        halo,
+        half,
         slots,
         sample_row(coefs, total_steps, first),
+        -time_step,
         total,
-        turned,
-    )
-
-    def store(field, value):
-        solved[field] = value
-
-    updated_fields(current, spectrum, total, coefs, counts, turn, total_steps, first, store)
+    )
+    for s in range(samples):
+        base = s * total_steps
+        for i, (k, re, im) in enumerate(frequencies(total_steps)):
+            active = counts[k] > turn + 1
+            rate_real = thetas[2 * i, s : s + 1, :]
+            value, rest_real = current[base + re], total[base + re]
+            change = rate_real * rest_real
+            if im is not None:
+                rate_imag = thetas[2 * i + 1, s : s + 1, :]
+                other, rest_imag = current[base + im], total[base + im]
+                change = change - rate_imag * rest_imag
+                solved[base + im] = jnp.where(
+                    active, other + (rate_real * rest_imag + rate_imag * rest_real), other
+                )
+            solved[base + re] = jnp.where(active, value + change, value)
     if not last:
         pack_fields(solved, even_slots(slots), send_ref[...], (pack0, pack1))
         return
@@ -732,10 +860,12 @@
     cube = (samples, dofs, elems)
     forcing = forcing.reshape(cube)
     iterate = iterate.reshape(cube)
-    earlier = lax.ppermute(iterate, "tm", [(i, (i + 1) % devs) for i in range(devs)])
+    onward = [(i, (i + 1) % devs) for i in range(devs)]
     rows = half * dofs
     copies = 2 * (half // group_size(half))
-    pack0, pack1, send, conduct, iterate = run(
+    (
+        pack0, pack1, send, conduct, low, high, face_nbr, grad_mats, face_mats, counts_line
+    ) = run(
         prepare_kernel,
         (
             iterate,
@@ -744,13 +874,22 @@
             gen_vector.reshape(1, -1),
             kappa_mean.reshape(1, -1),
             kappa_modes,
+            face_nbr,
+            grad_mats,
+            face_mats,
+            sweep_counts.reshape(1, -1),
         ),
         [
             ((rows + half, 2 * halo), f32),
             ((rows + half, 2 * halo), f32),
             ((2 * elems, 4 * halo), bf16),
             ((samples, elems), f32),
-            (cube, f32),
+            ((half, dofs, elems), f32),
+            ((half, dofs, elems), f32),
+            (face_nbr.shape, i32),
+            (grad_mats.shape, f32),
+            (face_mats.shape, f32),
+            ((1, sweep_counts.shape[0]), i32),
         ],
         [
             (halo_send.shape, i32),
@@ -760,25 +899,34 @@
             (kappa_modes.shape, f32),
             pltpu.SemaphoreType.DMA((5,)),
             pltpu.SemaphoreType.DMA((copies,)),
+            pltpu.SemaphoreType.DMA((4,)),
         ],
-        in_hbm=range(6),
+        in_hbm=range(10),
     )
     arrived0 = neighbour_swap(pack0, 0)
     arrived1 = neighbour_swap(pack1, 1)
+    earlier_high = lax.ppermute(high, "tm", onward)
+    if two_chips(devs):
+        earlier_low = time_swap(low, 1)
+    else:
+        earlier_low = lax.ppermute(low, "tm", onward)
     blocks_wide = (FACES + 1) * dofs
     splits = lambda count: [((count, blocks_wide, elems), bf16)] * 2
-    local, coefs, picks, blocks, face_blocks, halo_picks, general, counts = run(
+    (
+        local, coefs, picks, blocks, face_blocks, halo_picks, general, counts, facing
+    ) = run(
         first_local_kernel,
-        (iterate, conduct, face_nbr, grad_mats, face_mats, sweep_counts.reshape(1, -1)),
+        (low, high, conduct, face_nbr, grad_mats, face_mats, counts_line),
         [
             (cube, f32),
             ((FACES + 2, samples, elems), f32),
             ((elems, FACES * elems), bf16),
             ((2 * dofs, blocks_wide), bf16),
             ((FACES, 2 * dofs, dofs), bf16),
-            ((2, 2 * halo, 2 * elems), bf16),
+            ((4 * halo, 2 * elems), bf16),
             ((1,), i32),
             (sweep_counts.shape, i32),
+            ((2, half, 2 * halo), f32),
         ],
         splits(samples) + [((blocks_wide, 2 * dofs), f32)],
         out_smem=(6, 7),
@@ -791,8 +939,10 @@
         functools.partial(residual_kernel, total_steps=total_steps, groups=groups),
         (
             forcing,
-            iterate,
-            earlier,
+            low,
+            high,
+            earlier_low,
+            earlier_high,
             local,
             arrived0,
             arrived1,
@@ -801,67 +951,73 @@
             blocks,
             face_blocks,
             halo_picks,
+            facing,
             general,
         ),
         [piece] * (groups * devs) + [((FACES + 2, samples, elems), f32)],
-        [(cube, f32), ((rows, 2 * halo), f32), ((samples, elems), f32)],
-        in_smem=(11,),
+        [(cube, f32), ((samples, elems), f32)],
+        in_smem=(14,),
     )
     fields = share * total_steps
     swept = share * (total_steps - 1)
-    some = (fields, dofs, elems)
-    turned = ((((swept + 1) // 2) * dofs, 2 * halo), f32)
+    pairs = (swept + 1) // 2
+    some = ((fields, dofs, elems), f32)
+    packed = ((pairs * dofs, 2 * halo), f32)
     restored = []
     for at in range(groups):
         mine = dict(total_steps=total_steps, at=at, groups=groups)
         pieces = [time_swap(scaled[at * devs + turn], turn) for turn in range(devs)]
         spectrum, current, pack0, pack1 = run(
             functools.partial(spectrum_kernel, **mine),
-            (counts, coefs, send, *pieces),
-            [(some, f32), (some, f32), turned, turned],
+            (counts, coefs, send, low, earlier_low, *pieces),
+            [some, some, packed, packed],
             [((total_steps, share, dofs, elems), f32)],
             in_smem=(0,),
         )
         for turn in range(MAXS - 1):
             arrived0 = neighbour_swap(pack0, 0)
             arrived1 = neighbour_swap(pack1, 1)
-            (local,) = run(
-                functools.partial(sweep_local_kernel, **mine),
-                (counts, current, coefs, picks, blocks),
-                [(some, f32)],
-                splits(swept),
+            inner, *tables = run(
+                functools.partial(sweep_local_kernel, first_turn=turn == 0, **mine),
+                (counts, current, spectrum, coefs, picks, blocks, halo_picks),
+                [some]
+                + [
+                    ((2 * len(frequencies(total_steps)), share, elems), f32),
+                    ((2, pairs, 2 * halo), f32),
+                ]
+                * (turn == 0),
+                [some] + splits(swept),
                 in_smem=(0,),
                 flops=3 * 10**9 // groups,
             )
+            if turn == 0:
+                thetas, scales = tables
             last = turn == MAXS - 2
             inputs = (
                 counts,
                 general,
                 current,
-                spectrum,
-                local,
+                inner,
                 arrived0,
                 arrived1,
                 coefs,
                 face_nbr,
                 face_blocks,
                 halo_picks,
+                thetas,
+                scales,
             )
             kernel = functools.partial(sweep_update_kernel, turn=turn, last=last, **mine)
             if last:
                 series = run(
-                    kernel,
-                    inputs,
-                    [piece] * devs,
-                    [(some, f32), turned, (some, f32)],
-                    in_smem=(0, 1),
+                    kernel, inputs, [piece] * devs, [some, some], in_smem=(0, 1)
                 )
             else:
                 current, pack0, pack1 = run(
                     kernel,
                     inputs + (send,),
-                    [(some, f32), turned, turned],
-                    [(some, f32), turned],
+                    [some, packed, packed],
+                    [some],
                     in_smem=(0, 1),
                 )
         restored += [time_swap(series[turn], turn) for turn in range(devs)]

time: 69.1 us -> 66.9 us (0.968)
  waiting for transfers between devices: 29.3 us -> 26.6 us
  starting transfers between devices: 15.5 us -> 16.4 us
    ppermute x6 -> x7, starting transfers between devices: 4.5 us -> 6.48 us  [time_swap(): return value if turn == 0 else lax.ppermute(value, 'tm', pairs)]
    ppermute x6, waiting for transfers between devices: 4.35 us -> 2.95 us  [neighbour_swap(): return lax.ppermute(value, axes, pairs)]
    ppermute x1, waiting for transfers between devices: 1.23 us -> 0.01 us  [per_device(): earlier_high = lax.ppermute(high, 'tm', onward)]
    ppermute x6, starting transfers between devices: 10.5 us -> 9.41 us  [neighbour_swap(): return lax.ppermute(value, axes, pairs)]
    ppermute x6 -> x7, waiting for transfers between devices: 23.8 us -> 23.7 us  [time_swap(): return value if turn == 0 else lax.ppermute(value, 'tm', pairs)]
  transfers between devices with their start and end apart: 13 -> 14, of which waited for: 9 -> 8; matrix products, arithmetic and copies ran while one was open for 0% -> 0% of each run, Pallas kernels for 18% -> 17%
where the time goes in v3:
time: 66.9 us; the launch traced here: 66.3 us
  waiting for transfers between devices  26.6 us (40%)
  Pallas kernels  23.1 us (35%)
  starting transfers between devices  16.4 us (25%)
    ppermute x7, waiting for transfers between devices, time_swap(): return value if turn == 0 else lax.ppermute(value, 'tm', pairs)  23.7 us
    pallas_call x9, Pallas kernels, run(): pl.pallas_call(kernel, out_shape=[jax.ShapeDtypeStruct(*o) for o in outs]...  23.1 us
    ppermute x6, starting transfers between devices, neighbour_swap(): return lax.ppermute(value, axes, pairs)  9.41 us
    ppermute x7, starting transfers between devices, time_swap(): return value if turn == 0 else lax.ppermute(value, 'tm', pairs)  6.48 us
    ppermute x6, waiting for transfers between devices, neighbour_swap(): return lax.ppermute(value, axes, pairs)  2.95 us
  transfers between devices with their start and end apart: 14, of which 8 were waited for; matrix products, arithmetic and copies ran while one was open for 0% of the time, Pallas kernels for 17%

profile of v3, /device:TPU:0, one launch (start us, length us, event | category | flops | bytes accessed | tf_op | source)
XLA Modules:
  0.0 66.3 jit_solution(10494386950086670797)
XLA Ops:
  0.0 2.5 %shard_map.109 = (f32[520,128]{1,0:T(8,128)S(1)}, f32[520,128]{1,0:T(8,128)S(1)}, bf16[512,256]{1,0:T(8,128)(2,1)S(1)}, f32[16,256]{1,0:T(8,128)S(1)}, f32[8,64,...) custom-call(f32[16,64,256]{2,1,0:T(8,128)} %bitcast.10, ...), custom_call_target="tpu_custom_call" | custom-call | flops 1000000000 | bytes 4194304 | tf_op jit(solution)/shard_map/pallas_call | solution.py:806
  2.5 0.5 collective-permute-start.1
  3.0 2.6 %collective-permute-start = (f32[8,64,256]{2,1,0:T(8,128)S(1)}, f32[8,64,256]{2,1,0:T(8,128)S(1)}, u32[]{:S(2)}, u32[]{:S(2)}) collective-permute-start(f32[8,64,256]{2,1,0:T(8,128)S(1)} %get-tuple-element.43.low_fields.own), channel_id=1, source_target_pairs={{0,4},{4,0},{8,12},{12,8},{1,5},{5,1},{9,13},{13,9},{2,6},{6,2},{1... | collective-permute-start | bytes 1572872 | tf_op jit(solution)/shard_map/ppermute | solution.py:838
  5.6 1.6 %collective-permute-start.2 = (f32[520,128]{1,0:T(8,128)S(1)}, f32[520,128]{1,0:T(8,128)S(1)}, u32[]{:S(2)}, u32[]{:S(2)}) collective-permute-start(f32[520,128]{1,0:T(8,128)S(1)} %get-tuple-element.53), channel_id=1, source_target_pairs={{0,1},{1,0},{2,3},{3,2},{4,20},{5,6},{6,5},{7,23},{8,9},{9,8},{10,... | collective-permute-start | bytes 798728 | tf_op jit(solution)/shard_map/ppermute | solution.py:832
  7.2 1.5 %collective-permute-start.3 = (f32[520,128]{1,0:T(8,128)S(1)}, f32[520,128]{1,0:T(8,128)S(1)}, u32[]{:S(2)}, u32[]{:S(2)}) collective-permute-start(f32[520,128]{1,0:T(8,128)S(1)} %get-tuple-element.54), channel_id=1, source_target_pairs={{0,16},{1,2},{2,1},{3,19},{4,5},{5,4},{6,7},{7,6},{8,24},{9,10},{1... | collective-permute-start | bytes 798728 | tf_op jit(solution)/shard_map/ppermute | solution.py:832
  8.7 0.0 copy-start
  8.7 4.4 %shard_map.110 = (f32[16,64,256]{2,1,0:T(8,128)S(1)}, f32[8,16,256]{2,1,0:T(8,128)S(1)}, bf16[256,1536]{1,0:T(8,128)(2,1)S(1)}, bf16[128,448]{1,0:T(8,128)(2,1)S...) custom-call(f32[8,64,256]{2,1,0:T(8,128)S(1)} %get-tuple-element.43., ...), custom_call_target="tpu_custom_call" | custom-call | flops 4000000000 | bytes 4194304 | tf_op jit(solution)/shard_map/pallas_call | solution.py:806
  13.0 1.5 %collective-permute-done.2.arrived0 = f32[520,128]{1,0:T(8,128)S(1)} collective-permute-done((f32[520,128]{1,0:T(8,128)S(1)}, f32[520,128]{1,0:T(8,128)S(1)}, u32[]{:S(2)}, u32[]{:S(2)}) %collective-permute-start.2) | collective-permute-done | bytes 266272 | tf_op jit(solution)/shard_map/ppermute | solution.py:832
  14.6 0.0 collective-permute-done.3.arrived1
  14.6 0.0 collective-permute-done.1.earlier_high
  14.6 0.0 collective-permute-done.earlier_low.near
  14.6 0.0 copy-done
  14.6 2.3 %shard_map.111 = (f32[4,64,256]{2,1,0:T(8,128)S(1)}, f32[4,64,256]{2,1,0:T(8,128)S(1)}, f32[4,64,256]{2,1,0:T(8,128)S(1)}, f32[4,64,256]{2,1,0:T(8,128)S(1)}, f32[8,16,256]{2,1,0:T(8,128)S(1)}) custom-call(f32[16,64,256]{2,1,0:T(8,128)S(1)} %bitcast.9, f32[8,64,256]{2,1,0:T(8,128)S(1)} %get-tuple-element.43.low_fields.own, ...), custom_call_target="tpu_custom_call" | custom-call | flops 1000000000 | bytes 4194304 | tf_op jit(solution)/shard_map/pallas_call | solution.py:806
  16.9 0.2 collective-permute-start.4
  17.1 0.1 collective-permute-start.5
  17.1 1.7 %collective-permute-start.6 = (f32[4,64,256]{2,1,0:T(8,128)S(1)}, f32[4,64,256]{2,1,0:T(8,128)S(1)}, u32[]{:S(2)}, u32[]{:S(2)}) collective-permute-start(f32[4,64,256]{2,1,0:T(8,128)S(1)} %get-tuple-element.65), channel_id=1, source_target_pairs={{0,12},{4,8},{8,4},{12,0},{1,13},{5,9},{9,5},{13,1},{2,14},{6,10},... | collective-permute-start | bytes 786440 | tf_op jit(solution)/shard_map/ppermute | solution.py:838
  18.8 0.0 collective-permute-done.4.rest_1_
  18.8 7.3 %collective-permute-done.5.rest_2_ = f32[4,64,256]{2,1,0:T(8,128)S(1)} collective-permute-done((f32[4,64,256]{2,1,0:T(8,128)S(1)}, f32[4,64,256]{2,1,0:T(8,128)S(1)}, u32[]{:S(2)}, u32[]{:S(2)}) %collective-permute-start.5) | collective-permute-done | bytes 262176 | tf_op jit(solution)/shard_map/ppermute | solution.py:838
  26.2 4.7 %collective-permute-done.6.rest_3_ = f32[4,64,256]{2,1,0:T(8,128)S(1)} collective-permute-done((f32[4,64,256]{2,1,0:T(8,128)S(1)}, f32[4,64,256]{2,1,0:T(8,128)S(1)}, u32[]{:S(2)}, u32[]{:S(2)}) %collective-permute-start.6) | collective-permute-done | bytes 262176 | tf_op jit(solution)/shard_map/ppermute | solution.py:838
  30.8 1.3 %shard_map.112 = (f32[16,64,256]{2,1,0:T(8,128)S(1)}, f32[16,64,256]{2,1,0:T(8,128)S(1)}, f32[384,128]{1,0:T(8,128)S(1)}, f32[384,128]{1,0:T(8,128)S(1)}) custom-call(s32[4]{0:T(128)S(1)} %get-tuple-element.50.counts, f32[8,16,256]{2,1,0:T(8,128)S(1)} %get-tuple-element.60.coefs, bf16[512,256]{1,0:T(8,128)(2,1)S(1)} %get-tuple-element.61.send_ref.rest_0_, ...), custom_call_target="tpu_custom_call" | custom-call | flops 1000000000 | bytes 4194304 | tf_op jit(solution)/shard_map/pallas_call | solution.py:806
  32.2 1.5 %collective-permute-start.7 = (f32[384,128]{1,0:T(8,128)S(1)}, f32[384,128]{1,0:T(8,128)S(1)}, u32[]{:S(2)}, u32[]{:S(2)}) collective-permute-start(f32[384,128]{1,0:T(8,128)S(1)} %get-tuple-element.70), channel_id=1, source_target_pairs={{0,1},{1,0},{2,3},{3,2},{4,20},{5,6},{6,5},{7,23},{8,9},{9,8},{10,... | collective-permute-start | bytes 589832 | tf_op jit(solution)/shard_map/ppermute | solution.py:832
  33.6 1.5 %collective-permute-start.8 = (f32[384,128]{1,0:T(8,128)S(1)}, f32[384,128]{1,0:T(8,128)S(1)}, u32[]{:S(2)}, u32[]{:S(2)}) collective-permute-start(f32[384,128]{1,0:T(8,128)S(1)} %get-tuple-element.71), channel_id=1, source_target_pairs={{0,16},{1,2},{2,1},{3,19},{4,5},{5,4},{6,7},{7,6},{8,24},{9,10},{1... | collective-permute-start | bytes 589832 | tf_op jit(solution)/shard_map/ppermute | solution.py:832
  35.1 3.5 %shard_map.113 = (f32[16,64,256]{2,1,0:T(8,128)S(1)}, f32[6,4,256]{2,1,0:T(4,128)S(1)}, f32[2,6,128]{2,1,0:T(8,128)S(1)}) custom-call(s32[4]{0:T(128)S(1)} %get-tuple-element.50.counts, f32[16,64,256]{2,1,0:T(8,128)S(1)} %get-tuple-element.66.fields.current, f32[16,64,256]{2,1,0:T(8,128)S(1)} %get-tuple-element.67.spectrum, ...), custom_call_target="tpu_custom_call" | custom-call | flops 3000000000 | bytes 4194304 | tf_op jit(solution)/shard_map/pallas_call | solution.py:806
  38.6 0.7 %collective-permute-done.7.arrived0 = f32[384,128]{1,0:T(8,128)S(1)} collective-permute-done((f32[384,128]{1,0:T(8,128)S(1)}, f32[384,128]{1,0:T(8,128)S(1)}, u32[]{:S(2)}, u32[]{:S(2)}) %collective-permute-start.7) | collective-permute-done | bytes 196640 | tf_op jit(solution)/shard_map/ppermute | solution.py:832
  39.4 0.0 collective-permute-done.8.arrived1
  39.4 2.7 %shard_map.114 = (f32[16,64,256]{2,1,0:T(8,128)S(1)}, f32[384,128]{1,0:T(8,128)S(1)}, f32[384,128]{1,0:T(8,128)S(1)}) custom-call(s32[4]{0:T(128)S(1)} %get-tuple-element.50.counts, s32[1]{0:T(128)} %get-tuple-element.51.general, f32[16,64,256]{2,1,0:T(8,128)S(1)} %get-tuple-element.66.fields.current, f32[16,64,256]{2,1,0:T(8,128)S(1)} %get-tuple-element.69.inner, ...), custom_call_target="tpu_custom_call" | custom-call | flops 1000000000 | bytes 4194304 | tf_op jit(solution)/shard_map/pallas_call | solution.py:806
  42.1 1.6 %collective-permute-start.9 = (f32[384,128]{1,0:T(8,128)S(1)}, f32[384,128]{1,0:T(8,128)S(1)}, u32[]{:S(2)}, u32[]{:S(2)}) collective-permute-start(f32[384,128]{1,0:T(8,128)S(1)} %get-tuple-element.75), channel_id=1, source_target_pairs={{0,1},{1,0},{2,3},{3,2},{4,20},{5,6},{6,5},{7,23},{8,9},{9,8},{10,... | collective-permute-start | bytes 589832 | tf_op jit(solution)/shard_map/ppermute | solution.py:832
  43.7 1.7 %collective-permute-start.10 = (f32[384,128]{1,0:T(8,128)S(1)}, f32[384,128]{1,0:T(8,128)S(1)}, u32[]{:S(2)}, u32[]{:S(2)}) collective-permute-start(f32[384,128]{1,0:T(8,128)S(1)} %get-tuple-element.76), channel_id=1, source_target_pairs={{0,16},{1,2},{2,1},{3,19},{4,5},{5,4},{6,7},{7,6},{8,24},{9,10},{1... | collective-permute-start | bytes 589832 | tf_op jit(solution)/shard_map/ppermute | solution.py:832
  45.4 3.3 %shard_map.115.inner = f32[16,64,256]{2,1,0:T(8,128)S(1)} custom-call(s32[4]{0:T(128)S(1)} %get-tuple-element.50.counts, f32[16,64,256]{2,1,0:T(8,128)S(1)} %get-tuple-element.74.fields.current, f32[16,64,256]{2,1,0:T(8,128)S(1)} %get-tuple-element.67.spectrum, f32[8,16,256]{2,1,0:T(8,128)S(1)} %get-tuple-element.60.coefs, ...), custom_call_target="tpu_custom_call" | custom-call | flops 3000000000 | bytes 4194304 | tf_op jit(solution)/shard_map/pallas_call | solution.py:806
  48.7 0.5 collective-permute-done.9.arrived0
  49.2 0.2 collective-permute-done.10.arrived1
  49.4 2.2 %shard_map.116 = (f32[4,64,256]{2,1,0:T(8,128)S(1)}, f32[4,64,256]{2,1,0:T(8,128)S(1)}, f32[4,64,256]{2,1,0:T(8,128)S(1)}, f32[4,64,256]{2,1,0:T(8,128)S(1)}) custom-call(s32[4]{0:T(128)S(1)} %get-tuple-element.50.counts, s32[1]{0:T(128)} %get-tuple-element.51.general, f32[16,64,256]{2,1,0:T(8,128)S(1)} %get-tuple-element.74.fields.current, ...), custom_call_target="tpu_custom_call" | custom-call | flops 1000000000 | bytes 4194304 | tf_op jit(solution)/shard_map/pallas_call | solution.py:806
  51.6 0.4 collective-permute-start.11
  52.0 0.4 collective-permute-start.12
  52.4 1.1 %collective-permute-start.13 = (f32[4,64,256]{2,1,0:T(8,128)S(1)}, f32[4,64,256]{2,1,0:T(8,128)S(1)}, u32[]{:S(2)}, u32[]{:S(2)}) collective-permute-start(f32[4,64,256]{2,1,0:T(8,128)S(1)} %get-tuple-element.80), channel_id=1, source_target_pairs={{0,12},{4,8},{8,4},{12,0},{1,13},{5,9},{9,5},{13,1},{2,14},{6,10},... | collective-permute-start | bytes 786440 | tf_op jit(solution)/shard_map/ppermute | solution.py:838
  53.5 0.0 collective-permute-done.11.rest_1_
  53.5 7.6 %collective-permute-done.12.rest_2_ = f32[4,64,256]{2,1,0:T(8,128)S(1)} collective-permute-done((f32[4,64,256]{2,1,0:T(8,128)S(1)}, f32[4,64,256]{2,1,0:T(8,128)S(1)}, u32[]{:S(2)}, u32[]{:S(2)}) %collective-permute-start.12) | collective-permute-done | bytes 262176 | tf_op jit(solution)/shard_map/ppermute | solution.py:838
  61.1 4.0 %collective-permute-done.13.rest_3_ = f32[4,64,256]{2,1,0:T(8,128)S(1)} collective-permute-done((f32[4,64,256]{2,1,0:T(8,128)S(1)}, f32[4,64,256]{2,1,0:T(8,128)S(1)}, u32[]{:S(2)}, u32[]{:S(2)}) %collective-permute-start.13) | collective-permute-done | bytes 262176 | tf_op jit(solution)/shard_map/ppermute | solution.py:838
  65.2 1.0 %shard_map.117 = f32[16,64,256]{2,1,0:T(8,128)} custom-call(f32[4,64,256]{2,1,0:T(8,128)S(1)} %get-tuple-element.77.rest_0_, f32[4,64,256]{2,1,0:T(8,128)S(1)} %collective-permute-done.11.rest_1_, f32[4,64,256]{2,1,0:T(8,128)S(1)} %collective-permute-done.12.rest_2_, f32[4,64,256]{2,1,0:T(8,128)S(1)} %collective-permute-done.13.rest_3_), custom_call_target="tpu_custom_call" | custom-call | flops 1000000000 | bytes 4194304 | tf_op jit(solution)/shard_map/pallas_call | solution.py:806
Async XLA Ops:
  2.5 12.1 %collective-permute-start.1 = (f32[8,64,256]{2,1,0:T(8,128)S(1)}, f32[8,64,256]{2,1,0:T(8,128)S(1)}, u32[]{:S(2)}, u32[]{:S(2)}) collective-permute-start(f32[8,64,256]{2,1,0:T(8,128)S(1)} %get-tuple-element.44.high_fields), channel_id=1, source_target_pairs={{0,4},{4,8},{8,12},{12,0},{1,5},{5,9},{9,13},{13,1},{2,6},{6,10},{... | collective-permute-start | bytes 1572872 | tf_op jit(solution)/shard_map/ppermute | solution.py:908
  3.0 11.6 %collective-permute-start = (f32[8,64,256]{2,1,0:T(8,128)S(1)}, f32[8,64,256]{2,1,0:T(8,128)S(1)}, u32[]{:S(2)}, u32[]{:S(2)}) collective-permute-start(f32[8,64,256]{2,1,0:T(8,128)S(1)} %get-tuple-element.43.low_fields.own), channel_id=1, source_target_pairs={{0,4},{4,0},{8,12},{12,8},{1,5},{5,1},{9,13},{13,9},{2,6},{6,2},{1... | collective-permute-start | bytes 1572872 | tf_op jit(solution)/shard_map/ppermute | solution.py:838
  5.6 9.0 %collective-permute-start.2 = (f32[520,128]{1,0:T(8,128)S(1)}, f32[520,128]{1,0:T(8,128)S(1)}, u32[]{:S(2)}, u32[]{:S(2)}) collective-permute-start(f32[520,128]{1,0:T(8,128)S(1)} %get-tuple-element.53), channel_id=1, source_target_pairs={{0,1},{1,0},{2,3},{3,2},{4,20},{5,6},{6,5},{7,23},{8,9},{9,8},{10,... | collective-permute-start | bytes 798728 | tf_op jit(solution)/shard_map/ppermute | solution.py:832
  7.2 7.4 %collective-permute-start.3 = (f32[520,128]{1,0:T(8,128)S(1)}, f32[520,128]{1,0:T(8,128)S(1)}, u32[]{:S(2)}, u32[]{:S(2)}) collective-permute-start(f32[520,128]{1,0:T(8,128)S(1)} %get-tuple-element.54), channel_id=1, source_target_pairs={{0,16},{1,2},{2,1},{3,19},{4,5},{5,4},{6,7},{7,6},{8,24},{9,10},{1... | collective-permute-start | bytes 798728 | tf_op jit(solution)/shard_map/ppermute | solution.py:832
  8.7 5.9 %copy-start = (f32[16,1,64,256]{3,2,1,0:T(8,128)S(1)}, f32[16,1,64,256]{3,2,1,0:T(8,128)}, u32[]{:S(2)}) copy-start(f32[16,1,64,256]{3,2,1,0:T(8,128)} %param.11) | copy-start | bytes 3145732
  16.9 2.0 %collective-permute-start.4 = (f32[4,64,256]{2,1,0:T(8,128)S(1)}, f32[4,64,256]{2,1,0:T(8,128)S(1)}, u32[]{:S(2)}, u32[]{:S(2)}) collective-permute-start(f32[4,64,256]{2,1,0:T(8,128)S(1)} %get-tuple-element.63), channel_id=1, source_target_pairs={{0,4},{4,0},{8,12},{12,8},{1,5},{5,1},{9,13},{13,9},{2,6},{6,2},{1... | collective-permute-start | bytes 786440 | tf_op jit(solution)/shard_map/ppermute | solution.py:838
  17.1 9.1 %collective-permute-start.5 = (f32[4,64,256]{2,1,0:T(8,128)S(1)}, f32[4,64,256]{2,1,0:T(8,128)S(1)}, u32[]{:S(2)}, u32[]{:S(2)}) collective-permute-start(f32[4,64,256]{2,1,0:T(8,128)S(1)} %get-tuple-element.64), channel_id=1, source_target_pairs={{0,8},{4,12},{8,0},{12,4},{1,9},{5,13},{9,1},{13,5},{2,10},{6,14},... | collective-permute-start | bytes 786440 | tf_op jit(solution)/shard_map/ppermute | solution.py:838
  17.1 13.7 %collective-permute-start.6 = (f32[4,64,256]{2,1,0:T(8,128)S(1)}, f32[4,64,256]{2,1,0:T(8,128)S(1)}, u32[]{:S(2)}, u32[]{:S(2)}) collective-permute-start(f32[4,64,256]{2,1,0:T(8,128)S(1)} %get-tuple-element.65), channel_id=1, source_target_pairs={{0,12},{4,8},{8,4},{12,0},{1,13},{5,9},{9,5},{13,1},{2,14},{6,10},... | collective-permute-start | bytes 786440 | tf_op jit(solution)/shard_map/ppermute | solution.py:838
  32.2 7.2 %collective-permute-start.7 = (f32[384,128]{1,0:T(8,128)S(1)}, f32[384,128]{1,0:T(8,128)S(1)}, u32[]{:S(2)}, u32[]{:S(2)}) collective-permute-start(f32[384,128]{1,0:T(8,128)S(1)} %get-tuple-element.70), channel_id=1, source_target_pairs={{0,1},{1,0},{2,3},{3,2},{4,20},{5,6},{6,5},{7,23},{8,9},{9,8},{10,... | collective-permute-start | bytes 589832 | tf_op jit(solution)/shard_map/ppermute | solution.py:832
  33.6 5.8 %collective-permute-start.8 = (f32[384,128]{1,0:T(8,128)S(1)}, f32[384,128]{1,0:T(8,128)S(1)}, u32[]{:S(2)}, u32[]{:S(2)}) collective-permute-start(f32[384,128]{1,0:T(8,128)S(1)} %get-tuple-element.71), channel_id=1, source_target_pairs={{0,16},{1,2},{2,1},{3,19},{4,5},{5,4},{6,7},{7,6},{8,24},{9,10},{1... | collective-permute-start | bytes 589832 | tf_op jit(solution)/shard_map/ppermute | solution.py:832
  42.1 7.1 %collective-permute-start.9 = (f32[384,128]{1,0:T(8,128)S(1)}, f32[384,128]{1,0:T(8,128)S(1)}, u32[]{:S(2)}, u32[]{:S(2)}) collective-permute-start(f32[384,128]{1,0:T(8,128)S(1)} %get-tuple-element.75), channel_id=1, source_target_pairs={{0,1},{1,0},{2,3},{3,2},{4,20},{5,6},{6,5},{7,23},{8,9},{9,8},{10,... | collective-permute-start | bytes 589832 | tf_op jit(solution)/shard_map/ppermute | solution.py:832
  43.7 5.7 %collective-permute-start.10 = (f32[384,128]{1,0:T(8,128)S(1)}, f32[384,128]{1,0:T(8,128)S(1)}, u32[]{:S(2)}, u32[]{:S(2)}) collective-permute-start(f32[384,128]{1,0:T(8,128)S(1)} %get-tuple-element.76), channel_id=1, source_target_pairs={{0,16},{1,2},{2,1},{3,19},{4,5},{5,4},{6,7},{7,6},{8,24},{9,10},{1... | collective-permute-start | bytes 589832 | tf_op jit(solution)/shard_map/ppermute | solution.py:832
  51.6 1.9 %collective-permute-start.11 = (f32[4,64,256]{2,1,0:T(8,128)S(1)}, f32[4,64,256]{2,1,0:T(8,128)S(1)}, u32[]{:S(2)}, u32[]{:S(2)}) collective-permute-start(f32[4,64,256]{2,1,0:T(8,128)S(1)} %get-tuple-element.78), channel_id=1, source_target_pairs={{0,4},{4,0},{8,12},{12,8},{1,5},{5,1},{9,13},{13,9},{2,6},{6,2},{1... | collective-permute-start | bytes 786440 | tf_op jit(solution)/shard_map/ppermute | solution.py:838
  52.0 9.2 %collective-permute-start.12 = (f32[4,64,256]{2,1,0:T(8,128)S(1)}, f32[4,64,256]{2,1,0:T(8,128)S(1)}, u32[]{:S(2)}, u32[]{:S(2)}) collective-permute-start(f32[4,64,256]{2,1,0:T(8,128)S(1)} %get-tuple-element.79), channel_id=1, source_target_pairs={{0,8},{4,12},{8,0},{12,4},{1,9},{5,13},{9,1},{13,5},{2,10},{6,14},... | collective-permute-start | bytes 786440 | tf_op jit(solution)/shard_map/ppermute | solution.py:838
  52.4 12.8 %collective-permute-start.13 = (f32[4,64,256]{2,1,0:T(8,128)S(1)}, f32[4,64,256]{2,1,0:T(8,128)S(1)}, u32[]{:S(2)}, u32[]{:S(2)}) collective-permute-start(f32[4,64,256]{2,1,0:T(8,128)S(1)} %get-tuple-element.80), channel_id=1, source_target_pairs={{0,12},{4,8},{8,4},{12,0},{1,13},{5,9},{9,5},{13,1},{2,14},{6,10},... | collective-permute-start | bytes 786440 | tf_op jit(solution)/shard_map/ppermute | solution.py:838

commit v4 on v3

--- a/solution.py
+++ b/solution.py
@@ -233,15 +233,12 @@
     blocks,
     face_blocks,
     halo_picks,
-    general,
-    counts,
+    flags,
     facing,
     high,
     low,
     wide,
 ):
-    for k in range(counts.shape[0]):
-        counts[k] = counts_in[0, k]
     iterate = Halves(low_fields, high_fields)
     samples, dofs, elems = iterate.shape
     halo = halo_picks.shape[0] // 4
@@ -294,7 +291,14 @@
     crossing = crossing + jnp.max(
         jnp.where((fifth >= elems) & (fifth < elems + halo), 1, 0)
     )
-    general[0] = crossing
+    lane = lax.broadcasted_iota(i32, flags.shape, 1)
+    line = jnp.where(lane == 0, crossing, 0)
+    skip = jnp.int32(0)
+    for k in range(counts_in.shape[1]):
+        line = jnp.where(lane == 2 + k, counts_in[0, k], line)
+    for k, re, _ in frequencies(counts_in.shape[1]):
+        skip = jnp.where(counts_in[0, k] == 1, re, skip)
+    flags[...] = jnp.where(lane == 1, skip, line)
     local_part(
         iterate,
         list(range(samples)),
@@ -353,10 +357,10 @@
     return got
 
 
-def other_sides(general, even, face_nbr, halo, body):
+def other_sides(flags, even, face_nbr, halo, body):
     elems = face_nbr.shape[1]
 
-    @pl.when(general[0] > 0)
+    @pl.when(flags[0, 0] > 0)
     def _():
         for which, (usual, base) in enumerate(sides(even, elems, halo)):
 
@@ -375,7 +379,7 @@
     return slice(row, row + dofs), slice(col, col + elems)
 
 
-def add_others(arrived, even, general, face_nbr, face_blocks, halo, half, slots, coef_row, factor, total):
+def add_others(arrived, even, flags, face_nbr, face_blocks, halo, half, slots, coef_row, factor, total):
     elems = face_nbr.shape[1]
     dofs = total.shape[1]
 
@@ -389,7 +393,7 @@
                     field = slots[t]
                     total[field] = total[field] + factor * coef_row(face, t) * got[:, cols]
 
-    other_sides(general, even, face_nbr, halo, body)
+    other_sides(flags, even, face_nbr, halo, body)
 
 
 def residual_kernel(
@@ -407,7 +411,7 @@
     face_blocks,
     halo_picks,
     facing,
-    general,
+    flags,
     *rest,
     total_steps,
     groups,
@@ -443,7 +447,7 @@
         coefs[face] = coefs[face] + coupling
         extra[...] = extra[...] + coupling
 
-    other_sides(general, even, face_nbr, halo, add_coupling)
+    other_sides(flags, even, face_nbr, halo, add_coupling)
     coefs[FACES] = coefs[FACES] + extra[...]
     volume = blocks[:, 0 : 2 * dofs][:, :dofs]
     brought = usual_halo(
@@ -459,7 +463,7 @@
     add_others(
         arrived,
         even,
-        general,
+        flags,
         face_nbr,
         face_blocks,
         halo,
@@ -554,10 +558,8 @@
     ]
 
 
-def kept_slots(counts, samples, total_steps):
-    skip = jnp.int32(0)
-    for k, re, _ in frequencies(total_steps):
-        skip = jnp.where(counts[k] == 1, re, skip)
+def kept_slots(flags, samples, total_steps):
+    skip = flags[0, 1]
     kept = total_steps - 1
     slots = []
     for t in range(samples * kept):
@@ -580,7 +582,7 @@
 
 
 def spectrum_kernel(
-    counts, coefs, send_ref, own, near, *rest, total_steps, at, groups
+    flags, coefs, send_ref, own, near, *rest, total_steps, at, groups
 ):
     arrived, (spectrum, first_w, pack0, pack1, pieces) = (
         rest[:total_steps],
@@ -613,12 +615,12 @@
                 spectrum[base + im] = imag
                 first_w[base + re] = rate_real * real - rate_imag * imag
                 first_w[base + im] = rate_real * imag + rate_imag * real
-    slots = kept_slots(counts, samples, total_steps)
+    slots = kept_slots(flags, samples, total_steps)
     pack_fields(first_w, even_slots(slots), send_ref[...], (pack0, pack1))
 
 
 def sweep_local_kernel(
-    counts,
+    flags,
     fields,
     spectrum,
     coefs,
@@ -638,7 +640,7 @@
     elems = fields.shape[2]
     samples = fields.shape[0] // total_steps
     first = my_first(samples, at, groups)
-    slots = kept_slots(counts, samples, total_steps)
+    slots = kept_slots(flags, samples, total_steps)
     row = sample_row(coefs, total_steps, first)
     if first_turn:
         halo = halo_picks.shape[0] // 4
@@ -680,8 +682,7 @@
 
 
 def sweep_update_kernel(
-    counts,
-    general,
+    flags,
     current,
     inner,
     arrived0,
@@ -707,7 +708,7 @@
     fields, dofs, elems = current.shape
     samples = fields // total_steps
     first = my_first(samples, at, groups)
-    slots = kept_slots(counts, samples, total_steps)
+    slots = kept_slots(flags, samples, total_steps)
     arrived = (arrived0, arrived1)
     halo = halo_picks.shape[0] // 4
     half = scales.shape[1]
@@ -723,7 +724,7 @@
     add_others(
         arrived,
         even,
-        general,
+        flags,
         face_nbr,
         face_blocks,
         halo,
@@ -736,7 +737,7 @@
     for s in range(samples):
         base = s * total_steps
         for i, (k, re, im) in enumerate(frequencies(total_steps)):
-            active = counts[k] > turn + 1
+            active = flags[0, 2 + k] > turn + 1
             rate_real = thetas[2 * i, s : s + 1, :]
             value, rest_real = current[base + re], total[base + re]
             change = rate_real * rest_real
@@ -788,16 +789,13 @@
 
 
 vmem = pl.BlockSpec(memory_space=pltpu.VMEM)
-smem = pl.BlockSpec(memory_space=pltpu.SMEM)
 
 
 def run(
-    kernel, inputs, outs, scratch=(), in_smem=(), out_smem=(), in_hbm=(), out_hbm=(), flops=10**9
+    kernel, inputs, outs, scratch=(), in_hbm=(), out_hbm=(), flops=10**9
 ):
-    def spec(i, small, outside=()):
-        if i in outside:
-            return pl.BlockSpec(memory_space=pltpu.HBM)
-        return smem if i in small else vmem
+    def spec(i, outside):
+        return pl.BlockSpec(memory_space=pltpu.HBM) if i in outside else vmem
 
     inputs = [
         pltpu.with_memory_space_constraint(value, pltpu.HBM) if i in in_hbm else value
@@ -806,8 +804,8 @@
     return pl.pallas_call(
         kernel,
         out_shape=[jax.ShapeDtypeStruct(*o) for o in outs],
-        in_specs=[spec(i, in_smem, in_hbm) for i in range(len(inputs))],
-        out_specs=[spec(i, out_smem, out_hbm) for i in range(len(outs))],
+        in_specs=[spec(i, in_hbm) for i in range(len(inputs))],
+        out_specs=[spec(i, out_hbm) for i in range(len(outs))],
         scratch_shapes=[pltpu.VMEM(*s) if isinstance(s, tuple) else s for s in scratch],
         compiler_params=pltpu.CompilerParams(vmem_limit_bytes=40 << 20),
         cost_estimate=pl.CostEstimate(flops=flops, bytes_accessed=1 << 22, transcendentals=0),
@@ -913,7 +911,7 @@
     blocks_wide = (FACES + 1) * dofs
     splits = lambda count: [((count, blocks_wide, elems), bf16)] * 2
     (
-        local, coefs, picks, blocks, face_blocks, halo_picks, general, counts, facing
+        local, coefs, picks, blocks, face_blocks, halo_picks, flags, facing
     ) = run(
         first_local_kernel,
         (low, high, conduct, face_nbr, grad_mats, face_mats, counts_line),
@@ -924,12 +922,10 @@
             ((2 * dofs, blocks_wide), bf16),
             ((FACES, 2 * dofs, dofs), bf16),
             ((4 * halo, 2 * elems), bf16),
-            ((1,), i32),
-            (sweep_counts.shape, i32),
+            ((1, 2 * halo), i32),
             ((2, half, 2 * halo), f32),
         ],
         splits(samples) + [((blocks_wide, 2 * dofs), f32)],
-        out_smem=(6, 7),
         flops=4 * 10**9,
     )
     groups = GROUPS if part % GROUPS == 0 else 1
@@ -952,11 +948,10 @@
             face_blocks,
             halo_picks,
             facing,
-            general,
+            flags,
         ),
         [piece] * (groups * devs) + [((FACES + 2, samples, elems), f32)],
         [(cube, f32), ((samples, elems), f32)],
-        in_smem=(14,),
     )
     fields = share * total_steps
     swept = share * (total_steps - 1)
@@ -969,17 +964,16 @@
         pieces = [time_swap(scaled[at * devs + turn], turn) for turn in range(devs)]
         spectrum, current, pack0, pack1 = run(
             functools.partial(spectrum_kernel, **mine),
-            (counts, coefs, send, low, earlier_low, *pieces),
+            (flags, coefs, send, low, earlier_low, *pieces),
             [some, some, packed, packed],
             [((total_steps, share, dofs, elems), f32)],
-            in_smem=(0,),
         )
         for turn in range(MAXS - 1):
             arrived0 = neighbour_swap(pack0, 0)
             arrived1 = neighbour_swap(pack1, 1)
             inner, *tables = run(
                 functools.partial(sweep_local_kernel, first_turn=turn == 0, **mine),
-                (counts, current, spectrum, coefs, picks, blocks, halo_picks),
+                (flags, current, spectrum, coefs, picks, blocks, halo_picks),
                 [some]
                 + [
                     ((2 * len(frequencies(total_steps)), share, elems), f32),
@@ -987,15 +981,13 @@
                 ]
                 * (turn == 0),
                 [some] + splits(swept),
-                in_smem=(0,),
-                flops=3 * 10**9 // groups,
+                    flops=3 * 10**9 // groups,
             )
             if turn == 0:
                 thetas, scales = tables
             last = turn == MAXS - 2
             inputs = (
-                counts,
-                general,
+                flags,
                 current,
                 inner,
                 arrived0,
@@ -1010,7 +1002,7 @@
             kernel = functools.partial(sweep_update_kernel, turn=turn, last=last, **mine)
             if last:
                 series = run(
-                    kernel, inputs, [piece] * devs, [some, some], in_smem=(0, 1)
+                    kernel, inputs, [piece] * devs, [some, some]
                 )
             else:
                 current, pack0, pack1 = run(
@@ -1018,7 +1010,6 @@
                     inputs + (send,),
                     [some, packed, packed],
                     [some],
-                    in_smem=(0, 1),
                 )
         restored += [time_swap(series[turn], turn) for turn in range(devs)]
     (out,) = run(

time: 66.9 us -> 63.6 us (0.951)
  Pallas kernels: 23.1 us -> 18.5 us
  waiting for transfers between devices: 26.6 us -> 27.9 us
    pallas_call x9, Pallas kernels: 23.1 us -> 18.5 us  [run(): pl.pallas_call(kernel, out_shape=[jax.ShapeDtypeStruct(*o) for o in outs]...]
    ppermute x6, waiting for transfers between devices: 2.95 us -> 4.21 us  [neighbour_swap(): return lax.ppermute(value, axes, pairs)]
  transfers between devices with their start and end apart: 14 -> 14, of which waited for: 8 -> 8; matrix products, arithmetic and copies ran while one was open for 0% -> 0% of each run, Pallas kernels for 17% -> 16%
where the time goes in v4:
time: 63.6 us; the launch traced here: 63.1 us
  waiting for transfers between devices  27.9 us (44%)
  Pallas kernels  18.5 us (29%)
  starting transfers between devices  16.4 us (26%)
    ppermute x7, waiting for transfers between devices, time_swap(): return value if turn == 0 else lax.ppermute(value, 'tm', pairs)  23.7 us
    pallas_call x9, Pallas kernels, run(): pl.pallas_call(kernel, out_shape=[jax.ShapeDtypeStruct(*o) for o in outs]...  18.5 us
    ppermute x6, starting transfers between devices, neighbour_swap(): return lax.ppermute(value, axes, pairs)  9.43 us
    ppermute x7, starting transfers between devices, time_swap(): return value if turn == 0 else lax.ppermute(value, 'tm', pairs)  6.48 us
    ppermute x6, waiting for transfers between devices, neighbour_swap(): return lax.ppermute(value, axes, pairs)  4.21 us
  transfers between devices with their start and end apart: 14, of which 8 were waited for; matrix products, arithmetic and copies ran while one was open for 0% of the time, Pallas kernels for 16%

profile of v4, /device:TPU:0, one launch (start us, length us, event | category | flops | bytes accessed | tf_op | source)
XLA Modules:
  0.0 63.1 jit_solution(15592851134722911918)
XLA Ops:
  0.0 2.5 %shard_map.109 = (f32[520,128]{1,0:T(8,128)S(1)}, f32[520,128]{1,0:T(8,128)S(1)}, bf16[512,256]{1,0:T(8,128)(2,1)S(1)}, f32[16,256]{1,0:T(8,128)S(1)}, f32[8,64,...) custom-call(f32[16,64,256]{2,1,0:T(8,128)} %bitcast.10, ...), custom_call_target="tpu_custom_call" | custom-call | flops 1000000000 | bytes 4194304 | tf_op jit(solution)/shard_map/pallas_call | solution.py:804
  2.5 0.5 collective-permute-start.1
  3.0 2.6 %collective-permute-start = (f32[8,64,256]{2,1,0:T(8,128)S(1)}, f32[8,64,256]{2,1,0:T(8,128)S(1)}, u32[]{:S(2)}, u32[]{:S(2)}) collective-permute-start(f32[8,64,256]{2,1,0:T(8,128)S(1)} %get-tuple-element.42.low_fields.own), channel_id=1, source_target_pairs={{0,4},{4,0},{8,12},{12,8},{1,5},{5,1},{9,13},{13,9},{2,6},{6,2},{1... | collective-permute-start | bytes 1572872 | tf_op jit(solution)/shard_map/ppermute | solution.py:836
  5.6 1.6 %collective-permute-start.2 = (f32[520,128]{1,0:T(8,128)S(1)}, f32[520,128]{1,0:T(8,128)S(1)}, u32[]{:S(2)}, u32[]{:S(2)}) collective-permute-start(f32[520,128]{1,0:T(8,128)S(1)} %get-tuple-element.51), channel_id=1, source_target_pairs={{0,1},{1,0},{2,3},{3,2},{4,20},{5,6},{6,5},{7,23},{8,9},{9,8},{10,... | collective-permute-start | bytes 798728 | tf_op jit(solution)/shard_map/ppermute | solution.py:830
  7.2 1.5 %collective-permute-start.3 = (f32[520,128]{1,0:T(8,128)S(1)}, f32[520,128]{1,0:T(8,128)S(1)}, u32[]{:S(2)}, u32[]{:S(2)}) collective-permute-start(f32[520,128]{1,0:T(8,128)S(1)} %get-tuple-element.52), channel_id=1, source_target_pairs={{0,16},{1,2},{2,1},{3,19},{4,5},{5,4},{6,7},{7,6},{8,24},{9,10},{1... | collective-permute-start | bytes 798728 | tf_op jit(solution)/shard_map/ppermute | solution.py:830
  8.7 0.0 copy-start
  8.7 4.0 %shard_map.110 = (f32[16,64,256]{2,1,0:T(8,128)S(1)}, f32[8,16,256]{2,1,0:T(8,128)S(1)}, bf16[256,1536]{1,0:T(8,128)(2,1)S(1)}, bf16[128,448]{1,0:T(8,128)(2,1)S...) custom-call(f32[8,64,256]{2,1,0:T(8,128)S(1)} %get-tuple-element.42., ...), custom_call_target="tpu_custom_call" | custom-call | flops 4000000000 | bytes 4194304 | tf_op jit(solution)/shard_map/pallas_call | solution.py:804
  12.7 1.9 %collective-permute-done.2.arrived0 = f32[520,128]{1,0:T(8,128)S(1)} collective-permute-done((f32[520,128]{1,0:T(8,128)S(1)}, f32[520,128]{1,0:T(8,128)S(1)}, u32[]{:S(2)}, u32[]{:S(2)}) %collective-permute-start.2) | collective-permute-done | bytes 266272 | tf_op jit(solution)/shard_map/ppermute | solution.py:830
  14.6 0.0 collective-permute-done.3.arrived1
  14.6 0.0 collective-permute-done.1.earlier_high
  14.6 0.0 collective-permute-done.earlier_low.near
  14.6 0.0 copy-done
  14.6 1.7 %shard_map.111 = (f32[4,64,256]{2,1,0:T(8,128)S(1)}, f32[4,64,256]{2,1,0:T(8,128)S(1)}, f32[4,64,256]{2,1,0:T(8,128)S(1)}, f32[4,64,256]{2,1,0:T(8,128)S(1)}, f32[8,16,256]{2,1,0:T(8,128)S(1)}) custom-call(f32[16,64,256]{2,1,0:T(8,128)S(1)} %bitcast.9, f32[8,64,256]{2,1,0:T(8,128)S(1)} %get-tuple-element.42.low_fields.own, ...), custom_call_target="tpu_custom_call" | custom-call | flops 1000000000 | bytes 4194304 | tf_op jit(solution)/shard_map/pallas_call | solution.py:804
  16.3 0.2 collective-permute-start.4
  16.4 0.1 collective-permute-start.5
  16.5 1.7 %collective-permute-start.6 = (f32[4,64,256]{2,1,0:T(8,128)S(1)}, f32[4,64,256]{2,1,0:T(8,128)S(1)}, u32[]{:S(2)}, u32[]{:S(2)}) collective-permute-start(f32[4,64,256]{2,1,0:T(8,128)S(1)} %get-tuple-element.63), channel_id=1, source_target_pairs={{0,12},{4,8},{8,4},{12,0},{1,13},{5,9},{9,5},{13,1},{2,14},{6,10},... | collective-permute-start | bytes 786440 | tf_op jit(solution)/shard_map/ppermute | solution.py:836
  18.2 0.0 collective-permute-done.4.rest_1_
  18.2 7.3 %collective-permute-done.5.rest_2_ = f32[4,64,256]{2,1,0:T(8,128)S(1)} collective-permute-done((f32[4,64,256]{2,1,0:T(8,128)S(1)}, f32[4,64,256]{2,1,0:T(8,128)S(1)}, u32[]{:S(2)}, u32[]{:S(2)}) %collective-permute-start.5) | collective-permute-done | bytes 262176 | tf_op jit(solution)/shard_map/ppermute | solution.py:836
  25.6 4.7 %collective-permute-done.6.rest_3_ = f32[4,64,256]{2,1,0:T(8,128)S(1)} collective-permute-done((f32[4,64,256]{2,1,0:T(8,128)S(1)}, f32[4,64,256]{2,1,0:T(8,128)S(1)}, u32[]{:S(2)}, u32[]{:S(2)}) %collective-permute-start.6) | collective-permute-done | bytes 262176 | tf_op jit(solution)/shard_map/ppermute | solution.py:836
  30.2 0.8 %shard_map.112 = (f32[16,64,256]{2,1,0:T(8,128)S(1)}, f32[16,64,256]{2,1,0:T(8,128)S(1)}, f32[384,128]{1,0:T(8,128)S(1)}, f32[384,128]{1,0:T(8,128)S(1)}) custom-call(s32[1,128]{1,0:T(1,128)S(1)} %get-tuple-element.49.flags, f32[8,16,256]{2,1,0:T(8,128)S(1)} %get-tuple-element.58.coefs, bf16[512,256]{1,0:T(8,128)(2,1)S(1)} %get-tuple-element.59.send_ref.rest_0_, ...), custom_call_target="tpu_custom_call" | custom-call | flops 1000000000 | bytes 4194304 | tf_op jit(solution)/shard_map/pallas_call | solution.py:804
  31.1 1.5 %collective-permute-start.7 = (f32[384,128]{1,0:T(8,128)S(1)}, f32[384,128]{1,0:T(8,128)S(1)}, u32[]{:S(2)}, u32[]{:S(2)}) collective-permute-start(f32[384,128]{1,0:T(8,128)S(1)} %get-tuple-element.68), channel_id=1, source_target_pairs={{0,1},{1,0},{2,3},{3,2},{4,20},{5,6},{6,5},{7,23},{8,9},{9,8},{10,... | collective-permute-start | bytes 589832 | tf_op jit(solution)/shard_map/ppermute | solution.py:830
  32.6 1.5 %collective-permute-start.8 = (f32[384,128]{1,0:T(8,128)S(1)}, f32[384,128]{1,0:T(8,128)S(1)}, u32[]{:S(2)}, u32[]{:S(2)}) collective-permute-start(f32[384,128]{1,0:T(8,128)S(1)} %get-tuple-element.69), channel_id=1, source_target_pairs={{0,16},{1,2},{2,1},{3,19},{4,5},{5,4},{6,7},{7,6},{8,24},{9,10},{1... | collective-permute-start | bytes 589832 | tf_op jit(solution)/shard_map/ppermute | solution.py:830
  34.1 3.0 %shard_map.113 = (f32[16,64,256]{2,1,0:T(8,128)S(1)}, f32[6,4,256]{2,1,0:T(4,128)S(1)}, f32[2,6,128]{2,1,0:T(8,128)S(1)}) custom-call(s32[1,128]{1,0:T(1,128)S(1)} %get-tuple-element.49.flags, f32[16,64,256]{2,1,0:T(8,128)S(1)} %get-tuple-element.64.fields.current, f32[16,64,256]{2,1,0:T(8,128)S(1)} %get-tuple-element.65.spectrum, ...), custom_call_target="tpu_custom_call" | custom-call | flops 3000000000 | bytes 4194304 | tf_op jit(solution)/shard_map/pallas_call | solution.py:804
  37.1 1.2 %collective-permute-done.7.arrived0 = f32[384,128]{1,0:T(8,128)S(1)} collective-permute-done((f32[384,128]{1,0:T(8,128)S(1)}, f32[384,128]{1,0:T(8,128)S(1)}, u32[]{:S(2)}, u32[]{:S(2)}) %collective-permute-start.7) | collective-permute-done | bytes 196640 | tf_op jit(solution)/shard_map/ppermute | solution.py:830
  38.3 0.0 collective-permute-done.8.arrived1
  38.3 1.5 %shard_map.114 = (f32[16,64,256]{2,1,0:T(8,128)S(1)}, f32[384,128]{1,0:T(8,128)S(1)}, f32[384,128]{1,0:T(8,128)S(1)}) custom-call(s32[1,128]{1,0:T(1,128)S(1)} %get-tuple-element.49.flags, f32[16,64,256]{2,1,0:T(8,128)S(1)} %get-tuple-element.64.fields.current, f32[16,64,256]{2,1,0:T(8,128)S(1)} %get-tuple-element.67.inner, ...), custom_call_target="tpu_custom_call" | custom-call | flops 1000000000 | bytes 4194304 | tf_op jit(solution)/shard_map/pallas_call | solution.py:804
  39.9 1.6 %collective-permute-start.9 = (f32[384,128]{1,0:T(8,128)S(1)}, f32[384,128]{1,0:T(8,128)S(1)}, u32[]{:S(2)}, u32[]{:S(2)}) collective-permute-start(f32[384,128]{1,0:T(8,128)S(1)} %get-tuple-element.73), channel_id=1, source_target_pairs={{0,1},{1,0},{2,3},{3,2},{4,20},{5,6},{6,5},{7,23},{8,9},{9,8},{10,... | collective-permute-start | bytes 589832 | tf_op jit(solution)/shard_map/ppermute | solution.py:830
  41.5 1.7 %collective-permute-start.10 = (f32[384,128]{1,0:T(8,128)S(1)}, f32[384,128]{1,0:T(8,128)S(1)}, u32[]{:S(2)}, u32[]{:S(2)}) collective-permute-start(f32[384,128]{1,0:T(8,128)S(1)} %get-tuple-element.74), channel_id=1, source_target_pairs={{0,16},{1,2},{2,1},{3,19},{4,5},{5,4},{6,7},{7,6},{8,24},{9,10},{1... | collective-permute-start | bytes 589832 | tf_op jit(solution)/shard_map/ppermute | solution.py:830
  43.2 2.9 %shard_map.115.inner = f32[16,64,256]{2,1,0:T(8,128)S(1)} custom-call(s32[1,128]{1,0:T(1,128)S(1)} %get-tuple-element.49.flags, f32[16,64,256]{2,1,0:T(8,128)S(1)} %get-tuple-element.72.fields.current, f32[16,64,256]{2,1,0:T(8,128)S(1)} %get-tuple-element.65.spectrum, f32[8,16,256]{2,1,0:T(8,128)S(1)} %get-tuple-element.58.coefs, ...), custom_call_target="tpu_custom_call" | custom-call | flops 3000000000 | bytes 4194304 | tf_op jit(solution)/shard_map/pallas_call | solution.py:804
  46.1 0.9 %collective-permute-done.9.arrived0 = f32[384,128]{1,0:T(8,128)S(1)} collective-permute-done((f32[384,128]{1,0:T(8,128)S(1)}, f32[384,128]{1,0:T(8,128)S(1)}, u32[]{:S(2)}, u32[]{:S(2)}) %collective-permute-start.9) | collective-permute-done | bytes 196640 | tf_op jit(solution)/shard_map/ppermute | solution.py:830
  47.0 0.2 collective-permute-done.10.arrived1
  47.2 1.1 %shard_map.116 = (f32[4,64,256]{2,1,0:T(8,128)S(1)}, f32[4,64,256]{2,1,0:T(8,128)S(1)}, f32[4,64,256]{2,1,0:T(8,128)S(1)}, f32[4,64,256]{2,1,0:T(8,128)S(1)}) custom-call(s32[1,128]{1,0:T(1,128)S(1)} %get-tuple-element.49.flags, f32[16,64,256]{2,1,0:T(8,128)S(1)} %get-tuple-element.72.fields.current, f32[16,64,256]{2,1,0:T(8,128)S(1)} %shard_map.115.inner, ...), custom_call_target="tpu_custom_call" | custom-call | flops 1000000000 | bytes 4194304 | tf_op jit(solution)/shard_map/pallas_call | solution.py:804
  48.3 0.4 collective-permute-start.11
  48.7 0.5 collective-permute-start.12
  49.2 1.1 %collective-permute-start.13 = (f32[4,64,256]{2,1,0:T(8,128)S(1)}, f32[4,64,256]{2,1,0:T(8,128)S(1)}, u32[]{:S(2)}, u32[]{:S(2)}) collective-permute-start(f32[4,64,256]{2,1,0:T(8,128)S(1)} %get-tuple-element.78), channel_id=1, source_target_pairs={{0,12},{4,8},{8,4},{12,0},{1,13},{5,9},{9,5},{13,1},{2,14},{6,10},... | collective-permute-start | bytes 786440 | tf_op jit(solution)/shard_map/ppermute | solution.py:836
  50.2 0.0 collective-permute-done.11.rest_1_
  50.2 7.7 %collective-permute-done.12.rest_2_ = f32[4,64,256]{2,1,0:T(8,128)S(1)} collective-permute-done((f32[4,64,256]{2,1,0:T(8,128)S(1)}, f32[4,64,256]{2,1,0:T(8,128)S(1)}, u32[]{:S(2)}, u32[]{:S(2)}) %collective-permute-start.12) | collective-permute-done | bytes 262176 | tf_op jit(solution)/shard_map/ppermute | solution.py:836
  57.9 4.0 %collective-permute-done.13.rest_3_ = f32[4,64,256]{2,1,0:T(8,128)S(1)} collective-permute-done((f32[4,64,256]{2,1,0:T(8,128)S(1)}, f32[4,64,256]{2,1,0:T(8,128)S(1)}, u32[]{:S(2)}, u32[]{:S(2)}) %collective-permute-start.13) | collective-permute-done | bytes 262176 | tf_op jit(solution)/shard_map/ppermute | solution.py:836
  61.9 1.0 %shard_map.117 = f32[16,64,256]{2,1,0:T(8,128)} custom-call(f32[4,64,256]{2,1,0:T(8,128)S(1)} %get-tuple-element.75.rest_0_, f32[4,64,256]{2,1,0:T(8,128)S(1)} %collective-permute-done.11.rest_1_, f32[4,64,256]{2,1,0:T(8,128)S(1)} %collective-permute-done.12.rest_2_, f32[4,64,256]{2,1,0:T(8,128)S(1)} %collective-permute-done.13.rest_3_), custom_call_target="tpu_custom_call" | custom-call | flops 1000000000 | bytes 4194304 | tf_op jit(solution)/shard_map/pallas_call | solution.py:804
Async XLA Ops:
  2.5 12.1 %collective-permute-start.1 = (f32[8,64,256]{2,1,0:T(8,128)S(1)}, f32[8,64,256]{2,1,0:T(8,128)S(1)}, u32[]{:S(2)}, u32[]{:S(2)}) collective-permute-start(f32[8,64,256]{2,1,0:T(8,128)S(1)} %get-tuple-element.43.high_fields), channel_id=1, source_target_pairs={{0,4},{4,8},{8,12},{12,0},{1,5},{5,9},{9,13},{13,1},{2,6},{6,10},{... | collective-permute-start | bytes 1572872 | tf_op jit(solution)/shard_map/ppermute | solution.py:906
  3.0 11.6 %collective-permute-start = (f32[8,64,256]{2,1,0:T(8,128)S(1)}, f32[8,64,256]{2,1,0:T(8,128)S(1)}, u32[]{:S(2)}, u32[]{:S(2)}) collective-permute-start(f32[8,64,256]{2,1,0:T(8,128)S(1)} %get-tuple-element.42.low_fields.own), channel_id=1, source_target_pairs={{0,4},{4,0},{8,12},{12,8},{1,5},{5,1},{9,13},{13,9},{2,6},{6,2},{1... | collective-permute-start | bytes 1572872 | tf_op jit(solution)/shard_map/ppermute | solution.py:836
  5.6 9.0 %collective-permute-start.2 = (f32[520,128]{1,0:T(8,128)S(1)}, f32[520,128]{1,0:T(8,128)S(1)}, u32[]{:S(2)}, u32[]{:S(2)}) collective-permute-start(f32[520,128]{1,0:T(8,128)S(1)} %get-tuple-element.51), channel_id=1, source_target_pairs={{0,1},{1,0},{2,3},{3,2},{4,20},{5,6},{6,5},{7,23},{8,9},{9,8},{10,... | collective-permute-start | bytes 798728 | tf_op jit(solution)/shard_map/ppermute | solution.py:830
  7.2 7.4 %collective-permute-start.3 = (f32[520,128]{1,0:T(8,128)S(1)}, f32[520,128]{1,0:T(8,128)S(1)}, u32[]{:S(2)}, u32[]{:S(2)}) collective-permute-start(f32[520,128]{1,0:T(8,128)S(1)} %get-tuple-element.52), channel_id=1, source_target_pairs={{0,16},{1,2},{2,1},{3,19},{4,5},{5,4},{6,7},{7,6},{8,24},{9,10},{1... | collective-permute-start | bytes 798728 | tf_op jit(solution)/shard_map/ppermute | solution.py:830
  8.7 5.9 %copy-start = (f32[16,1,64,256]{3,2,1,0:T(8,128)S(1)}, f32[16,1,64,256]{3,2,1,0:T(8,128)}, u32[]{:S(2)}) copy-start(f32[16,1,64,256]{3,2,1,0:T(8,128)} %param.11) | copy-start | bytes 3145732
  16.3 2.0 %collective-permute-start.4 = (f32[4,64,256]{2,1,0:T(8,128)S(1)}, f32[4,64,256]{2,1,0:T(8,128)S(1)}, u32[]{:S(2)}, u32[]{:S(2)}) collective-permute-start(f32[4,64,256]{2,1,0:T(8,128)S(1)} %get-tuple-element.61), channel_id=1, source_target_pairs={{0,4},{4,0},{8,12},{12,8},{1,5},{5,1},{9,13},{13,9},{2,6},{6,2},{1... | collective-permute-start | bytes 786440 | tf_op jit(solution)/shard_map/ppermute | solution.py:836
  16.4 9.1 %collective-permute-start.5 = (f32[4,64,256]{2,1,0:T(8,128)S(1)}, f32[4,64,256]{2,1,0:T(8,128)S(1)}, u32[]{:S(2)}, u32[]{:S(2)}) collective-permute-start(f32[4,64,256]{2,1,0:T(8,128)S(1)} %get-tuple-element.62), channel_id=1, source_target_pairs={{0,8},{4,12},{8,0},{12,4},{1,9},{5,13},{9,1},{13,5},{2,10},{6,14},... | collective-permute-start | bytes 786440 | tf_op jit(solution)/shard_map/ppermute | solution.py:836
  16.5 13.7 %collective-permute-start.6 = (f32[4,64,256]{2,1,0:T(8,128)S(1)}, f32[4,64,256]{2,1,0:T(8,128)S(1)}, u32[]{:S(2)}, u32[]{:S(2)}) collective-permute-start(f32[4,64,256]{2,1,0:T(8,128)S(1)} %get-tuple-element.63), channel_id=1, source_target_pairs={{0,12},{4,8},{8,4},{12,0},{1,13},{5,9},{9,5},{13,1},{2,14},{6,10},... | collective-permute-start | bytes 786440 | tf_op jit(solution)/shard_map/ppermute | solution.py:836
  31.1 7.2 %collective-permute-start.7 = (f32[384,128]{1,0:T(8,128)S(1)}, f32[384,128]{1,0:T(8,128)S(1)}, u32[]{:S(2)}, u32[]{:S(2)}) collective-permute-start(f32[384,128]{1,0:T(8,128)S(1)} %get-tuple-element.68), channel_id=1, source_target_pairs={{0,1},{1,0},{2,3},{3,2},{4,20},{5,6},{6,5},{7,23},{8,9},{9,8},{10,... | collective-permute-start | bytes 589832 | tf_op jit(solution)/shard_map/ppermute | solution.py:830
  32.6 5.7 %collective-permute-start.8 = (f32[384,128]{1,0:T(8,128)S(1)}, f32[384,128]{1,0:T(8,128)S(1)}, u32[]{:S(2)}, u32[]{:S(2)}) collective-permute-start(f32[384,128]{1,0:T(8,128)S(1)} %get-tuple-element.69), channel_id=1, source_target_pairs={{0,16},{1,2},{2,1},{3,19},{4,5},{5,4},{6,7},{7,6},{8,24},{9,10},{1... | collective-permute-start | bytes 589832 | tf_op jit(solution)/shard_map/ppermute | solution.py:830
  39.9 7.1 %collective-permute-start.9 = (f32[384,128]{1,0:T(8,128)S(1)}, f32[384,128]{1,0:T(8,128)S(1)}, u32[]{:S(2)}, u32[]{:S(2)}) collective-permute-start(f32[384,128]{1,0:T(8,128)S(1)} %get-tuple-element.73), channel_id=1, source_target_pairs={{0,1},{1,0},{2,3},{3,2},{4,20},{5,6},{6,5},{7,23},{8,9},{9,8},{10,... | collective-permute-start | bytes 589832 | tf_op jit(solution)/shard_map/ppermute | solution.py:830
  41.5 5.7 %collective-permute-start.10 = (f32[384,128]{1,0:T(8,128)S(1)}, f32[384,128]{1,0:T(8,128)S(1)}, u32[]{:S(2)}, u32[]{:S(2)}) collective-permute-start(f32[384,128]{1,0:T(8,128)S(1)} %get-tuple-element.74), channel_id=1, source_target_pairs={{0,16},{1,2},{2,1},{3,19},{4,5},{5,4},{6,7},{7,6},{8,24},{9,10},{1... | collective-permute-start | bytes 589832 | tf_op jit(solution)/shard_map/ppermute | solution.py:830
  48.3 1.9 %collective-permute-start.11 = (f32[4,64,256]{2,1,0:T(8,128)S(1)}, f32[4,64,256]{2,1,0:T(8,128)S(1)}, u32[]{:S(2)}, u32[]{:S(2)}) collective-permute-start(f32[4,64,256]{2,1,0:T(8,128)S(1)} %get-tuple-element.76), channel_id=1, source_target_pairs={{0,4},{4,0},{8,12},{12,8},{1,5},{5,1},{9,13},{13,9},{2,6},{6,2},{1... | collective-permute-start | bytes 786440 | tf_op jit(solution)/shard_map/ppermute | solution.py:836
  48.7 9.2 %collective-permute-start.12 = (f32[4,64,256]{2,1,0:T(8,128)S(1)}, f32[4,64,256]{2,1,0:T(8,128)S(1)}, u32[]{:S(2)}, u32[]{:S(2)}) collective-permute-start(f32[4,64,256]{2,1,0:T(8,128)S(1)} %get-tuple-element.77), channel_id=1, source_target_pairs={{0,8},{4,12},{8,0},{12,4},{1,9},{5,13},{9,1},{13,5},{2,10},{6,14},... | collective-permute-start | bytes 786440 | tf_op jit(solution)/shard_map/ppermute | solution.py:836
  49.2 12.7 %collective-permute-start.13 = (f32[4,64,256]{2,1,0:T(8,128)S(1)}, f32[4,64,256]{2,1,0:T(8,128)S(1)}, u32[]{:S(2)}, u32[]{:S(2)}) collective-permute-start(f32[4,64,256]{2,1,0:T(8,128)S(1)} %get-tuple-element.78), channel_id=1, source_target_pairs={{0,12},{4,8},{8,4},{12,0},{1,13},{5,9},{9,5},{13,1},{2,14},{6,10},... | collective-permute-start | bytes 786440 | tf_op jit(solution)/shard_map/ppermute | solution.py:836

commit v5 on v4

--- a/solution.py
+++ b/solution.py
@@ -15,7 +15,7 @@
 highest = lax.Precision.HIGHEST
 f32, bf16, i32 = jnp.float32, jnp.bfloat16, jnp.int32
 FACES = 6
-GROUPS = 1
+GROUPS = 2
 
 
 def dot(a, b):
@@ -159,7 +159,7 @@
     ]
     for copy in small + large + later:
         copy.start()
-    for copy in small:
+    for copy in small + large:
         copy.wait()
     even = space_even()
     down = jnp.concatenate([halo_send[0:1, :]] * 2, axis=1)
@@ -185,9 +185,7 @@
     got = exact_select(jnp.concatenate([conduct[:half], conduct[half:]], axis=1), send)
     pack0[half * dofs :, :] = got[:, : 2 * halo]
     pack1[half * dofs :, :] = got[:, 2 * halo :]
-    for at, j in enumerate(range(0, half, size)):
-        large[2 * at].wait()
-        large[2 * at + 1].wait()
+    for j in range(0, half, size):
         left = list(range(j, j + size))
         pack_group(iterate, left, [half + i for i in left], send, j, (pack0, pack1))
     for copy in later:
@@ -558,14 +556,23 @@
     ]
 
 
-def kept_slots(flags, samples, total_steps):
+def slot_order(samples, total_steps, inner):
+    size = samples // inner
+    lists = [
+        [(g * size + s, i) for s in range(size) for i in range(total_steps - 1)]
+        for g in range(inner)
+    ]
+    if inner == 1:
+        return lists[0]
+    middle = len(lists[0]) // 2
+    return [pair for part in lists for pair in part[:middle]] + [
+        pair for part in lists for pair in part[middle:]
+    ]
+
+
+def kept_slots(flags, order, total_steps):
     skip = flags[0, 1]
-    kept = total_steps - 1
-    slots = []
-    for t in range(samples * kept):
-        s, i = divmod(t, kept)
-        slots.append(s * total_steps + jnp.where(skip <= i, i + 1, i))
-    return slots
+    return [s * total_steps + jnp.where(skip <= i, i + 1, i) for s, i in order]
 
 
 def even_slots(slots):
@@ -576,18 +583,14 @@
     return (lax.axis_index("tm") * groups + at) * samples
 
 
-def sample_row(coefs, total_steps, first):
-    kept = total_steps - 1
-    return lambda f, t: coefs[f, pl.ds(first + t // kept, 1), :]
+def sample_row(coefs, order, first):
+    return lambda f, t: coefs[f, pl.ds(first + order[t][0], 1), :]
 
 
 def spectrum_kernel(
     flags, coefs, send_ref, own, near, *rest, total_steps, at, groups
 ):
-    arrived, (spectrum, first_w, pack0, pack1, pieces) = (
-        rest[:total_steps],
-        rest[total_steps:],
-    )
+    arrived, (spectrum, first_w, pack0, pack1, pieces) = rest[:total_steps], rest[-5:]
     samples = arrived[0].shape[0]
     first = my_first(samples, at, groups)
     rank = lax.axis_index("tm")
@@ -615,14 +618,13 @@
                 spectrum[base + im] = imag
                 first_w[base + re] = rate_real * real - rate_imag * imag
                 first_w[base + im] = rate_real * imag + rate_imag * real
-    slots = kept_slots(flags, samples, total_steps)
+    slots = kept_slots(flags, slot_order(samples, total_steps, 1), total_steps)
     pack_fields(first_w, even_slots(slots), send_ref[...], (pack0, pack1))
 
 
 def sweep_local_kernel(
     flags,
     fields,
-    spectrum,
     coefs,
     picks,
     blocks,
@@ -632,7 +634,9 @@
     at,
     groups,
     first_turn,
+    inner,
 ):
+    spectra, rest = rest[:inner], rest[inner:]
     if first_turn:
         out, thetas, scales, total, high, low = rest
     else:
@@ -640,8 +644,9 @@
     elems = fields.shape[2]
     samples = fields.shape[0] // total_steps
     first = my_first(samples, at, groups)
-    slots = kept_slots(flags, samples, total_steps)
-    row = sample_row(coefs, total_steps, first)
+    order = slot_order(samples, total_steps, inner)
+    slots = kept_slots(flags, order, total_steps)
+    row = sample_row(coefs, order, first)
     if first_turn:
         halo = halo_picks.shape[0] // 4
         half = scales.shape[1]
@@ -668,14 +673,16 @@
     local_part(fields, slots, row, picks, blocks, total, high, low)
     for s in range(samples):
         base = s * total_steps
+        spectrum = spectra[s // (samples // inner)]
+        own = s % (samples // inner) * total_steps
         for k, re, im in frequencies(total_steps):
             shift_real, shift_imag = shift_of(k, total_steps)
             value = fields[base + re]
-            kept = spectrum[base + re] - (shift_real * value + time_step * total[base + re])
+            kept = spectrum[own + re] - (shift_real * value + time_step * total[base + re])
             if im is not None:
                 other = fields[base + im]
                 kept = kept + shift_imag * other
-                out[base + im] = spectrum[base + im] - (
+                out[base + im] = spectrum[own + im] - (
                     shift_real * other + shift_imag * value + time_step * total[base + im]
                 )
             out[base + re] = kept
@@ -683,72 +690,87 @@
 
 def sweep_update_kernel(
     flags,
-    current,
-    inner,
-    arrived0,
-    arrived1,
     coefs,
     face_nbr,
     face_blocks,
     halo_picks,
-    thetas,
-    scales,
     *rest,
     turn,
     total_steps,
     last,
-    at,
-    groups,
+    parts,
+    tables,
 ):
     even = space_even()
+    take = lambda count: (rest[:count], rest[count:])
+    currents, rest = take(parts)
+    inners, rest = take(parts)
+    arrived0, rest = take(parts)
+    arrived1, rest = take(parts)
+    thetas, rest = take(tables)
+    scale_refs, rest = take(tables)
     if last:
         outs, (total, solved) = rest[:total_steps], rest[total_steps:]
     else:
         send_ref, solved, pack0, pack1, total = rest
-    fields, dofs, elems = current.shape
-    samples = fields // total_steps
-    first = my_first(samples, at, groups)
-    slots = kept_slots(flags, samples, total_steps)
-    arrived = (arrived0, arrived1)
+    fields, dofs, elems = currents[0].shape
+    part_samples = fields // total_steps
+    samples = parts * part_samples
+    table_samples = samples // tables
+    first = my_first(samples, 0, 1)
     halo = halo_picks.shape[0] // 4
-    half = scales.shape[1]
     usual = sides(even, elems, halo)
-    brought = usual_halo(
-        arrived,
-        [scales[w] for w in range(2)],
-        [face_blocks[usual[w][0]] for w in range(2)],
-        halo_picks[...],
-    )
-    for t, field in enumerate(slots):
-        total[field] = inner[field] - brought[pair_place(t, half, dofs, elems)]
-    add_others(
-        arrived,
-        even,
-        flags,
-        face_nbr,
-        face_blocks,
-        halo,
-        half,
-        slots,
-        sample_row(coefs, total_steps, first),
-        -time_step,
-        total,
-    )
+    for part in range(parts):
+        per = tables // parts
+        mine = scale_refs[part * per : (part + 1) * per]
+        scales = [jnp.concatenate([ref[w] for ref in mine], axis=0) for w in range(2)]
+        half = scales[0].shape[0]
+        arrived = (arrived0[part], arrived1[part])
+        order = slot_order(part_samples, total_steps, per)
+        slots = kept_slots(flags, order, total_steps)
+        brought = usual_halo(
+            arrived,
+            scales,
+            [face_blocks[usual[w][0]] for w in range(2)],
+            halo_picks[...],
+        )
+        for t, field in enumerate(slots):
+            total[part * fields + field] = (
+                inners[part][field] - brought[pair_place(t, half, dofs, elems)]
+            )
+        add_others(
+            arrived,
+            even,
+            flags,
+            face_nbr,
+            face_blocks,
+            halo,
+            half,
+            [part * fields + field for field in slots],
+            sample_row(coefs, order, first + part * part_samples),
+            -time_step,
+            total,
+        )
     for s in range(samples):
         base = s * total_steps
+        current = currents[s // part_samples]
+        own = s % part_samples * total_steps
+        theta = thetas[s // table_samples]
+        line = slice(s % table_samples, s % table_samples + 1)
         for i, (k, re, im) in enumerate(frequencies(total_steps)):
             active = flags[0, 2 + k] > turn + 1
-            rate_real = thetas[2 * i, s : s + 1, :]
-            value, rest_real = current[base + re], total[base + re]
+            rate_real = theta[2 * i, line, :]
+            value, rest_real = current[own + re], total[base + re]
             change = rate_real * rest_real
             if im is not None:
-                rate_imag = thetas[2 * i + 1, s : s + 1, :]
-                other, rest_imag = current[base + im], total[base + im]
+                rate_imag = theta[2 * i + 1, line, :]
+                other, rest_imag = current[own + im], total[base + im]
                 change = change - rate_imag * rest_imag
                 solved[base + im] = jnp.where(
                     active, other + (rate_real * rest_imag + rate_imag * rest_real), other
                 )
             solved[base + re] = jnp.where(active, value + change, value)
+    slots = kept_slots(flags, slot_order(samples, total_steps, tables), total_steps)
     if not last:
         pack_fields(solved, even_slots(slots), send_ref[...], (pack0, pack1))
         return
@@ -771,17 +793,17 @@
             out[s] = total[step * samples + s]
 
 
-def assemble_kernel(*rest, total_steps, groups):
-    pieces, (out, done) = rest[:-2], rest[-2:]
+def assemble_kernel(*rest, turns, total_steps):
+    count = len(turns)
+    pieces, (out, done) = rest[:count], rest[-2:]
     size = pieces[0].shape[0]
     rank = lax.axis_index("tm")
-    copies = []
-    for which, piece in enumerate(pieces):
-        at, turn = divmod(which, total_steps)
-        first = (partner(rank, turn, total_steps) * groups + at) * size
-        copies.append(
-            pltpu.make_async_copy(piece, out.at[pl.ds(first, size)], done.at[which])
-        )
+    copies = [
+        pltpu.make_async_copy(
+            piece, out.at[pl.ds(partner(rank, turn, total_steps) * size, size)], done.at[which]
+        )
+        for which, (turn, piece) in enumerate(zip(turns, pieces))
+    ]
     for copy in copies:
         copy.start()
     for copy in copies:
@@ -792,7 +814,7 @@
 
 
 def run(
-    kernel, inputs, outs, scratch=(), in_hbm=(), out_hbm=(), flops=10**9
+    kernel, inputs, outs, scratch=(), in_hbm=(), out_hbm=(), aliases=(), flops=10**9
 ):
     def spec(i, outside):
         return pl.BlockSpec(memory_space=pltpu.HBM) if i in outside else vmem
@@ -806,6 +828,7 @@
         out_shape=[jax.ShapeDtypeStruct(*o) for o in outs],
         in_specs=[spec(i, in_hbm) for i in range(len(inputs))],
         out_specs=[spec(i, out_hbm) for i in range(len(outs))],
+        input_output_aliases=dict(aliases),
         scratch_shapes=[pltpu.VMEM(*s) if isinstance(s, tuple) else s for s in scratch],
         compiler_params=pltpu.CompilerParams(vmem_limit_bytes=40 << 20),
         cost_estimate=pl.CostEstimate(flops=flops, bytes_accessed=1 << 22, transcendentals=0),
@@ -928,7 +951,9 @@
         splits(samples) + [((blocks_wide, 2 * dofs), f32)],
         flops=4 * 10**9,
     )
-    groups = GROUPS if part % GROUPS == 0 else 1
+    groups = GROUPS
+    if part % groups or (part // groups * (total_steps - 1)) % 2:
+        groups = 1
     share = part // groups
     piece = ((share, dofs, elems), f32)
     *scaled, coefs = run(
@@ -953,72 +978,91 @@
         [piece] * (groups * devs) + [((FACES + 2, samples, elems), f32)],
         [(cube, f32), ((samples, elems), f32)],
     )
-    fields = share * total_steps
-    swept = share * (total_steps - 1)
-    pairs = (swept + 1) // 2
-    some = ((fields, dofs, elems), f32)
-    packed = ((pairs * dofs, 2 * halo), f32)
-    restored = []
+    sizes = lambda share: (
+        ((share * total_steps, dofs, elems), f32),
+        (((share * (total_steps - 1) + 1) // 2 * dofs, 2 * halo), f32),
+        (share * (total_steps - 1) + 1) // 2,
+    )
+    some, packed, pairs = sizes(share)
+    currents, spectra, inners, arrived0, arrived1, thetas, scales = ([] for _ in range(7))
     for at in range(groups):
         mine = dict(total_steps=total_steps, at=at, groups=groups)
         pieces = [time_swap(scaled[at * devs + turn], turn) for turn in range(devs)]
         spectrum, current, pack0, pack1 = run(
             functools.partial(spectrum_kernel, **mine),
-            (flags, coefs, send, low, earlier_low, *pieces),
+            (flags, coefs, send, low, earlier_low, *pieces, *thetas[-1:]),
             [some, some, packed, packed],
             [((total_steps, share, dofs, elems), f32)],
         )
-        for turn in range(MAXS - 1):
-            arrived0 = neighbour_swap(pack0, 0)
-            arrived1 = neighbour_swap(pack1, 1)
-            inner, *tables = run(
-                functools.partial(sweep_local_kernel, first_turn=turn == 0, **mine),
-                (flags, current, spectrum, coefs, picks, blocks, halo_picks),
-                [some]
-                + [
-                    ((2 * len(frequencies(total_steps)), share, elems), f32),
-                    ((2, pairs, 2 * halo), f32),
-                ]
-                * (turn == 0),
-                [some] + splits(swept),
-                    flops=3 * 10**9 // groups,
-            )
-            if turn == 0:
-                thetas, scales = tables
-            last = turn == MAXS - 2
-            inputs = (
-                flags,
-                current,
-                inner,
-                arrived0,
-                arrived1,
-                coefs,
-                face_nbr,
-                face_blocks,
-                halo_picks,
-                thetas,
-                scales,
-            )
-            kernel = functools.partial(sweep_update_kernel, turn=turn, last=last, **mine)
-            if last:
-                series = run(
-                    kernel, inputs, [piece] * devs, [some, some]
-                )
-            else:
-                current, pack0, pack1 = run(
-                    kernel,
-                    inputs + (send,),
-                    [some, packed, packed],
-                    [some],
-                )
-        restored += [time_swap(series[turn], turn) for turn in range(devs)]
-    (out,) = run(
-        functools.partial(assemble_kernel, total_steps=total_steps, groups=groups),
-        tuple(restored),
-        [(cube, f32)],
-        [pltpu.SemaphoreType.DMA((len(restored),))],
-        out_hbm=(0,),
-    )
+        arrived0.append(neighbour_swap(pack0, 0))
+        arrived1.append(neighbour_swap(pack1, 1))
+        inner, theta, scale = run(
+            functools.partial(sweep_local_kernel, first_turn=True, inner=1, **mine),
+            (flags, current, coefs, picks, blocks, halo_picks, spectrum),
+            [
+                some,
+                ((2 * len(frequencies(total_steps)), share, elems), f32),
+                ((2, pairs, 2 * halo), f32),
+            ],
+            [some] + splits(share * (total_steps - 1)),
+            flops=3 * 10**9 // groups,
+        )
+        currents.append(current)
+        spectra.append(spectrum)
+        inners.append(inner)
+        thetas.append(theta)
+        scales.append(scale)
+    some, packed, pairs = sizes(part)
+    tables = (flags, coefs, face_nbr, face_blocks, halo_picks)
+    update = lambda turn, parts: functools.partial(
+        sweep_update_kernel,
+        turn=turn,
+        total_steps=total_steps,
+        last=turn == MAXS - 2,
+        parts=parts,
+        tables=groups,
+    )
+    current, pack0, pack1 = run(
+        update(0, groups),
+        (*tables, *currents, *inners, *arrived0, *arrived1, *thetas, *scales, send),
+        [some, packed, packed],
+        [some],
+    )
+    arrived0 = neighbour_swap(pack0, 0)
+    arrived1 = neighbour_swap(pack1, 1)
+    (inner,) = run(
+        functools.partial(
+            sweep_local_kernel,
+            first_turn=False,
+            inner=groups,
+            total_steps=total_steps,
+            at=0,
+            groups=1,
+        ),
+        (flags, current, coefs, picks, blocks, halo_picks, *spectra),
+        [some],
+        [some] + splits(part * (total_steps - 1)),
+        flops=3 * 10**9,
+    )
+    series = run(
+        update(1, 1),
+        (*tables, current, inner, arrived0, arrived1, *thetas, *scales),
+        [((part, dofs, elems), f32)] * devs,
+        [some, some],
+    )
+    restored = [time_swap(series[turn], turn) for turn in range(devs)]
+    out = None
+    for turns in (range(devs - 1), range(devs - 1, devs)):
+        inputs = [restored[turn] for turn in turns] + ([] if out is None else [out])
+        (out,) = run(
+            functools.partial(assemble_kernel, turns=turns, total_steps=total_steps),
+            tuple(inputs),
+            [(cube, f32)],
+            [pltpu.SemaphoreType.DMA((len(turns),))],
+            in_hbm=() if out is None else (len(turns),),
+            out_hbm=(0,),
+            aliases=() if out is None else ((len(turns), 0),),
+        )
     return out.reshape(samples, steps_dev, dofs, elems)
 
 

time: 63.6 us -> 62.1 us (0.976)
  waiting for transfers between devices: 27.9 us -> 21.7 us
  starting transfers between devices: 16.4 us -> 20.3 us
  Pallas kernels: 18.5 us -> 19.7 us
    ppermute x7 -> x10, waiting for transfers between devices: 23.7 us -> 16 us  [time_swap(): return value if turn == 0 else lax.ppermute(value, 'tm', pairs)]
    ppermute x6 -> x8, starting transfers between devices: 9.43 us -> 11.4 us  [neighbour_swap(): return lax.ppermute(value, axes, pairs)]
    ppermute x7 -> x10, starting transfers between devices: 6.48 us -> 8.37 us  [time_swap(): return value if turn == 0 else lax.ppermute(value, 'tm', pairs)]
    ppermute x6 -> x8, waiting for transfers between devices: 4.21 us -> 5.69 us  [neighbour_swap(): return lax.ppermute(value, axes, pairs)]
    pallas_call x9 -> x12, Pallas kernels: 18.5 us -> 19.7 us  [run(): pl.pallas_call(kernel, out_shape=[jax.ShapeDtypeStruct(*o) for o in outs]...]
  transfers between devices with their start and end apart: 14 -> 19, of which waited for: 8 -> 8; matrix products, arithmetic and copies ran while one was open for 0% -> 0% of each run, Pallas kernels for 16% -> 20%
where the time goes in v5:
time: 62.1 us; the launch traced here: 62 us
  waiting for transfers between devices  21.7 us (35%)
  starting transfers between devices  20.3 us (33%)
  Pallas kernels  19.7 us (32%)
    pallas_call x12, Pallas kernels, run(): pl.pallas_call(kernel, out_shape=[jax.ShapeDtypeStruct(*o) for o in outs]...  19.7 us
    ppermute x10, waiting for transfers between devices, time_swap(): return value if turn == 0 else lax.ppermute(value, 'tm', pairs)  16 us
    ppermute x8, starting transfers between devices, neighbour_swap(): return lax.ppermute(value, axes, pairs)  11.4 us
    ppermute x10, starting transfers between devices, time_swap(): return value if turn == 0 else lax.ppermute(value, 'tm', pairs)  8.37 us
    ppermute x8, waiting for transfers between devices, neighbour_swap(): return lax.ppermute(value, axes, pairs)  5.69 us
  transfers between devices with their start and end apart: 19, of which 8 were waited for; matrix products, arithmetic and copies ran while one was open for 0% of the time, Pallas kernels for 20%

profile of v5, /device:TPU:0, one launch (start us, length us, event | category | flops | bytes accessed | tf_op | source)
XLA Modules:
  0.0 62.0 jit_solution(17208187095106863154)
XLA Ops:
  0.0 2.2 %shard_map.109 = (f32[520,128]{1,0:T(8,128)S(1)}, f32[520,128]{1,0:T(8,128)S(1)}, bf16[512,256]{1,0:T(8,128)(2,1)S(1)}, f32[16,256]{1,0:T(8,128)S(1)}, f32[8,64,...) custom-call(f32[16,64,256]{2,1,0:T(8,128)} %bitcast.10, ...), custom_call_target="tpu_custom_call" | custom-call | flops 1000000000 | bytes 4194304 | tf_op jit(solution)/shard_map/pallas_call | solution.py:826
  2.2 0.5 collective-permute-start.1
  2.7 2.6 %collective-permute-start = (f32[8,64,256]{2,1,0:T(8,128)S(1)}, f32[8,64,256]{2,1,0:T(8,128)S(1)}, u32[]{:S(2)}, u32[]{:S(2)}) collective-permute-start(f32[8,64,256]{2,1,0:T(8,128)S(1)} %get-tuple-element.53.low_fields.own), channel_id=1, source_target_pairs={{0,4},{4,0},{8,12},{12,8},{1,5},{5,1},{9,13},{13,9},{2,6},{6,2},{1... | collective-permute-start | bytes 1572872 | tf_op jit(solution)/shard_map/ppermute | solution.py:859
  5.3 1.6 %collective-permute-start.2 = (f32[520,128]{1,0:T(8,128)S(1)}, f32[520,128]{1,0:T(8,128)S(1)}, u32[]{:S(2)}, u32[]{:S(2)}) collective-permute-start(f32[520,128]{1,0:T(8,128)S(1)} %get-tuple-element.62), channel_id=1, source_target_pairs={{0,1},{1,0},{2,3},{3,2},{4,20},{5,6},{6,5},{7,23},{8,9},{9,8},{10,... | collective-permute-start | bytes 798728 | tf_op jit(solution)/shard_map/ppermute | solution.py:853
  6.8 1.5 %collective-permute-start.3 = (f32[520,128]{1,0:T(8,128)S(1)}, f32[520,128]{1,0:T(8,128)S(1)}, u32[]{:S(2)}, u32[]{:S(2)}) collective-permute-start(f32[520,128]{1,0:T(8,128)S(1)} %get-tuple-element.63), channel_id=1, source_target_pairs={{0,16},{1,2},{2,1},{3,19},{4,5},{5,4},{6,7},{7,6},{8,24},{9,10},{1... | collective-permute-start | bytes 798728 | tf_op jit(solution)/shard_map/ppermute | solution.py:853
  8.4 0.0 copy-start
  8.4 4.0 %shard_map.110 = (f32[16,64,256]{2,1,0:T(8,128)S(1)}, f32[8,16,256]{2,1,0:T(8,128)S(1)}, bf16[256,1536]{1,0:T(8,128)(2,1)S(1)}, bf16[128,448]{1,0:T(8,128)(2,1)S...) custom-call(f32[8,64,256]{2,1,0:T(8,128)S(1)} %get-tuple-element.53., ...), custom_call_target="tpu_custom_call" | custom-call | flops 4000000000 | bytes 4194304 | tf_op jit(solution)/shard_map/pallas_call | solution.py:826
  12.3 1.9 %collective-permute-done.2.arrived0 = f32[520,128]{1,0:T(8,128)S(1)} collective-permute-done((f32[520,128]{1,0:T(8,128)S(1)}, f32[520,128]{1,0:T(8,128)S(1)}, u32[]{:S(2)}, u32[]{:S(2)}) %collective-permute-start.2) | collective-permute-done | bytes 266272 | tf_op jit(solution)/shard_map/ppermute | solution.py:853
  14.3 0.0 collective-permute-done.3.arrived1
  14.3 0.0 collective-permute-done.1.earlier_high
  14.3 0.0 collective-permute-done.earlier_low.near
  14.3 0.0 copy-done
  14.3 1.7 %shard_map.111 = (f32[2,64,256]{2,1,0:T(8,128)S(1)}, f32[2,64,256]{2,1,0:T(8,128)S(1)}, f32[2,64,256]{2,1,0:T(8,128)S(1)}, f32[2,64,256]{2,1,0:T(8,128)S(1)}, f3...) custom-call(f32[16,64,256]{2,1,0:T(8,128)S(1)} %bitcast.9, ...), custom_call_target="tpu_custom_call" | custom-call | flops 1000000000 | bytes 4194304 | tf_op jit(solution)/shard_map/pallas_call | solution.py:826
  16.0 0.2 collective-permute-start.4
  16.1 0.1 collective-permute-start.5
  16.2 1.7 %collective-permute-start.6 = (f32[2,64,256]{2,1,0:T(8,128)S(1)}, f32[2,64,256]{2,1,0:T(8,128)S(1)}, u32[]{:S(2)}, u32[]{:S(2)}) collective-permute-start(f32[2,64,256]{2,1,0:T(8,128)S(1)} %get-tuple-element.74), channel_id=1, source_target_pairs={{0,12},{4,8},{8,4},{12,0},{1,13},{5,9},{9,5},{13,1},{2,14},{6,10},... | collective-permute-start | bytes 393224 | tf_op jit(solution)/shard_map/ppermute | solution.py:859
  17.9 0.4 collective-permute-start.7
  18.3 0.1 collective-permute-start.8
  18.4 0.0 collective-permute-done.4.rest_1_
  18.4 1.4 %collective-permute-start.9 = (f32[2,64,256]{2,1,0:T(8,128)S(1)}, f32[2,64,256]{2,1,0:T(8,128)S(1)}, u32[]{:S(2)}, u32[]{:S(2)}) collective-permute-start(f32[2,64,256]{2,1,0:T(8,128)S(1)} %get-tuple-element.79), channel_id=1, source_target_pairs={{0,12},{4,8},{8,4},{12,0},{1,13},{5,9},{9,5},{13,1},{2,14},{6,10},... | collective-permute-start | bytes 393224 | tf_op jit(solution)/shard_map/ppermute | solution.py:859
  19.8 2.7 %collective-permute-done.5.rest_2_ = f32[2,64,256]{2,1,0:T(8,128)S(1)} collective-permute-done((f32[2,64,256]{2,1,0:T(8,128)S(1)}, f32[2,64,256]{2,1,0:T(8,128)S(1)}, u32[]{:S(2)}, u32[]{:S(2)}) %collective-permute-start.5) | collective-permute-done | bytes 131104 | tf_op jit(solution)/shard_map/ppermute | solution.py:859
  22.4 1.9 %collective-permute-done.6.rest_3_ = f32[2,64,256]{2,1,0:T(8,128)S(1)} collective-permute-done((f32[2,64,256]{2,1,0:T(8,128)S(1)}, f32[2,64,256]{2,1,0:T(8,128)S(1)}, u32[]{:S(2)}, u32[]{:S(2)}) %collective-permute-start.6) | collective-permute-done | bytes 131104 | tf_op jit(solution)/shard_map/ppermute | solution.py:859
  24.3 0.4 shard_map.112
  24.7 1.5 %collective-permute-start.10 = (f32[192,128]{1,0:T(8,128)S(1)}, f32[192,128]{1,0:T(8,128)S(1)}, u32[]{:S(2)}, u32[]{:S(2)}) collective-permute-start(f32[192,128]{1,0:T(8,128)S(1)} %get-tuple-element.87), channel_id=1, source_target_pairs={{0,1},{1,0},{2,3},{3,2},{4,20},{5,6},{6,5},{7,23},{8,9},{9,8},{10,... | collective-permute-start | bytes 294920 | tf_op jit(solution)/shard_map/ppermute | solution.py:853
  26.2 1.5 %collective-permute-start.12 = (f32[192,128]{1,0:T(8,128)S(1)}, f32[192,128]{1,0:T(8,128)S(1)}, u32[]{:S(2)}, u32[]{:S(2)}) collective-permute-start(f32[192,128]{1,0:T(8,128)S(1)} %get-tuple-element.89), channel_id=1, source_target_pairs={{0,16},{1,2},{2,1},{3,19},{4,5},{5,4},{6,7},{7,6},{8,24},{9,10},{1... | collective-permute-start | bytes 294920 | tf_op jit(solution)/shard_map/ppermute | solution.py:853
  27.7 1.8 %shard_map.113 = (f32[8,64,256]{2,1,0:T(8,128)S(1)}, f32[6,2,256]{2,1,0:T(2,128)S(1)}, f32[2,3,128]{2,1,0:T(4,128)S(1)}) custom-call(s32[1,128]{1,0:T(1,128)S(1)} %get-tuple-element.60.flags, f32[8,64,256]{2,1,0:T(8,128)S(1)} %get-tuple-element.75.fields.rest_0_, f32[8,16,256]{2,1,0:T(8,128)S(1)} %get-tuple-element.69.coefs, ...), custom_call_target="tpu_custom_call" | custom-call | flops 1500000000 | bytes 4194304 | tf_op jit(solution)/shard_map/pallas_call | solution.py:826
  29.5 0.0 collective-permute-done.7.rest_1_
  29.5 0.0 collective-permute-done.8.rest_2_
  29.5 0.4 collective-permute-done.9.rest_3_
  29.9 0.4 shard_map.114
  30.3 1.5 %collective-permute-start.11 = (f32[192,128]{1,0:T(8,128)S(1)}, f32[192,128]{1,0:T(8,128)S(1)}, u32[]{:S(2)}, u32[]{:S(2)}) collective-permute-start(f32[192,128]{1,0:T(8,128)S(1)} %get-tuple-element.88), channel_id=1, source_target_pairs={{0,1},{1,0},{2,3},{3,2},{4,20},{5,6},{6,5},{7,23},{8,9},{9,8},{10,... | collective-permute-start | bytes 294920 | tf_op jit(solution)/shard_map/ppermute | solution.py:853
  31.8 1.5 %collective-permute-start.13 = (f32[192,128]{1,0:T(8,128)S(1)}, f32[192,128]{1,0:T(8,128)S(1)}, u32[]{:S(2)}, u32[]{:S(2)}) collective-permute-start(f32[192,128]{1,0:T(8,128)S(1)} %get-tuple-element.90), channel_id=1, source_target_pairs={{0,16},{1,2},{2,1},{3,19},{4,5},{5,4},{6,7},{7,6},{8,24},{9,10},{1... | collective-permute-start | bytes 294920 | tf_op jit(solution)/shard_map/ppermute | solution.py:853
  33.3 1.8 %shard_map.115 = (f32[8,64,256]{2,1,0:T(8,128)S(1)}, f32[6,2,256]{2,1,0:T(2,128)S(1)}, f32[2,3,128]{2,1,0:T(4,128)S(1)}) custom-call(s32[1,128]{1,0:T(1,128)S(1)} %get-tuple-element.60.flags, f32[8,64,256]{2,1,0:T(8,128)S(1)} %get-tuple-element.83.fields.rest_1_, f32[8,16,256]{2,1,0:T(8,128)S(1)} %get-tuple-element.69.coefs, ...), custom_call_target="tpu_custom_call" | custom-call | flops 1500000000 | bytes 4194304 | tf_op jit(solution)/shard_map/pallas_call | solution.py:826
  35.1 0.0 collective-permute-done.10.rest_4_
  35.1 0.0 collective-permute-done.12.rest_6_
  35.1 0.0 collective-permute-done.11.rest_5_
  35.2 1.3 %collective-permute-done.13.rest_7_ = f32[192,128]{1,0:T(8,128)S(1)} collective-permute-done((f32[192,128]{1,0:T(8,128)S(1)}, f32[192,128]{1,0:T(8,128)S(1)}, u32[]{:S(2)}, u32[]{:S(2)}) %collective-permute-start.13) | collective-permute-done | bytes 98336 | tf_op jit(solution)/shard_map/ppermute | solution.py:853
  36.4 1.8 %shard_map.116 = (f32[16,64,256]{2,1,0:T(8,128)S(1)}, f32[384,128]{1,0:T(8,128)S(1)}, f32[384,128]{1,0:T(8,128)S(1)}) custom-call(s32[1,128]{1,0:T(1,128)S(1)} %get-tuple-element.60.flags, f32[8,16,256]{2,1,0:T(8,128)S(1)} %get-tuple-element.69.coefs, s32[6,256]{1,0:T(8,128)S(1)} %get-tuple-element.56.face_nbr, ...), custom_call_target="tpu_custom_call" | custom-call | flops 1000000000 | bytes 4194304 | tf_op jit(solution)/shard_map/pallas_call | solution.py:826
  38.3 1.3 %collective-permute-start.14 = (f32[384,128]{1,0:T(8,128)S(1)}, f32[384,128]{1,0:T(8,128)S(1)}, u32[]{:S(2)}, u32[]{:S(2)}) collective-permute-start(f32[384,128]{1,0:T(8,128)S(1)} %get-tuple-element.95), channel_id=1, source_target_pairs={{0,1},{1,0},{2,3},{3,2},{4,20},{5,6},{6,5},{7,23},{8,9},{9,8},{10,... | collective-permute-start | bytes 589832 | tf_op jit(solution)/shard_map/ppermute | solution.py:853
  39.6 1.1 %collective-permute-start.15 = (f32[384,128]{1,0:T(8,128)S(1)}, f32[384,128]{1,0:T(8,128)S(1)}, u32[]{:S(2)}, u32[]{:S(2)}) collective-permute-start(f32[384,128]{1,0:T(8,128)S(1)} %get-tuple-element.96), channel_id=1, source_target_pairs={{0,16},{1,2},{2,1},{3,19},{4,5},{5,4},{6,7},{7,6},{8,24},{9,10},{1... | collective-permute-start | bytes 589832 | tf_op jit(solution)/shard_map/ppermute | solution.py:853
  40.7 2.9 %shard_map.117.rest_1_ = f32[16,64,256]{2,1,0:T(8,128)S(1)} custom-call(s32[1,128]{1,0:T(1,128)S(1)} %get-tuple-element.60.flags, f32[16,64,256]{2,1,0:T(8,128)S(1)} %get-tuple-element.94.fields.rest_0_, f32[8,16,256]{2,1,0:T(8,128)S(1)} %get-tuple-element.69.coefs, bf16[256,1536]{1,0:T(8,128)(2,1)S(1)} %get-tuple-element.80.picks, ...), custom_call_target="tpu_custom_call" | custom-call | flops 3000000000 | bytes 4194304 | tf_op jit(solution)/shard_map/pallas_call | solution.py:826
  43.6 2.5 %collective-permute-done.14.rest_2_ = f32[384,128]{1,0:T(8,128)S(1)} collective-permute-done((f32[384,128]{1,0:T(8,128)S(1)}, f32[384,128]{1,0:T(8,128)S(1)}, u32[]{:S(2)}, u32[]{:S(2)}) %collective-permute-start.14) | collective-permute-done | bytes 196640 | tf_op jit(solution)/shard_map/ppermute | solution.py:853
  46.0 0.0 collective-permute-done.15.rest_3_
  46.0 1.1 %shard_map.118 = (f32[4,64,256]{2,1,0:T(8,128)S(1)}, f32[4,64,256]{2,1,0:T(8,128)S(1)}, f32[4,64,256]{2,1,0:T(8,128)S(1)}, f32[4,64,256]{2,1,0:T(8,128)S(1)}) custom-call(s32[1,128]{1,0:T(1,128)S(1)} %get-tuple-element.60.flags, f32[8,16,256]{2,1,0:T(8,128)S(1)} %get-tuple-element.69.coefs, s32[6,256]{1,0:T(8,128)S(1)} %get-tuple-element.56.face_nbr, ...), custom_call_target="tpu_custom_call" | custom-call | flops 1000000000 | bytes 4194304 | tf_op jit(solution)/shard_map/pallas_call | solution.py:826
  47.2 0.2 collective-permute-start.17
  47.4 0.5 collective-permute-start.18
  47.9 1.3 %collective-permute-start.16 = (f32[4,64,256]{2,1,0:T(8,128)S(1)}, f32[4,64,256]{2,1,0:T(8,128)S(1)}, u32[]{:S(2)}, u32[]{:S(2)}) collective-permute-start(f32[4,64,256]{2,1,0:T(8,128)S(1)} %get-tuple-element.97), channel_id=1, source_target_pairs={{0,12},{4,8},{8,4},{12,0},{1,13},{5,9},{9,5},{13,1},{2,14},{6,10},... | collective-permute-start | bytes 786440 | tf_op jit(solution)/shard_map/ppermute | solution.py:859
  49.1 0.0 collective-permute-done.17.rest_1_
  49.1 7.3 %collective-permute-done.18.rest_2_ = f32[4,64,256]{2,1,0:T(8,128)S(1)} collective-permute-done((f32[4,64,256]{2,1,0:T(8,128)S(1)}, f32[4,64,256]{2,1,0:T(8,128)S(1)}, u32[]{:S(2)}, u32[]{:S(2)}) %collective-permute-start.18) | collective-permute-done | bytes 262176 | tf_op jit(solution)/shard_map/ppermute | solution.py:859
  56.5 0.9 %shard_map.119.rest_1_ = f32[16,64,256]{2,1,0:T(8,128)} custom-call(f32[4,64,256]{2,1,0:T(8,128)S(1)} %get-tuple-element.98.rest_0_, f32[4,64,256]{2,1,0:T(8,128)S(1)} %collective-permute-done.17.rest_1_, f32[4,64,256]{2,1,0:T(8,128)S(1)} %collective-permute-done.18.rest_2_), custom_call_target="tpu_custom_call" | custom-call | flops 1000000000 | bytes 4194304 | tf_op jit(solution)/shard_map/pallas_call | solution.py:826
  57.4 3.8 %collective-permute-done.16.rest_0_ = f32[4,64,256]{2,1,0:T(8,128)S(1)} collective-permute-done((f32[4,64,256]{2,1,0:T(8,128)S(1)}, f32[4,64,256]{2,1,0:T(8,128)S(1)}, u32[]{:S(2)}, u32[]{:S(2)}) %collective-permute-start.16) | collective-permute-done | bytes 262176 | tf_op jit(solution)/shard_map/ppermute | solution.py:859
  61.1 0.7 %shard_map.120 = f32[16,64,256]{2,1,0:T(8,128)} custom-call(f32[4,64,256]{2,1,0:T(8,128)S(1)} %collective-permute-done.16.rest_0_, f32[16,64,256]{2,1,0:T(8,128)} %shard_map.119.rest_1_), custom_call_target="tpu_custom_call", output_to_operand_aliasing={{}: (1, {})} | custom-call | flops 1000000000 | bytes 4194304 | tf_op jit(solution)/shard_map/pallas_call | solution.py:826
Async XLA Ops:
  2.2 12.1 %collective-permute-start.1 = (f32[8,64,256]{2,1,0:T(8,128)S(1)}, f32[8,64,256]{2,1,0:T(8,128)S(1)}, u32[]{:S(2)}, u32[]{:S(2)}) collective-permute-start(f32[8,64,256]{2,1,0:T(8,128)S(1)} %get-tuple-element.54.high_fields), channel_id=1, source_target_pairs={{0,4},{4,8},{8,12},{12,0},{1,5},{5,9},{9,13},{13,1},{2,6},{6,10},{... | collective-permute-start | bytes 1572872 | tf_op jit(solution)/shard_map/ppermute | solution.py:929
  2.7 11.6 %collective-permute-start = (f32[8,64,256]{2,1,0:T(8,128)S(1)}, f32[8,64,256]{2,1,0:T(8,128)S(1)}, u32[]{:S(2)}, u32[]{:S(2)}) collective-permute-start(f32[8,64,256]{2,1,0:T(8,128)S(1)} %get-tuple-element.53.low_fields.own), channel_id=1, source_target_pairs={{0,4},{4,0},{8,12},{12,8},{1,5},{5,1},{9,13},{13,9},{2,6},{6,2},{1... | collective-permute-start | bytes 1572872 | tf_op jit(solution)/shard_map/ppermute | solution.py:859
  5.3 9.0 %collective-permute-start.2 = (f32[520,128]{1,0:T(8,128)S(1)}, f32[520,128]{1,0:T(8,128)S(1)}, u32[]{:S(2)}, u32[]{:S(2)}) collective-permute-start(f32[520,128]{1,0:T(8,128)S(1)} %get-tuple-element.62), channel_id=1, source_target_pairs={{0,1},{1,0},{2,3},{3,2},{4,20},{5,6},{6,5},{7,23},{8,9},{9,8},{10,... | collective-permute-start | bytes 798728 | tf_op jit(solution)/shard_map/ppermute | solution.py:853
  6.8 7.4 %collective-permute-start.3 = (f32[520,128]{1,0:T(8,128)S(1)}, f32[520,128]{1,0:T(8,128)S(1)}, u32[]{:S(2)}, u32[]{:S(2)}) collective-permute-start(f32[520,128]{1,0:T(8,128)S(1)} %get-tuple-element.63), channel_id=1, source_target_pairs={{0,16},{1,2},{2,1},{3,19},{4,5},{5,4},{6,7},{7,6},{8,24},{9,10},{1... | collective-permute-start | bytes 798728 | tf_op jit(solution)/shard_map/ppermute | solution.py:853
  8.4 5.9 %copy-start = (f32[16,1,64,256]{3,2,1,0:T(8,128)S(1)}, f32[16,1,64,256]{3,2,1,0:T(8,128)}, u32[]{:S(2)}) copy-start(f32[16,1,64,256]{3,2,1,0:T(8,128)} %param.11) | copy-start | bytes 3145732
  16.0 2.4 %collective-permute-start.4 = (f32[2,64,256]{2,1,0:T(8,128)S(1)}, f32[2,64,256]{2,1,0:T(8,128)S(1)}, u32[]{:S(2)}, u32[]{:S(2)}) collective-permute-start(f32[2,64,256]{2,1,0:T(8,128)S(1)} %get-tuple-element.72), channel_id=1, source_target_pairs={{0,4},{4,0},{8,12},{12,8},{1,5},{5,1},{9,13},{13,9},{2,6},{6,2},{1... | collective-permute-start | bytes 393224 | tf_op jit(solution)/shard_map/ppermute | solution.py:859
  16.1 6.3 %collective-permute-start.5 = (f32[2,64,256]{2,1,0:T(8,128)S(1)}, f32[2,64,256]{2,1,0:T(8,128)S(1)}, u32[]{:S(2)}, u32[]{:S(2)}) collective-permute-start(f32[2,64,256]{2,1,0:T(8,128)S(1)} %get-tuple-element.73), channel_id=1, source_target_pairs={{0,8},{4,12},{8,0},{12,4},{1,9},{5,13},{9,1},{13,5},{2,10},{6,14},... | collective-permute-start | bytes 393224 | tf_op jit(solution)/shard_map/ppermute | solution.py:859
  16.2 8.1 %collective-permute-start.6 = (f32[2,64,256]{2,1,0:T(8,128)S(1)}, f32[2,64,256]{2,1,0:T(8,128)S(1)}, u32[]{:S(2)}, u32[]{:S(2)}) collective-permute-start(f32[2,64,256]{2,1,0:T(8,128)S(1)} %get-tuple-element.74), channel_id=1, source_target_pairs={{0,12},{4,8},{8,4},{12,0},{1,13},{5,9},{9,5},{13,1},{2,14},{6,10},... | collective-permute-start | bytes 393224 | tf_op jit(solution)/shard_map/ppermute | solution.py:859
  17.9 11.6 %collective-permute-start.7 = (f32[2,64,256]{2,1,0:T(8,128)S(1)}, f32[2,64,256]{2,1,0:T(8,128)S(1)}, u32[]{:S(2)}, u32[]{:S(2)}) collective-permute-start(f32[2,64,256]{2,1,0:T(8,128)S(1)} %get-tuple-element.77), channel_id=1, source_target_pairs={{0,4},{4,0},{8,12},{12,8},{1,5},{5,1},{9,13},{13,9},{2,6},{6,2},{1... | collective-permute-start | bytes 393224 | tf_op jit(solution)/shard_map/ppermute | solution.py:859
  18.3 11.3 %collective-permute-start.8 = (f32[2,64,256]{2,1,0:T(8,128)S(1)}, f32[2,64,256]{2,1,0:T(8,128)S(1)}, u32[]{:S(2)}, u32[]{:S(2)}) collective-permute-start(f32[2,64,256]{2,1,0:T(8,128)S(1)} %get-tuple-element.78), channel_id=1, source_target_pairs={{0,8},{4,12},{8,0},{12,4},{1,9},{5,13},{9,1},{13,5},{2,10},{6,14},... | collective-permute-start | bytes 393224 | tf_op jit(solution)/shard_map/ppermute | solution.py:859
  18.4 11.5 %collective-permute-start.9 = (f32[2,64,256]{2,1,0:T(8,128)S(1)}, f32[2,64,256]{2,1,0:T(8,128)S(1)}, u32[]{:S(2)}, u32[]{:S(2)}) collective-permute-start(f32[2,64,256]{2,1,0:T(8,128)S(1)} %get-tuple-element.79), channel_id=1, source_target_pairs={{0,12},{4,8},{8,4},{12,0},{1,13},{5,9},{9,5},{13,1},{2,14},{6,10},... | collective-permute-start | bytes 393224 | tf_op jit(solution)/shard_map/ppermute | solution.py:859
  24.7 10.4 %collective-permute-start.10 = (f32[192,128]{1,0:T(8,128)S(1)}, f32[192,128]{1,0:T(8,128)S(1)}, u32[]{:S(2)}, u32[]{:S(2)}) collective-permute-start(f32[192,128]{1,0:T(8,128)S(1)} %get-tuple-element.87), channel_id=1, source_target_pairs={{0,1},{1,0},{2,3},{3,2},{4,20},{5,6},{6,5},{7,23},{8,9},{9,8},{10,... | collective-permute-start | bytes 294920 | tf_op jit(solution)/shard_map/ppermute | solution.py:853
  26.2 9.0 %collective-permute-start.12 = (f32[192,128]{1,0:T(8,128)S(1)}, f32[192,128]{1,0:T(8,128)S(1)}, u32[]{:S(2)}, u32[]{:S(2)}) collective-permute-start(f32[192,128]{1,0:T(8,128)S(1)} %get-tuple-element.89), channel_id=1, source_target_pairs={{0,16},{1,2},{2,1},{3,19},{4,5},{5,4},{6,7},{7,6},{8,24},{9,10},{1... | collective-permute-start | bytes 294920 | tf_op jit(solution)/shard_map/ppermute | solution.py:853
  30.3 4.8 %collective-permute-start.11 = (f32[192,128]{1,0:T(8,128)S(1)}, f32[192,128]{1,0:T(8,128)S(1)}, u32[]{:S(2)}, u32[]{:S(2)}) collective-permute-start(f32[192,128]{1,0:T(8,128)S(1)} %get-tuple-element.88), channel_id=1, source_target_pairs={{0,1},{1,0},{2,3},{3,2},{4,20},{5,6},{6,5},{7,23},{8,9},{9,8},{10,... | collective-permute-start | bytes 294920 | tf_op jit(solution)/shard_map/ppermute | solution.py:853
  31.8 4.6 %collective-permute-start.13 = (f32[192,128]{1,0:T(8,128)S(1)}, f32[192,128]{1,0:T(8,128)S(1)}, u32[]{:S(2)}, u32[]{:S(2)}) collective-permute-start(f32[192,128]{1,0:T(8,128)S(1)} %get-tuple-element.90), channel_id=1, source_target_pairs={{0,16},{1,2},{2,1},{3,19},{4,5},{5,4},{6,7},{7,6},{8,24},{9,10},{1... | collective-permute-start | bytes 294920 | tf_op jit(solution)/shard_map/ppermute | solution.py:853
  38.3 7.7 %collective-permute-start.14 = (f32[384,128]{1,0:T(8,128)S(1)}, f32[384,128]{1,0:T(8,128)S(1)}, u32[]{:S(2)}, u32[]{:S(2)}) collective-permute-start(f32[384,128]{1,0:T(8,128)S(1)} %get-tuple-element.95), channel_id=1, source_target_pairs={{0,1},{1,0},{2,3},{3,2},{4,20},{5,6},{6,5},{7,23},{8,9},{9,8},{10,... | collective-permute-start | bytes 589832 | tf_op jit(solution)/shard_map/ppermute | solution.py:853
  39.6 6.4 %collective-permute-start.15 = (f32[384,128]{1,0:T(8,128)S(1)}, f32[384,128]{1,0:T(8,128)S(1)}, u32[]{:S(2)}, u32[]{:S(2)}) collective-permute-start(f32[384,128]{1,0:T(8,128)S(1)} %get-tuple-element.96), channel_id=1, source_target_pairs={{0,16},{1,2},{2,1},{3,19},{4,5},{5,4},{6,7},{7,6},{8,24},{9,10},{1... | collective-permute-start | bytes 589832 | tf_op jit(solution)/shard_map/ppermute | solution.py:853
  47.2 2.0 %collective-permute-start.17 = (f32[4,64,256]{2,1,0:T(8,128)S(1)}, f32[4,64,256]{2,1,0:T(8,128)S(1)}, u32[]{:S(2)}, u32[]{:S(2)}) collective-permute-start(f32[4,64,256]{2,1,0:T(8,128)S(1)} %get-tuple-element.99), channel_id=1, source_target_pairs={{0,4},{4,0},{8,12},{12,8},{1,5},{5,1},{9,13},{13,9},{2,6},{6,2},{1... | collective-permute-start | bytes 786440 | tf_op jit(solution)/shard_map/ppermute | solution.py:859
  47.4 9.1 %collective-permute-start.18 = (f32[4,64,256]{2,1,0:T(8,128)S(1)}, f32[4,64,256]{2,1,0:T(8,128)S(1)}, u32[]{:S(2)}, u32[]{:S(2)}) collective-permute-start(f32[4,64,256]{2,1,0:T(8,128)S(1)} %get-tuple-element.100), channel_id=1, source_target_pairs={{0,8},{4,12},{8,0},{12,4},{1,9},{5,13},{9,1},{13,5},{2,10},{6,14},... | collective-permute-start | bytes 786440 | tf_op jit(solution)/shard_map/ppermute | solution.py:859
  47.9 13.3 %collective-permute-start.16 = (f32[4,64,256]{2,1,0:T(8,128)S(1)}, f32[4,64,256]{2,1,0:T(8,128)S(1)}, u32[]{:S(2)}, u32[]{:S(2)}) collective-permute-start(f32[4,64,256]{2,1,0:T(8,128)S(1)} %get-tuple-element.97), channel_id=1, source_target_pairs={{0,12},{4,8},{8,4},{12,0},{1,13},{5,9},{9,5},{13,1},{2,14},{6,10},... | collective-permute-start | bytes 786440 | tf_op jit(solution)/shard_map/ppermute | solution.py:859

commit v6 on v5

--- a/solution.py
+++ b/solution.py
@@ -192,12 +192,12 @@
         copy.wait()
 
 
-def local_part(fields, slots, coef_row, picks, blocks, out, high, low):
-    dofs, elems = fields.shape[1], fields.shape[2]
+def local_part(read, slots, coef_row, picks, blocks, out, high, low):
+    dofs, elems = out.shape[1], out.shape[2]
     size = group_size(len(slots))
     for first in range(0, len(slots), size):
         group = range(first, first + size)
-        values = [fields[slots[t]] for t in group]
+        values = [read(t) for t in group]
         hi, lo = split(jnp.concatenate(values, axis=0))
         for t, value in zip(group, values):
             a, b = split(value * coef_row(FACES, t))
@@ -298,7 +298,7 @@
         skip = jnp.where(counts_in[0, k] == 1, re, skip)
     flags[...] = jnp.where(lane == 1, skip, line)
     local_part(
-        iterate,
+        lambda t: iterate[t],
         list(range(samples)),
         lambda f, t: coefs[f, t : t + 1, :],
         picks,
@@ -319,16 +319,16 @@
     return jnp.concatenate([x[:, :width], x[:, width:]], axis=0)
 
 
-def usual_halo(arrived, scales, blocks, picks):
+def usual_halo(arrived, scales, blocks, picks, chosen=None):
     dofs = blocks[0].shape[1]
     columns = []
     for which in range(2):
         value = arrived[which]
         width = value.shape[1]
-        pairs = scales[which].shape[0]
+        chosen = range(scales[which].shape[0]) if chosen is None else chosen
+        pairs = len(chosen)
         scaled = [
-            value[j * dofs : (j + 1) * dofs, :] * scales[which][j : j + 1, :]
-            for j in range(pairs)
+            value[j * dofs : (j + 1) * dofs, :] * scales[which][j : j + 1, :] for j in chosen
         ]
         got = times_block(blocks[which], jnp.concatenate(scaled, axis=1))
         columns.append(
@@ -377,15 +377,16 @@
     return slice(row, row + dofs), slice(col, col + elems)
 
 
-def add_others(arrived, even, flags, face_nbr, face_blocks, halo, half, slots, coef_row, factor, total):
+def add_others(arrived, even, flags, face_nbr, face_blocks, halo, chosen, slots, coef_row, factor, total):
     elems = face_nbr.shape[1]
     dofs = total.shape[1]
 
     def body(which, face, pick):
         block = face_blocks[face]
-        for j in range(half):
+        half = len(chosen)
+        for i, j in enumerate(chosen):
             got = other_halo(arrived[which][j * dofs : (j + 1) * dofs, :], block, pick)
-            for t in (j, half + j):
+            for t in (i, half + i):
                 if t < len(slots):
                     cols = slice(t // half * elems, (t // half + 1) * elems)
                     field = slots[t]
@@ -413,49 +414,62 @@
     *rest,
     total_steps,
     groups,
+    at,
 ):
-    outs = rest[: groups * total_steps]
-    coefs, total, extra = rest[groups * total_steps :]
+    samples, dofs, elems = forcing.shape
+    if at == 0:
+        outs, (coefs, extra, total) = rest[:total_steps], rest[total_steps:]
+    else:
+        extra, outs, total = rest[0], rest[1 : total_steps + 1], rest[-1]
+        coefs = coefs_in
     iterate = Halves(low_fields, high_fields)
-    samples, dofs, elems = forcing.shape
     halo = halo_picks.shape[0] // 4
     half = samples // 2
+    part = samples // total_steps
+    size = part // groups
+    chosen = [j for j in range(half) if j % part // size == at]
+    mine = chosen + [half + j for j in chosen]
     even = space_even()
     usual = sides(even, elems, halo)
     arrived = (arrived0, arrived1)
-    coefs[...] = coefs_in[...]
-    conduct = coefs_in[FACES + 1]
     scales = [0.5 * (facing[w] + arrived[w][half * dofs :, :]) for w in range(2)]
-    couplings = [
-        stacked_halves(
-            exact_select(scales[w], halo_picks[w * 2 * halo : (w + 1) * 2 * halo, :])
-        )
-        for w in range(2)
-    ]
-    extra[...] = couplings[0] + couplings[1]
-    for w in range(2):
-        coefs[usual[w][0]] = coefs[usual[w][0]] + couplings[w]
-
-    def add_coupling(which, face, pick):
-        got = exact_select(arrived[which][half * dofs :, :], pick)
-        nbr = face_nbr[pl.ds(face, 1), :]
-        base = usual[which][1]
-        here = (nbr >= base) & (nbr < base + halo)
-        coupling = jnp.where(here, 0.5 * (conduct + stacked_halves(got)), 0.0)
-        coefs[face] = coefs[face] + coupling
-        extra[...] = extra[...] + coupling
-
-    other_sides(flags, even, face_nbr, halo, add_coupling)
-    coefs[FACES] = coefs[FACES] + extra[...]
+    if at == 0:
+        coefs[...] = coefs_in[...]
+        conduct = coefs_in[FACES + 1]
+        couplings = [
+            stacked_halves(
+                exact_select(scales[w], halo_picks[w * 2 * halo : (w + 1) * 2 * halo, :])
+            )
+            for w in range(2)
+        ]
+        extra[...] = couplings[0] + couplings[1]
+        for w in range(2):
+            coefs[usual[w][0]] = coefs[usual[w][0]] + couplings[w]
+
+        def add_coupling(which, face, pick):
+            got = exact_select(arrived[which][half * dofs :, :], pick)
+            nbr = face_nbr[pl.ds(face, 1), :]
+            base = usual[which][1]
+            here = (nbr >= base) & (nbr < base + halo)
+            coupling = jnp.where(here, 0.5 * (conduct + stacked_halves(got)), 0.0)
+            coefs[face] = coefs[face] + coupling
+            extra[...] = extra[...] + coupling
+
+        other_sides(flags, even, face_nbr, halo, add_coupling)
+        coefs[FACES] = coefs[FACES] + extra[...]
     volume = blocks[:, 0 : 2 * dofs][:, :dofs]
     brought = usual_halo(
-        arrived, scales, [face_blocks[usual[w][0]] for w in range(2)], halo_picks[...]
-    )
-    for j in range(samples):
+        arrived,
+        scales,
+        [face_blocks[usual[w][0]] for w in range(2)],
+        halo_picks[...],
+        chosen,
+    )
+    for t, j in enumerate(mine):
         value = iterate[j]
         total[j] = value + time_step * (
             local[j]
-            + brought[pair_place(j, half, dofs, elems)]
+            + brought[pair_place(t, len(chosen), dofs, elems)]
             + times_block(volume, value * extra[j : j + 1, :])
         )
     add_others(
@@ -465,9 +479,9 @@
         face_nbr,
         face_blocks,
         halo,
-        half,
-        list(range(samples)),
-        lambda f, t: coefs[f, t : t + 1, :],
+        chosen,
+        mine,
+        lambda f, t: coefs[f, mine[t] : mine[t] + 1, :],
         time_step,
         total,
     )
@@ -477,9 +491,7 @@
         weight = jnp.where(step == n, jnp.float32(alpha_circ ** (n / total_steps)), weight)
     gate_high = jnp.where(step > 0, weight, 0.0)
     gate_low = jnp.where(step % 2 == 1, weight, 0.0) if two_chips(total_steps) else gate_high
-    size = samples // (groups * total_steps)
-    for which, out in enumerate(outs):
-        at, turn = divmod(which, total_steps)
+    for turn, out in enumerate(outs):
         first = (partner(step, turn, total_steps) * groups + at) * size
         for i in range(size):
             j = first + i
@@ -624,7 +636,6 @@
 
 def sweep_local_kernel(
     flags,
-    fields,
     coefs,
     picks,
     blocks,
@@ -636,13 +647,14 @@
     first_turn,
     inner,
 ):
-    spectra, rest = rest[:inner], rest[inner:]
+    fields, spectra, rest = rest[:inner], rest[inner : 2 * inner], rest[2 * inner :]
     if first_turn:
         out, thetas, scales, total, high, low = rest
     else:
         out, total, high, low = rest
-    elems = fields.shape[2]
-    samples = fields.shape[0] // total_steps
+    elems = fields[0].shape[2]
+    each = fields[0].shape[0] // total_steps
+    samples = inner * each
     first = my_first(samples, at, groups)
     order = slot_order(samples, total_steps, inner)
     slots = kept_slots(flags, order, total_steps)
@@ -670,17 +682,22 @@
             thetas[2 * i] = rate_real
             if im is not None:
                 thetas[2 * i + 1] = rate_imag
-    local_part(fields, slots, row, picks, blocks, total, high, low)
+
+    def read(t):
+        which = order[t][0] // each
+        return fields[which][slots[t] - which * each * total_steps]
+
+    local_part(read, slots, row, picks, blocks, total, high, low)
     for s in range(samples):
         base = s * total_steps
-        spectrum = spectra[s // (samples // inner)]
-        own = s % (samples // inner) * total_steps
+        spectrum, current = spectra[s // each], fields[s // each]
+        own = s % each * total_steps
         for k, re, im in frequencies(total_steps):
             shift_real, shift_imag = shift_of(k, total_steps)
-            value = fields[base + re]
+            value = current[own + re]
             kept = spectrum[own + re] - (shift_real * value + time_step * total[base + re])
             if im is not None:
-                other = fields[base + im]
+                other = current[own + im]
                 kept = kept + shift_imag * other
                 out[base + im] = spectrum[own + im] - (
                     shift_real * other + shift_imag * value + time_step * total[base + im]
@@ -698,65 +715,57 @@
     turn,
     total_steps,
     last,
-    parts,
-    tables,
+    sources,
+    at,
+    groups,
 ):
     even = space_even()
     take = lambda count: (rest[:count], rest[count:])
-    currents, rest = take(parts)
-    inners, rest = take(parts)
-    arrived0, rest = take(parts)
-    arrived1, rest = take(parts)
-    thetas, rest = take(tables)
-    scale_refs, rest = take(tables)
+    (inner, arrived0, arrived1), rest = take(3)
+    currents, rest = take(sources)
+    thetas, rest = take(sources)
+    scale_refs, rest = take(sources)
     if last:
         outs, (total, solved) = rest[:total_steps], rest[total_steps:]
     else:
-        send_ref, solved, pack0, pack1, total = rest
-    fields, dofs, elems = currents[0].shape
-    part_samples = fields // total_steps
-    samples = parts * part_samples
-    table_samples = samples // tables
-    first = my_first(samples, 0, 1)
+        send_ref, *before, solved, pack0, pack1, total = rest
+    fields, dofs, elems = inner.shape
+    samples = fields // total_steps
+    each = samples // sources
+    first = my_first(samples, at, groups)
     halo = halo_picks.shape[0] // 4
     usual = sides(even, elems, halo)
-    for part in range(parts):
-        per = tables // parts
-        mine = scale_refs[part * per : (part + 1) * per]
-        scales = [jnp.concatenate([ref[w] for ref in mine], axis=0) for w in range(2)]
-        half = scales[0].shape[0]
-        arrived = (arrived0[part], arrived1[part])
-        order = slot_order(part_samples, total_steps, per)
-        slots = kept_slots(flags, order, total_steps)
-        brought = usual_halo(
-            arrived,
-            scales,
-            [face_blocks[usual[w][0]] for w in range(2)],
-            halo_picks[...],
-        )
-        for t, field in enumerate(slots):
-            total[part * fields + field] = (
-                inners[part][field] - brought[pair_place(t, half, dofs, elems)]
-            )
-        add_others(
-            arrived,
-            even,
-            flags,
-            face_nbr,
-            face_blocks,
-            halo,
-            half,
-            [part * fields + field for field in slots],
-            sample_row(coefs, order, first + part * part_samples),
-            -time_step,
-            total,
-        )
+    scales = [jnp.concatenate([ref[w] for ref in scale_refs], axis=0) for w in range(2)]
+    half = scales[0].shape[0]
+    arrived = (arrived0, arrived1)
+    order = slot_order(samples, total_steps, sources)
+    slots = kept_slots(flags, order, total_steps)
+    brought = usual_halo(
+        arrived,
+        scales,
+        [face_blocks[usual[w][0]] for w in range(2)],
+        halo_picks[...],
+    )
+    for t, field in enumerate(slots):
+        total[field] = inner[field] - brought[pair_place(t, half, dofs, elems)]
+    add_others(
+        arrived,
+        even,
+        flags,
+        face_nbr,
+        face_blocks,
+        halo,
+        range(half),
+        slots,
+        sample_row(coefs, order, first),
+        -time_step,
+        total,
+    )
     for s in range(samples):
         base = s * total_steps
-        current = currents[s // part_samples]
-        own = s % part_samples * total_steps
-        theta = thetas[s // table_samples]
-        line = slice(s % table_samples, s % table_samples + 1)
+        current, theta = currents[s // each], thetas[s // each]
+        own = s % each * total_steps
+        line = slice(s % each, s % each + 1)
         for i, (k, re, im) in enumerate(frequencies(total_steps)):
             active = flags[0, 2 + k] > turn + 1
             rate_real = theta[2 * i, line, :]
@@ -770,9 +779,17 @@
                     active, other + (rate_real * rest_imag + rate_imag * rest_real), other
                 )
             solved[base + re] = jnp.where(active, value + change, value)
-    slots = kept_slots(flags, slot_order(samples, total_steps, tables), total_steps)
     if not last:
-        pack_fields(solved, even_slots(slots), send_ref[...], (pack0, pack1))
+        rows = half * dofs
+        start = at * rows if before else 0
+        for ref, out in zip(before, (pack0, pack1)):
+            out[:start, :] = ref[...]
+        pack_fields(
+            solved,
+            even_slots(slots),
+            send_ref[...],
+            [out.at[start : start + rows] for out in (pack0, pack1)],
+        )
         return
     rank = lax.axis_index("tm")
     for s in range(samples):
@@ -956,28 +973,35 @@
         groups = 1
     share = part // groups
     piece = ((share, dofs, elems), f32)
-    *scaled, coefs = run(
-        functools.partial(residual_kernel, total_steps=total_steps, groups=groups),
-        (
-            forcing,
-            low,
-            high,
-            earlier_low,
-            earlier_high,
-            local,
-            arrived0,
-            arrived1,
-            coefs,
-            face_nbr,
-            blocks,
-            face_blocks,
-            halo_picks,
-            facing,
-            flags,
-        ),
-        [piece] * (groups * devs) + [((FACES + 2, samples, elems), f32)],
-        [(cube, f32), ((samples, elems), f32)],
-    )
+    scaled, extra = [], ()
+    for at in range(groups):
+        results = run(
+            functools.partial(residual_kernel, total_steps=total_steps, groups=groups, at=at),
+            (
+                forcing,
+                low,
+                high,
+                earlier_low,
+                earlier_high,
+                local,
+                arrived0,
+                arrived1,
+                coefs,
+                face_nbr,
+                blocks,
+                face_blocks,
+                halo_picks,
+                facing,
+                flags,
+                *extra,
+            ),
+            [piece] * devs
+            + [((FACES + 2, samples, elems), f32), ((samples, elems), f32)] * (at == 0),
+            [(cube, f32)],
+        )
+        scaled += results[:devs]
+        if at == 0:
+            coefs, extra = results[devs], (results[devs + 1],)
     sizes = lambda share: (
         ((share * total_steps, dofs, elems), f32),
         (((share * (total_steps - 1) + 1) // 2 * dofs, 2 * halo), f32),
@@ -998,7 +1022,7 @@
         arrived1.append(neighbour_swap(pack1, 1))
         inner, theta, scale = run(
             functools.partial(sweep_local_kernel, first_turn=True, inner=1, **mine),
-            (flags, current, coefs, picks, blocks, halo_picks, spectrum),
+            (flags, coefs, picks, blocks, halo_picks, current, spectrum),
             [
                 some,
                 ((2 * len(frequencies(total_steps)), share, elems), f32),
@@ -1012,24 +1036,38 @@
         inners.append(inner)
         thetas.append(theta)
         scales.append(scale)
+    tables = (flags, coefs, face_nbr, face_blocks, halo_picks)
+    after, packs = [], ()
+    for at in range(groups):
+        rows = (at + 1) * pairs * dofs
+        current, *packs = run(
+            functools.partial(
+                sweep_update_kernel,
+                turn=0,
+                total_steps=total_steps,
+                last=False,
+                sources=1,
+                at=at,
+                groups=groups,
+            ),
+            (
+                *tables,
+                inners[at],
+                arrived0[at],
+                arrived1[at],
+                currents[at],
+                thetas[at],
+                scales[at],
+                send,
+                *packs,
+            ),
+            [some] + [((rows, 2 * halo), f32)] * 2,
+            [some],
+        )
+        after.append(current)
     some, packed, pairs = sizes(part)
-    tables = (flags, coefs, face_nbr, face_blocks, halo_picks)
-    update = lambda turn, parts: functools.partial(
-        sweep_update_kernel,
-        turn=turn,
-        total_steps=total_steps,
-        last=turn == MAXS - 2,
-        parts=parts,
-        tables=groups,
-    )
-    current, pack0, pack1 = run(
-        update(0, groups),
-        (*tables, *currents, *inners, *arrived0, *arrived1, *thetas, *scales, send),
-        [some, packed, packed],
-        [some],
-    )
-    arrived0 = neighbour_swap(pack0, 0)
-    arrived1 = neighbour_swap(pack1, 1)
+    arrived0 = neighbour_swap(packs[0], 0)
+    arrived1 = neighbour_swap(packs[1], 1)
     (inner,) = run(
         functools.partial(
             sweep_local_kernel,
@@ -1039,14 +1077,22 @@
             at=0,
             groups=1,
         ),
-        (flags, current, coefs, picks, blocks, halo_picks, *spectra),
+        (flags, coefs, picks, blocks, halo_picks, *after, *spectra),
         [some],
         [some] + splits(part * (total_steps - 1)),
         flops=3 * 10**9,
     )
     series = run(
-        update(1, 1),
-        (*tables, current, inner, arrived0, arrived1, *thetas, *scales),
+        functools.partial(
+            sweep_update_kernel,
+            turn=1,
+            total_steps=total_steps,
+            last=True,
+            sources=groups,
+            at=0,
+            groups=1,
+        ),
+        (*tables, inner, arrived0, arrived1, *after, *thetas, *scales),
         [((part, dofs, elems), f32)] * devs,
         [some, some],
     )

time: 62.1 us -> 60.5 us (0.974)
  waiting for transfers between devices: 21.7 us -> 19.4 us
    ppermute x10, waiting for transfers between devices: 16 us -> 14.8 us  [time_swap(): return value if turn == 0 else lax.ppermute(value, 'tm', pairs)]
    ppermute x8, waiting for transfers between devices: 5.69 us -> 4.58 us  [neighbour_swap(): return lax.ppermute(value, axes, pairs)]
    pallas_call x12 -> x14, Pallas kernels: 19.7 us -> 20.1 us  [run(): pl.pallas_call(kernel, out_shape=[jax.ShapeDtypeStruct(*o) for o in outs]...]
  transfers between devices with their start and end apart: 19 -> 19, of which waited for: 8 -> 8; matrix products, arithmetic and copies ran while one was open for 0% -> 0% of each run, Pallas kernels for 20% -> 23%
where the time goes in v6:
time: 60.5 us; the launch traced here: 60.4 us
  starting transfers between devices  20.6 us (34%)
  Pallas kernels  20.1 us (33%)
  waiting for transfers between devices  19.4 us (32%)
    pallas_call x14, Pallas kernels, run(): pl.pallas_call(kernel, out_shape=[jax.ShapeDtypeStruct(*o) for o in outs]...  20.1 us
    ppermute x10, waiting for transfers between devices, time_swap(): return value if turn == 0 else lax.ppermute(value, 'tm', pairs)  14.8 us
    ppermute x8, starting transfers between devices, neighbour_swap(): return lax.ppermute(value, axes, pairs)  11.6 us
    ppermute x10, starting transfers between devices, time_swap(): return value if turn == 0 else lax.ppermute(value, 'tm', pairs)  8.42 us
    ppermute x8, waiting for transfers between devices, neighbour_swap(): return lax.ppermute(value, axes, pairs)  4.58 us
  transfers between devices with their start and end apart: 19, of which 8 were waited for; matrix products, arithmetic and copies ran while one was open for 0% of the time, Pallas kernels for 23%

profile of v6, /device:TPU:0, one launch (start us, length us, event | category | flops | bytes accessed | tf_op | source)
XLA Modules:
  0.0 60.4 jit_solution(6814580388019319126)
XLA Ops:
  0.0 2.2 %shard_map.109 = (f32[520,128]{1,0:T(8,128)S(1)}, f32[520,128]{1,0:T(8,128)S(1)}, bf16[512,256]{1,0:T(8,128)(2,1)S(1)}, f32[16,256]{1,0:T(8,128)S(1)}, f32[8,64,...) custom-call(f32[16,64,256]{2,1,0:T(8,128)} %bitcast.11, ...), custom_call_target="tpu_custom_call" | custom-call | flops 1000000000 | bytes 4194304 | tf_op jit(solution)/shard_map/pallas_call | solution.py:843
  2.2 0.5 collective-permute-start.1
  2.7 2.6 %collective-permute-start = (f32[8,64,256]{2,1,0:T(8,128)S(1)}, f32[8,64,256]{2,1,0:T(8,128)S(1)}, u32[]{:S(2)}, u32[]{:S(2)}) collective-permute-start(f32[8,64,256]{2,1,0:T(8,128)S(1)} %get-tuple-element.57.low_fields.own), channel_id=1, source_target_pairs={{0,4},{4,0},{8,12},{12,8},{1,5},{5,1},{9,13},{13,9},{2,6},{6,2},{1... | collective-permute-start | bytes 1572872 | tf_op jit(solution)/shard_map/ppermute | solution.py:876
  5.3 1.6 %collective-permute-start.2 = (f32[520,128]{1,0:T(8,128)S(1)}, f32[520,128]{1,0:T(8,128)S(1)}, u32[]{:S(2)}, u32[]{:S(2)}) collective-permute-start(f32[520,128]{1,0:T(8,128)S(1)} %get-tuple-element.66), channel_id=1, source_target_pairs={{0,1},{1,0},{2,3},{3,2},{4,20},{5,6},{6,5},{7,23},{8,9},{9,8},{10,... | collective-permute-start | bytes 798728 | tf_op jit(solution)/shard_map/ppermute | solution.py:870
  6.8 1.5 %collective-permute-start.3 = (f32[520,128]{1,0:T(8,128)S(1)}, f32[520,128]{1,0:T(8,128)S(1)}, u32[]{:S(2)}, u32[]{:S(2)}) collective-permute-start(f32[520,128]{1,0:T(8,128)S(1)} %get-tuple-element.67), channel_id=1, source_target_pairs={{0,16},{1,2},{2,1},{3,19},{4,5},{5,4},{6,7},{7,6},{8,24},{9,10},{1... | collective-permute-start | bytes 798728 | tf_op jit(solution)/shard_map/ppermute | solution.py:870
  8.4 0.0 copy-start
  8.4 4.0 %shard_map.110 = (f32[16,64,256]{2,1,0:T(8,128)S(1)}, f32[8,16,256]{2,1,0:T(8,128)S(1)}, bf16[256,1536]{1,0:T(8,128)(2,1)S(1)}, bf16[128,448]{1,0:T(8,128)(2,1)S...) custom-call(f32[8,64,256]{2,1,0:T(8,128)S(1)} %get-tuple-element.57., ...), custom_call_target="tpu_custom_call" | custom-call | flops 4000000000 | bytes 4194304 | tf_op jit(solution)/shard_map/pallas_call | solution.py:843
  12.3 1.9 %collective-permute-done.2.arrived0 = f32[520,128]{1,0:T(8,128)S(1)} collective-permute-done((f32[520,128]{1,0:T(8,128)S(1)}, f32[520,128]{1,0:T(8,128)S(1)}, u32[]{:S(2)}, u32[]{:S(2)}) %collective-permute-start.2) | collective-permute-done | bytes 266272 | tf_op jit(solution)/shard_map/ppermute | solution.py:870
  14.3 0.0 collective-permute-done.3.arrived1
  14.3 0.0 collective-permute-done.1.earlier_high
  14.3 0.0 collective-permute-done.earlier_low.near
  14.3 0.0 copy-done
  14.3 1.1 %shard_map.111 = (f32[2,64,256]{2,1,0:T(8,128)S(1)}, f32[2,64,256]{2,1,0:T(8,128)S(1)}, f32[2,64,256]{2,1,0:T(8,128)S(1)}, f32[2,64,256]{2,1,0:T(8,128)S(1)}, f3...) custom-call(f32[16,64,256]{2,1,0:T(8,128)S(1)} %bitcast.9, f32[8,64,256]{2,1,0:T(8,128)S(1)} %get-tuple-element.57.low_fields.own, ...), custom_call_target="tpu_custom_call" | custom-call | flops 1000000000 | bytes 4194304 | tf_op jit(solution)/shard_map/pallas_call | solution.py:843
  15.4 0.2 collective-permute-start.4
  15.6 0.1 collective-permute-start.5
  15.6 1.7 %collective-permute-start.6 = (f32[2,64,256]{2,1,0:T(8,128)S(1)}, f32[2,64,256]{2,1,0:T(8,128)S(1)}, u32[]{:S(2)}, u32[]{:S(2)}) collective-permute-start(f32[2,64,256]{2,1,0:T(8,128)S(1)} %get-tuple-element.79), channel_id=1, source_target_pairs={{0,12},{4,8},{8,4},{12,0},{1,13},{5,9},{9,5},{13,1},{2,14},{6,10},... | collective-permute-start | bytes 393224 | tf_op jit(solution)/shard_map/ppermute | solution.py:876
  17.4 1.1 %shard_map.115 = (f32[2,64,256]{2,1,0:T(8,128)S(1)}, f32[2,64,256]{2,1,0:T(8,128)S(1)}, f32[2,64,256]{2,1,0:T(8,128)S(1)}, f32[2,64,256]{2,1,0:T(8,128)S(1)}) custom-call(f32[16,64,256]{2,1,0:T(8,128)S(1)} %bitcast.10, f32[8,64,256]{2,1,0:T(8,128)S(1)} %get-tuple-element.57.low_fields.own, f32[8,64,256]{2,1,0:T(8,128)S(1)} %get-tuple-element.58.high_fields, ...), custom_call_target="tpu_custom_call" | custom-call | flops 1000000000 | bytes 4194304 | tf_op jit(solution)/shard_map/pallas_call | solution.py:843
  18.4 0.4 collective-permute-start.9
  18.8 0.1 collective-permute-start.10
  18.9 0.0 collective-permute-done.4.rest_1_
  18.9 1.4 %collective-permute-start.11 = (f32[2,64,256]{2,1,0:T(8,128)S(1)}, f32[2,64,256]{2,1,0:T(8,128)S(1)}, u32[]{:S(2)}, u32[]{:S(2)}) collective-permute-start(f32[2,64,256]{2,1,0:T(8,128)S(1)} %get-tuple-element.92), channel_id=1, source_target_pairs={{0,12},{4,8},{8,4},{12,0},{1,13},{5,9},{9,5},{13,1},{2,14},{6,10},... | collective-permute-start | bytes 393224 | tf_op jit(solution)/shard_map/ppermute | solution.py:876
  20.3 1.5 %collective-permute-done.5.rest_2_ = f32[2,64,256]{2,1,0:T(8,128)S(1)} collective-permute-done((f32[2,64,256]{2,1,0:T(8,128)S(1)}, f32[2,64,256]{2,1,0:T(8,128)S(1)}, u32[]{:S(2)}, u32[]{:S(2)}) %collective-permute-start.5) | collective-permute-done | bytes 131104 | tf_op jit(solution)/shard_map/ppermute | solution.py:876
  21.9 1.9 %collective-permute-done.6.rest_3_ = f32[2,64,256]{2,1,0:T(8,128)S(1)} collective-permute-done((f32[2,64,256]{2,1,0:T(8,128)S(1)}, f32[2,64,256]{2,1,0:T(8,128)S(1)}, u32[]{:S(2)}, u32[]{:S(2)}) %collective-permute-start.6) | collective-permute-done | bytes 131104 | tf_op jit(solution)/shard_map/ppermute | solution.py:876
  23.7 0.4 shard_map.112
  24.1 1.5 %collective-permute-start.7 = (f32[192,128]{1,0:T(8,128)S(1)}, f32[192,128]{1,0:T(8,128)S(1)}, u32[]{:S(2)}, u32[]{:S(2)}) collective-permute-start(f32[192,128]{1,0:T(8,128)S(1)} %get-tuple-element.83), channel_id=1, source_target_pairs={{0,1},{1,0},{2,3},{3,2},{4,20},{5,6},{6,5},{7,23},{8,9},{9,8},{10,... | collective-permute-start | bytes 294920 | tf_op jit(solution)/shard_map/ppermute | solution.py:870
  25.6 1.5 %collective-permute-start.8 = (f32[192,128]{1,0:T(8,128)S(1)}, f32[192,128]{1,0:T(8,128)S(1)}, u32[]{:S(2)}, u32[]{:S(2)}) collective-permute-start(f32[192,128]{1,0:T(8,128)S(1)} %get-tuple-element.84), channel_id=1, source_target_pairs={{0,16},{1,2},{2,1},{3,19},{4,5},{5,4},{6,7},{7,6},{8,24},{9,10},{1... | collective-permute-start | bytes 294920 | tf_op jit(solution)/shard_map/ppermute | solution.py:870
  27.1 1.8 %shard_map.113 = (f32[8,64,256]{2,1,0:T(8,128)S(1)}, f32[6,2,256]{2,1,0:T(2,128)S(1)}, f32[2,3,128]{2,1,0:T(4,128)S(1)}) custom-call(s32[1,128]{1,0:T(1,128)S(1)} %get-tuple-element.64.flags, f32[8,16,256]{2,1,0:T(8,128)S(1)} %get-tuple-element.73.coefs.coefs_in, bf16[256,1536]{1,0:T(8,128)(2,1)S(1)} %get-tuple-element.74.picks, ...), custom_call_target="tpu_custom_call" | custom-call | flops 1500000000 | bytes 4194304 | tf_op jit(solution)/shard_map/pallas_call | solution.py:843
  29.0 0.0 collective-permute-done.9.rest_1_
  29.0 0.0 collective-permute-done.10.rest_2_
  29.0 0.4 collective-permute-done.11.rest_3_
  29.4 0.4 shard_map.116
  29.7 1.5 %collective-permute-start.12 = (f32[192,128]{1,0:T(8,128)S(1)}, f32[192,128]{1,0:T(8,128)S(1)}, u32[]{:S(2)}, u32[]{:S(2)}) collective-permute-start(f32[192,128]{1,0:T(8,128)S(1)} %get-tuple-element.96), channel_id=1, source_target_pairs={{0,1},{1,0},{2,3},{3,2},{4,20},{5,6},{6,5},{7,23},{8,9},{9,8},{10,... | collective-permute-start | bytes 294920 | tf_op jit(solution)/shard_map/ppermute | solution.py:870
  31.3 1.5 %collective-permute-start.13 = (f32[192,128]{1,0:T(8,128)S(1)}, f32[192,128]{1,0:T(8,128)S(1)}, u32[]{:S(2)}, u32[]{:S(2)}) collective-permute-start(f32[192,128]{1,0:T(8,128)S(1)} %get-tuple-element.97), channel_id=1, source_target_pairs={{0,16},{1,2},{2,1},{3,19},{4,5},{5,4},{6,7},{7,6},{8,24},{9,10},{1... | collective-permute-start | bytes 294920 | tf_op jit(solution)/shard_map/ppermute | solution.py:870
  32.7 1.8 %shard_map.117 = (f32[8,64,256]{2,1,0:T(8,128)S(1)}, f32[6,2,256]{2,1,0:T(2,128)S(1)}, f32[2,3,128]{2,1,0:T(4,128)S(1)}) custom-call(s32[1,128]{1,0:T(1,128)S(1)} %get-tuple-element.64.flags, f32[8,16,256]{2,1,0:T(8,128)S(1)} %get-tuple-element.73.coefs.coefs_in, bf16[256,1536]{1,0:T(8,128)(2,1)S(1)} %get-tuple-element.74.picks, ...), custom_call_target="tpu_custom_call" | custom-call | flops 1500000000 | bytes 4194304 | tf_op jit(solution)/shard_map/pallas_call | solution.py:843
  34.6 0.0 collective-permute-done.7.rest_1_
  34.6 0.0 collective-permute-done.8.rest_2_
  34.6 0.9 %shard_map.114 = (f32[8,64,256]{2,1,0:T(8,128)S(1)}, f32[192,128]{1,0:T(8,128)S(1)}, f32[192,128]{1,0:T(8,128)S(1)}) custom-call(s32[1,128]{1,0:T(1,128)S(1)} %get-tuple-element.64.flags, f32[8,16,256]{2,1,0:T(8,128)S(1)} %get-tuple-element.73.coefs.coefs_in, s32[6,256]{1,0:T(8,128)S(1)} %get-tuple-element.60.face_nbr, ...), custom_call_target="tpu_custom_call" | custom-call | flops 1000000000 | bytes 4194304 | tf_op jit(solution)/shard_map/pallas_call | solution.py:843
  35.5 0.0 collective-permute-done.12.rest_1_
  35.5 0.4 collective-permute-done.13.rest_2_
  35.9 0.9 %shard_map.118 = (f32[8,64,256]{2,1,0:T(8,128)S(1)}, f32[384,128]{1,0:T(8,128)S(1)}, f32[384,128]{1,0:T(8,128)S(1)}) custom-call(s32[1,128]{1,0:T(1,128)S(1)} %get-tuple-element.64.flags, f32[8,16,256]{2,1,0:T(8,128)S(1)} %get-tuple-element.73.coefs.coefs_in, s32[6,256]{1,0:T(8,128)S(1)} %get-tuple-element.60.face_nbr, ...), custom_call_target="tpu_custom_call" | custom-call | flops 1000000000 | bytes 4194304 | tf_op jit(solution)/shard_map/pallas_call | solution.py:843
  36.7 1.5 %collective-permute-start.14 = (f32[384,128]{1,0:T(8,128)S(1)}, f32[384,128]{1,0:T(8,128)S(1)}, u32[]{:S(2)}, u32[]{:S(2)}) collective-permute-start(f32[384,128]{1,0:T(8,128)S(1)} %get-tuple-element.103), channel_id=1, source_target_pairs={{0,1},{1,0},{2,3},{3,2},{4,20},{5,6},{6,5},{7,23},{8,9},{9,8},{10,... | collective-permute-start | bytes 589832 | tf_op jit(solution)/shard_map/ppermute | solution.py:870
  38.2 1.1 %collective-permute-start.15 = (f32[384,128]{1,0:T(8,128)S(1)}, f32[384,128]{1,0:T(8,128)S(1)}, u32[]{:S(2)}, u32[]{:S(2)}) collective-permute-start(f32[384,128]{1,0:T(8,128)S(1)} %get-tuple-element.104), channel_id=1, source_target_pairs={{0,16},{1,2},{2,1},{3,19},{4,5},{5,4},{6,7},{7,6},{8,24},{9,10},{1... | collective-permute-start | bytes 589832 | tf_op jit(solution)/shard_map/ppermute | solution.py:870
  39.3 2.9 %shard_map.119.rest_0_ = f32[16,64,256]{2,1,0:T(8,128)S(1)} custom-call(s32[1,128]{1,0:T(1,128)S(1)} %get-tuple-element.64.flags, f32[8,16,256]{2,1,0:T(8,128)S(1)} %get-tuple-element.73.coefs.coefs_in, bf16[256,1536]{1,0:T(8,128)(2,1)S(1)} %get-tuple-element.74.picks, bf16[128,448]{1,0:T(8,128)(2,1)S(1)} %get-tuple-element.69.blocks, ...), custom_call_target="tpu_custom_call" | custom-call | flops 3000000000 | bytes 4194304 | tf_op jit(solution)/shard_map/pallas_call | solution.py:843
  42.3 2.2 %collective-permute-done.14.rest_1_ = f32[384,128]{1,0:T(8,128)S(1)} collective-permute-done((f32[384,128]{1,0:T(8,128)S(1)}, f32[384,128]{1,0:T(8,128)S(1)}, u32[]{:S(2)}, u32[]{:S(2)}) %collective-permute-start.14) | collective-permute-done | bytes 196640 | tf_op jit(solution)/shard_map/ppermute | solution.py:870
  44.5 0.0 collective-permute-done.15.rest_2_
  44.5 1.1 %shard_map.120 = (f32[4,64,256]{2,1,0:T(8,128)S(1)}, f32[4,64,256]{2,1,0:T(8,128)S(1)}, f32[4,64,256]{2,1,0:T(8,128)S(1)}, f32[4,64,256]{2,1,0:T(8,128)S(1)}) custom-call(s32[1,128]{1,0:T(1,128)S(1)} %get-tuple-element.64.flags, f32[8,16,256]{2,1,0:T(8,128)S(1)} %get-tuple-element.73.coefs.coefs_in, s32[6,256]{1,0:T(8,128)S(1)} %get-tuple-element.60.face_nbr, ...), custom_call_target="tpu_custom_call" | custom-call | flops 1000000000 | bytes 4194304 | tf_op jit(solution)/shard_map/pallas_call | solution.py:843
  45.6 0.2 collective-permute-start.17
  45.8 0.6 collective-permute-start.18
  46.3 1.2 %collective-permute-start.16 = (f32[4,64,256]{2,1,0:T(8,128)S(1)}, f32[4,64,256]{2,1,0:T(8,128)S(1)}, u32[]{:S(2)}, u32[]{:S(2)}) collective-permute-start(f32[4,64,256]{2,1,0:T(8,128)S(1)} %get-tuple-element.105), channel_id=1, source_target_pairs={{0,12},{4,8},{8,4},{12,0},{1,13},{5,9},{9,5},{13,1},{2,14},{6,10},... | collective-permute-start | bytes 786440 | tf_op jit(solution)/shard_map/ppermute | solution.py:876
  47.5 0.0 collective-permute-done.17.rest_1_
  47.6 7.3 %collective-permute-done.18.rest_2_ = f32[4,64,256]{2,1,0:T(8,128)S(1)} collective-permute-done((f32[4,64,256]{2,1,0:T(8,128)S(1)}, f32[4,64,256]{2,1,0:T(8,128)S(1)}, u32[]{:S(2)}, u32[]{:S(2)}) %collective-permute-start.18) | collective-permute-done | bytes 262176 | tf_op jit(solution)/shard_map/ppermute | solution.py:876
  54.9 0.9 %shard_map.121.rest_1_ = f32[16,64,256]{2,1,0:T(8,128)} custom-call(f32[4,64,256]{2,1,0:T(8,128)S(1)} %get-tuple-element.106.rest_0_, f32[4,64,256]{2,1,0:T(8,128)S(1)} %collective-permute-done.17.rest_1_, f32[4,64,256]{2,1,0:T(8,128)S(1)} %collective-permute-done.18.rest_2_), custom_call_target="tpu_custom_call" | custom-call | flops 1000000000 | bytes 4194304 | tf_op jit(solution)/shard_map/pallas_call | solution.py:843
  55.8 3.8 %collective-permute-done.16.rest_0_ = f32[4,64,256]{2,1,0:T(8,128)S(1)} collective-permute-done((f32[4,64,256]{2,1,0:T(8,128)S(1)}, f32[4,64,256]{2,1,0:T(8,128)S(1)}, u32[]{:S(2)}, u32[]{:S(2)}) %collective-permute-start.16) | collective-permute-done | bytes 262176 | tf_op jit(solution)/shard_map/ppermute | solution.py:876
  59.5 0.7 %shard_map.122 = f32[16,64,256]{2,1,0:T(8,128)} custom-call(f32[4,64,256]{2,1,0:T(8,128)S(1)} %collective-permute-done.16.rest_0_, f32[16,64,256]{2,1,0:T(8,128)} %shard_map.121.rest_1_), custom_call_target="tpu_custom_call", output_to_operand_aliasing={{}: (1, {})} | custom-call | flops 1000000000 | bytes 4194304 | tf_op jit(solution)/shard_map/pallas_call | solution.py:843
Async XLA Ops:
  2.2 12.1 %collective-permute-start.1 = (f32[8,64,256]{2,1,0:T(8,128)S(1)}, f32[8,64,256]{2,1,0:T(8,128)S(1)}, u32[]{:S(2)}, u32[]{:S(2)}) collective-permute-start(f32[8,64,256]{2,1,0:T(8,128)S(1)} %get-tuple-element.58.high_fields), channel_id=1, source_target_pairs={{0,4},{4,8},{8,12},{12,0},{1,5},{5,9},{9,13},{13,1},{2,6},{6,10},{... | collective-permute-start | bytes 1572872 | tf_op jit(solution)/shard_map/ppermute | solution.py:946
  2.7 11.6 %collective-permute-start = (f32[8,64,256]{2,1,0:T(8,128)S(1)}, f32[8,64,256]{2,1,0:T(8,128)S(1)}, u32[]{:S(2)}, u32[]{:S(2)}) collective-permute-start(f32[8,64,256]{2,1,0:T(8,128)S(1)} %get-tuple-element.57.low_fields.own), channel_id=1, source_target_pairs={{0,4},{4,0},{8,12},{12,8},{1,5},{5,1},{9,13},{13,9},{2,6},{6,2},{1... | collective-permute-start | bytes 1572872 | tf_op jit(solution)/shard_map/ppermute | solution.py:876
  5.3 9.0 %collective-permute-start.2 = (f32[520,128]{1,0:T(8,128)S(1)}, f32[520,128]{1,0:T(8,128)S(1)}, u32[]{:S(2)}, u32[]{:S(2)}) collective-permute-start(f32[520,128]{1,0:T(8,128)S(1)} %get-tuple-element.66), channel_id=1, source_target_pairs={{0,1},{1,0},{2,3},{3,2},{4,20},{5,6},{6,5},{7,23},{8,9},{9,8},{10,... | collective-permute-start | bytes 798728 | tf_op jit(solution)/shard_map/ppermute | solution.py:870
  6.8 7.4 %collective-permute-start.3 = (f32[520,128]{1,0:T(8,128)S(1)}, f32[520,128]{1,0:T(8,128)S(1)}, u32[]{:S(2)}, u32[]{:S(2)}) collective-permute-start(f32[520,128]{1,0:T(8,128)S(1)} %get-tuple-element.67), channel_id=1, source_target_pairs={{0,16},{1,2},{2,1},{3,19},{4,5},{5,4},{6,7},{7,6},{8,24},{9,10},{1... | collective-permute-start | bytes 798728 | tf_op jit(solution)/shard_map/ppermute | solution.py:870
  8.4 5.9 %copy-start = (f32[16,1,64,256]{3,2,1,0:T(8,128)S(1)}, f32[16,1,64,256]{3,2,1,0:T(8,128)}, u32[]{:S(2)}) copy-start(f32[16,1,64,256]{3,2,1,0:T(8,128)} %param.11) | copy-start | bytes 3145732
  15.4 3.5 %collective-permute-start.4 = (f32[2,64,256]{2,1,0:T(8,128)S(1)}, f32[2,64,256]{2,1,0:T(8,128)S(1)}, u32[]{:S(2)}, u32[]{:S(2)}) collective-permute-start(f32[2,64,256]{2,1,0:T(8,128)S(1)} %get-tuple-element.77), channel_id=1, source_target_pairs={{0,4},{4,0},{8,12},{12,8},{1,5},{5,1},{9,13},{13,9},{2,6},{6,2},{1... | collective-permute-start | bytes 393224 | tf_op jit(solution)/shard_map/ppermute | solution.py:876
  15.6 6.3 %collective-permute-start.5 = (f32[2,64,256]{2,1,0:T(8,128)S(1)}, f32[2,64,256]{2,1,0:T(8,128)S(1)}, u32[]{:S(2)}, u32[]{:S(2)}) collective-permute-start(f32[2,64,256]{2,1,0:T(8,128)S(1)} %get-tuple-element.78), channel_id=1, source_target_pairs={{0,8},{4,12},{8,0},{12,4},{1,9},{5,13},{9,1},{13,5},{2,10},{6,14},... | collective-permute-start | bytes 393224 | tf_op jit(solution)/shard_map/ppermute | solution.py:876
  15.6 8.1 %collective-permute-start.6 = (f32[2,64,256]{2,1,0:T(8,128)S(1)}, f32[2,64,256]{2,1,0:T(8,128)S(1)}, u32[]{:S(2)}, u32[]{:S(2)}) collective-permute-start(f32[2,64,256]{2,1,0:T(8,128)S(1)} %get-tuple-element.79), channel_id=1, source_target_pairs={{0,12},{4,8},{8,4},{12,0},{1,13},{5,9},{9,5},{13,1},{2,14},{6,10},... | collective-permute-start | bytes 393224 | tf_op jit(solution)/shard_map/ppermute | solution.py:876
  18.4 10.6 %collective-permute-start.9 = (f32[2,64,256]{2,1,0:T(8,128)S(1)}, f32[2,64,256]{2,1,0:T(8,128)S(1)}, u32[]{:S(2)}, u32[]{:S(2)}) collective-permute-start(f32[2,64,256]{2,1,0:T(8,128)S(1)} %get-tuple-element.90), channel_id=1, source_target_pairs={{0,4},{4,0},{8,12},{12,8},{1,5},{5,1},{9,13},{13,9},{2,6},{6,2},{1... | collective-permute-start | bytes 393224 | tf_op jit(solution)/shard_map/ppermute | solution.py:876
  18.8 10.2 %collective-permute-start.10 = (f32[2,64,256]{2,1,0:T(8,128)S(1)}, f32[2,64,256]{2,1,0:T(8,128)S(1)}, u32[]{:S(2)}, u32[]{:S(2)}) collective-permute-start(f32[2,64,256]{2,1,0:T(8,128)S(1)} %get-tuple-element.91), channel_id=1, source_target_pairs={{0,8},{4,12},{8,0},{12,4},{1,9},{5,13},{9,1},{13,5},{2,10},{6,14},... | collective-permute-start | bytes 393224 | tf_op jit(solution)/shard_map/ppermute | solution.py:876
  18.9 10.4 %collective-permute-start.11 = (f32[2,64,256]{2,1,0:T(8,128)S(1)}, f32[2,64,256]{2,1,0:T(8,128)S(1)}, u32[]{:S(2)}, u32[]{:S(2)}) collective-permute-start(f32[2,64,256]{2,1,0:T(8,128)S(1)} %get-tuple-element.92), channel_id=1, source_target_pairs={{0,12},{4,8},{8,4},{12,0},{1,13},{5,9},{9,5},{13,1},{2,14},{6,10},... | collective-permute-start | bytes 393224 | tf_op jit(solution)/shard_map/ppermute | solution.py:876
  24.1 10.5 %collective-permute-start.7 = (f32[192,128]{1,0:T(8,128)S(1)}, f32[192,128]{1,0:T(8,128)S(1)}, u32[]{:S(2)}, u32[]{:S(2)}) collective-permute-start(f32[192,128]{1,0:T(8,128)S(1)} %get-tuple-element.83), channel_id=1, source_target_pairs={{0,1},{1,0},{2,3},{3,2},{4,20},{5,6},{6,5},{7,23},{8,9},{9,8},{10,... | collective-permute-start | bytes 294920 | tf_op jit(solution)/shard_map/ppermute | solution.py:870
  25.6 9.0 %collective-permute-start.8 = (f32[192,128]{1,0:T(8,128)S(1)}, f32[192,128]{1,0:T(8,128)S(1)}, u32[]{:S(2)}, u32[]{:S(2)}) collective-permute-start(f32[192,128]{1,0:T(8,128)S(1)} %get-tuple-element.84), channel_id=1, source_target_pairs={{0,16},{1,2},{2,1},{3,19},{4,5},{5,4},{6,7},{7,6},{8,24},{9,10},{1... | collective-permute-start | bytes 294920 | tf_op jit(solution)/shard_map/ppermute | solution.py:870
  29.7 5.7 %collective-permute-start.12 = (f32[192,128]{1,0:T(8,128)S(1)}, f32[192,128]{1,0:T(8,128)S(1)}, u32[]{:S(2)}, u32[]{:S(2)}) collective-permute-start(f32[192,128]{1,0:T(8,128)S(1)} %get-tuple-element.96), channel_id=1, source_target_pairs={{0,1},{1,0},{2,3},{3,2},{4,20},{5,6},{6,5},{7,23},{8,9},{9,8},{10,... | collective-permute-start | bytes 294920 | tf_op jit(solution)/shard_map/ppermute | solution.py:870
  31.3 4.6 %collective-permute-start.13 = (f32[192,128]{1,0:T(8,128)S(1)}, f32[192,128]{1,0:T(8,128)S(1)}, u32[]{:S(2)}, u32[]{:S(2)}) collective-permute-start(f32[192,128]{1,0:T(8,128)S(1)} %get-tuple-element.97), channel_id=1, source_target_pairs={{0,16},{1,2},{2,1},{3,19},{4,5},{5,4},{6,7},{7,6},{8,24},{9,10},{1... | collective-permute-start | bytes 294920 | tf_op jit(solution)/shard_map/ppermute | solution.py:870
  36.7 7.7 %collective-permute-start.14 = (f32[384,128]{1,0:T(8,128)S(1)}, f32[384,128]{1,0:T(8,128)S(1)}, u32[]{:S(2)}, u32[]{:S(2)}) collective-permute-start(f32[384,128]{1,0:T(8,128)S(1)} %get-tuple-element.103), channel_id=1, source_target_pairs={{0,1},{1,0},{2,3},{3,2},{4,20},{5,6},{6,5},{7,23},{8,9},{9,8},{10,... | collective-permute-start | bytes 589832 | tf_op jit(solution)/shard_map/ppermute | solution.py:870
  38.2 6.3 %collective-permute-start.15 = (f32[384,128]{1,0:T(8,128)S(1)}, f32[384,128]{1,0:T(8,128)S(1)}, u32[]{:S(2)}, u32[]{:S(2)}) collective-permute-start(f32[384,128]{1,0:T(8,128)S(1)} %get-tuple-element.104), channel_id=1, source_target_pairs={{0,16},{1,2},{2,1},{3,19},{4,5},{5,4},{6,7},{7,6},{8,24},{9,10},{1... | collective-permute-start | bytes 589832 | tf_op jit(solution)/shard_map/ppermute | solution.py:870
  45.6 2.0 %collective-permute-start.17 = (f32[4,64,256]{2,1,0:T(8,128)S(1)}, f32[4,64,256]{2,1,0:T(8,128)S(1)}, u32[]{:S(2)}, u32[]{:S(2)}) collective-permute-start(f32[4,64,256]{2,1,0:T(8,128)S(1)} %get-tuple-element.107), channel_id=1, source_target_pairs={{0,4},{4,0},{8,12},{12,8},{1,5},{5,1},{9,13},{13,9},{2,6},{6,2},{1... | collective-permute-start | bytes 786440 | tf_op jit(solution)/shard_map/ppermute | solution.py:876
  45.8 9.1 %collective-permute-start.18 = (f32[4,64,256]{2,1,0:T(8,128)S(1)}, f32[4,64,256]{2,1,0:T(8,128)S(1)}, u32[]{:S(2)}, u32[]{:S(2)}) collective-permute-start(f32[4,64,256]{2,1,0:T(8,128)S(1)} %get-tuple-element.108), channel_id=1, source_target_pairs={{0,8},{4,12},{8,0},{12,4},{1,9},{5,13},{9,1},{13,5},{2,10},{6,14},... | collective-permute-start | bytes 786440 | tf_op jit(solution)/shard_map/ppermute | solution.py:876
  46.3 13.2 %collective-permute-start.16 = (f32[4,64,256]{2,1,0:T(8,128)S(1)}, f32[4,64,256]{2,1,0:T(8,128)S(1)}, u32[]{:S(2)}, u32[]{:S(2)}) collective-permute-start(f32[4,64,256]{2,1,0:T(8,128)S(1)} %get-tuple-element.105), channel_id=1, source_target_pairs={{0,12},{4,8},{8,4},{12,0},{1,13},{5,9},{9,5},{13,1},{2,14},{6,10},... | collective-permute-start | bytes 786440 | tf_op jit(solution)/shard_map/ppermute | solution.py:876

commit v7 on v6

--- a/solution.py
+++ b/solution.py
@@ -651,7 +651,7 @@
     if first_turn:
         out, thetas, scales, total, high, low = rest
     else:
-        out, total, high, low = rest
+        out, total, high, low = rest[-4:]
     elems = fields[0].shape[2]
     each = fields[0].shape[0] // total_steps
     samples = inner * each
@@ -810,17 +810,17 @@
             out[s] = total[step * samples + s]
 
 
-def assemble_kernel(*rest, turns, total_steps):
-    count = len(turns)
+def assemble_kernel(*rest, places, total_steps, groups):
+    count = len(places)
     pieces, (out, done) = rest[:count], rest[-2:]
     size = pieces[0].shape[0]
     rank = lax.axis_index("tm")
-    copies = [
-        pltpu.make_async_copy(
-            piece, out.at[pl.ds(partner(rank, turn, total_steps) * size, size)], done.at[which]
-        )
-        for which, (turn, piece) in enumerate(zip(turns, pieces))
-    ]
+    copies = []
+    for which, ((at, turn), piece) in enumerate(zip(places, pieces)):
+        first = (partner(rank, turn, total_steps) * groups + at) * size
+        copies.append(
+            pltpu.make_async_copy(piece, out.at[pl.ds(first, size)], done.at[which])
+        )
     for copy in copies:
         copy.start()
     for copy in copies:
@@ -1037,19 +1037,12 @@
         thetas.append(theta)
         scales.append(scale)
     tables = (flags, coefs, face_nbr, face_blocks, halo_picks)
-    after, packs = [], ()
+    restored = {}
+    arrived = []
     for at in range(groups):
-        rows = (at + 1) * pairs * dofs
+        mine = dict(total_steps=total_steps, at=at, groups=groups)
         current, *packs = run(
-            functools.partial(
-                sweep_update_kernel,
-                turn=0,
-                total_steps=total_steps,
-                last=False,
-                sources=1,
-                at=at,
-                groups=groups,
-            ),
+            functools.partial(sweep_update_kernel, turn=0, last=False, sources=1, **mine),
             (
                 *tables,
                 inners[at],
@@ -1059,55 +1052,44 @@
                 thetas[at],
                 scales[at],
                 send,
-                *packs,
             ),
-            [some] + [((rows, 2 * halo), f32)] * 2,
+            [some, packed, packed],
             [some],
         )
-        after.append(current)
-    some, packed, pairs = sizes(part)
-    arrived0 = neighbour_swap(packs[0], 0)
-    arrived1 = neighbour_swap(packs[1], 1)
-    (inner,) = run(
-        functools.partial(
-            sweep_local_kernel,
-            first_turn=False,
-            inner=groups,
-            total_steps=total_steps,
-            at=0,
-            groups=1,
-        ),
-        (flags, coefs, picks, blocks, halo_picks, *after, *spectra),
-        [some],
-        [some] + splits(part * (total_steps - 1)),
-        flops=3 * 10**9,
-    )
-    series = run(
-        functools.partial(
-            sweep_update_kernel,
-            turn=1,
-            total_steps=total_steps,
-            last=True,
-            sources=groups,
-            at=0,
-            groups=1,
-        ),
-        (*tables, inner, arrived0, arrived1, *after, *thetas, *scales),
-        [((part, dofs, elems), f32)] * devs,
-        [some, some],
-    )
-    restored = [time_swap(series[turn], turn) for turn in range(devs)]
+        currents[at] = current
+        arrived.append([neighbour_swap(pack, which) for which, pack in enumerate(packs)])
+    series = ()
+    for at in range(groups):
+        mine = dict(total_steps=total_steps, at=at, groups=groups)
+        (inner,) = run(
+            functools.partial(sweep_local_kernel, first_turn=False, inner=1, **mine),
+            (flags, coefs, picks, blocks, halo_picks, currents[at], spectra[at], *series[:1]),
+            [some],
+            [some] + splits(share * (total_steps - 1)),
+            flops=3 * 10**9 // groups,
+        )
+        series = run(
+            functools.partial(sweep_update_kernel, turn=1, last=True, sources=1, **mine),
+            (*tables, inner, *arrived[at], currents[at], thetas[at], scales[at]),
+            [piece] * devs,
+            [some, some],
+        )
+        for turn in range(devs):
+            restored[at, turn] = time_swap(series[turn], turn)
     out = None
-    for turns in (range(devs - 1), range(devs - 1, devs)):
-        inputs = [restored[turn] for turn in turns] + ([] if out is None else [out])
+    places = list(restored)
+    for chosen in (places[:-1], places[-1:]):
+        inputs = [restored[place] for place in chosen] + ([] if out is None else [out])
         (out,) = run(
-            functools.partial(assemble_kernel, turns=turns, total_steps=total_steps),
+            functools.partial(
+                assemble_kernel, places=chosen, total_steps=total_steps, groups=groups
+            ),
             tuple(inputs),
             [(cube, f32)],
-            [pltpu.SemaphoreType.DMA((len(turns),))],
-            in_hbm=() if out is None else (len(turns),),
+            [pltpu.SemaphoreType.DMA((len(chosen),))],
+            in_hbm=() if out is None else (len(chosen),),
             out_hbm=(0,),
-            aliases=() if out is None else ((len(turns), 0),),
+            aliases=() if out is None else ((len(chosen), 0),),
         )
     return out.reshape(samples, steps_dev, dofs, elems)
 

time: 60.5 us -> 58.3 us (0.964)
  waiting for transfers between devices: 19.4 us -> 12.4 us
  starting transfers between devices: 20.6 us -> 24.5 us
  Pallas kernels: 20.1 us -> 21 us
    ppermute x10 -> x13, waiting for transfers between devices: 14.8 us -> 10.4 us  [time_swap(): return value if turn == 0 else lax.ppermute(value, 'tm', pairs)]
    ppermute x8 -> x10, waiting for transfers between devices: 4.58 us -> 2.01 us  [neighbour_swap(): return lax.ppermute(value, axes, pairs)]
    ppermute x8 -> x10, starting transfers between devices: 11.6 us -> 13.6 us  [neighbour_swap(): return lax.ppermute(value, axes, pairs)]
    ppermute x10 -> x13, starting transfers between devices: 8.42 us -> 10.3 us  [time_swap(): return value if turn == 0 else lax.ppermute(value, 'tm', pairs)]
    pallas_call x14 -> x16, Pallas kernels: 20.1 us -> 21 us  [run(): pl.pallas_call(kernel, out_shape=[jax.ShapeDtypeStruct(*o) for o in outs]...]
  transfers between devices with their start and end apart: 19 -> 24, of which waited for: 8 -> 8; matrix products, arithmetic and copies ran while one was open for 0% -> 0% of each run, Pallas kernels for 23% -> 29%
where the time goes in v7:
time: 58.3 us; the launch traced here: 58.2 us
  starting transfers between devices  24.5 us (42%)
  Pallas kernels  21 us (36%)
  waiting for transfers between devices  12.4 us (21%)
    pallas_call x16, Pallas kernels, run(): pl.pallas_call(kernel, out_shape=[jax.ShapeDtypeStruct(*o) for o in outs]...  21 us
    ppermute x10, starting transfers between devices, neighbour_swap(): return lax.ppermute(value, axes, pairs)  13.6 us
    ppermute x13, waiting for transfers between devices, time_swap(): return value if turn == 0 else lax.ppermute(value, 'tm', pairs)  10.4 us
    ppermute x13, starting transfers between devices, time_swap(): return value if turn == 0 else lax.ppermute(value, 'tm', pairs)  10.3 us
    ppermute x10, waiting for transfers between devices, neighbour_swap(): return lax.ppermute(value, axes, pairs)  2.01 us
  transfers between devices with their start and end apart: 24, of which 8 were waited for; matrix products, arithmetic and copies ran while one was open for 0% of the time, Pallas kernels for 29%

profile of v7, /device:TPU:0, one launch (start us, length us, event | category | flops | bytes accessed | tf_op | source)
XLA Modules:
  0.0 58.2 jit_solution(1725024390745504919)
XLA Ops:
  0.0 2.1 %shard_map.109 = (f32[520,128]{1,0:T(8,128)S(1)}, f32[520,128]{1,0:T(8,128)S(1)}, bf16[512,256]{1,0:T(8,128)(2,1)S(1)}, f32[16,256]{1,0:T(8,128)S(1)}, f32[8,64,...) custom-call(f32[16,64,256]{2,1,0:T(8,128)} %bitcast.11, ...), custom_call_target="tpu_custom_call" | custom-call | flops 1000000000 | bytes 4194304 | tf_op jit(solution)/shard_map/pallas_call | solution.py:843
  2.2 0.5 collective-permute-start.1
  2.7 2.6 %collective-permute-start = (f32[8,64,256]{2,1,0:T(8,128)S(1)}, f32[8,64,256]{2,1,0:T(8,128)S(1)}, u32[]{:S(2)}, u32[]{:S(2)}) collective-permute-start(f32[8,64,256]{2,1,0:T(8,128)S(1)} %get-tuple-element.61.low_fields.own), channel_id=1, source_target_pairs={{0,4},{4,0},{8,12},{12,8},{1,5},{5,1},{9,13},{13,9},{2,6},{6,2},{1... | collective-permute-start | bytes 1572872 | tf_op jit(solution)/shard_map/ppermute | solution.py:876
  5.3 1.6 %collective-permute-start.2 = (f32[520,128]{1,0:T(8,128)S(1)}, f32[520,128]{1,0:T(8,128)S(1)}, u32[]{:S(2)}, u32[]{:S(2)}) collective-permute-start(f32[520,128]{1,0:T(8,128)S(1)} %get-tuple-element.70), channel_id=1, source_target_pairs={{0,1},{1,0},{2,3},{3,2},{4,20},{5,6},{6,5},{7,23},{8,9},{9,8},{10,... | collective-permute-start | bytes 798728 | tf_op jit(solution)/shard_map/ppermute | solution.py:870
  6.8 1.5 %collective-permute-start.3 = (f32[520,128]{1,0:T(8,128)S(1)}, f32[520,128]{1,0:T(8,128)S(1)}, u32[]{:S(2)}, u32[]{:S(2)}) collective-permute-start(f32[520,128]{1,0:T(8,128)S(1)} %get-tuple-element.71), channel_id=1, source_target_pairs={{0,16},{1,2},{2,1},{3,19},{4,5},{5,4},{6,7},{7,6},{8,24},{9,10},{1... | collective-permute-start | bytes 798728 | tf_op jit(solution)/shard_map/ppermute | solution.py:870
  8.4 4.0 %shard_map.110 = (f32[16,64,256]{2,1,0:T(8,128)S(1)}, f32[8,16,256]{2,1,0:T(8,128)S(1)}, bf16[256,1536]{1,0:T(8,128)(2,1)S(1)}, bf16[128,448]{1,0:T(8,128)(2,1)S...) custom-call(f32[8,64,256]{2,1,0:T(8,128)S(1)} %get-tuple-element.61., ...), custom_call_target="tpu_custom_call" | custom-call | flops 4000000000 | bytes 4194304 | tf_op jit(solution)/shard_map/pallas_call | solution.py:843
  12.3 1.9 %collective-permute-done.2.arrived0 = f32[520,128]{1,0:T(8,128)S(1)} collective-permute-done((f32[520,128]{1,0:T(8,128)S(1)}, f32[520,128]{1,0:T(8,128)S(1)}, u32[]{:S(2)}, u32[]{:S(2)}) %collective-permute-start.2) | collective-permute-done | bytes 266272 | tf_op jit(solution)/shard_map/ppermute | solution.py:870
  14.3 0.0 collective-permute-done.3.arrived1
  14.3 0.0 collective-permute-done.1.earlier_high
  14.3 0.0 collective-permute-done.earlier_low.near
  14.3 1.1 %shard_map.111 = (f32[2,64,256]{2,1,0:T(8,128)S(1)}, f32[2,64,256]{2,1,0:T(8,128)S(1)}, f32[2,64,256]{2,1,0:T(8,128)S(1)}, f32[2,64,256]{2,1,0:T(8,128)S(1)}, f3...) custom-call(f32[16,64,256]{2,1,0:T(8,128)S(1)} %bitcast.9, f32[8,64,256]{2,1,0:T(8,128)S(1)} %get-tuple-element.61.low_fields.own, ...), custom_call_target="tpu_custom_call" | custom-call | flops 1000000000 | bytes 4194304 | tf_op jit(solution)/shard_map/pallas_call | solution.py:843
  15.4 0.2 collective-permute-start.7
  15.6 0.1 collective-permute-start.8
  15.6 1.7 %collective-permute-start.9 = (f32[2,64,256]{2,1,0:T(8,128)S(1)}, f32[2,64,256]{2,1,0:T(8,128)S(1)}, u32[]{:S(2)}, u32[]{:S(2)}) collective-permute-start(f32[2,64,256]{2,1,0:T(8,128)S(1)} %get-tuple-element.88), channel_id=1, source_target_pairs={{0,12},{4,8},{8,4},{12,0},{1,13},{5,9},{9,5},{13,1},{2,14},{6,10},... | collective-permute-start | bytes 393224 | tf_op jit(solution)/shard_map/ppermute | solution.py:876
  17.3 1.1 %shard_map.112 = (f32[2,64,256]{2,1,0:T(8,128)S(1)}, f32[2,64,256]{2,1,0:T(8,128)S(1)}, f32[2,64,256]{2,1,0:T(8,128)S(1)}, f32[2,64,256]{2,1,0:T(8,128)S(1)}) custom-call(f32[16,64,256]{2,1,0:T(8,128)S(1)} %bitcast.10, f32[8,64,256]{2,1,0:T(8,128)S(1)} %get-tuple-element.61.low_fields.own, f32[8,64,256]{2,1,0:T(8,128)S(1)} %get-tuple-element.62.high_fields, ...), custom_call_target="tpu_custom_call" | custom-call | flops 1000000000 | bytes 4194304 | tf_op jit(solution)/shard_map/pallas_call | solution.py:843
  18.4 0.4 collective-permute-start.4
  18.8 0.1 collective-permute-start.5
  18.9 0.0 collective-permute-done.7.rest_1_
  18.9 1.4 %collective-permute-start.6 = (f32[2,64,256]{2,1,0:T(8,128)S(1)}, f32[2,64,256]{2,1,0:T(8,128)S(1)}, u32[]{:S(2)}, u32[]{:S(2)}) collective-permute-start(f32[2,64,256]{2,1,0:T(8,128)S(1)} %get-tuple-element.84), channel_id=1, source_target_pairs={{0,12},{4,8},{8,4},{12,0},{1,13},{5,9},{9,5},{13,1},{2,14},{6,10},... | collective-permute-start | bytes 393224 | tf_op jit(solution)/shard_map/ppermute | solution.py:876
  20.3 1.5 %collective-permute-done.8.rest_2_ = f32[2,64,256]{2,1,0:T(8,128)S(1)} collective-permute-done((f32[2,64,256]{2,1,0:T(8,128)S(1)}, f32[2,64,256]{2,1,0:T(8,128)S(1)}, u32[]{:S(2)}, u32[]{:S(2)}) %collective-permute-start.8) | collective-permute-done | bytes 131104 | tf_op jit(solution)/shard_map/ppermute | solution.py:876
  21.9 1.9 %collective-permute-done.9.rest_3_ = f32[2,64,256]{2,1,0:T(8,128)S(1)} collective-permute-done((f32[2,64,256]{2,1,0:T(8,128)S(1)}, f32[2,64,256]{2,1,0:T(8,128)S(1)}, u32[]{:S(2)}, u32[]{:S(2)}) %collective-permute-start.9) | collective-permute-done | bytes 131104 | tf_op jit(solution)/shard_map/ppermute | solution.py:876
  23.7 0.4 shard_map.113
  24.1 1.5 %collective-permute-start.12 = (f32[192,128]{1,0:T(8,128)S(1)}, f32[192,128]{1,0:T(8,128)S(1)}, u32[]{:S(2)}, u32[]{:S(2)}) collective-permute-start(f32[192,128]{1,0:T(8,128)S(1)} %get-tuple-element.101), channel_id=1, source_target_pairs={{0,1},{1,0},{2,3},{3,2},{4,20},{5,6},{6,5},{7,23},{8,9},{9,8},{10,... | collective-permute-start | bytes 294920 | tf_op jit(solution)/shard_map/ppermute | solution.py:870
  25.6 1.5 %collective-permute-start.13 = (f32[192,128]{1,0:T(8,128)S(1)}, f32[192,128]{1,0:T(8,128)S(1)}, u32[]{:S(2)}, u32[]{:S(2)}) collective-permute-start(f32[192,128]{1,0:T(8,128)S(1)} %get-tuple-element.102), channel_id=1, source_target_pairs={{0,16},{1,2},{2,1},{3,19},{4,5},{5,4},{6,7},{7,6},{8,24},{9,10},{1... | collective-permute-start | bytes 294920 | tf_op jit(solution)/shard_map/ppermute | solution.py:870
  27.1 1.8 %shard_map.114 = (f32[8,64,256]{2,1,0:T(8,128)S(1)}, f32[6,2,256]{2,1,0:T(2,128)S(1)}, f32[2,3,128]{2,1,0:T(4,128)S(1)}) custom-call(s32[1,128]{1,0:T(1,128)S(1)} %get-tuple-element.68.flags, f32[8,16,256]{2,1,0:T(8,128)S(1)} %get-tuple-element.77.coefs_in.coefs, bf16[256,1536]{1,0:T(8,128)(2,1)S(1)} %get-tuple-element.78.picks, ...), custom_call_target="tpu_custom_call" | custom-call | flops 1500000000 | bytes 4194304 | tf_op jit(solution)/shard_map/pallas_call | solution.py:843
  28.9 0.0 collective-permute-done.4.rest_1_
  29.0 0.0 collective-permute-done.5.rest_2_
  29.0 0.4 collective-permute-done.6.rest_3_
  29.3 0.4 shard_map.115
  29.7 1.5 %collective-permute-start.10 = (f32[192,128]{1,0:T(8,128)S(1)}, f32[192,128]{1,0:T(8,128)S(1)}, u32[]{:S(2)}, u32[]{:S(2)}) collective-permute-start(f32[192,128]{1,0:T(8,128)S(1)} %get-tuple-element.95), channel_id=1, source_target_pairs={{0,1},{1,0},{2,3},{3,2},{4,20},{5,6},{6,5},{7,23},{8,9},{9,8},{10,... | collective-permute-start | bytes 294920 | tf_op jit(solution)/shard_map/ppermute | solution.py:870
  31.2 1.5 %collective-permute-start.11 = (f32[192,128]{1,0:T(8,128)S(1)}, f32[192,128]{1,0:T(8,128)S(1)}, u32[]{:S(2)}, u32[]{:S(2)}) collective-permute-start(f32[192,128]{1,0:T(8,128)S(1)} %get-tuple-element.96), channel_id=1, source_target_pairs={{0,16},{1,2},{2,1},{3,19},{4,5},{5,4},{6,7},{7,6},{8,24},{9,10},{1... | collective-permute-start | bytes 294920 | tf_op jit(solution)/shard_map/ppermute | solution.py:870
  32.7 1.8 %shard_map.116 = (f32[8,64,256]{2,1,0:T(8,128)S(1)}, f32[6,2,256]{2,1,0:T(2,128)S(1)}, f32[2,3,128]{2,1,0:T(4,128)S(1)}) custom-call(s32[1,128]{1,0:T(1,128)S(1)} %get-tuple-element.68.flags, f32[8,16,256]{2,1,0:T(8,128)S(1)} %get-tuple-element.77.coefs_in.coefs, bf16[256,1536]{1,0:T(8,128)(2,1)S(1)} %get-tuple-element.78.picks, ...), custom_call_target="tpu_custom_call" | custom-call | flops 1500000000 | bytes 4194304 | tf_op jit(solution)/shard_map/pallas_call | solution.py:843
  34.6 0.0 collective-permute-done.12.rest_1_
  34.6 0.0 collective-permute-done.13.rest_2_
  34.6 0.9 %shard_map.118 = (f32[8,64,256]{2,1,0:T(8,128)S(1)}, f32[192,128]{1,0:T(8,128)S(1)}, f32[192,128]{1,0:T(8,128)S(1)}) custom-call(s32[1,128]{1,0:T(1,128)S(1)} %get-tuple-element.68.flags, f32[8,16,256]{2,1,0:T(8,128)S(1)} %get-tuple-element.77.coefs_in.coefs, s32[6,256]{1,0:T(8,128)S(1)} %get-tuple-element.64.face_nbr, ...), custom_call_target="tpu_custom_call" | custom-call | flops 1000000000 | bytes 4194304 | tf_op jit(solution)/shard_map/pallas_call | solution.py:843
  35.4 1.9 %collective-permute-start.14 = (f32[192,128]{1,0:T(8,128)S(1)}, f32[192,128]{1,0:T(8,128)S(1)}, u32[]{:S(2)}, u32[]{:S(2)}) collective-permute-start(f32[192,128]{1,0:T(8,128)S(1)} %get-tuple-element.105), channel_id=1, source_target_pairs={{0,1},{1,0},{2,3},{3,2},{4,20},{5,6},{6,5},{7,23},{8,9},{9,8},{10,... | collective-permute-start | bytes 294920 | tf_op jit(solution)/shard_map/ppermute | solution.py:870
  37.3 1.1 %collective-permute-start.15 = (f32[192,128]{1,0:T(8,128)S(1)}, f32[192,128]{1,0:T(8,128)S(1)}, u32[]{:S(2)}, u32[]{:S(2)}) collective-permute-start(f32[192,128]{1,0:T(8,128)S(1)} %get-tuple-element.106), channel_id=1, source_target_pairs={{0,16},{1,2},{2,1},{3,19},{4,5},{5,4},{6,7},{7,6},{8,24},{9,10},{1... | collective-permute-start | bytes 294920 | tf_op jit(solution)/shard_map/ppermute | solution.py:870
  38.4 0.0 collective-permute-done.10.rest_1_
  38.4 0.0 collective-permute-done.11.rest_2_
  38.4 0.9 %shard_map.117 = (f32[8,64,256]{2,1,0:T(8,128)S(1)}, f32[192,128]{1,0:T(8,128)S(1)}, f32[192,128]{1,0:T(8,128)S(1)}) custom-call(s32[1,128]{1,0:T(1,128)S(1)} %get-tuple-element.68.flags, f32[8,16,256]{2,1,0:T(8,128)S(1)} %get-tuple-element.77.coefs_in.coefs, s32[6,256]{1,0:T(8,128)S(1)} %get-tuple-element.64.face_nbr, ...), custom_call_target="tpu_custom_call" | custom-call | flops 1000000000 | bytes 4194304 | tf_op jit(solution)/shard_map/pallas_call | solution.py:843
  39.3 0.5 collective-permute-start.16
  39.7 1.2 %collective-permute-start.17 = (f32[192,128]{1,0:T(8,128)S(1)}, f32[192,128]{1,0:T(8,128)S(1)}, u32[]{:S(2)}, u32[]{:S(2)}) collective-permute-start(f32[192,128]{1,0:T(8,128)S(1)} %get-tuple-element.109), channel_id=1, source_target_pairs={{0,16},{1,2},{2,1},{3,19},{4,5},{5,4},{6,7},{7,6},{8,24},{9,10},{1... | collective-permute-start | bytes 294920 | tf_op jit(solution)/shard_map/ppermute | solution.py:870
  40.9 1.7 %shard_map.119.rest_0_ = f32[8,64,256]{2,1,0:T(8,128)S(1)} custom-call(s32[1,128]{1,0:T(1,128)S(1)} %get-tuple-element.68.flags, f32[8,16,256]{2,1,0:T(8,128)S(1)} %get-tuple-element.77.coefs_in.coefs, bf16[256,1536]{1,0:T(8,128)(2,1)S(1)} %get-tuple-element.78.picks, bf16[128,448]{1,0:T(8,128)(2,1)S(1)} %get-tuple-element.73.blocks, ...), custom_call_target="tpu_custom_call" | custom-call | flops 1500000000 | bytes 4194304 | tf_op jit(solution)/shard_map/pallas_call | solution.py:843
  42.6 0.0 collective-permute-done.14.rest_1_
  42.6 0.0 collective-permute-done.15.rest_2_
  42.7 0.7 %shard_map.120 = (f32[2,64,256]{2,1,0:T(8,128)S(1)}, f32[2,64,256]{2,1,0:T(8,128)S(1)}, f32[2,64,256]{2,1,0:T(8,128)S(1)}, f32[2,64,256]{2,1,0:T(8,128)S(1)}) custom-call(s32[1,128]{1,0:T(1,128)S(1)} %get-tuple-element.68.flags, f32[8,16,256]{2,1,0:T(8,128)S(1)} %get-tuple-element.77.coefs_in.coefs, s32[6,256]{1,0:T(8,128)S(1)} %get-tuple-element.64.face_nbr, ...), custom_call_target="tpu_custom_call" | custom-call | flops 1000000000 | bytes 4194304 | tf_op jit(solution)/shard_map/pallas_call | solution.py:843
  43.4 0.1 collective-permute-start.19
  43.5 0.7 %collective-permute-start.20 = (f32[2,64,256]{2,1,0:T(8,128)S(1)}, f32[2,64,256]{2,1,0:T(8,128)S(1)}, u32[]{:S(2)}, u32[]{:S(2)}) collective-permute-start(f32[2,64,256]{2,1,0:T(8,128)S(1)} %get-tuple-element.112), channel_id=1, source_target_pairs={{0,8},{4,12},{8,0},{12,4},{1,9},{5,13},{9,1},{13,5},{2,10},{6,14},... | collective-permute-start | bytes 393224 | tf_op jit(solution)/shard_map/ppermute | solution.py:876
  44.2 1.2 %collective-permute-start.21 = (f32[2,64,256]{2,1,0:T(8,128)S(1)}, f32[2,64,256]{2,1,0:T(8,128)S(1)}, u32[]{:S(2)}, u32[]{:S(2)}) collective-permute-start(f32[2,64,256]{2,1,0:T(8,128)S(1)} %get-tuple-element.113), channel_id=1, source_target_pairs={{0,12},{4,8},{8,4},{12,0},{1,13},{5,9},{9,5},{13,1},{2,14},{6,10},... | collective-permute-start | bytes 393224 | tf_op jit(solution)/shard_map/ppermute | solution.py:876
  45.4 1.7 %shard_map.121.rest_0_ = f32[8,64,256]{2,1,0:T(8,128)S(1)} custom-call(s32[1,128]{1,0:T(1,128)S(1)} %get-tuple-element.68.flags, f32[8,16,256]{2,1,0:T(8,128)S(1)} %get-tuple-element.77.coefs_in.coefs, bf16[256,1536]{1,0:T(8,128)(2,1)S(1)} %get-tuple-element.78.picks, bf16[128,448]{1,0:T(8,128)(2,1)S(1)} %get-tuple-element.73.blocks, ...), custom_call_target="tpu_custom_call" | custom-call | flops 1500000000 | bytes 4194304 | tf_op jit(solution)/shard_map/pallas_call | solution.py:843
  47.1 0.0 collective-permute-done.16.rest_1_
  47.1 0.0 collective-permute-done.17.rest_2_
  47.1 0.8 %shard_map.122 = (f32[2,64,256]{2,1,0:T(8,128)S(1)}, f32[2,64,256]{2,1,0:T(8,128)S(1)}, f32[2,64,256]{2,1,0:T(8,128)S(1)}, f32[2,64,256]{2,1,0:T(8,128)S(1)}) custom-call(s32[1,128]{1,0:T(1,128)S(1)} %get-tuple-element.68.flags, f32[8,16,256]{2,1,0:T(8,128)S(1)} %get-tuple-element.77.coefs_in.coefs, s32[6,256]{1,0:T(8,128)S(1)} %get-tuple-element.64.face_nbr, ...), custom_call_target="tpu_custom_call" | custom-call | flops 1000000000 | bytes 4194304 | tf_op jit(solution)/shard_map/pallas_call | solution.py:843
  47.8 0.4 collective-permute-start.22
  48.3 0.6 %collective-permute-start.23 = (f32[2,64,256]{2,1,0:T(8,128)S(1)}, f32[2,64,256]{2,1,0:T(8,128)S(1)}, u32[]{:S(2)}, u32[]{:S(2)}) collective-permute-start(f32[2,64,256]{2,1,0:T(8,128)S(1)} %get-tuple-element.116), channel_id=1, source_target_pairs={{0,8},{4,12},{8,0},{12,4},{1,9},{5,13},{9,1},{13,5},{2,10},{6,14},... | collective-permute-start | bytes 393224 | tf_op jit(solution)/shard_map/ppermute | solution.py:876
  48.9 0.0 collective-permute-done.19.rest_1_
  48.9 0.9 %collective-permute-start.18 = (f32[2,64,256]{2,1,0:T(8,128)S(1)}, f32[2,64,256]{2,1,0:T(8,128)S(1)}, u32[]{:S(2)}, u32[]{:S(2)}) collective-permute-start(f32[2,64,256]{2,1,0:T(8,128)S(1)} %get-tuple-element.110), channel_id=1, source_target_pairs={{0,12},{4,8},{8,4},{12,0},{1,13},{5,9},{9,5},{13,1},{2,14},{6,10},... | collective-permute-start | bytes 393224 | tf_op jit(solution)/shard_map/ppermute | solution.py:876
  49.8 0.1 collective-permute-done.20.rest_2_
  49.9 1.9 %collective-permute-done.21.rest_3_ = f32[2,64,256]{2,1,0:T(8,128)S(1)} collective-permute-done((f32[2,64,256]{2,1,0:T(8,128)S(1)}, f32[2,64,256]{2,1,0:T(8,128)S(1)}, u32[]{:S(2)}, u32[]{:S(2)}) %collective-permute-start.21) | collective-permute-done | bytes 131104 | tf_op jit(solution)/shard_map/ppermute | solution.py:876
  51.8 0.0 collective-permute-done.22.rest_5_
  51.8 3.7 %collective-permute-done.23.rest_6_ = f32[2,64,256]{2,1,0:T(8,128)S(1)} collective-permute-done((f32[2,64,256]{2,1,0:T(8,128)S(1)}, f32[2,64,256]{2,1,0:T(8,128)S(1)}, u32[]{:S(2)}, u32[]{:S(2)}) %collective-permute-start.23) | collective-permute-done | bytes 131104 | tf_op jit(solution)/shard_map/ppermute | solution.py:876
  55.5 1.0 %shard_map.123.rest_1_ = f32[16,64,256]{2,1,0:T(8,128)} custom-call(f32[2,64,256]{2,1,0:T(8,128)S(1)} %get-tuple-element.107.rest_2_.rest_0_, f32[2,64,256]{2,1,0:T(8,128)S(1)} %collective-permute-done.19.rest_1_, f32[2,64,256]{2,1,0:T(8,128)S(1)} %collective-permute-done.20.rest_2_, f32[2,64,256]{2,1,0:T(8,128)S(1)} %collective-permute-done.21.rest_3_, ...), custom_call_target="tpu_custom_call" | custom-call | flops 1000000000 | bytes 4194304 | tf_op jit(solution)/shard_map/pallas_call | solution.py:843
  56.5 0.9 %collective-permute-done.18.rest_0_ = f32[2,64,256]{2,1,0:T(8,128)S(1)} collective-permute-done((f32[2,64,256]{2,1,0:T(8,128)S(1)}, f32[2,64,256]{2,1,0:T(8,128)S(1)}, u32[]{:S(2)}, u32[]{:S(2)}) %collective-permute-start.18) | collective-permute-done | bytes 131104 | tf_op jit(solution)/shard_map/ppermute | solution.py:876
  57.4 0.7 %shard_map.124 = f32[16,64,256]{2,1,0:T(8,128)} custom-call(f32[2,64,256]{2,1,0:T(8,128)S(1)} %collective-permute-done.18.rest_0_, f32[16,64,256]{2,1,0:T(8,128)} %shard_map.123.rest_1_), custom_call_target="tpu_custom_call", output_to_operand_aliasing={{}: (1, {})} | custom-call | flops 1000000000 | bytes 4194304 | tf_op jit(solution)/shard_map/pallas_call | solution.py:843
  (2 shorter events, 0.0 us)
Async XLA Ops:
  2.2 12.1 %collective-permute-start.1 = (f32[8,64,256]{2,1,0:T(8,128)S(1)}, f32[8,64,256]{2,1,0:T(8,128)S(1)}, u32[]{:S(2)}, u32[]{:S(2)}) collective-permute-start(f32[8,64,256]{2,1,0:T(8,128)S(1)} %get-tuple-element.62.high_fields), channel_id=1, source_target_pairs={{0,4},{4,8},{8,12},{12,0},{1,5},{5,9},{9,13},{13,1},{2,6},{6,10},{... | collective-permute-start | bytes 1572872 | tf_op jit(solution)/shard_map/ppermute | solution.py:946
  2.7 11.6 %collective-permute-start = (f32[8,64,256]{2,1,0:T(8,128)S(1)}, f32[8,64,256]{2,1,0:T(8,128)S(1)}, u32[]{:S(2)}, u32[]{:S(2)}) collective-permute-start(f32[8,64,256]{2,1,0:T(8,128)S(1)} %get-tuple-element.61.low_fields.own), channel_id=1, source_target_pairs={{0,4},{4,0},{8,12},{12,8},{1,5},{5,1},{9,13},{13,9},{2,6},{6,2},{1... | collective-permute-start | bytes 1572872 | tf_op jit(solution)/shard_map/ppermute | solution.py:876
  5.3 9.0 %collective-permute-start.2 = (f32[520,128]{1,0:T(8,128)S(1)}, f32[520,128]{1,0:T(8,128)S(1)}, u32[]{:S(2)}, u32[]{:S(2)}) collective-permute-start(f32[520,128]{1,0:T(8,128)S(1)} %get-tuple-element.70), channel_id=1, source_target_pairs={{0,1},{1,0},{2,3},{3,2},{4,20},{5,6},{6,5},{7,23},{8,9},{9,8},{10,... | collective-permute-start | bytes 798728 | tf_op jit(solution)/shard_map/ppermute | solution.py:870
  6.8 7.4 %collective-permute-start.3 = (f32[520,128]{1,0:T(8,128)S(1)}, f32[520,128]{1,0:T(8,128)S(1)}, u32[]{:S(2)}, u32[]{:S(2)}) collective-permute-start(f32[520,128]{1,0:T(8,128)S(1)} %get-tuple-element.71), channel_id=1, source_target_pairs={{0,16},{1,2},{2,1},{3,19},{4,5},{5,4},{6,7},{7,6},{8,24},{9,10},{1... | collective-permute-start | bytes 798728 | tf_op jit(solution)/shard_map/ppermute | solution.py:870
  8.4 5.9 %copy-start = (f32[16,1,64,256]{3,2,1,0:T(8,128)S(1)}, f32[16,1,64,256]{3,2,1,0:T(8,128)}, u32[]{:S(2)}) copy-start(f32[16,1,64,256]{3,2,1,0:T(8,128)} %param.11) | copy-start | bytes 3145732
  15.4 3.5 %collective-permute-start.7 = (f32[2,64,256]{2,1,0:T(8,128)S(1)}, f32[2,64,256]{2,1,0:T(8,128)S(1)}, u32[]{:S(2)}, u32[]{:S(2)}) collective-permute-start(f32[2,64,256]{2,1,0:T(8,128)S(1)} %get-tuple-element.86), channel_id=1, source_target_pairs={{0,4},{4,0},{8,12},{12,8},{1,5},{5,1},{9,13},{13,9},{2,6},{6,2},{1... | collective-permute-start | bytes 393224 | tf_op jit(solution)/shard_map/ppermute | solution.py:876
  15.6 6.3 %collective-permute-start.8 = (f32[2,64,256]{2,1,0:T(8,128)S(1)}, f32[2,64,256]{2,1,0:T(8,128)S(1)}, u32[]{:S(2)}, u32[]{:S(2)}) collective-permute-start(f32[2,64,256]{2,1,0:T(8,128)S(1)} %get-tuple-element.87), channel_id=1, source_target_pairs={{0,8},{4,12},{8,0},{12,4},{1,9},{5,13},{9,1},{13,5},{2,10},{6,14},... | collective-permute-start | bytes 393224 | tf_op jit(solution)/shard_map/ppermute | solution.py:876
  15.6 8.1 %collective-permute-start.9 = (f32[2,64,256]{2,1,0:T(8,128)S(1)}, f32[2,64,256]{2,1,0:T(8,128)S(1)}, u32[]{:S(2)}, u32[]{:S(2)}) collective-permute-start(f32[2,64,256]{2,1,0:T(8,128)S(1)} %get-tuple-element.88), channel_id=1, source_target_pairs={{0,12},{4,8},{8,4},{12,0},{1,13},{5,9},{9,5},{13,1},{2,14},{6,10},... | collective-permute-start | bytes 393224 | tf_op jit(solution)/shard_map/ppermute | solution.py:876
  18.4 10.6 %collective-permute-start.4 = (f32[2,64,256]{2,1,0:T(8,128)S(1)}, f32[2,64,256]{2,1,0:T(8,128)S(1)}, u32[]{:S(2)}, u32[]{:S(2)}) collective-permute-start(f32[2,64,256]{2,1,0:T(8,128)S(1)} %get-tuple-element.82), channel_id=1, source_target_pairs={{0,4},{4,0},{8,12},{12,8},{1,5},{5,1},{9,13},{13,9},{2,6},{6,2},{1... | collective-permute-start | bytes 393224 | tf_op jit(solution)/shard_map/ppermute | solution.py:876
  18.8 10.1 %collective-permute-start.5 = (f32[2,64,256]{2,1,0:T(8,128)S(1)}, f32[2,64,256]{2,1,0:T(8,128)S(1)}, u32[]{:S(2)}, u32[]{:S(2)}) collective-permute-start(f32[2,64,256]{2,1,0:T(8,128)S(1)} %get-tuple-element.83), channel_id=1, source_target_pairs={{0,8},{4,12},{8,0},{12,4},{1,9},{5,13},{9,1},{13,5},{2,10},{6,14},... | collective-permute-start | bytes 393224 | tf_op jit(solution)/shard_map/ppermute | solution.py:876
  18.9 10.4 %collective-permute-start.6 = (f32[2,64,256]{2,1,0:T(8,128)S(1)}, f32[2,64,256]{2,1,0:T(8,128)S(1)}, u32[]{:S(2)}, u32[]{:S(2)}) collective-permute-start(f32[2,64,256]{2,1,0:T(8,128)S(1)} %get-tuple-element.84), channel_id=1, source_target_pairs={{0,12},{4,8},{8,4},{12,0},{1,13},{5,9},{9,5},{13,1},{2,14},{6,10},... | collective-permute-start | bytes 393224 | tf_op jit(solution)/shard_map/ppermute | solution.py:876
  24.1 10.4 %collective-permute-start.12 = (f32[192,128]{1,0:T(8,128)S(1)}, f32[192,128]{1,0:T(8,128)S(1)}, u32[]{:S(2)}, u32[]{:S(2)}) collective-permute-start(f32[192,128]{1,0:T(8,128)S(1)} %get-tuple-element.101), channel_id=1, source_target_pairs={{0,1},{1,0},{2,3},{3,2},{4,20},{5,6},{6,5},{7,23},{8,9},{9,8},{10,... | collective-permute-start | bytes 294920 | tf_op jit(solution)/shard_map/ppermute | solution.py:870
  25.6 9.0 %collective-permute-start.13 = (f32[192,128]{1,0:T(8,128)S(1)}, f32[192,128]{1,0:T(8,128)S(1)}, u32[]{:S(2)}, u32[]{:S(2)}) collective-permute-start(f32[192,128]{1,0:T(8,128)S(1)} %get-tuple-element.102), channel_id=1, source_target_pairs={{0,16},{1,2},{2,1},{3,19},{4,5},{5,4},{6,7},{7,6},{8,24},{9,10},{1... | collective-permute-start | bytes 294920 | tf_op jit(solution)/shard_map/ppermute | solution.py:870
  29.7 8.7 %collective-permute-start.10 = (f32[192,128]{1,0:T(8,128)S(1)}, f32[192,128]{1,0:T(8,128)S(1)}, u32[]{:S(2)}, u32[]{:S(2)}) collective-permute-start(f32[192,128]{1,0:T(8,128)S(1)} %get-tuple-element.95), channel_id=1, source_target_pairs={{0,1},{1,0},{2,3},{3,2},{4,20},{5,6},{6,5},{7,23},{8,9},{9,8},{10,... | collective-permute-start | bytes 294920 | tf_op jit(solution)/shard_map/ppermute | solution.py:870
  31.2 7.1 %collective-permute-start.11 = (f32[192,128]{1,0:T(8,128)S(1)}, f32[192,128]{1,0:T(8,128)S(1)}, u32[]{:S(2)}, u32[]{:S(2)}) collective-permute-start(f32[192,128]{1,0:T(8,128)S(1)} %get-tuple-element.96), channel_id=1, source_target_pairs={{0,16},{1,2},{2,1},{3,19},{4,5},{5,4},{6,7},{7,6},{8,24},{9,10},{1... | collective-permute-start | bytes 294920 | tf_op jit(solution)/shard_map/ppermute | solution.py:870
  35.4 7.2 %collective-permute-start.14 = (f32[192,128]{1,0:T(8,128)S(1)}, f32[192,128]{1,0:T(8,128)S(1)}, u32[]{:S(2)}, u32[]{:S(2)}) collective-permute-start(f32[192,128]{1,0:T(8,128)S(1)} %get-tuple-element.105), channel_id=1, source_target_pairs={{0,1},{1,0},{2,3},{3,2},{4,20},{5,6},{6,5},{7,23},{8,9},{9,8},{10,... | collective-permute-start | bytes 294920 | tf_op jit(solution)/shard_map/ppermute | solution.py:870
  37.3 5.4 %collective-permute-start.15 = (f32[192,128]{1,0:T(8,128)S(1)}, f32[192,128]{1,0:T(8,128)S(1)}, u32[]{:S(2)}, u32[]{:S(2)}) collective-permute-start(f32[192,128]{1,0:T(8,128)S(1)} %get-tuple-element.106), channel_id=1, source_target_pairs={{0,16},{1,2},{2,1},{3,19},{4,5},{5,4},{6,7},{7,6},{8,24},{9,10},{1... | collective-permute-start | bytes 294920 | tf_op jit(solution)/shard_map/ppermute | solution.py:870
  39.3 7.8 %collective-permute-start.16 = (f32[192,128]{1,0:T(8,128)S(1)}, f32[192,128]{1,0:T(8,128)S(1)}, u32[]{:S(2)}, u32[]{:S(2)}) collective-permute-start(f32[192,128]{1,0:T(8,128)S(1)} %get-tuple-element.108), channel_id=1, source_target_pairs={{0,1},{1,0},{2,3},{3,2},{4,20},{5,6},{6,5},{7,23},{8,9},{9,8},{10,... | collective-permute-start | bytes 294920 | tf_op jit(solution)/shard_map/ppermute | solution.py:870
  39.7 7.4 %collective-permute-start.17 = (f32[192,128]{1,0:T(8,128)S(1)}, f32[192,128]{1,0:T(8,128)S(1)}, u32[]{:S(2)}, u32[]{:S(2)}) collective-permute-start(f32[192,128]{1,0:T(8,128)S(1)} %get-tuple-element.109), channel_id=1, source_target_pairs={{0,16},{1,2},{2,1},{3,19},{4,5},{5,4},{6,7},{7,6},{8,24},{9,10},{1... | collective-permute-start | bytes 294920 | tf_op jit(solution)/shard_map/ppermute | solution.py:870
  43.4 5.4 %collective-permute-start.19 = (f32[2,64,256]{2,1,0:T(8,128)S(1)}, f32[2,64,256]{2,1,0:T(8,128)S(1)}, u32[]{:S(2)}, u32[]{:S(2)}) collective-permute-start(f32[2,64,256]{2,1,0:T(8,128)S(1)} %get-tuple-element.111), channel_id=1, source_target_pairs={{0,4},{4,0},{8,12},{12,8},{1,5},{5,1},{9,13},{13,9},{2,6},{6,2},{1... | collective-permute-start | bytes 393224 | tf_op jit(solution)/shard_map/ppermute | solution.py:876
  43.5 6.4 %collective-permute-start.20 = (f32[2,64,256]{2,1,0:T(8,128)S(1)}, f32[2,64,256]{2,1,0:T(8,128)S(1)}, u32[]{:S(2)}, u32[]{:S(2)}) collective-permute-start(f32[2,64,256]{2,1,0:T(8,128)S(1)} %get-tuple-element.112), channel_id=1, source_target_pairs={{0,8},{4,12},{8,0},{12,4},{1,9},{5,13},{9,1},{13,5},{2,10},{6,14},... | collective-permute-start | bytes 393224 | tf_op jit(solution)/shard_map/ppermute | solution.py:876
  44.2 7.6 %collective-permute-start.21 = (f32[2,64,256]{2,1,0:T(8,128)S(1)}, f32[2,64,256]{2,1,0:T(8,128)S(1)}, u32[]{:S(2)}, u32[]{:S(2)}) collective-permute-start(f32[2,64,256]{2,1,0:T(8,128)S(1)} %get-tuple-element.113), channel_id=1, source_target_pairs={{0,12},{4,8},{8,4},{12,0},{1,13},{5,9},{9,5},{13,1},{2,14},{6,10},... | collective-permute-start | bytes 393224 | tf_op jit(solution)/shard_map/ppermute | solution.py:876
  47.8 3.9 %collective-permute-start.22 = (f32[2,64,256]{2,1,0:T(8,128)S(1)}, f32[2,64,256]{2,1,0:T(8,128)S(1)}, u32[]{:S(2)}, u32[]{:S(2)}) collective-permute-start(f32[2,64,256]{2,1,0:T(8,128)S(1)} %get-tuple-element.115), channel_id=1, source_target_pairs={{0,4},{4,0},{8,12},{12,8},{1,5},{5,1},{9,13},{13,9},{2,6},{6,2},{1... | collective-permute-start | bytes 393224 | tf_op jit(solution)/shard_map/ppermute | solution.py:876
  48.3 7.2 %collective-permute-start.23 = (f32[2,64,256]{2,1,0:T(8,128)S(1)}, f32[2,64,256]{2,1,0:T(8,128)S(1)}, u32[]{:S(2)}, u32[]{:S(2)}) collective-permute-start(f32[2,64,256]{2,1,0:T(8,128)S(1)} %get-tuple-element.116), channel_id=1, source_target_pairs={{0,8},{4,12},{8,0},{12,4},{1,9},{5,13},{9,1},{13,5},{2,10},{6,14},... | collective-permute-start | bytes 393224 | tf_op jit(solution)/shard_map/ppermute | solution.py:876
  48.9 8.5 %collective-permute-start.18 = (f32[2,64,256]{2,1,0:T(8,128)S(1)}, f32[2,64,256]{2,1,0:T(8,128)S(1)}, u32[]{:S(2)}, u32[]{:S(2)}) collective-permute-start(f32[2,64,256]{2,1,0:T(8,128)S(1)} %get-tuple-element.110), channel_id=1, source_target_pairs={{0,12},{4,8},{8,4},{12,0},{1,13},{5,9},{9,5},{13,1},{2,14},{6,10},... | collective-permute-start | bytes 393224 | tf_op jit(solution)/shard_map/ppermute | solution.py:876

commit v8 on v7

--- a/solution.py
+++ b/solution.py
@@ -194,7 +194,7 @@
 
 def local_part(read, slots, coef_row, picks, blocks, out, high, low):
     dofs, elems = out.shape[1], out.shape[2]
-    size = group_size(len(slots))
+    size = next(size for size in (8, 6, 4, 3, 2, 1) if len(slots) % size == 0)
     for first in range(0, len(slots), size):
         group = range(first, first + size)
         values = [read(t) for t in group]

time: 58.3 us -> 58.3 us (level)
  Pallas kernels: 21 us -> 20 us
  waiting for transfers between devices: 12.4 us -> 13.3 us
    pallas_call x16, Pallas kernels: 21 us -> 20 us  [run(): pl.pallas_call(kernel, out_shape=[jax.ShapeDtypeStruct(*o) for o in outs]...]
    ppermute x13, waiting for transfers between devices: 10.4 us -> 11 us  [time_swap(): return value if turn == 0 else lax.ppermute(value, 'tm', pairs)]
  transfers between devices with their start and end apart: 24 -> 24, of which waited for: 8 -> 9; matrix products, arithmetic and copies ran while one was open for 0% -> 0% of each run, Pallas kernels for 29% -> 28%
where the time goes in v8:
time: 58.3 us; the launch traced here: 58.1 us
  starting transfers between devices  24.5 us (42%)
  Pallas kernels  20 us (34%)
  waiting for transfers between devices  13.3 us (23%)
    pallas_call x16, Pallas kernels, run(): pl.pallas_call(kernel, out_shape=[jax.ShapeDtypeStruct(*o) for o in outs]...  20 us
    ppermute x10, starting transfers between devices, neighbour_swap(): return lax.ppermute(value, axes, pairs)  13.6 us
    ppermute x13, waiting for transfers between devices, time_swap(): return value if turn == 0 else lax.ppermute(value, 'tm', pairs)  11 us
    ppermute x13, starting transfers between devices, time_swap(): return value if turn == 0 else lax.ppermute(value, 'tm', pairs)  10.3 us
    ppermute x10, waiting for transfers between devices, neighbour_swap(): return lax.ppermute(value, axes, pairs)  2.24 us
  transfers between devices with their start and end apart: 24, of which 9 were waited for; matrix products, arithmetic and copies ran while one was open for 0% of the time, Pallas kernels for 28%

profile of v8, /device:TPU:0, one launch (start us, length us, event | category | flops | bytes accessed | tf_op | source)
XLA Modules:
  0.0 58.1 jit_solution(536630261435721154)
XLA Ops:
  0.0 2.1 %shard_map.109 = (f32[520,128]{1,0:T(8,128)S(1)}, f32[520,128]{1,0:T(8,128)S(1)}, bf16[512,256]{1,0:T(8,128)(2,1)S(1)}, f32[16,256]{1,0:T(8,128)S(1)}, f32[8,64,...) custom-call(f32[16,64,256]{2,1,0:T(8,128)} %bitcast.11, ...), custom_call_target="tpu_custom_call" | custom-call | flops 1000000000 | bytes 4194304 | tf_op jit(solution)/shard_map/pallas_call | solution.py:843
  2.2 0.5 collective-permute-start.1
  2.7 2.6 %collective-permute-start = (f32[8,64,256]{2,1,0:T(8,128)S(1)}, f32[8,64,256]{2,1,0:T(8,128)S(1)}, u32[]{:S(2)}, u32[]{:S(2)}) collective-permute-start(f32[8,64,256]{2,1,0:T(8,128)S(1)} %get-tuple-element.61.low_fields.own), channel_id=1, source_target_pairs={{0,4},{4,0},{8,12},{12,8},{1,5},{5,1},{9,13},{13,9},{2,6},{6,2},{1... | collective-permute-start | bytes 1572872 | tf_op jit(solution)/shard_map/ppermute | solution.py:876
  5.3 1.6 %collective-permute-start.2 = (f32[520,128]{1,0:T(8,128)S(1)}, f32[520,128]{1,0:T(8,128)S(1)}, u32[]{:S(2)}, u32[]{:S(2)}) collective-permute-start(f32[520,128]{1,0:T(8,128)S(1)} %get-tuple-element.70), channel_id=1, source_target_pairs={{0,1},{1,0},{2,3},{3,2},{4,20},{5,6},{6,5},{7,23},{8,9},{9,8},{10,... | collective-permute-start | bytes 798728 | tf_op jit(solution)/shard_map/ppermute | solution.py:870
  6.8 1.5 %collective-permute-start.3 = (f32[520,128]{1,0:T(8,128)S(1)}, f32[520,128]{1,0:T(8,128)S(1)}, u32[]{:S(2)}, u32[]{:S(2)}) collective-permute-start(f32[520,128]{1,0:T(8,128)S(1)} %get-tuple-element.71), channel_id=1, source_target_pairs={{0,16},{1,2},{2,1},{3,19},{4,5},{5,4},{6,7},{7,6},{8,24},{9,10},{1... | collective-permute-start | bytes 798728 | tf_op jit(solution)/shard_map/ppermute | solution.py:870
  8.4 4.0 %shard_map.110 = (f32[16,64,256]{2,1,0:T(8,128)S(1)}, f32[8,16,256]{2,1,0:T(8,128)S(1)}, bf16[256,1536]{1,0:T(8,128)(2,1)S(1)}, bf16[128,448]{1,0:T(8,128)(2,1)S...) custom-call(f32[8,64,256]{2,1,0:T(8,128)S(1)} %get-tuple-element.61., ...), custom_call_target="tpu_custom_call" | custom-call | flops 4000000000 | bytes 4194304 | tf_op jit(solution)/shard_map/pallas_call | solution.py:843
  12.3 1.9 %collective-permute-done.2.arrived0 = f32[520,128]{1,0:T(8,128)S(1)} collective-permute-done((f32[520,128]{1,0:T(8,128)S(1)}, f32[520,128]{1,0:T(8,128)S(1)}, u32[]{:S(2)}, u32[]{:S(2)}) %collective-permute-start.2) | collective-permute-done | bytes 266272 | tf_op jit(solution)/shard_map/ppermute | solution.py:870
  14.3 0.0 collective-permute-done.3.arrived1
  14.3 0.0 collective-permute-done.1.earlier_high
  14.3 0.0 collective-permute-done.earlier_low.near
  14.3 1.1 %shard_map.111 = (f32[2,64,256]{2,1,0:T(8,128)S(1)}, f32[2,64,256]{2,1,0:T(8,128)S(1)}, f32[2,64,256]{2,1,0:T(8,128)S(1)}, f32[2,64,256]{2,1,0:T(8,128)S(1)}, f3...) custom-call(f32[16,64,256]{2,1,0:T(8,128)S(1)} %bitcast.9, f32[8,64,256]{2,1,0:T(8,128)S(1)} %get-tuple-element.61.low_fields.own, ...), custom_call_target="tpu_custom_call" | custom-call | flops 1000000000 | bytes 4194304 | tf_op jit(solution)/shard_map/pallas_call | solution.py:843
  15.4 0.2 collective-permute-start.7
  15.6 0.1 collective-permute-start.8
  15.6 1.7 %collective-permute-start.9 = (f32[2,64,256]{2,1,0:T(8,128)S(1)}, f32[2,64,256]{2,1,0:T(8,128)S(1)}, u32[]{:S(2)}, u32[]{:S(2)}) collective-permute-start(f32[2,64,256]{2,1,0:T(8,128)S(1)} %get-tuple-element.88), channel_id=1, source_target_pairs={{0,12},{4,8},{8,4},{12,0},{1,13},{5,9},{9,5},{13,1},{2,14},{6,10},... | collective-permute-start | bytes 393224 | tf_op jit(solution)/shard_map/ppermute | solution.py:876
  17.3 0.9 %shard_map.112 = (f32[2,64,256]{2,1,0:T(8,128)S(1)}, f32[2,64,256]{2,1,0:T(8,128)S(1)}, f32[2,64,256]{2,1,0:T(8,128)S(1)}, f32[2,64,256]{2,1,0:T(8,128)S(1)}) custom-call(f32[16,64,256]{2,1,0:T(8,128)S(1)} %bitcast.10, f32[8,64,256]{2,1,0:T(8,128)S(1)} %get-tuple-element.61.low_fields.own, f32[8,64,256]{2,1,0:T(8,128)S(1)} %get-tuple-element.62.high_fields, ...), custom_call_target="tpu_custom_call" | custom-call | flops 1000000000 | bytes 4194304 | tf_op jit(solution)/shard_map/pallas_call | solution.py:843
  18.2 0.4 collective-permute-start.4
  18.6 0.1 collective-permute-start.5
  18.7 0.0 collective-permute-done.7.rest_1_
  18.7 1.4 %collective-permute-start.6 = (f32[2,64,256]{2,1,0:T(8,128)S(1)}, f32[2,64,256]{2,1,0:T(8,128)S(1)}, u32[]{:S(2)}, u32[]{:S(2)}) collective-permute-start(f32[2,64,256]{2,1,0:T(8,128)S(1)} %get-tuple-element.84), channel_id=1, source_target_pairs={{0,12},{4,8},{8,4},{12,0},{1,13},{5,9},{9,5},{13,1},{2,14},{6,10},... | collective-permute-start | bytes 393224 | tf_op jit(solution)/shard_map/ppermute | solution.py:876
  20.1 1.7 %collective-permute-done.8.rest_2_ = f32[2,64,256]{2,1,0:T(8,128)S(1)} collective-permute-done((f32[2,64,256]{2,1,0:T(8,128)S(1)}, f32[2,64,256]{2,1,0:T(8,128)S(1)}, u32[]{:S(2)}, u32[]{:S(2)}) %collective-permute-start.8) | collective-permute-done | bytes 131104 | tf_op jit(solution)/shard_map/ppermute | solution.py:876
  21.9 1.9 %collective-permute-done.9.rest_3_ = f32[2,64,256]{2,1,0:T(8,128)S(1)} collective-permute-done((f32[2,64,256]{2,1,0:T(8,128)S(1)}, f32[2,64,256]{2,1,0:T(8,128)S(1)}, u32[]{:S(2)}, u32[]{:S(2)}) %collective-permute-start.9) | collective-permute-done | bytes 131104 | tf_op jit(solution)/shard_map/ppermute | solution.py:876
  23.7 0.4 shard_map.113
  24.1 1.5 %collective-permute-start.12 = (f32[192,128]{1,0:T(8,128)S(1)}, f32[192,128]{1,0:T(8,128)S(1)}, u32[]{:S(2)}, u32[]{:S(2)}) collective-permute-start(f32[192,128]{1,0:T(8,128)S(1)} %get-tuple-element.101), channel_id=1, source_target_pairs={{0,1},{1,0},{2,3},{3,2},{4,20},{5,6},{6,5},{7,23},{8,9},{9,8},{10,... | collective-permute-start | bytes 294920 | tf_op jit(solution)/shard_map/ppermute | solution.py:870
  25.6 1.5 %collective-permute-start.13 = (f32[192,128]{1,0:T(8,128)S(1)}, f32[192,128]{1,0:T(8,128)S(1)}, u32[]{:S(2)}, u32[]{:S(2)}) collective-permute-start(f32[192,128]{1,0:T(8,128)S(1)} %get-tuple-element.102), channel_id=1, source_target_pairs={{0,16},{1,2},{2,1},{3,19},{4,5},{5,4},{6,7},{7,6},{8,24},{9,10},{1... | collective-permute-start | bytes 294920 | tf_op jit(solution)/shard_map/ppermute | solution.py:870
  27.1 1.6 %shard_map.114 = (f32[8,64,256]{2,1,0:T(8,128)S(1)}, f32[6,2,256]{2,1,0:T(2,128)S(1)}, f32[2,3,128]{2,1,0:T(4,128)S(1)}) custom-call(s32[1,128]{1,0:T(1,128)S(1)} %get-tuple-element.68.flags, f32[8,16,256]{2,1,0:T(8,128)S(1)} %get-tuple-element.77.coefs_in.coefs, bf16[256,1536]{1,0:T(8,128)(2,1)S(1)} %get-tuple-element.78.picks, ...), custom_call_target="tpu_custom_call" | custom-call | flops 1500000000 | bytes 4194304 | tf_op jit(solution)/shard_map/pallas_call | solution.py:843
  28.7 0.0 collective-permute-done.4.rest_1_
  28.7 0.0 collective-permute-done.5.rest_2_
  28.7 0.6 %collective-permute-done.6.rest_3_ = f32[2,64,256]{2,1,0:T(8,128)S(1)} collective-permute-done((f32[2,64,256]{2,1,0:T(8,128)S(1)}, f32[2,64,256]{2,1,0:T(8,128)S(1)}, u32[]{:S(2)}, u32[]{:S(2)}) %collective-permute-start.6) | collective-permute-done | bytes 131104 | tf_op jit(solution)/shard_map/ppermute | solution.py:876
  29.3 0.4 shard_map.115
  29.7 1.5 %collective-permute-start.10 = (f32[192,128]{1,0:T(8,128)S(1)}, f32[192,128]{1,0:T(8,128)S(1)}, u32[]{:S(2)}, u32[]{:S(2)}) collective-permute-start(f32[192,128]{1,0:T(8,128)S(1)} %get-tuple-element.95), channel_id=1, source_target_pairs={{0,1},{1,0},{2,3},{3,2},{4,20},{5,6},{6,5},{7,23},{8,9},{9,8},{10,... | collective-permute-start | bytes 294920 | tf_op jit(solution)/shard_map/ppermute | solution.py:870
  31.2 1.5 %collective-permute-start.11 = (f32[192,128]{1,0:T(8,128)S(1)}, f32[192,128]{1,0:T(8,128)S(1)}, u32[]{:S(2)}, u32[]{:S(2)}) collective-permute-start(f32[192,128]{1,0:T(8,128)S(1)} %get-tuple-element.96), channel_id=1, source_target_pairs={{0,16},{1,2},{2,1},{3,19},{4,5},{5,4},{6,7},{7,6},{8,24},{9,10},{1... | collective-permute-start | bytes 294920 | tf_op jit(solution)/shard_map/ppermute | solution.py:870
  32.7 1.6 %shard_map.116 = (f32[8,64,256]{2,1,0:T(8,128)S(1)}, f32[6,2,256]{2,1,0:T(2,128)S(1)}, f32[2,3,128]{2,1,0:T(4,128)S(1)}) custom-call(s32[1,128]{1,0:T(1,128)S(1)} %get-tuple-element.68.flags, f32[8,16,256]{2,1,0:T(8,128)S(1)} %get-tuple-element.77.coefs_in.coefs, bf16[256,1536]{1,0:T(8,128)(2,1)S(1)} %get-tuple-element.78.picks, ...), custom_call_target="tpu_custom_call" | custom-call | flops 1500000000 | bytes 4194304 | tf_op jit(solution)/shard_map/pallas_call | solution.py:843
  34.3 0.0 collective-permute-done.12.rest_1_
  34.3 0.0 collective-permute-done.13.rest_2_
  34.3 1.0 %shard_map.118 = (f32[8,64,256]{2,1,0:T(8,128)S(1)}, f32[192,128]{1,0:T(8,128)S(1)}, f32[192,128]{1,0:T(8,128)S(1)}) custom-call(s32[1,128]{1,0:T(1,128)S(1)} %get-tuple-element.68.flags, f32[8,16,256]{2,1,0:T(8,128)S(1)} %get-tuple-element.77.coefs_in.coefs, s32[6,256]{1,0:T(8,128)S(1)} %get-tuple-element.64.face_nbr, ...), custom_call_target="tpu_custom_call" | custom-call | flops 1000000000 | bytes 4194304 | tf_op jit(solution)/shard_map/pallas_call | solution.py:843
  35.4 1.9 %collective-permute-start.14 = (f32[192,128]{1,0:T(8,128)S(1)}, f32[192,128]{1,0:T(8,128)S(1)}, u32[]{:S(2)}, u32[]{:S(2)}) collective-permute-start(f32[192,128]{1,0:T(8,128)S(1)} %get-tuple-element.105), channel_id=1, source_target_pairs={{0,1},{1,0},{2,3},{3,2},{4,20},{5,6},{6,5},{7,23},{8,9},{9,8},{10,... | collective-permute-start | bytes 294920 | tf_op jit(solution)/shard_map/ppermute | solution.py:870
  37.2 1.1 %collective-permute-start.15 = (f32[192,128]{1,0:T(8,128)S(1)}, f32[192,128]{1,0:T(8,128)S(1)}, u32[]{:S(2)}, u32[]{:S(2)}) collective-permute-start(f32[192,128]{1,0:T(8,128)S(1)} %get-tuple-element.106), channel_id=1, source_target_pairs={{0,16},{1,2},{2,1},{3,19},{4,5},{5,4},{6,7},{7,6},{8,24},{9,10},{1... | collective-permute-start | bytes 294920 | tf_op jit(solution)/shard_map/ppermute | solution.py:870
  38.3 0.0 collective-permute-done.10.rest_1_
  38.3 0.0 collective-permute-done.11.rest_2_
  38.3 0.9 %shard_map.117 = (f32[8,64,256]{2,1,0:T(8,128)S(1)}, f32[192,128]{1,0:T(8,128)S(1)}, f32[192,128]{1,0:T(8,128)S(1)}) custom-call(s32[1,128]{1,0:T(1,128)S(1)} %get-tuple-element.68.flags, f32[8,16,256]{2,1,0:T(8,128)S(1)} %get-tuple-element.77.coefs_in.coefs, s32[6,256]{1,0:T(8,128)S(1)} %get-tuple-element.64.face_nbr, ...), custom_call_target="tpu_custom_call" | custom-call | flops 1000000000 | bytes 4194304 | tf_op jit(solution)/shard_map/pallas_call | solution.py:843
  39.2 0.5 collective-permute-start.16
  39.6 1.2 %collective-permute-start.17 = (f32[192,128]{1,0:T(8,128)S(1)}, f32[192,128]{1,0:T(8,128)S(1)}, u32[]{:S(2)}, u32[]{:S(2)}) collective-permute-start(f32[192,128]{1,0:T(8,128)S(1)} %get-tuple-element.109), channel_id=1, source_target_pairs={{0,16},{1,2},{2,1},{3,19},{4,5},{5,4},{6,7},{7,6},{8,24},{9,10},{1... | collective-permute-start | bytes 294920 | tf_op jit(solution)/shard_map/ppermute | solution.py:870
  40.8 1.5 %shard_map.119.rest_0_ = f32[8,64,256]{2,1,0:T(8,128)S(1)} custom-call(s32[1,128]{1,0:T(1,128)S(1)} %get-tuple-element.68.flags, f32[8,16,256]{2,1,0:T(8,128)S(1)} %get-tuple-element.77.coefs_in.coefs, bf16[256,1536]{1,0:T(8,128)(2,1)S(1)} %get-tuple-element.78.picks, bf16[128,448]{1,0:T(8,128)(2,1)S(1)} %get-tuple-element.73.blocks, ...), custom_call_target="tpu_custom_call" | custom-call | flops 1500000000 | bytes 4194304 | tf_op jit(solution)/shard_map/pallas_call | solution.py:843
  42.3 0.0 collective-permute-done.14.rest_1_
  42.3 0.3 collective-permute-done.15.rest_2_
  42.6 0.7 %shard_map.120 = (f32[2,64,256]{2,1,0:T(8,128)S(1)}, f32[2,64,256]{2,1,0:T(8,128)S(1)}, f32[2,64,256]{2,1,0:T(8,128)S(1)}, f32[2,64,256]{2,1,0:T(8,128)S(1)}) custom-call(s32[1,128]{1,0:T(1,128)S(1)} %get-tuple-element.68.flags, f32[8,16,256]{2,1,0:T(8,128)S(1)} %get-tuple-element.77.coefs_in.coefs, s32[6,256]{1,0:T(8,128)S(1)} %get-tuple-element.64.face_nbr, ...), custom_call_target="tpu_custom_call" | custom-call | flops 1000000000 | bytes 4194304 | tf_op jit(solution)/shard_map/pallas_call | solution.py:843
  43.3 0.1 collective-permute-start.19
  43.4 0.6 %collective-permute-start.20 = (f32[2,64,256]{2,1,0:T(8,128)S(1)}, f32[2,64,256]{2,1,0:T(8,128)S(1)}, u32[]{:S(2)}, u32[]{:S(2)}) collective-permute-start(f32[2,64,256]{2,1,0:T(8,128)S(1)} %get-tuple-element.112), channel_id=1, source_target_pairs={{0,8},{4,12},{8,0},{12,4},{1,9},{5,13},{9,1},{13,5},{2,10},{6,14},... | collective-permute-start | bytes 393224 | tf_op jit(solution)/shard_map/ppermute | solution.py:876
  44.0 1.3 %collective-permute-start.21 = (f32[2,64,256]{2,1,0:T(8,128)S(1)}, f32[2,64,256]{2,1,0:T(8,128)S(1)}, u32[]{:S(2)}, u32[]{:S(2)}) collective-permute-start(f32[2,64,256]{2,1,0:T(8,128)S(1)} %get-tuple-element.113), channel_id=1, source_target_pairs={{0,12},{4,8},{8,4},{12,0},{1,13},{5,9},{9,5},{13,1},{2,14},{6,10},... | collective-permute-start | bytes 393224 | tf_op jit(solution)/shard_map/ppermute | solution.py:876
  45.3 1.5 %shard_map.121.rest_0_ = f32[8,64,256]{2,1,0:T(8,128)S(1)} custom-call(s32[1,128]{1,0:T(1,128)S(1)} %get-tuple-element.68.flags, f32[8,16,256]{2,1,0:T(8,128)S(1)} %get-tuple-element.77.coefs_in.coefs, bf16[256,1536]{1,0:T(8,128)(2,1)S(1)} %get-tuple-element.78.picks, bf16[128,448]{1,0:T(8,128)(2,1)S(1)} %get-tuple-element.73.blocks, ...), custom_call_target="tpu_custom_call" | custom-call | flops 1500000000 | bytes 4194304 | tf_op jit(solution)/shard_map/pallas_call | solution.py:843
  46.8 0.0 collective-permute-done.16.rest_1_
  46.8 0.0 collective-permute-done.17.rest_2_
  46.8 0.8 %shard_map.122 = (f32[2,64,256]{2,1,0:T(8,128)S(1)}, f32[2,64,256]{2,1,0:T(8,128)S(1)}, f32[2,64,256]{2,1,0:T(8,128)S(1)}, f32[2,64,256]{2,1,0:T(8,128)S(1)}) custom-call(s32[1,128]{1,0:T(1,128)S(1)} %get-tuple-element.68.flags, f32[8,16,256]{2,1,0:T(8,128)S(1)} %get-tuple-element.77.coefs_in.coefs, s32[6,256]{1,0:T(8,128)S(1)} %get-tuple-element.64.face_nbr, ...), custom_call_target="tpu_custom_call" | custom-call | flops 1000000000 | bytes 4194304 | tf_op jit(solution)/shard_map/pallas_call | solution.py:843
  47.5 0.4 collective-permute-start.22
  47.9 0.5 collective-permute-start.23
  48.5 0.0 collective-permute-done.19.rest_1_
  48.5 1.0 %collective-permute-start.18 = (f32[2,64,256]{2,1,0:T(8,128)S(1)}, f32[2,64,256]{2,1,0:T(8,128)S(1)}, u32[]{:S(2)}, u32[]{:S(2)}) collective-permute-start(f32[2,64,256]{2,1,0:T(8,128)S(1)} %get-tuple-element.110), channel_id=1, source_target_pairs={{0,12},{4,8},{8,4},{12,0},{1,13},{5,9},{9,5},{13,1},{2,14},{6,10},... | collective-permute-start | bytes 393224 | tf_op jit(solution)/shard_map/ppermute | solution.py:876
  49.5 0.3 collective-permute-done.20.rest_2_
  49.8 1.9 %collective-permute-done.21.rest_3_ = f32[2,64,256]{2,1,0:T(8,128)S(1)} collective-permute-done((f32[2,64,256]{2,1,0:T(8,128)S(1)}, f32[2,64,256]{2,1,0:T(8,128)S(1)}, u32[]{:S(2)}, u32[]{:S(2)}) %collective-permute-start.21) | collective-permute-done | bytes 131104 | tf_op jit(solution)/shard_map/ppermute | solution.py:876
  51.7 0.0 collective-permute-done.22.rest_5_
  51.7 3.7 %collective-permute-done.23.rest_6_ = f32[2,64,256]{2,1,0:T(8,128)S(1)} collective-permute-done((f32[2,64,256]{2,1,0:T(8,128)S(1)}, f32[2,64,256]{2,1,0:T(8,128)S(1)}, u32[]{:S(2)}, u32[]{:S(2)}) %collective-permute-start.23) | collective-permute-done | bytes 131104 | tf_op jit(solution)/shard_map/ppermute | solution.py:876
  55.4 1.0 %shard_map.123.rest_1_ = f32[16,64,256]{2,1,0:T(8,128)} custom-call(f32[2,64,256]{2,1,0:T(8,128)S(1)} %get-tuple-element.107.rest_2_.rest_0_, f32[2,64,256]{2,1,0:T(8,128)S(1)} %collective-permute-done.19.rest_1_, f32[2,64,256]{2,1,0:T(8,128)S(1)} %collective-permute-done.20.rest_2_, f32[2,64,256]{2,1,0:T(8,128)S(1)} %collective-permute-done.21.rest_3_, ...), custom_call_target="tpu_custom_call" | custom-call | flops 1000000000 | bytes 4194304 | tf_op jit(solution)/shard_map/pallas_call | solution.py:843
  56.4 0.9 %collective-permute-done.18.rest_0_ = f32[2,64,256]{2,1,0:T(8,128)S(1)} collective-permute-done((f32[2,64,256]{2,1,0:T(8,128)S(1)}, f32[2,64,256]{2,1,0:T(8,128)S(1)}, u32[]{:S(2)}, u32[]{:S(2)}) %collective-permute-start.18) | collective-permute-done | bytes 131104 | tf_op jit(solution)/shard_map/ppermute | solution.py:876
  57.3 0.7 %shard_map.124 = f32[16,64,256]{2,1,0:T(8,128)} custom-call(f32[2,64,256]{2,1,0:T(8,128)S(1)} %collective-permute-done.18.rest_0_, f32[16,64,256]{2,1,0:T(8,128)} %shard_map.123.rest_1_), custom_call_target="tpu_custom_call", output_to_operand_aliasing={{}: (1, {})} | custom-call | flops 1000000000 | bytes 4194304 | tf_op jit(solution)/shard_map/pallas_call | solution.py:843
  (2 shorter events, 0.0 us)
Async XLA Ops:
  2.2 12.1 %collective-permute-start.1 = (f32[8,64,256]{2,1,0:T(8,128)S(1)}, f32[8,64,256]{2,1,0:T(8,128)S(1)}, u32[]{:S(2)}, u32[]{:S(2)}) collective-permute-start(f32[8,64,256]{2,1,0:T(8,128)S(1)} %get-tuple-element.62.high_fields), channel_id=1, source_target_pairs={{0,4},{4,8},{8,12},{12,0},{1,5},{5,9},{9,13},{13,1},{2,6},{6,10},{... | collective-permute-start | bytes 1572872 | tf_op jit(solution)/shard_map/ppermute | solution.py:946
  2.7 11.6 %collective-permute-start = (f32[8,64,256]{2,1,0:T(8,128)S(1)}, f32[8,64,256]{2,1,0:T(8,128)S(1)}, u32[]{:S(2)}, u32[]{:S(2)}) collective-permute-start(f32[8,64,256]{2,1,0:T(8,128)S(1)} %get-tuple-element.61.low_fields.own), channel_id=1, source_target_pairs={{0,4},{4,0},{8,12},{12,8},{1,5},{5,1},{9,13},{13,9},{2,6},{6,2},{1... | collective-permute-start | bytes 1572872 | tf_op jit(solution)/shard_map/ppermute | solution.py:876
  5.3 9.0 %collective-permute-start.2 = (f32[520,128]{1,0:T(8,128)S(1)}, f32[520,128]{1,0:T(8,128)S(1)}, u32[]{:S(2)}, u32[]{:S(2)}) collective-permute-start(f32[520,128]{1,0:T(8,128)S(1)} %get-tuple-element.70), channel_id=1, source_target_pairs={{0,1},{1,0},{2,3},{3,2},{4,20},{5,6},{6,5},{7,23},{8,9},{9,8},{10,... | collective-permute-start | bytes 798728 | tf_op jit(solution)/shard_map/ppermute | solution.py:870
  6.8 7.4 %collective-permute-start.3 = (f32[520,128]{1,0:T(8,128)S(1)}, f32[520,128]{1,0:T(8,128)S(1)}, u32[]{:S(2)}, u32[]{:S(2)}) collective-permute-start(f32[520,128]{1,0:T(8,128)S(1)} %get-tuple-element.71), channel_id=1, source_target_pairs={{0,16},{1,2},{2,1},{3,19},{4,5},{5,4},{6,7},{7,6},{8,24},{9,10},{1... | collective-permute-start | bytes 798728 | tf_op jit(solution)/shard_map/ppermute | solution.py:870
  8.4 5.9 %copy-start = (f32[16,1,64,256]{3,2,1,0:T(8,128)S(1)}, f32[16,1,64,256]{3,2,1,0:T(8,128)}, u32[]{:S(2)}) copy-start(f32[16,1,64,256]{3,2,1,0:T(8,128)} %param.11) | copy-start | bytes 3145732
  15.4 3.4 %collective-permute-start.7 = (f32[2,64,256]{2,1,0:T(8,128)S(1)}, f32[2,64,256]{2,1,0:T(8,128)S(1)}, u32[]{:S(2)}, u32[]{:S(2)}) collective-permute-start(f32[2,64,256]{2,1,0:T(8,128)S(1)} %get-tuple-element.86), channel_id=1, source_target_pairs={{0,4},{4,0},{8,12},{12,8},{1,5},{5,1},{9,13},{13,9},{2,6},{6,2},{1... | collective-permute-start | bytes 393224 | tf_op jit(solution)/shard_map/ppermute | solution.py:876
  15.6 6.3 %collective-permute-start.8 = (f32[2,64,256]{2,1,0:T(8,128)S(1)}, f32[2,64,256]{2,1,0:T(8,128)S(1)}, u32[]{:S(2)}, u32[]{:S(2)}) collective-permute-start(f32[2,64,256]{2,1,0:T(8,128)S(1)} %get-tuple-element.87), channel_id=1, source_target_pairs={{0,8},{4,12},{8,0},{12,4},{1,9},{5,13},{9,1},{13,5},{2,10},{6,14},... | collective-permute-start | bytes 393224 | tf_op jit(solution)/shard_map/ppermute | solution.py:876
  15.6 8.1 %collective-permute-start.9 = (f32[2,64,256]{2,1,0:T(8,128)S(1)}, f32[2,64,256]{2,1,0:T(8,128)S(1)}, u32[]{:S(2)}, u32[]{:S(2)}) collective-permute-start(f32[2,64,256]{2,1,0:T(8,128)S(1)} %get-tuple-element.88), channel_id=1, source_target_pairs={{0,12},{4,8},{8,4},{12,0},{1,13},{5,9},{9,5},{13,1},{2,14},{6,10},... | collective-permute-start | bytes 393224 | tf_op jit(solution)/shard_map/ppermute | solution.py:876
  18.2 10.5 %collective-permute-start.4 = (f32[2,64,256]{2,1,0:T(8,128)S(1)}, f32[2,64,256]{2,1,0:T(8,128)S(1)}, u32[]{:S(2)}, u32[]{:S(2)}) collective-permute-start(f32[2,64,256]{2,1,0:T(8,128)S(1)} %get-tuple-element.82), channel_id=1, source_target_pairs={{0,4},{4,0},{8,12},{12,8},{1,5},{5,1},{9,13},{13,9},{2,6},{6,2},{1... | collective-permute-start | bytes 393224 | tf_op jit(solution)/shard_map/ppermute | solution.py:876
  18.6 10.1 %collective-permute-start.5 = (f32[2,64,256]{2,1,0:T(8,128)S(1)}, f32[2,64,256]{2,1,0:T(8,128)S(1)}, u32[]{:S(2)}, u32[]{:S(2)}) collective-permute-start(f32[2,64,256]{2,1,0:T(8,128)S(1)} %get-tuple-element.83), channel_id=1, source_target_pairs={{0,8},{4,12},{8,0},{12,4},{1,9},{5,13},{9,1},{13,5},{2,10},{6,14},... | collective-permute-start | bytes 393224 | tf_op jit(solution)/shard_map/ppermute | solution.py:876
  18.7 10.6 %collective-permute-start.6 = (f32[2,64,256]{2,1,0:T(8,128)S(1)}, f32[2,64,256]{2,1,0:T(8,128)S(1)}, u32[]{:S(2)}, u32[]{:S(2)}) collective-permute-start(f32[2,64,256]{2,1,0:T(8,128)S(1)} %get-tuple-element.84), channel_id=1, source_target_pairs={{0,12},{4,8},{8,4},{12,0},{1,13},{5,9},{9,5},{13,1},{2,14},{6,10},... | collective-permute-start | bytes 393224 | tf_op jit(solution)/shard_map/ppermute | solution.py:876
  24.1 10.2 %collective-permute-start.12 = (f32[192,128]{1,0:T(8,128)S(1)}, f32[192,128]{1,0:T(8,128)S(1)}, u32[]{:S(2)}, u32[]{:S(2)}) collective-permute-start(f32[192,128]{1,0:T(8,128)S(1)} %get-tuple-element.101), channel_id=1, source_target_pairs={{0,1},{1,0},{2,3},{3,2},{4,20},{5,6},{6,5},{7,23},{8,9},{9,8},{10,... | collective-permute-start | bytes 294920 | tf_op jit(solution)/shard_map/ppermute | solution.py:870
  25.6 8.7 %collective-permute-start.13 = (f32[192,128]{1,0:T(8,128)S(1)}, f32[192,128]{1,0:T(8,128)S(1)}, u32[]{:S(2)}, u32[]{:S(2)}) collective-permute-start(f32[192,128]{1,0:T(8,128)S(1)} %get-tuple-element.102), channel_id=1, source_target_pairs={{0,16},{1,2},{2,1},{3,19},{4,5},{5,4},{6,7},{7,6},{8,24},{9,10},{1... | collective-permute-start | bytes 294920 | tf_op jit(solution)/shard_map/ppermute | solution.py:870
  29.7 8.6 %collective-permute-start.10 = (f32[192,128]{1,0:T(8,128)S(1)}, f32[192,128]{1,0:T(8,128)S(1)}, u32[]{:S(2)}, u32[]{:S(2)}) collective-permute-start(f32[192,128]{1,0:T(8,128)S(1)} %get-tuple-element.95), channel_id=1, source_target_pairs={{0,1},{1,0},{2,3},{3,2},{4,20},{5,6},{6,5},{7,23},{8,9},{9,8},{10,... | collective-permute-start | bytes 294920 | tf_op jit(solution)/shard_map/ppermute | solution.py:870
  31.2 7.1 %collective-permute-start.11 = (f32[192,128]{1,0:T(8,128)S(1)}, f32[192,128]{1,0:T(8,128)S(1)}, u32[]{:S(2)}, u32[]{:S(2)}) collective-permute-start(f32[192,128]{1,0:T(8,128)S(1)} %get-tuple-element.96), channel_id=1, source_target_pairs={{0,16},{1,2},{2,1},{3,19},{4,5},{5,4},{6,7},{7,6},{8,24},{9,10},{1... | collective-permute-start | bytes 294920 | tf_op jit(solution)/shard_map/ppermute | solution.py:870
  35.4 6.9 %collective-permute-start.14 = (f32[192,128]{1,0:T(8,128)S(1)}, f32[192,128]{1,0:T(8,128)S(1)}, u32[]{:S(2)}, u32[]{:S(2)}) collective-permute-start(f32[192,128]{1,0:T(8,128)S(1)} %get-tuple-element.105), channel_id=1, source_target_pairs={{0,1},{1,0},{2,3},{3,2},{4,20},{5,6},{6,5},{7,23},{8,9},{9,8},{10,... | collective-permute-start | bytes 294920 | tf_op jit(solution)/shard_map/ppermute | solution.py:870
  37.2 5.4 %collective-permute-start.15 = (f32[192,128]{1,0:T(8,128)S(1)}, f32[192,128]{1,0:T(8,128)S(1)}, u32[]{:S(2)}, u32[]{:S(2)}) collective-permute-start(f32[192,128]{1,0:T(8,128)S(1)} %get-tuple-element.106), channel_id=1, source_target_pairs={{0,16},{1,2},{2,1},{3,19},{4,5},{5,4},{6,7},{7,6},{8,24},{9,10},{1... | collective-permute-start | bytes 294920 | tf_op jit(solution)/shard_map/ppermute | solution.py:870
  39.2 7.6 %collective-permute-start.16 = (f32[192,128]{1,0:T(8,128)S(1)}, f32[192,128]{1,0:T(8,128)S(1)}, u32[]{:S(2)}, u32[]{:S(2)}) collective-permute-start(f32[192,128]{1,0:T(8,128)S(1)} %get-tuple-element.108), channel_id=1, source_target_pairs={{0,1},{1,0},{2,3},{3,2},{4,20},{5,6},{6,5},{7,23},{8,9},{9,8},{10,... | collective-permute-start | bytes 294920 | tf_op jit(solution)/shard_map/ppermute | solution.py:870
  39.6 7.1 %collective-permute-start.17 = (f32[192,128]{1,0:T(8,128)S(1)}, f32[192,128]{1,0:T(8,128)S(1)}, u32[]{:S(2)}, u32[]{:S(2)}) collective-permute-start(f32[192,128]{1,0:T(8,128)S(1)} %get-tuple-element.109), channel_id=1, source_target_pairs={{0,16},{1,2},{2,1},{3,19},{4,5},{5,4},{6,7},{7,6},{8,24},{9,10},{1... | collective-permute-start | bytes 294920 | tf_op jit(solution)/shard_map/ppermute | solution.py:870
  43.3 5.1 %collective-permute-start.19 = (f32[2,64,256]{2,1,0:T(8,128)S(1)}, f32[2,64,256]{2,1,0:T(8,128)S(1)}, u32[]{:S(2)}, u32[]{:S(2)}) collective-permute-start(f32[2,64,256]{2,1,0:T(8,128)S(1)} %get-tuple-element.111), channel_id=1, source_target_pairs={{0,4},{4,0},{8,12},{12,8},{1,5},{5,1},{9,13},{13,9},{2,6},{6,2},{1... | collective-permute-start | bytes 393224 | tf_op jit(solution)/shard_map/ppermute | solution.py:876
  43.4 6.4 %collective-permute-start.20 = (f32[2,64,256]{2,1,0:T(8,128)S(1)}, f32[2,64,256]{2,1,0:T(8,128)S(1)}, u32[]{:S(2)}, u32[]{:S(2)}) collective-permute-start(f32[2,64,256]{2,1,0:T(8,128)S(1)} %get-tuple-element.112), channel_id=1, source_target_pairs={{0,8},{4,12},{8,0},{12,4},{1,9},{5,13},{9,1},{13,5},{2,10},{6,14},... | collective-permute-start | bytes 393224 | tf_op jit(solution)/shard_map/ppermute | solution.py:876
  44.0 7.7 %collective-permute-start.21 = (f32[2,64,256]{2,1,0:T(8,128)S(1)}, f32[2,64,256]{2,1,0:T(8,128)S(1)}, u32[]{:S(2)}, u32[]{:S(2)}) collective-permute-start(f32[2,64,256]{2,1,0:T(8,128)S(1)} %get-tuple-element.113), channel_id=1, source_target_pairs={{0,12},{4,8},{8,4},{12,0},{1,13},{5,9},{9,5},{13,1},{2,14},{6,10},... | collective-permute-start | bytes 393224 | tf_op jit(solution)/shard_map/ppermute | solution.py:876
  47.5 4.2 %collective-permute-start.22 = (f32[2,64,256]{2,1,0:T(8,128)S(1)}, f32[2,64,256]{2,1,0:T(8,128)S(1)}, u32[]{:S(2)}, u32[]{:S(2)}) collective-permute-start(f32[2,64,256]{2,1,0:T(8,128)S(1)} %get-tuple-element.115), channel_id=1, source_target_pairs={{0,4},{4,0},{8,12},{12,8},{1,5},{5,1},{9,13},{13,9},{2,6},{6,2},{1... | collective-permute-start | bytes 393224 | tf_op jit(solution)/shard_map/ppermute | solution.py:876
  47.9 7.5 %collective-permute-start.23 = (f32[2,64,256]{2,1,0:T(8,128)S(1)}, f32[2,64,256]{2,1,0:T(8,128)S(1)}, u32[]{:S(2)}, u32[]{:S(2)}) collective-permute-start(f32[2,64,256]{2,1,0:T(8,128)S(1)} %get-tuple-element.116), channel_id=1, source_target_pairs={{0,8},{4,12},{8,0},{12,4},{1,9},{5,13},{9,1},{13,5},{2,10},{6,14},... | collective-permute-start | bytes 393224 | tf_op jit(solution)/shard_map/ppermute | solution.py:876
  48.5 8.8 %collective-permute-start.18 = (f32[2,64,256]{2,1,0:T(8,128)S(1)}, f32[2,64,256]{2,1,0:T(8,128)S(1)}, u32[]{:S(2)}, u32[]{:S(2)}) collective-permute-start(f32[2,64,256]{2,1,0:T(8,128)S(1)} %get-tuple-element.110), channel_id=1, source_target_pairs={{0,12},{4,8},{8,4},{12,0},{1,13},{5,9},{9,5},{13,1},{2,14},{6,10},... | collective-permute-start | bytes 393224 | tf_op jit(solution)/shard_map/ppermute | solution.py:876
